TPU v7x, 32 devices: a whole 2x2x4 slice. The times are simulated.
32 devices in a mesh: groups: 2 (over y), seq: 4 (over z), head: 4 (over x, core).
Axes of the slice: x: 2, y: 2, z: 4, core: 2. Of those that a mesh axis runs over, the one named last changes fastest.
Arguments:
- query_latent_rows: bfloat16 [640, 1536], P(('groups', 'seq')), parts along dimension 0, may hold values from -6 to 6
- key_value_latents: bfloat16 [640, 576], P(('groups', 'seq')), parts along dimension 0, may hold values from -500 to 500
- positions: int32 [640], P(('groups', 'seq')), parts along dimension 0, may hold values from 130752 to 131071, as said below
- query_up_weight: bfloat16 [1536, 12288], P('seq', 'head'), may hold values from -0.15625 to 0.15625
- adapter_down_factor: bfloat16 [3072, 64], P(('groups', 'seq')), parts along dimension 0, may hold values from -0.75 to 0.75
- adapter_up_factor: bfloat16 [128, 12288], P('groups', 'head'), parts along dimension 0, may hold values from -0.15625 to 0.15625
- head_key_up_weight: bfloat16 [64, 128, 512], P('head'), may hold values from -0.5 to 0.5
- head_value_up_weight: bfloat16 [64, 512, 128], P('head'), may hold values from -0.25 to 0.25
- output_projection_weight: bfloat16 [8192, 7168], P('head', 'seq'), may hold values from -0.0625 to 0.0625
Outputs:
- merged_weight: bfloat16 [3072, 12288], P(('groups', 'seq'), 'head'), parts along dimension 0
- mixed: bfloat16 [640, 7168], P(('groups', 'head'), 'seq'), parts along dimension 0
There are 2 independent parts, one for each index of `groups`. A program takes and returns all parts, laid end to end along the dimension named above; an argument that names none is the same for every part. Nothing has to cross between parts.
Inputs may be any that keep to these rules, and one draw needn't show every extreme that they name: positions are distinct; each aligned block of 80 rows holds 80 consecutive positions in rising order, and the blocks together cover the last 320 positions of the prompt in an order drawn from the seed.
All inputs are finite; a program needn't handle non-finite values.
Results may differ from a plain program's by a relative error of at most 0.015.
The roundings to bfloat16 on the way count: a program that leaves them out, or rounds other values in their place, can miss the bound.
Values may be sent and summed in bfloat16 or wider, within the bound.
No kernel may reach another device: no remote copies, remote signals or barrier semaphores. Data moves between devices by JAX's collectives and lax.ppermute only.
A program may use at most 64 MiB of HBM per device.

v0:
```python
import math

import jax
import jax.numpy as jnp
from jax import lax
from jax.sharding import PartitionSpec as P


def on_device(
    query_latent_rows,
    key_value_latents,
    positions,
    query_up_weight,
    adapter_down_factor,
    adapter_up_factor,
    head_key_up_weight,
    head_value_up_weight,
    output_projection_weight,
):
    merged_query_weight = (
        query_up_weight.astype(jnp.float32)
        + jnp.dot(adapter_down_factor, adapter_up_factor, preferred_element_type=jnp.float32)
    ).astype(jnp.bfloat16)
    tok_rows = query_latent_rows.shape[0]
    queries = jnp.dot(
        query_latent_rows,
        lax.all_gather(merged_query_weight, "seq", axis=0, tiled=True),
        preferred_element_type=jnp.float32,
    )
    heads_dev = head_key_up_weight.shape[0]
    nope_dim = head_key_up_weight.shape[1]
    kv_rank = head_key_up_weight.shape[2]
    lat_width = key_value_latents.shape[1]
    score_scale = 1.0 / math.sqrt(nope_dim + lat_width - kv_rank)
    queries = queries.astype(jnp.bfloat16).reshape(tok_rows, heads_dev, -1)
    absorbed = jnp.einsum(
        "thn,hnk->thk",
        queries[:, :, :nope_dim],
        head_key_up_weight,
        preferred_element_type=jnp.float32,
    ).astype(jnp.bfloat16)
    full_query = jnp.concatenate([absorbed, queries[:, :, nope_dim:]], axis=2).reshape(
        tok_rows * heads_dev, lat_width
    )
    query_pos = jnp.repeat(positions, heads_dev)
    q_count = tok_rows * heads_dev
    row_max = jnp.full((q_count,), -1e30, jnp.float32)
    key_rows = lax.all_gather(key_value_latents, "seq", axis=0, tiled=True)
    key_pos = lax.all_gather(positions, "seq", axis=0, tiled=True)
    visible = key_pos[None, :] <= query_pos[:, None]
    scores = (
        lax.dot_general(
            full_query, key_rows, (((1,), (1,)), ((), ())), preferred_element_type=jnp.float32
        )
        * score_scale
    )
    scores = jnp.where(visible, scores, jnp.float32(-1e30))
    new_max = jnp.maximum(row_max, jnp.max(scores, axis=1))
    weights = jnp.where(visible, jnp.exp(scores - new_max[:, None]), jnp.float32(0.0))
    row_sum = jnp.sum(weights, axis=1)
    running = jnp.dot(
        weights.astype(jnp.bfloat16), key_rows[:, :kv_rank], preferred_element_type=jnp.float32
    )
    row_max, row_sum, running = (new_max, row_sum, running)
    context_output = (
        (running / row_sum[:, None]).astype(jnp.bfloat16).reshape(tok_rows, heads_dev, kv_rank)
    )
    heads_out = (
        jnp.einsum(
            "euw,uwz->euz", context_output, head_value_up_weight, preferred_element_type=jnp.float32
        )
        .astype(jnp.bfloat16)
        .reshape(tok_rows, -1)
    )
    partial_value = jnp.dot(
        lax.all_gather(heads_out, "seq", axis=0, tiled=True),
        output_projection_weight,
        preferred_element_type=jnp.float32,
    )
    mixed = lax.psum_scatter(
        partial_value.astype(jnp.bfloat16), "head", scatter_dimension=0, tiled=True
    )
    return (merged_query_weight, mixed)


def solution(mesh):
    placed = (
        P(("groups", "seq"), None),
        P(("groups", "seq"), None),
        P(("groups", "seq")),
        P("seq", "head"),
        P(("groups", "seq"), None),
        P("groups", "head"),
        P("head", None, None),
        P("head", None, None),
        P("head", "seq"),
    )
    return jax.shard_map(
        on_device,
        mesh=mesh,
        in_specs=placed,
        out_specs=(P(("groups", "seq"), "head"), P(("groups", "head"), "seq")),
        check_vma=False,
    )
```

profile of v0, /device:TPU:0, one launch (start us, length us, event | category | flops | bytes accessed | tf_op | source)
XLA Modules:
  0.0 269.1 jit_solution(17031424686050613375)
XLA Ops:
  7.2 0.0 all-gather.3.cloned.1.call-start
  7.2 4.1 %add_convert_fusion = bf16[384,3072]{1,0:T(8,128)(2,1)} fusion(bf16[384,3072]{1,0:T(8,128)(2,1)} %param.12, bf16[384,64]{0,1:T(8,128)(2,1)} %param.13, bf16[64,3072]{1,0:T(8,128)(2,1)} %param.14), kind=kOutput, calls=%fused_computation | convolution fusion | flops 154533888 | bytes 5160960 | tf_op jit(solution)/shard_map/dot_general | solution.py:22
  11.4 0.0 all-gather.3.cloned.1.call-update
  11.4 0.0 all-gather.5.cloned.1.call-start
  11.5 0.6 copy-done.5
  12.0 0.1 broadcast_in_dim.16
  12.1 0.1 le.16
  12.2 0.6 dynamic-slice
  13.4 0.2 dynamic-update-slice
  13.7 9.9 %all-reduce = s32[320]{0:T(512)S(1)} all-reduce(s32[320]{0:T(512)S(1)} %dynamic-update-slice), channel_id=1, replica_groups=mesh['groups'=2,'seq'=4,'head'=4] {'seq'}, use_global_device_ids=true, to_apply=%add | all-reduce | flops 320 | bytes 2560
  23.6 24.7 %all_gather.14 = bf16[320,576]{1,0:T(8,128)(2,1)} all-gather(bf16[80,576]{1,0:T(8,128)(2,1)S(1)} %copy-done.4), channel_id=1, replica_groups=mesh['groups'=2,'seq'=4,'head'=4] {'seq'}, dimensions={0}, use_global_device_ids=true | all-gather | bytes 460800 | tf_op jit(solution)/shard_map/all_gather | solution.py:48
  48.3 138.0 %all-gather.3.cloned.1.call-done = bf16[1536,3072]{1,0:T(8,128)(2,1)} async-done(((bf16[384,3072]{1,0:T(8,128)(2,1)}), bf16[1536,3072]{1,0:T(8,128)(2,1)}) %all-gather.3.cloned.1.call-update) | async-done | bytes 9437200 | tf_op jit(solution)/shard_map/all_gather | solution.py:27
  186.3 5.4 %fusion = bf16[80,3072]{1,0:T(8,128)(2,1)S(1)} fusion(bf16[80,1536]{1,0:T(8,128)(2,1)S(1)} %copy-done.2, bf16[1536,3072]{1,0:T(8,128)(2,1)} %all-gather.3.cloned.1.call-done), kind=kOutput, calls=%fused_computation.2 | convolution fusion | flops 755220480 | bytes 10174464 | tf_op jit(solution)/shard_map/dot_general | solution.py:25
  191.8 0.7 reshape.22
  192.5 0.1 slice.12
  192.6 0.1 slice.13
  192.6 0.1 copy.20
  192.7 0.5 fusion.3
  193.2 0.1 pad_maximum_fusion
  193.4 0.3 copy.16
  193.7 0.7 copy-done.3
  194.4 0.9 fusion.22
  195.2 0.3 fusion.6
  195.6 1.0 fusion.1
  196.6 0.6 copy-done.1
  197.2 1.6 fusion.11
  198.8 0.8 copy.31
  199.6 0.0 all-gather.5.cloned.1.call-update
  199.6 0.0 reduce-scatter.2.cloned.1.call-start
  199.7 31.2 %all-gather.5.cloned.1.call-done = bf16[320,2048]{1,0:T(8,128)(2,1)} async-done(((bf16[80,2048]{1,0:T(8,128)(2,1)}), bf16[320,2048]{1,0:T(8,128)(2,1)}) %all-gather.5.cloned.1.call-update) | async-done | bytes 1310736 | tf_op jit(solution)/shard_map/all_gather | solution.py:76
  230.9 7.0 %convolution_convert_fusion.1 = bf16[320,1792]{1,0:T(8,128)(2,1)} fusion(bf16[320,2048]{1,0:T(8,128)(2,1)} %all-gather.5.cloned.1.call-done, bf16[2048,1792]{1,0:T(8,128)(2,1)} %param.17), kind=kOutput, calls=%fused_computation.7 | convolution fusion | flops 2349383680 | bytes 9797632 | tf_op jit(solution)/shard_map/dot_general | solution.py:75
  237.9 24.6 %reduce-scatter.2.cloned.1.call-done = bf16[80,1792]{1,0:T(8,128)(2,1)} async-done(((bf16[320,1792]{1,0:T(8,128)(2,1)}), bf16[80,1792]{1,0:T(8,128)(2,1)}) %reduce-scatter.2.cloned.1.call-update) | async-done | bytes 286736 | tf_op jit(solution)/shard_map/reduce_scatter | solution.py:80
  (14 shorter events, 0.1 us)
Async XLA Ops:
  7.2 185.5 %copy-start = (bf16[16,128,512]{2,1,0:T(8,128)(2,1)S(1)}, bf16[16,128,512]{2,1,0:T(8,128)(2,1)}, u32[]{:S(2)}) copy-start(bf16[16,128,512]{2,1,0:T(8,128)(2,1)} %param.15) | copy-start | bytes 6291460
  7.2 179.1 %all-gather.3.cloned.1.call-start = ((), (), s32[]{:S(2)}) async-start(), calls=%async_computation.1 | async-start | bytes 11796480 | tf_op jit(solution)/shard_map/all_gather | solution.py:27
  11.4 0.7 copy-start.5
  11.4 0.8 copy-start.6
  11.4 12.2 %copy-start.4 = (bf16[80,576]{1,0:T(8,128)(2,1)S(1)}, bf16[80,576]{1,0:T(8,128)(2,1)}, u32[]{:S(2)}) copy-start(bf16[80,576]{1,0:T(8,128)(2,1)} %param.10) | copy-start | bytes 276484
  11.4 174.9 %copy-start.2 = (bf16[80,1536]{1,0:T(8,128)(2,1)S(1)}, bf16[80,1536]{1,0:T(8,128)(2,1)}, u32[]{:S(2)}) copy-start(bf16[80,1536]{1,0:T(8,128)(2,1)} %param.9) | copy-start | bytes 737284
  11.4 219.5 %all-gather.5.cloned.1.call-start = ((), (), s32[]{:S(2)}) async-start(), calls=%async_computation.2 | async-start | bytes 1638400 | tf_op jit(solution)/shard_map/all_gather | solution.py:76
  193.4 1.0 copy-start.3
  195.6 1.6 copy-start.1
  199.6 63.0 %reduce-scatter.2.cloned.1.call-start = ((), (), s32[]{:S(2)}) async-start(), calls=%async_computation.3 | async-start | bytes 1433600 | tf_op jit(solution)/shard_map/reduce_scatter | solution.py:80
Sparse Core Ops, SparseCore 0:
  11.5 174.7 all-gather.2
  199.8 31.0 all-gather.4
  238.1 24.4 reduce-scatter.1
where the time goes:
time: 269 us
  waiting for transfers between devices  194 us (72%)
  blocking collectives  34.6 us (13%)
  matrix products  20.6 us (8%)
  between operations  14.5 us (5%)
  local copies, waits for them, and re-layouts  4.86 us (2%)
    all_gather x1, waiting for transfers between devices, on_device(): lax.all_gather(merged_query_weight, 'seq', axis=0, tiled=True)  138 us
    all_gather x1, waiting for transfers between devices, on_device(): lax.all_gather(heads_out, 'seq', axis=0, tiled=True)  31.2 us
    all_gather x1, blocking collectives, on_device(): key_rows = lax.all_gather(key_value_latents, 'seq', axis=0, tiled=True)  24.7 us
    reduce_scatter x1, waiting for transfers between devices, on_device(): lax.psum_scatter(partial_value.astype(jnp.bfloat16), 'head', scatter_dime...  24.6 us
    unnamed x1, blocking collectives  9.89 us
    dot_general x1, matrix products, on_device(): jnp.dot(lax.all_gather(heads_out, 'seq', axis=0, tiled=True), output_proj...  7.03 us
    dot_general x1, matrix products, on_device(): jnp.dot(query_latent_rows, lax.all_gather(merged_query_weight, 'seq', axi...  5.43 us
  transfers between devices with their start and end apart: 3, of which 3 were waited for; matrix products, arithmetic and copies ran while one was open for 0% of the time, Pallas kernels for 0%

commit v1 on v0

--- a/solution.py
+++ b/solution.py
@@ -1,9 +1,15 @@
+import functools
 import math
 
 import jax
 import jax.numpy as jnp
 from jax import lax
+from jax.experimental import pallas as pl
+from jax.experimental.pallas import tpu as pltpu
 from jax.sharding import PartitionSpec as P
+
+CHUNKS = 2
+VMEM_BYTES = 50 * 1024 * 1024
 
 
 def on_device(
@@ -83,6 +89,274 @@
     return (merged_query_weight, mixed)
 
 
+def cyclic(n, k):
+    return [(i, (i + k) % n) for i in range(n)]
+
+
+def flipped(n, bit):
+    return [(i, i ^ bit) for i in range(n)]
+
+
+def call(body, outs, blocks, scalars, args, scratch=(), flops=0, moved=0):
+    def whole(shape):
+        return pl.BlockSpec(tuple(shape), lambda i, sc: (0,) * len(shape))
+
+    return pl.pallas_call(
+        body,
+        out_shape=outs,
+        grid_spec=pltpu.PrefetchScalarGridSpec(
+            num_scalar_prefetch=1,
+            grid=(1,),
+            in_specs=[whole(a.shape) if b is None else b for a, b in zip(args, blocks)],
+            out_specs=jax.tree.map(lambda o: whole(o.shape), outs),
+            scratch_shapes=list(scratch),
+        ),
+        compiler_params=pltpu.CompilerParams(vmem_limit_bytes=VMEM_BYTES),
+        cost_estimate=pl.CostEstimate(flops=flops, bytes_accessed=moved, transcendentals=0),
+    )(scalars, *args)
+
+
+def unpack_body(n, nh, tok, kq, vq, aq, sc, x_ref, kv_ref, a_ref, *rest):
+    stacks, (xo, kvo, ao) = rest[:nh], rest[nh:]
+    s, h = sc[0], sc[2]
+    kvr = vq * nh
+    depth = a_ref.shape[0]
+    row = pl.multiple_of(s * tok, 16)
+    xo[pl.ds(row, tok), :] = x_ref[...]
+    kvo[pl.ds(row, tok), :] = kv_ref[...]
+    ao[pl.ds(pl.multiple_of(s * depth, 16), depth), :] = a_ref[...]
+    third = aq // 3
+    unit = tok + third
+    rope = kvo.shape[1] - kvr
+    rank = ao.shape[1]
+    for j in range(nh):
+        hh = h ^ j
+        ref = stacks[j]
+        for k in range(1, n):
+            src = lax.rem(s - k + n, n)
+            row = pl.multiple_of(src * tok, 16)
+            base = (k - 1) * unit
+            xo[pl.ds(row, tok), pl.ds(pl.multiple_of(hh * kq, 128), kq)] = ref[base : base + tok, :kq]
+            kvo[pl.ds(row, tok), pl.ds(pl.multiple_of(hh * vq, 128), vq)] = ref[base : base + tok, kq : kq + vq]
+            for i in range(3):
+                piece = ref[base + tok : base + unit, i * 128 : (i + 1) * 128]
+                arow = pl.multiple_of(src * depth + hh * aq + i * third, 16)
+                ao[pl.ds(arow, third), :] = piece[:, :rank]
+                if j == 0:
+                    rows = min(third, tok - i * third)
+                    krow = pl.multiple_of(src * tok + i * third, 16)
+                    kvo[pl.ds(krow, rows), kvr:] = piece[:rows, rank : rank + rope]
+
+
+def attend_body(n, nope, scale, sc, x_ref, a_ref, b_ref, w_ref, kv_ref, pr_ref, pc_ref, ku_ref, vu_ref, *rest):
+    moved, out, merged = rest[: 2 * (n - 1)], rest[-2], rest[-1]
+    s, g = sc[0], sc[1]
+    depth = w_ref.shape[0]
+    half = depth // 2
+    up = b_ref[...]
+
+    def merge(w, begin):
+        rows = w.shape[0]
+        at = pl.ds(pl.multiple_of(begin, 16), rows)
+        add = jnp.dot(a_ref[at, :], up, preferred_element_type=jnp.float32)
+        merged[at, :] = (w.astype(jnp.float32) + add).astype(jnp.bfloat16)
+
+    merge(w_ref[...], s * depth)
+    for k in range(1, n):
+        src = lax.rem(s - k + n, n)
+        merge(moved[k - 1][...], src * depth + g * half)
+        merge(moved[n - 2 + k][...], src * depth + (1 - g) * half)
+    q = jnp.dot(x_ref[...], merged[...], preferred_element_type=jnp.float32)
+    heads, kvr = vu_ref.shape[0], vu_ref.shape[1]
+    vdim = vu_ref.shape[2]
+    width = q.shape[1] // heads
+    lat, rope_key = kv_ref[:, :kvr], kv_ref[:, kvr:]
+    visible = pr_ref[...] <= pc_ref[...]
+    nt = (((1,), (1,)), ((), ()))
+    for j in range(heads):
+        qn = q[:, j * width : j * width + nope].astype(jnp.bfloat16)
+        qr = q[:, j * width + nope : (j + 1) * width].astype(jnp.bfloat16)
+        absorbed = jnp.dot(qn, ku_ref[j], preferred_element_type=jnp.float32).astype(jnp.bfloat16)
+        scores = lax.dot_general(absorbed, lat, nt, preferred_element_type=jnp.float32)
+        scores = scores + lax.dot_general(qr, rope_key, nt, preferred_element_type=jnp.float32)
+        scores = jnp.where(visible, scores * scale, jnp.float32(-1e30))
+        top = jnp.max(scores, axis=1, keepdims=True)
+        e = jnp.where(visible, jnp.exp(scores - top), jnp.float32(0.0))
+        total = jnp.sum(e, axis=1, keepdims=True)
+        ctx = jnp.dot(e.astype(jnp.bfloat16), lat, preferred_element_type=jnp.float32)
+        ctx = (ctx / total).astype(jnp.bfloat16)
+        ho = jnp.dot(ctx, vu_ref[j], preferred_element_type=jnp.float32)
+        out[:, j * vdim : (j + 1) * vdim] = ho.astype(jnp.bfloat16)
+
+
+def gather_slots(n, sc, slots, lhs):
+    s = sc[0]
+    width = slots[0].shape[1]
+    for k in range(n):
+        src = lax.rem(s - k + n, n)
+        lhs[:, pl.ds(pl.multiple_of(src * width, 128), width)] = slots[k][...]
+
+
+def first_body(n, sc, w_ref, *rest):
+    slots, acc, lhs = rest[:n], rest[n], rest[n + 1]
+    gather_slots(n, sc, slots, lhs)
+    w = w_ref[...].reshape(lhs.shape[1], w_ref.shape[-1])
+    acc[...] = jnp.dot(lhs[...], w, preferred_element_type=jnp.float32)
+
+
+def last_body(n, nh, tok, sc, w_ref, acc, *rest):
+    slots, (keep, send), lhs, tot = rest[:n], rest[n : n + 2], rest[n + 2], rest[n + 3]
+    gather_slots(n, sc, slots, lhs)
+    w = w_ref[...].reshape(lhs.shape[1], w_ref.shape[-1])
+    tot[...] = acc[...] + jnp.dot(lhs[...], w, preferred_element_type=jnp.float32)
+    core = sc[2] % 2
+    for i in range(nh // 2):
+        mine = pl.ds(pl.multiple_of((2 * i + core) * tok, 16), tok)
+        theirs = pl.ds(pl.multiple_of((2 * i + 1 - core) * tok, 16), tok)
+        keep[i * tok : (i + 1) * tok, :] = tot[mine, :]
+        send[i * tok : (i + 1) * tok, :] = tot[theirs, :].astype(jnp.bfloat16)
+
+
+def by_heads(x, kv, pos, wq, down, up, ku, vu, wo):
+    n, nh = lax.axis_size("seq"), lax.axis_size("head")
+    s, g, h = lax.axis_index("seq"), lax.axis_index("groups"), lax.axis_index("head")
+    sc = jnp.stack([s, g, h]).astype(jnp.int32)
+    tok, depth = x.shape
+    heads, nope, kvr = ku.shape
+    vdim = vu.shape[2]
+    rope = kv.shape[1] - kvr
+    rank = down.shape[1]
+    rows, cols = wq.shape
+    half = rows // 2
+    tokens = n * tok
+    mine = heads // n
+    per = mine // CHUNKS
+    wide = per * (cols // heads)
+    bf = jnp.bfloat16
+
+    kq, vq, aq = depth // nh, kvr // nh, rows // nh
+    third = aq // 3
+    xs = lax.dynamic_slice(x, (0, h * kq), (tok, kq))
+    vs = lax.dynamic_slice(kv, (0, h * vq), (tok, vq))
+    as_ = lax.dynamic_slice(down, (h * aq, 0), (aq, rank))
+    tail = jnp.concatenate([as_, jnp.pad(kv[:, kvr:], ((0, aq - tok), (0, 0)))], axis=1)
+    tail = jnp.concatenate([tail[i * third : (i + 1) * third] for i in range(3)], axis=1)
+    tail = jnp.pad(tail, ((0, 0), (0, kq + vq - tail.shape[1])))
+    pack = jnp.concatenate([jnp.concatenate([xs, vs], axis=1), tail], axis=0)
+    packs = [lax.ppermute(pack, "seq", cyclic(n, k)) for k in range(1, n)]
+    others = [lax.ppermute(pos, "seq", cyclic(n, k)) for k in range(1, n)]
+
+    received = []
+    for c in range(CHUNKS):
+        got = []
+        for k in range(1, n):
+            at = lax.rem(s + k, n) * (mine * (cols // heads)) + c * wide
+            piece = lax.dynamic_slice(wq, (g * half, at), (half, wide))
+            got.append(lax.ppermute(piece, "seq", cyclic(n, k)))
+        received.append(got)
+    passed = [[lax.ppermute(p, "groups", cyclic(2, 1)) for p in got] for got in received]
+
+    stack = jnp.concatenate(packs, axis=0)
+    bit = 1
+    stacks = [stack]
+    across = lax.ppermute(stack, "head", flipped(nh, 2))
+    stacks = [
+        stack,
+        lax.ppermute(stack, "head", flipped(nh, 1)),
+        across,
+        lax.ppermute(across, "head", flipped(nh, 1)),
+    ]
+    x_all, kv_all, a_all = call(
+        functools.partial(unpack_body, n, nh, tok, kq, vq, aq),
+        (
+            jax.ShapeDtypeStruct((tokens, depth), bf),
+            jax.ShapeDtypeStruct((tokens, kv.shape[1]), bf),
+            jax.ShapeDtypeStruct((n * rows, rank), bf),
+        ),
+        [None] * (3 + nh),
+        sc,
+        [x, kv, down] + stacks,
+        moved=4 * x.size * n * 2,
+    )
+    around = jnp.concatenate([o for o in others[::-1]] + [pos] + [o for o in others[::-1]] + [pos])
+    pos_all = lax.dynamic_slice(around, ((n - 1 - s) * tok,), (tokens,))
+    pr, pc = pos_all[None, :], pos_all[:, None]
+
+    merged = (
+        wq.astype(jnp.float32) + jnp.dot(down, up, preferred_element_type=jnp.float32)
+    ).astype(bf)
+
+    scale = 1.0 / math.sqrt(nope + rope)
+    slots = []
+    for c in range(CHUNKS):
+        def column(i, sc, c=c):
+            return (0, sc[0] * CHUNKS + c)
+
+        def leading(i, sc, c=c):
+            return (sc[0] * CHUNKS + c, 0, 0)
+
+        args = [x_all, a_all, up, wq, kv_all, pr, pc, ku, vu] + received[c] + passed[c]
+        blocks = [None] * len(args)
+        blocks[2] = pl.BlockSpec((rank, wide), column)
+        blocks[3] = pl.BlockSpec((rows, wide), column)
+        blocks[7] = pl.BlockSpec((per, nope, kvr), leading)
+        blocks[8] = pl.BlockSpec((per, kvr, vdim), leading)
+        ho = call(
+            functools.partial(attend_body, n, nope, scale),
+            jax.ShapeDtypeStruct((tokens, per * vdim), bf),
+            blocks,
+            sc,
+            args,
+            scratch=[pltpu.VMEM((n * rows, wide), bf)],
+            flops=2 * tokens * per * (depth * wide // per + 2 * nope * kvr + 2 * tokens * kvr),
+            moved=4 * n * rows * wide,
+        )
+        slots.append([ho] + [lax.ppermute(ho, "seq", cyclic(n, k)) for k in range(1, n)])
+
+    w4 = wo.reshape(n, CHUNKS, per * vdim, wo.shape[1])
+    wide_out = wo.shape[1]
+    acc = None
+    for c in range(CHUNKS):
+        spec = pl.BlockSpec((n, None, per * vdim, wide_out), lambda i, sc, c=c: (0, c, 0, 0))
+        lhs = pltpu.VMEM((tokens, n * per * vdim), bf)
+        cost = dict(flops=2 * tokens * n * per * vdim * wide_out, moved=w4.size * 2 // CHUNKS)
+        if c < CHUNKS - 1:
+            acc = call(
+                functools.partial(first_body, n),
+                jax.ShapeDtypeStruct((tokens, wide_out), jnp.float32),
+                [spec] + [None] * n,
+                sc,
+                [w4] + slots[c],
+                scratch=[lhs],
+                **cost,
+            )
+        else:
+            keep, send = call(
+                functools.partial(last_body, n, nh, tok),
+                (
+                    jax.ShapeDtypeStruct((nh // 2 * tok, wide_out), jnp.float32),
+                    jax.ShapeDtypeStruct((nh // 2 * tok, wide_out), bf),
+                ),
+                [spec] + [None] * (n + 1),
+                sc,
+                [w4, acc] + slots[c],
+                scratch=[lhs, pltpu.VMEM((tokens, wide_out), jnp.float32)],
+                **cost,
+            )
+    got = lax.ppermute(send, "head", flipped(nh, 1))
+    pair = (keep + got.astype(jnp.float32)).reshape(nh // 2, tok, wide_out)
+    side = h // 2
+    out = lax.dynamic_index_in_dim(pair, side, 0, keepdims=False)
+    away = lax.dynamic_index_in_dim(pair, 1 - side, 0, keepdims=False).astype(bf)
+    out = out + lax.ppermute(away, "head", flipped(nh, 2)).astype(jnp.float32)
+    return merged, out.astype(bf)
+
+
+def fits(mesh, heads, tok):
+    n, nh = mesh.shape["seq"], mesh.shape["head"]
+    return mesh.shape["groups"] == 2 and nh == 4 and heads % (nh * n * CHUNKS) == 0 and tok % 16 == 0
+
+
 def solution(mesh):
     placed = (
         P(("groups", "seq"), None),
@@ -95,8 +369,13 @@
         P("head", None, None),
         P("head", "seq"),
     )
+
+    def local(*args):
+        heads = args[6].shape[0] * mesh.shape["head"]
+        return (by_heads if fits(mesh, heads, args[0].shape[0]) else on_device)(*args)
+
     return jax.shard_map(
-        on_device,
+        local,
         mesh=mesh,
         in_specs=placed,
         out_specs=(P(("groups", "seq"), "head"), P(("groups", "head"), "seq")),

time: 269 us -> 127 us (0.47)
  waiting for transfers between devices: 194 us -> 47.7 us
  starting transfers between devices: 0.12 us -> 46.6 us
  blocking collectives: 34.6 us -> 0 us
  Pallas kernels: 0 us -> 18.9 us
  matrix products: 20.6 us -> 2.2 us
  between operations: 14.5 us -> 0.89 us
  local copies, waits for them, and re-layouts: 4.86 us -> 8.46 us
    all_gather x2 -> x0, waiting for transfers between devices: 169 us -> none  [the longest x1 138 us: on_device(): lax.all_gather(merged_query_weight, 'seq', axis=0, tiled=True)]
    ppermute x0 -> x29, waiting for transfers between devices: none -> 47.7 us  [the longest x1 8.35 us: by_heads(): across = lax.ppermute(stack, 'head', flipped(nh, 2))]
    ppermute x0 -> x29, starting transfers between devices: none -> 46.6 us  [the longest x6 12 us: by_heads(): lax.ppermute(ho, 'seq', cyclic(n, k))]
    all_gather x1 -> x0, blocking collectives: 24.7 us -> none  [on_device(): key_rows = lax.all_gather(key_value_latents, 'seq', axis=0, tiled=True)]
    reduce_scatter x1 -> x0, waiting for transfers between devices: 24.6 us -> none  [on_device(): lax.psum_scatter(partial_value.astype(jnp.bfloat16), 'head', scatter_dime...]
    pallas_call x0 -> x5, Pallas kernels: none -> 18.9 us  [call(): pl.pallas_call(body, out_shape=outs, grid_spec=pltpu.PrefetchScalarGridSp...]
    dot_general x7 -> x1, matrix products: 20.6 us -> 2.2 us  [by_heads(): jnp.dot(down, up, preferred_element_type=jnp.float32)]
    unnamed x1 -> x0, blocking collectives: 9.89 us -> none
  transfers between devices with their start and end apart: 3 -> 29, of which waited for: 3 -> 14; matrix products, arithmetic and copies ran while one was open for 0% -> 4% of each run, Pallas kernels for 0% -> 11%
where the time goes in v1:
time: 127 us; the launch traced here: 126 us
  waiting for transfers between devices  47.7 us (38%)
  starting transfers between devices  46.6 us (37%)
  Pallas kernels  18.9 us (15%)
  local copies, waits for them, and re-layouts  8.46 us (7%)
  matrix products  2.2 us (2%)
    pallas_call x5, Pallas kernels, call(): pl.pallas_call(body, out_shape=outs, grid_spec=pltpu.PrefetchScalarGridSp...  18.9 us
    ppermute x6, starting transfers between devices, by_heads(): lax.ppermute(ho, 'seq', cyclic(n, k))  12 us
    ppermute x3, starting transfers between devices, by_heads(): others = [lax.ppermute(pos, 'seq', cyclic(n, k)) for k in range(1, n)]  9.58 us
    ppermute x1, waiting for transfers between devices, by_heads(): across = lax.ppermute(stack, 'head', flipped(nh, 2))  8.35 us
    ppermute x6, starting transfers between devices, by_heads(): got.append(lax.ppermute(piece, 'seq', cyclic(n, k)))  8.09 us
    ppermute x6, waiting for transfers between devices, by_heads(): got.append(lax.ppermute(piece, 'seq', cyclic(n, k)))  7.9 us
    ppermute x3, waiting for transfers between devices, by_heads(): others = [lax.ppermute(pos, 'seq', cyclic(n, k)) for k in range(1, n)]  7.65 us
    ppermute x3, starting transfers between devices, by_heads(): packs = [lax.ppermute(pack, 'seq', cyclic(n, k)) for k in range(1, n)]  7.01 us
  transfers between devices with their start and end apart: 29, of which 14 were waited for; matrix products, arithmetic and copies ran while one was open for 4% of the time, Pallas kernels for 11%

profile of v1, /device:TPU:0, one launch (start us, length us, event | category | flops | bytes accessed | tf_op | source)
XLA Modules:
  0.0 125.8 jit_solution(4823468873537893917)
XLA Ops:
  4.2 3.1 %collective-permute-start = (bf16[112,512]{1,0:T(8,128)(2,1)S(1)}, bf16[112,512]{1,0:T(8,128)(2,1)S(1)}, u32[]{:S(2)}, u32[]{:S(2)}) collective-permute-start(bf16[112,512]{1,0:T(8,128)(2,1)S(1)} %pad_maximum_fusion), channel_id=1, source_target_pairs={{0,4},{4,8},{8,12},{12,0},{1,5},{5,9},{9,13},{13,1},{2,6},{6,10},{... | collective-permute-start | bytes 344072 | tf_op jit(solution)/shard_map/ppermute | solution.py:246
  7.3 2.6 %collective-permute-start.1 = (bf16[112,512]{1,0:T(8,128)(2,1)S(1)}, bf16[112,512]{1,0:T(8,128)(2,1)S(1)}, u32[]{:S(2)}, u32[]{:S(2)}) collective-permute-start(bf16[112,512]{1,0:T(8,128)(2,1)S(1)} %pad_maximum_fusion), channel_id=1, source_target_pairs={{0,8},{4,12},{8,0},{12,4},{1,9},{5,13},{9,1},{13,5},{2,10},{6,14},... | collective-permute-start | bytes 344072 | tf_op jit(solution)/shard_map/ppermute | solution.py:246
  11.2 2.2 %collective-permute-done = bf16[112,512]{1,0:T(8,128)(2,1)S(1)} collective-permute-done((bf16[112,512]{1,0:T(8,128)(2,1)S(1)}, bf16[112,512]{1,0:T(8,128)(2,1)S(1)}, u32[]{:S(2)}, u32[]{:S(2)}) %collective-permute-start) | collective-permute-done | bytes 114720 | tf_op jit(solution)/shard_map/ppermute | solution.py:246
  13.4 4.1 %collective-permute-done.1 = bf16[112,512]{1,0:T(8,128)(2,1)S(1)} collective-permute-done((bf16[112,512]{1,0:T(8,128)(2,1)S(1)}, bf16[112,512]{1,0:T(8,128)(2,1)S(1)}, u32[]{:S(2)}, u32[]{:S(2)}) %collective-permute-start.1) | collective-permute-done | bytes 114720 | tf_op jit(solution)/shard_map/ppermute | solution.py:246
  17.5 1.6 %collective-permute-start.4 = (bf16[336,512]{1,0:T(8,128)(2,1)S(1)}, bf16[336,512]{1,0:T(8,128)(2,1)S(1)}, u32[]{:S(2)}, u32[]{:S(2)}) collective-permute-start(bf16[336,512]{1,0:T(8,128)(2,1)S(1)} %constant_dynamic-update-slice_fusion.rest_0_), channel_id=1, source_target_pairs={{0,2},{1,3},{2,0},{3,1},{4,6},{5,7},{6,4},{7,5},{8,10},{9,11},{10,... | collective-permute-start | bytes 1032200 | tf_op jit(solution)/shard_map/ppermute | solution.py:262
  19.1 8.4 %collective-permute-done.4.rest_2_ = bf16[336,512]{1,0:T(8,128)(2,1)S(1)} collective-permute-done((bf16[336,512]{1,0:T(8,128)(2,1)S(1)}, bf16[336,512]{1,0:T(8,128)(2,1)S(1)}, u32[]{:S(2)}, u32[]{:S(2)}) %collective-permute-start.4) | collective-permute-done | bytes 344096 | tf_op jit(solution)/shard_map/ppermute | solution.py:262
  27.5 2.0 %fusion.9 = (bf16[192,384]{1,0:T(8,128)(2,1)}, bf16[192,384]{1,0:T(8,128)(2,1)S(1)}, bf16[192,384]{1,0:T(8,128)(2,1)S(1)}, bf16[192,384]{1,0:T(8,128)(2,1)S(1)},...) fusion(bf16[384,3072]{1,0:T(8,128)(2,1)} %w_ref.3, s32[]{:T(128)S(6)} %select_n.54, s32[]{:T(128)S(6)} %select_n.60, ...), kind=kLoop, calls=%fused_computation.23 | loop fusion | bytes 1769500 | tf_op jit(solution)/shard_map/dynamic_slice | solution.py:254
  29.5 3.0 %collective-permute-start.18 = (bf16[192,384]{1,0:T(8,128)(2,1)S(1)}, bf16[192,384]{1,0:T(8,128)(2,1)S(1)}, u32[]{:S(2)}, u32[]{:S(2)}) collective-permute-start(bf16[192,384]{1,0:T(8,128)(2,1)S(1)} %get-tuple-element.14), channel_id=1, source_target_pairs={{0,4},{4,8},{8,12},{12,0},{1,5},{5,9},{9,13},{13,1},{2,6},{6,10},{... | collective-permute-start | bytes 442376 | tf_op jit(solution)/shard_map/ppermute | solution.py:255
  33.1 1.8 %collective-permute-start.6 = (s32[80]{0:T(128)S(1)}, s32[80]{0:T(128)S(1)}, u32[]{:S(2)}, u32[]{:S(2)}) collective-permute-start(s32[80]{0:T(128)S(1)} %copy-done.6), channel_id=1, source_target_pairs={{0,12},{4,0},{8,4},{12,8},{1,13},{5,1},{9,5},{13,9},{2,14},{6,2},{... | collective-permute-start | bytes 968 | tf_op jit(solution)/shard_map/ppermute | solution.py:247
  34.9 4.7 %collective-permute-done.6 = s32[80]{0:T(128)S(1)} collective-permute-done((s32[80]{0:T(128)S(1)}, s32[80]{0:T(128)S(1)}, u32[]{:S(2)}, u32[]{:S(2)}) %collective-permute-start.6) | collective-permute-done | bytes 352 | tf_op jit(solution)/shard_map/ppermute | solution.py:247
  39.5 4.0 %collective-permute-start.7 = (s32[80]{0:T(128)S(1)}, s32[80]{0:T(128)S(1)}, u32[]{:S(2)}, u32[]{:S(2)}) collective-permute-start(s32[80]{0:T(128)S(1)} %copy-done.6), channel_id=1, source_target_pairs={{0,8},{4,12},{8,0},{12,4},{1,9},{5,13},{9,1},{13,5},{2,10},{6,14},... | collective-permute-start | bytes 968 | tf_op jit(solution)/shard_map/ppermute | solution.py:247
  45.0 3.9 %collective-permute-start.8 = (s32[80]{0:T(128)S(1)}, s32[80]{0:T(128)S(1)}, u32[]{:S(2)}, u32[]{:S(2)}) collective-permute-start(s32[80]{0:T(128)S(1)} %copy-done.6), channel_id=1, source_target_pairs={{0,4},{4,8},{8,12},{12,0},{1,5},{5,9},{9,13},{13,1},{2,6},{6,10},{... | collective-permute-start | bytes 968 | tf_op jit(solution)/shard_map/ppermute | solution.py:247
  50.9 2.1 %collective-permute-start.9 = (bf16[192,384]{1,0:T(8,128)(2,1)S(1)}, bf16[192,384]{1,0:T(8,128)(2,1)S(1)}, u32[]{:S(2)}, u32[]{:S(2)}) collective-permute-start(bf16[192,384]{1,0:T(8,128)(2,1)S(1)} %get-tuple-element.17), channel_id=1, source_target_pairs={{0,4},{4,8},{8,12},{12,0},{1,5},{5,9},{9,13},{13,1},{2,6},{6,10},{... | collective-permute-start | bytes 442376 | tf_op jit(solution)/shard_map/ppermute | solution.py:255
  53.0 2.4 %collective-permute-start.11 = (bf16[192,384]{1,0:T(8,128)(2,1)S(1)}, bf16[192,384]{1,0:T(8,128)(2,1)S(1)}, u32[]{:S(2)}, u32[]{:S(2)}) collective-permute-start(bf16[192,384]{1,0:T(8,128)(2,1)S(1)} %get-tuple-element.15), channel_id=1, source_target_pairs={{0,12},{4,0},{8,4},{12,8},{1,13},{5,1},{9,5},{13,9},{2,14},{6,2},{... | collective-permute-start | bytes 442376 | tf_op jit(solution)/shard_map/ppermute | solution.py:255
  55.4 4.1 %collective-permute-done.9.rest_0_ = bf16[192,384]{1,0:T(8,128)(2,1)S(1)} collective-permute-done((bf16[192,384]{1,0:T(8,128)(2,1)S(1)}, bf16[192,384]{1,0:T(8,128)(2,1)S(1)}, u32[]{:S(2)}, u32[]{:S(2)}) %collective-permute-start.9) | collective-permute-done | bytes 147488 | tf_op jit(solution)/shard_map/ppermute | solution.py:255
  59.5 3.8 %collective-permute-done.10.rest_1_ = bf16[192,384]{1,0:T(8,128)(2,1)S(1)} collective-permute-done((bf16[192,384]{1,0:T(8,128)(2,1)S(1)}, bf16[192,384]{1,0:T(8,128)(2,1)S(1)}, u32[]{:S(2)}, u32[]{:S(2)}) %collective-permute-start.10) | collective-permute-done | bytes 147488 | tf_op jit(solution)/shard_map/ppermute | solution.py:255
  63.3 1.6 %collective-permute-start.12 = (bf16[192,384]{1,0:T(8,128)(2,1)S(1)}, bf16[192,384]{1,0:T(8,128)(2,1)S(1)}, u32[]{:S(2)}, u32[]{:S(2)}) collective-permute-start(bf16[192,384]{1,0:T(8,128)(2,1)S(1)} %collective-permute-done.9.rest_0_), channel_id=1, source_target_pairs={{0,16},{16,0},{1,17},{17,1},{2,18},{18,2},{3,19},{19,3},{4,20},{20... | collective-permute-start | bytes 442376 | tf_op jit(solution)/shard_map/ppermute | solution.py:257
  73.2 3.3 %collective-permute-done.14.rest_5_ = bf16[192,384]{1,0:T(8,128)(2,1)} collective-permute-done((bf16[192,384]{1,0:T(8,128)(2,1)S(1)}, bf16[192,384]{1,0:T(8,128)(2,1)}, u32[]{:S(2)}, u32[]{:S(2)}) %collective-permute-start.14) | collective-permute-done | bytes 147488 | tf_op jit(solution)/shard_map/ppermute | solution.py:257
  76.5 4.6 %shard_map.105.rest_0_ = bf16[320,256]{1,0:T(8,128)(2,1)S(1)} custom-call(s32[3]{0:T(128)S(1)} %pad_add_fusion.sc, bf16[320,1536]{1,0:T(8,128)(2,1)S(1)} %get-tuple-element.7.x_ref, bf16[1536,64]{1,0:T(8,128)(2,1)S(1)} %get-tuple-element.8.a_ref, bf16[64,3072]{1,0:T(8,128)(2,1)S(1)} %copy-done.1, bf16[384,3072]{1,0:T(8,128)(2,1)} %w_ref.3, ...), custom_call_target="tpu_custom_call" | custom-call | flops 964689920 | bytes 2359296 | tf_op jit(solution)/shard_map/pallas_call | solution.py:104
  81.1 4.1 %collective-permute-start.15 = (bf16[320,256]{1,0:T(8,128)(2,1)S(1)}, bf16[320,256]{1,0:T(8,128)(2,1)S(1)}, u32[]{:S(2)}, u32[]{:S(2)}) collective-permute-start(bf16[320,256]{1,0:T(8,128)(2,1)S(1)} %shard_map.105.rest_0_), channel_id=1, source_target_pairs={{0,4},{4,8},{8,12},{12,0},{1,5},{5,9},{9,13},{13,1},{2,6},{6,10},{... | collective-permute-start | bytes 491528 | tf_op jit(solution)/shard_map/ppermute | solution.py:314
  85.2 3.4 %collective-permute-start.16 = (bf16[320,256]{1,0:T(8,128)(2,1)S(1)}, bf16[320,256]{1,0:T(8,128)(2,1)S(1)}, u32[]{:S(2)}, u32[]{:S(2)}) collective-permute-start(bf16[320,256]{1,0:T(8,128)(2,1)S(1)} %shard_map.105.rest_0_), channel_id=1, source_target_pairs={{0,8},{4,12},{8,0},{12,4},{1,9},{5,13},{9,1},{13,5},{2,10},{6,14},... | collective-permute-start | bytes 491528 | tf_op jit(solution)/shard_map/ppermute | solution.py:314
  88.6 4.5 %shard_map.107.rest_0_ = bf16[320,256]{1,0:T(8,128)(2,1)S(1)} custom-call(s32[3]{0:T(128)S(1)} %pad_add_fusion.sc, bf16[320,1536]{1,0:T(8,128)(2,1)S(1)} %get-tuple-element.7.x_ref, bf16[1536,64]{1,0:T(8,128)(2,1)S(1)} %get-tuple-element.8.a_ref, bf16[64,3072]{1,0:T(8,128)(2,1)S(1)} %copy-done.1, bf16[384,3072]{1,0:T(8,128)(2,1)} %w_ref.3, ...), custom_call_target="tpu_custom_call" | custom-call | flops 964689920 | bytes 2359296 | tf_op jit(solution)/shard_map/pallas_call | solution.py:104
  93.1 2.0 %collective-permute-start.24 = (bf16[320,256]{1,0:T(8,128)(2,1)S(1)}, bf16[320,256]{1,0:T(8,128)(2,1)S(1)}, u32[]{:S(2)}, u32[]{:S(2)}) collective-permute-start(bf16[320,256]{1,0:T(8,128)(2,1)S(1)} %shard_map.107.rest_0_), channel_id=1, source_target_pairs={{0,4},{4,8},{8,12},{12,0},{1,5},{5,9},{9,13},{13,1},{2,6},{6,10},{... | collective-permute-start | bytes 491528 | tf_op jit(solution)/shard_map/ppermute | solution.py:314
  95.2 2.4 %collective-permute-start.26 = (bf16[320,256]{1,0:T(8,128)(2,1)S(1)}, bf16[320,256]{1,0:T(8,128)(2,1)S(1)}, u32[]{:S(2)}, u32[]{:S(2)}) collective-permute-start(bf16[320,256]{1,0:T(8,128)(2,1)S(1)} %shard_map.107.rest_0_), channel_id=1, source_target_pairs={{0,12},{4,0},{8,4},{12,8},{1,13},{5,1},{9,5},{13,9},{2,14},{6,2},{... | collective-permute-start | bytes 491528 | tf_op jit(solution)/shard_map/ppermute | solution.py:314
  97.6 3.8 %collective-permute-done.16.rest_2_ = bf16[320,256]{1,0:T(8,128)(2,1)S(1)} collective-permute-done((bf16[320,256]{1,0:T(8,128)(2,1)S(1)}, bf16[320,256]{1,0:T(8,128)(2,1)S(1)}, u32[]{:S(2)}, u32[]{:S(2)}) %collective-permute-start.16) | collective-permute-done | bytes 163872 | tf_op jit(solution)/shard_map/ppermute | solution.py:314
  101.4 4.0 %shard_map.106.acc = f32[320,1792]{1,0:T(8,128)S(1)} custom-call(s32[3]{0:T(128)S(1)} %pad_add_fusion.sc, bf16[4,2,256,1792]{3,2,1,0:T(8,128)(2,1)} %bitcast.13, bf16[320,256]{1,0:T(8,128)(2,1)S(1)} %shard_map.105.rest_0_, bf16[320,256]{1,0:T(8,128)(2,1)S(1)} %collective-permute-done.15.rest_1_, bf16[320,256]{1,0:T(8,128)(2,1)S(1)} %collective-permute-done.16.rest_2_, ...), custom_call_target="tpu_custom_call" | custom-call | flops 1174405120 | bytes 3670016 | tf_op jit(solution)/shard_map/pallas_call | solution.py:104
  106.8 2.1 %collective-permute-done.25.rest_2_ = bf16[320,256]{1,0:T(8,128)(2,1)S(1)} collective-permute-done((bf16[320,256]{1,0:T(8,128)(2,1)S(1)}, bf16[320,256]{1,0:T(8,128)(2,1)S(1)}, u32[]{:S(2)}, u32[]{:S(2)}) %collective-permute-start.25) | collective-permute-done | bytes 163872 | tf_op jit(solution)/shard_map/ppermute | solution.py:314
  108.9 5.0 %shard_map.108 = (f32[160,1792]{1,0:T(8,128)S(1)}, bf16[160,1792]{1,0:T(8,128)(2,1)S(1)}) custom-call(s32[3]{0:T(128)S(1)} %pad_add_fusion.sc, bf16[4,2,256,1792]{3,2,1,0:T(8,128)(2,1)} %bitcast.14, f32[320,1792]{1,0:T(8,128)} %copy-done, bf16[320,256]{1,0:T(8,128)(2,1)S(1)} %shard_map.107.rest_0_, bf16[320,256]{1,0:T(8,128)(2,1)S(1)} %collective-permute-done.24.rest_1_, ...), custom_call_target="tpu_custom_call" | custom-call | flops 1174405120 | bytes 3670016 | tf_op jit(solution)/shard_map/pallas_call | solution.py:104
  114.0 1.9 %collective-permute-done.27 = bf16[160,1792]{1,0:T(8,128)(2,1)S(1)} collective-permute-done((bf16[160,1792]{1,0:T(8,128)(2,1)S(1)}, bf16[160,1792]{1,0:T(8,128)(2,1)S(1)}, u32[]{:S(2)}, u32[]{:S(2)}) %collective-permute-start.27) | collective-permute-done | bytes 573472 | tf_op jit(solution)/shard_map/ppermute | solution.py:346
  116.1 1.6 %collective-permute-start.28 = (bf16[80,1792]{1,0:T(8,128)(2,1)S(1)}, bf16[80,1792]{1,0:T(8,128)(2,1)S(1)}, u32[]{:S(2)}, u32[]{:S(2)}) collective-permute-start(bf16[80,1792]{1,0:T(8,128)(2,1)S(1)} %fusion.1), channel_id=1, source_target_pairs={{0,2},{1,3},{2,0},{3,1},{4,6},{5,7},{6,4},{7,5},{8,10},{9,11},{10,... | collective-permute-start | bytes 860168 | tf_op jit(solution)/shard_map/ppermute | solution.py:351
  117.7 2.2 %add_convert_fusion = bf16[384,3072]{1,0:T(8,128)(2,1)} fusion(bf16[384,3072]{1,0:T(8,128)(2,1)S(1)} %copy-done.4, bf16[384,64]{0,1:T(8,128)(2,1)S(1)} %copy-done.5, bf16[64,3072]{1,0:T(8,128)(2,1)S(1)} %copy-done.1), kind=kOutput, calls=%fused_computation | convolution fusion | flops 154533888 | bytes 5160960 | tf_op jit(solution)/shard_map/dot_general | solution.py:286
  119.9 5.1 %collective-permute-done.28 = bf16[80,1792]{1,0:T(8,128)(2,1)S(1)} collective-permute-done((bf16[80,1792]{1,0:T(8,128)(2,1)S(1)}, bf16[80,1792]{1,0:T(8,128)(2,1)S(1)}, u32[]{:S(2)}, u32[]{:S(2)}) %collective-permute-start.28) | collective-permute-done | bytes 286752 | tf_op jit(solution)/shard_map/ppermute | solution.py:351
  (73 shorter events, 19.8 us)
Async XLA Ops:
  0.6 68.3 %copy-start.3 = (bf16[80,576]{1,0:T(8,128)(2,1)S(1)}, bf16[80,576]{1,0:T(8,128)(2,1)}, u32[]{:S(2)}) copy-start(bf16[80,576]{1,0:T(8,128)(2,1)} %kv_ref.1) | copy-start | bytes 276484
  0.6 68.3 %copy-start.2 = (bf16[80,1536]{1,0:T(8,128)(2,1)S(1)}, bf16[80,1536]{1,0:T(8,128)(2,1)}, u32[]{:S(2)}) copy-start(bf16[80,1536]{1,0:T(8,128)(2,1)} %x_ref.1) | copy-start | bytes 737284
  4.2 72.3 %copy-start.1 = (bf16[64,3072]{1,0:T(8,128)(2,1)S(1)}, bf16[64,3072]{1,0:T(8,128)(2,1)}, u32[]{:S(2)}) copy-start(bf16[64,3072]{1,0:T(8,128)(2,1)} %b_ref.3) | copy-start | bytes 1179652
  4.2 9.2 %collective-permute-start = (bf16[112,512]{1,0:T(8,128)(2,1)S(1)}, bf16[112,512]{1,0:T(8,128)(2,1)S(1)}, u32[]{:S(2)}, u32[]{:S(2)}) collective-permute-start(bf16[112,512]{1,0:T(8,128)(2,1)S(1)} %pad_maximum_fusion), channel_id=1, source_target_pairs={{0,4},{4,8},{8,12},{12,0},{1,5},{5,9},{9,13},{13,1},{2,6},{6,10},{... | collective-permute-start | bytes 344072 | tf_op jit(solution)/shard_map/ppermute | solution.py:246
  7.3 10.2 %collective-permute-start.1 = (bf16[112,512]{1,0:T(8,128)(2,1)S(1)}, bf16[112,512]{1,0:T(8,128)(2,1)S(1)}, u32[]{:S(2)}, u32[]{:S(2)}) collective-permute-start(bf16[112,512]{1,0:T(8,128)(2,1)S(1)} %pad_maximum_fusion), channel_id=1, source_target_pairs={{0,8},{4,12},{8,0},{12,4},{1,9},{5,13},{9,1},{13,5},{2,10},{6,14},... | collective-permute-start | bytes 344072 | tf_op jit(solution)/shard_map/ppermute | solution.py:246
  9.9 7.6 %collective-permute-start.2 = (bf16[112,512]{1,0:T(8,128)(2,1)S(1)}, bf16[112,512]{1,0:T(8,128)(2,1)S(1)}, u32[]{:S(2)}, u32[]{:S(2)}) collective-permute-start(bf16[112,512]{1,0:T(8,128)(2,1)S(1)} %pad_maximum_fusion), channel_id=1, source_target_pairs={{0,12},{4,0},{8,4},{12,8},{1,13},{5,1},{9,5},{13,9},{2,14},{6,2},{... | collective-permute-start | bytes 344072 | tf_op jit(solution)/shard_map/ppermute | solution.py:246
  17.5 10.0 %collective-permute-start.4 = (bf16[336,512]{1,0:T(8,128)(2,1)S(1)}, bf16[336,512]{1,0:T(8,128)(2,1)S(1)}, u32[]{:S(2)}, u32[]{:S(2)}) collective-permute-start(bf16[336,512]{1,0:T(8,128)(2,1)S(1)} %constant_dynamic-update-slice_fusion.rest_0_), channel_id=1, source_target_pairs={{0,2},{1,3},{2,0},{3,1},{4,6},{5,7},{6,4},{7,5},{8,10},{9,11},{10,... | collective-permute-start | bytes 1032200 | tf_op jit(solution)/shard_map/ppermute | solution.py:262
  19.1 46.7 %collective-permute-start.3 = (bf16[336,512]{1,0:T(8,128)(2,1)S(1)}, bf16[336,512]{1,0:T(8,128)(2,1)S(1)}, u32[]{:S(2)}, u32[]{:S(2)}) collective-permute-start(bf16[336,512]{1,0:T(8,128)(2,1)S(1)} %constant_dynamic-update-slice_fusion.rest_0_), channel_id=1, source_target_pairs={{0,1},{1,0},{2,3},{3,2},{4,5},{5,4},{6,7},{7,6},{8,9},{9,8},{10,11... | collective-permute-start | bytes 1032200 | tf_op jit(solution)/shard_map/ppermute | solution.py:265
  27.5 39.4 %collective-permute-start.5 = (bf16[336,512]{1,0:T(8,128)(2,1)S(1)}, bf16[336,512]{1,0:T(8,128)(2,1)S(1)}, u32[]{:S(2)}, u32[]{:S(2)}) collective-permute-start(bf16[336,512]{1,0:T(8,128)(2,1)S(1)} %collective-permute-done.4.rest_2_), channel_id=1, source_target_pairs={{0,1},{1,0},{2,3},{3,2},{4,5},{5,4},{6,7},{7,6},{8,9},{9,8},{10,11... | collective-permute-start | bytes 1032200 | tf_op jit(solution)/shard_map/ppermute | solution.py:267
  29.5 23.5 %collective-permute-start.18 = (bf16[192,384]{1,0:T(8,128)(2,1)S(1)}, bf16[192,384]{1,0:T(8,128)(2,1)S(1)}, u32[]{:S(2)}, u32[]{:S(2)}) collective-permute-start(bf16[192,384]{1,0:T(8,128)(2,1)S(1)} %get-tuple-element.14), channel_id=1, source_target_pairs={{0,4},{4,8},{8,12},{12,0},{1,5},{5,9},{9,13},{13,1},{2,6},{6,10},{... | collective-permute-start | bytes 442376 | tf_op jit(solution)/shard_map/ppermute | solution.py:255
  32.5 20.5 %collective-permute-start.19 = (bf16[192,384]{1,0:T(8,128)(2,1)S(1)}, bf16[192,384]{1,0:T(8,128)(2,1)S(1)}, u32[]{:S(2)}, u32[]{:S(2)}) collective-permute-start(bf16[192,384]{1,0:T(8,128)(2,1)S(1)} %get-tuple-element.13), channel_id=1, source_target_pairs={{0,8},{4,12},{8,0},{12,4},{1,9},{5,13},{9,1},{13,5},{2,10},{6,14},... | collective-permute-start | bytes 442376 | tf_op jit(solution)/shard_map/ppermute | solution.py:255
  33.1 6.4 %collective-permute-start.6 = (s32[80]{0:T(128)S(1)}, s32[80]{0:T(128)S(1)}, u32[]{:S(2)}, u32[]{:S(2)}) collective-permute-start(s32[80]{0:T(128)S(1)} %copy-done.6), channel_id=1, source_target_pairs={{0,12},{4,0},{8,4},{12,8},{1,13},{5,1},{9,5},{13,9},{2,14},{6,2},{... | collective-permute-start | bytes 968 | tf_op jit(solution)/shard_map/ppermute | solution.py:247
  39.5 5.5 %collective-permute-start.7 = (s32[80]{0:T(128)S(1)}, s32[80]{0:T(128)S(1)}, u32[]{:S(2)}, u32[]{:S(2)}) collective-permute-start(s32[80]{0:T(128)S(1)} %copy-done.6), channel_id=1, source_target_pairs={{0,8},{4,12},{8,0},{12,4},{1,9},{5,13},{9,1},{13,5},{2,10},{6,14},... | collective-permute-start | bytes 968 | tf_op jit(solution)/shard_map/ppermute | solution.py:247
  45.0 5.3 %collective-permute-start.8 = (s32[80]{0:T(128)S(1)}, s32[80]{0:T(128)S(1)}, u32[]{:S(2)}, u32[]{:S(2)}) collective-permute-start(s32[80]{0:T(128)S(1)} %copy-done.6), channel_id=1, source_target_pairs={{0,4},{4,8},{8,12},{12,0},{1,5},{5,9},{9,13},{13,1},{2,6},{6,10},{... | collective-permute-start | bytes 968 | tf_op jit(solution)/shard_map/ppermute | solution.py:247
  50.9 8.6 %collective-permute-start.9 = (bf16[192,384]{1,0:T(8,128)(2,1)S(1)}, bf16[192,384]{1,0:T(8,128)(2,1)S(1)}, u32[]{:S(2)}, u32[]{:S(2)}) collective-permute-start(bf16[192,384]{1,0:T(8,128)(2,1)S(1)} %get-tuple-element.17), channel_id=1, source_target_pairs={{0,4},{4,8},{8,12},{12,0},{1,5},{5,9},{9,13},{13,1},{2,6},{6,10},{... | collective-permute-start | bytes 442376 | tf_op jit(solution)/shard_map/ppermute | solution.py:255
  53.0 10.3 %collective-permute-start.10 = (bf16[192,384]{1,0:T(8,128)(2,1)S(1)}, bf16[192,384]{1,0:T(8,128)(2,1)S(1)}, u32[]{:S(2)}, u32[]{:S(2)}) collective-permute-start(bf16[192,384]{1,0:T(8,128)(2,1)S(1)} %get-tuple-element.16), channel_id=1, source_target_pairs={{0,8},{4,12},{8,0},{12,4},{1,9},{5,13},{9,1},{13,5},{2,10},{6,14},... | collective-permute-start | bytes 442376 | tf_op jit(solution)/shard_map/ppermute | solution.py:255
  53.0 11.9 %collective-permute-start.11 = (bf16[192,384]{1,0:T(8,128)(2,1)S(1)}, bf16[192,384]{1,0:T(8,128)(2,1)S(1)}, u32[]{:S(2)}, u32[]{:S(2)}) collective-permute-start(bf16[192,384]{1,0:T(8,128)(2,1)S(1)} %get-tuple-element.15), channel_id=1, source_target_pairs={{0,12},{4,0},{8,4},{12,8},{1,13},{5,1},{9,5},{13,9},{2,14},{6,2},{... | collective-permute-start | bytes 442376 | tf_op jit(solution)/shard_map/ppermute | solution.py:255
  59.5 10.3 %collective-permute-start.20 = (bf16[192,384]{1,0:T(8,128)(2,1)}, bf16[192,384]{1,0:T(8,128)(2,1)S(1)}, u32[]{:S(2)}, u32[]{:S(2)}) collective-permute-start(bf16[192,384]{1,0:T(8,128)(2,1)} %get-tuple-element.12), channel_id=1, source_target_pairs={{0,12},{4,0},{8,4},{12,8},{1,13},{5,1},{9,5},{13,9},{2,14},{6,2},{... | collective-permute-start | bytes 442376 | tf_op jit(solution)/shard_map/ppermute | solution.py:255
  63.3 7.6 %collective-permute-start.12 = (bf16[192,384]{1,0:T(8,128)(2,1)S(1)}, bf16[192,384]{1,0:T(8,128)(2,1)S(1)}, u32[]{:S(2)}, u32[]{:S(2)}) collective-permute-start(bf16[192,384]{1,0:T(8,128)(2,1)S(1)} %collective-permute-done.9.rest_0_), channel_id=1, source_target_pairs={{0,16},{16,0},{1,17},{17,1},{2,18},{18,2},{3,19},{19,3},{4,20},{20... | collective-permute-start | bytes 442376 | tf_op jit(solution)/shard_map/ppermute | solution.py:257
  64.8 8.4 %collective-permute-start.13 = (bf16[192,384]{1,0:T(8,128)(2,1)S(1)}, bf16[192,384]{1,0:T(8,128)(2,1)S(1)}, u32[]{:S(2)}, u32[]{:S(2)}) collective-permute-start(bf16[192,384]{1,0:T(8,128)(2,1)S(1)} %collective-permute-done.10.rest_1_), channel_id=1, source_target_pairs={{0,16},{16,0},{1,17},{17,1},{2,18},{18,2},{3,19},{19,3},{4,20},{20... | collective-permute-start | bytes 442376 | tf_op jit(solution)/shard_map/ppermute | solution.py:257
  65.8 10.7 %collective-permute-start.14 = (bf16[192,384]{1,0:T(8,128)(2,1)S(1)}, bf16[192,384]{1,0:T(8,128)(2,1)}, u32[]{:S(2)}, u32[]{:S(2)}) collective-permute-start(bf16[192,384]{1,0:T(8,128)(2,1)S(1)} %collective-permute-done.11.rest_2_), channel_id=1, source_target_pairs={{0,16},{16,0},{1,17},{17,1},{2,18},{18,2},{3,19},{19,3},{4,20},{20... | collective-permute-start | bytes 442376 | tf_op jit(solution)/shard_map/ppermute | solution.py:257
  66.9 21.7 %collective-permute-start.21 = (bf16[192,384]{1,0:T(8,128)(2,1)S(1)}, bf16[192,384]{1,0:T(8,128)(2,1)S(1)}, u32[]{:S(2)}, u32[]{:S(2)}) collective-permute-start(bf16[192,384]{1,0:T(8,128)(2,1)S(1)} %collective-permute-done.18.rest_0_), channel_id=1, source_target_pairs={{0,16},{16,0},{1,17},{17,1},{2,18},{18,2},{3,19},{19,3},{4,20},{20... | collective-permute-start | bytes 442376 | tf_op jit(solution)/shard_map/ppermute | solution.py:257
  69.8 18.8 %collective-permute-start.22 = (bf16[192,384]{1,0:T(8,128)(2,1)S(1)}, bf16[192,384]{1,0:T(8,128)(2,1)S(1)}, u32[]{:S(2)}, u32[]{:S(2)}) collective-permute-start(bf16[192,384]{1,0:T(8,128)(2,1)S(1)} %collective-permute-done.19.rest_1_), channel_id=1, source_target_pairs={{0,16},{16,0},{1,17},{17,1},{2,18},{18,2},{3,19},{19,3},{4,20},{20... | collective-permute-start | bytes 442376 | tf_op jit(solution)/shard_map/ppermute | solution.py:257
  70.9 17.7 %collective-permute-start.23 = (bf16[192,384]{1,0:T(8,128)(2,1)S(1)}, bf16[192,384]{1,0:T(8,128)(2,1)S(1)}, u32[]{:S(2)}, u32[]{:S(2)}) collective-permute-start(bf16[192,384]{1,0:T(8,128)(2,1)S(1)} %collective-permute-done.20.rest_2_), channel_id=1, source_target_pairs={{0,16},{16,0},{1,17},{17,1},{2,18},{18,2},{3,19},{19,3},{4,20},{20... | collective-permute-start | bytes 442376 | tf_op jit(solution)/shard_map/ppermute | solution.py:257
  81.1 14.1 %collective-permute-start.15 = (bf16[320,256]{1,0:T(8,128)(2,1)S(1)}, bf16[320,256]{1,0:T(8,128)(2,1)S(1)}, u32[]{:S(2)}, u32[]{:S(2)}) collective-permute-start(bf16[320,256]{1,0:T(8,128)(2,1)S(1)} %shard_map.105.rest_0_), channel_id=1, source_target_pairs={{0,4},{4,8},{8,12},{12,0},{1,5},{5,9},{9,13},{13,1},{2,6},{6,10},{... | collective-permute-start | bytes 491528 | tf_op jit(solution)/shard_map/ppermute | solution.py:314
  85.2 16.2 %collective-permute-start.16 = (bf16[320,256]{1,0:T(8,128)(2,1)S(1)}, bf16[320,256]{1,0:T(8,128)(2,1)S(1)}, u32[]{:S(2)}, u32[]{:S(2)}) collective-permute-start(bf16[320,256]{1,0:T(8,128)(2,1)S(1)} %shard_map.105.rest_0_), channel_id=1, source_target_pairs={{0,8},{4,12},{8,0},{12,4},{1,9},{5,13},{9,1},{13,5},{2,10},{6,14},... | collective-permute-start | bytes 491528 | tf_op jit(solution)/shard_map/ppermute | solution.py:314
  88.6 12.8 %collective-permute-start.17 = (bf16[320,256]{1,0:T(8,128)(2,1)S(1)}, bf16[320,256]{1,0:T(8,128)(2,1)S(1)}, u32[]{:S(2)}, u32[]{:S(2)}) collective-permute-start(bf16[320,256]{1,0:T(8,128)(2,1)S(1)} %shard_map.105.rest_0_), channel_id=1, source_target_pairs={{0,12},{4,0},{8,4},{12,8},{1,13},{5,1},{9,5},{13,9},{2,14},{6,2},{... | collective-permute-start | bytes 491528 | tf_op jit(solution)/shard_map/ppermute | solution.py:314
  93.1 13.6 %collective-permute-start.24 = (bf16[320,256]{1,0:T(8,128)(2,1)S(1)}, bf16[320,256]{1,0:T(8,128)(2,1)S(1)}, u32[]{:S(2)}, u32[]{:S(2)}) collective-permute-start(bf16[320,256]{1,0:T(8,128)(2,1)S(1)} %shard_map.107.rest_0_), channel_id=1, source_target_pairs={{0,4},{4,8},{8,12},{12,0},{1,5},{5,9},{9,13},{13,1},{2,6},{6,10},{... | collective-permute-start | bytes 491528 | tf_op jit(solution)/shard_map/ppermute | solution.py:314
  95.2 13.7 %collective-permute-start.25 = (bf16[320,256]{1,0:T(8,128)(2,1)S(1)}, bf16[320,256]{1,0:T(8,128)(2,1)S(1)}, u32[]{:S(2)}, u32[]{:S(2)}) collective-permute-start(bf16[320,256]{1,0:T(8,128)(2,1)S(1)} %shard_map.107.rest_0_), channel_id=1, source_target_pairs={{0,8},{4,12},{8,0},{12,4},{1,9},{5,13},{9,1},{13,5},{2,10},{6,14},... | collective-permute-start | bytes 491528 | tf_op jit(solution)/shard_map/ppermute | solution.py:314
  95.2 13.7 %collective-permute-start.26 = (bf16[320,256]{1,0:T(8,128)(2,1)S(1)}, bf16[320,256]{1,0:T(8,128)(2,1)S(1)}, u32[]{:S(2)}, u32[]{:S(2)}) collective-permute-start(bf16[320,256]{1,0:T(8,128)(2,1)S(1)} %shard_map.107.rest_0_), channel_id=1, source_target_pairs={{0,12},{4,0},{8,4},{12,8},{1,13},{5,1},{9,5},{13,9},{2,14},{6,2},{... | collective-permute-start | bytes 491528 | tf_op jit(solution)/shard_map/ppermute | solution.py:314
  113.9 2.0 %collective-permute-start.27 = (bf16[160,1792]{1,0:T(8,128)(2,1)S(1)}, bf16[160,1792]{1,0:T(8,128)(2,1)S(1)}, u32[]{:S(2)}, u32[]{:S(2)}) collective-permute-start(bf16[160,1792]{1,0:T(8,128)(2,1)S(1)} %get-tuple-element.11), channel_id=1, source_target_pairs={{0,1},{1,0},{2,3},{3,2},{4,5},{5,4},{6,7},{7,6},{8,9},{9,8},{10,11... | collective-permute-start | bytes 1720328 | tf_op jit(solution)/shard_map/ppermute | solution.py:346
  116.1 8.9 %collective-permute-start.28 = (bf16[80,1792]{1,0:T(8,128)(2,1)S(1)}, bf16[80,1792]{1,0:T(8,128)(2,1)S(1)}, u32[]{:S(2)}, u32[]{:S(2)}) collective-permute-start(bf16[80,1792]{1,0:T(8,128)(2,1)S(1)} %fusion.1), channel_id=1, source_target_pairs={{0,2},{1,3},{2,0},{3,1},{4,6},{5,7},{6,4},{7,5},{8,10},{9,11},{10,... | collective-permute-start | bytes 860168 | tf_op jit(solution)/shard_map/ppermute | solution.py:351
  (7 other events, 60.6 us)

commit v2 on v0

--- a/solution.py
+++ b/solution.py
@@ -1,9 +1,15 @@
+import functools
 import math
 
 import jax
 import jax.numpy as jnp
 from jax import lax
+from jax.experimental import pallas as pl
+from jax.experimental.pallas import tpu as pltpu
 from jax.sharding import PartitionSpec as P
+
+CHUNKS = 2
+VMEM_BYTES = 50 * 1024 * 1024
 
 
 def on_device(
@@ -83,6 +89,382 @@
     return (merged_query_weight, mixed)
 
 
+def cyclic(n, k):
+    return [(i, (i + k) % n) for i in range(n)]
+
+
+def flipped(n, bit):
+    return [(i, i ^ bit) for i in range(n)]
+
+
+def call(body, outs, args, blocks=None, out_blocks=None, steps=1, scratch=(), flops=0, moved=0):
+    whole = pl.BlockSpec(memory_space=pltpu.VMEM)
+    blocks = blocks or {}
+    return pl.pallas_call(
+        body,
+        out_shape=outs,
+        grid_spec=pltpu.PrefetchScalarGridSpec(
+            num_scalar_prefetch=1,
+            grid=(steps,),
+            in_specs=[blocks.get(i, whole) for i in range(len(args) - 1)],
+            out_specs=out_blocks if out_blocks is not None else jax.tree.map(lambda o: whole, outs),
+            scratch_shapes=list(scratch),
+        ),
+        compiler_params=pltpu.CompilerParams(vmem_limit_bytes=VMEM_BYTES),
+        cost_estimate=pl.CostEstimate(flops=flops, bytes_accessed=moved, transcendentals=0),
+    )(*args)
+
+
+def three_terms(p):
+    out = []
+    for _ in range(3):
+        t = p.astype(jnp.bfloat16).astype(jnp.float32)
+        out.append(t)
+        p = p - t
+    return out
+
+
+def pack_body(n, kq, vq, aq, wide, kvr, sc, x_ref, kv_ref, at_ref, pos_ref, w_ref, first, *rest):
+    others, turn, turned = rest[:-2], rest[-2], rest[-1]
+    h = sc[2]
+    tok = x_ref.shape[0]
+    rope = kv_ref.shape[1] - kvr
+    half = w_ref.shape[0]
+    pieces = 1 + len(others)
+    turn[...] = jnp.zeros_like(turn)
+    turn[:tok, :rope] = kv_ref[:, kvr:].astype(jnp.float32)
+    start = pos_ref[0:1, 0:1].astype(jnp.float32)
+    for i, t in enumerate(three_terms(start)):
+        turn[tok + i : tok + i + 1, :] = jnp.broadcast_to(t, (1, turn.shape[1]))
+    turned[...] = turn[...].T
+    xs = x_ref[:, pl.ds(pl.multiple_of(h * kq, 128), kq)]
+    ats = at_ref[pl.ds(pl.multiple_of(h * aq, 16), aq), :]
+    keys = kv_ref[:, pl.ds(pl.multiple_of(h * vq, 128), vq)]
+    ropes = turned[pl.ds(pl.multiple_of(h * aq, 16), aq), :].astype(jnp.bfloat16)
+    third = (tok + aq) // 3
+    tail = jnp.concatenate([keys, ropes], axis=0)
+    for j in range(n):
+        at = j * pieces * wide
+        first[j, :half, :] = w_ref[:, at : at + wide]
+        first[j, half : half + tok, :] = xs
+        first[j, half + tok : half + tok + aq, :] = ats
+        for i in range(3):
+            first[j, half + tok + aq :, i * vq : (i + 1) * vq] = tail[i * third : (i + 1) * third]
+        for c, other in enumerate(others):
+            at = (j * pieces + c + 1) * wide
+            other[j] = w_ref[:, at : at + wide]
+
+
+def split_body(n, half, sc, u_ref, *outs):
+    for k in range(1, n):
+        src = lax.rem(sc[0] - k + n, n)
+        outs[0][k - 1] = u_ref[src, :half]
+        if len(outs) > 1:
+            outs[1][k - 1] = u_ref[src, half:]
+
+
+def unpack_body(n, nh, kq, vq, aq, kvr, sc, x_ref, kv_ref, at_ref, pos_ref, *rest):
+    stacks, (xo, kvo, ao, bias), turn = rest[:nh], rest[nh : nh + 4], rest[nh + 4]
+    s, h = sc[0], sc[2]
+    tok, depth = x_ref.shape[0], at_ref.shape[1]
+    rope = kv_ref.shape[1] - kvr
+    third = (tok + aq) // 3
+    tokens = bias.shape[0]
+    row = pl.multiple_of(s * tok, 16)
+    xo[pl.ds(row, tok), :] = x_ref[...]
+    kvo[pl.ds(row, tok), :] = kv_ref[...]
+    ao[:, pl.ds(pl.multiple_of(s * depth, 128), depth)] = at_ref[...]
+    starts = [(s, pos_ref[0:1, 0:1].astype(jnp.float32))]
+    turn[...] = jnp.zeros_like(turn)
+    for k in range(1, n):
+        src = lax.rem(s - k + n, n)
+        rows = pl.ds(pl.multiple_of(src * tok, 16), tok)
+        for j in range(nh):
+            hh = h ^ j
+            got = stacks[j].at[k - 1]
+            xo[rows, pl.ds(pl.multiple_of(hh * kq, 128), kq)] = got[:tok, :]
+            arow = pl.ds(pl.multiple_of(hh * aq, 16), aq)
+            ao[arow, pl.ds(pl.multiple_of(src * depth, 128), depth)] = got[tok : tok + aq, :]
+            tail = jnp.concatenate([got[tok + aq :, i * vq : (i + 1) * vq] for i in range(3)], axis=0)
+            kvo[rows, pl.ds(pl.multiple_of(hh * vq, 128), vq)] = tail[:tok]
+            turn[arow, :] = tail[tok:].astype(jnp.float32)
+        turned = turn[...].T
+        kvo[rows, kvr:] = turned[:tok, :rope].astype(jnp.bfloat16)
+        starts.append((src, turned[tok : tok + 1, :1] + turned[tok + 1 : tok + 2, :1] + turned[tok + 2 : tok + 3, :1]))
+
+    def places(shape, dim):
+        index = lax.broadcasted_iota(jnp.int32, shape, dim)
+        block = index // tok
+        out = (index - block * tok).astype(jnp.float32)
+        for src, start in starts:
+            out = out + jnp.where(block == src, start, 0.0)
+        return out
+
+    seen = places((1, tokens), 1) <= places((tokens, 1), 0)
+    bias[...] = jnp.where(seen, 0.0, -1e30)
+
+
+def attend_body(n, nope, scale, sc, x_ref, at_ref, b_ref, w_ref, kv_ref, bias_ref, ku_ref, vu_ref, u_ref, y_ref, out, raw):
+    s, g = sc[0], sc[1]
+    depth = w_ref.shape[0]
+    half = depth // 2
+    raw[pl.ds(pl.multiple_of(s * depth, 16), depth), :] = w_ref[...]
+    for k in range(1, n):
+        src = lax.rem(s - k + n, n)
+        raw[pl.ds(pl.multiple_of(src * depth + g * half, 16), half), :] = u_ref[src, :half]
+        raw[pl.ds(pl.multiple_of(src * depth + (1 - g) * half, 16), half), :] = y_ref[k - 1]
+    add = lax.dot_general(
+        at_ref[...], b_ref[...], (((0,), (0,)), ((), ())), preferred_element_type=jnp.float32
+    )
+    merged = (raw[...].astype(jnp.float32) + add).astype(jnp.bfloat16)
+    q = jnp.dot(x_ref[...], merged, preferred_element_type=jnp.float32)
+    heads, kvr, vdim = vu_ref.shape
+    width = q.shape[1] // heads
+    lat, rope_key = kv_ref[:, :kvr], kv_ref[:, kvr:]
+    bias = bias_ref[...]
+    nt = (((1,), (1,)), ((), ()))
+    for j in range(heads):
+        qn = q[:, j * width : j * width + nope].astype(jnp.bfloat16)
+        qr = q[:, j * width + nope : (j + 1) * width].astype(jnp.bfloat16)
+        absorbed = jnp.dot(qn, ku_ref[j], preferred_element_type=jnp.float32).astype(jnp.bfloat16)
+        scores = lax.dot_general(absorbed, lat, nt, preferred_element_type=jnp.float32)
+        scores = scores + lax.dot_general(qr, rope_key, nt, preferred_element_type=jnp.float32)
+        scores = scores * scale + bias
+        top = jnp.max(scores, axis=1, keepdims=True)
+        e = jnp.exp(scores - top)
+        total = jnp.sum(e, axis=1, keepdims=True)
+        ctx = jnp.dot(e.astype(jnp.bfloat16), lat, preferred_element_type=jnp.float32)
+        ctx = (ctx / total).astype(jnp.bfloat16)
+        ho = jnp.dot(ctx, vu_ref[j], preferred_element_type=jnp.float32)
+        out[:, j * vdim : (j + 1) * vdim] = ho.astype(jnp.bfloat16)
+
+
+def gather_line(x):
+    left = lax.ppermute(x, "seq", [(0, 1), (1, 2), (2, 3)])
+    right = lax.ppermute(x, "seq", [(1, 0), (2, 1), (3, 2)])
+    two = lax.ppermute(x, "seq", cyclic(4, 2))
+    three = lax.ppermute(two, "seq", [(2, 3), (1, 0)])
+    return [x, left, right, two, three]
+
+
+def place_line(s, slots, lhs):
+    own, left, right, two, three = slots
+    width = own.shape[1]
+
+    def put(src, ref):
+        lhs[:, pl.ds(pl.multiple_of(src * width, 128), width)] = ref[...]
+
+    put(s, own)
+    put(lax.rem(s + 2, 4), two)
+
+    @pl.when(s > 0)
+    def _():
+        put(s - 1, left)
+
+    @pl.when(s < 3)
+    def _():
+        put(s + 1, right)
+
+    @pl.when((s == 0) | (s == 3))
+    def _():
+        put(3 - s, three)
+
+
+def first_body(sc, w_ref, *rest):
+    slots, acc, lhs = rest[:5], rest[5], rest[6]
+
+    @pl.when(pl.program_id(0) == 0)
+    def _():
+        place_line(sc[0], slots, lhs)
+
+    w = w_ref[...].reshape(lhs.shape[1], w_ref.shape[-1])
+    acc[...] = jnp.dot(lhs[...], w, preferred_element_type=jnp.float32)
+
+
+def last_body(nh, tok, sc, w_ref, acc, *rest):
+    slots, (keep, send), lhs, tot = rest[:5], rest[5:7], rest[7], rest[8]
+
+    @pl.when(pl.program_id(0) == 0)
+    def _():
+        place_line(sc[0], slots, lhs)
+
+    w = w_ref[...].reshape(lhs.shape[1], w_ref.shape[-1])
+    tot[...] = acc[...] + jnp.dot(lhs[...], w, preferred_element_type=jnp.float32)
+    core = sc[2] % 2
+    for i in range(nh // 2):
+        mine = pl.ds(pl.multiple_of((2 * i + core) * tok, 16), tok)
+        theirs = pl.ds(pl.multiple_of((2 * i + 1 - core) * tok, 16), tok)
+        keep[i * tok : (i + 1) * tok, :] = tot[mine, :]
+        send[i * tok : (i + 1) * tok, :] = tot[theirs, :].astype(jnp.bfloat16)
+
+
+def by_heads(x, kv, pos, wq, down, up, ku, vu, wo):
+    n, nh = lax.axis_size("seq"), lax.axis_size("head")
+    s, g, h = lax.axis_index("seq"), lax.axis_index("groups"), lax.axis_index("head")
+    sc = jnp.stack([s, g, h]).astype(jnp.int32)
+    bf, f32 = jnp.bfloat16, jnp.float32
+    tok, depth = x.shape
+    heads, nope, kvr = ku.shape
+    vdim = vu.shape[2]
+    rope = kv.shape[1] - kvr
+    rank = down.shape[1]
+    rows, cols = wq.shape
+    half = rows // 2
+    tokens = n * tok
+    per = heads // n // CHUNKS
+    wide = per * (cols // heads)
+    kq, vq, aq = depth // nh, kvr // nh, rank // nh
+    extra = tok + aq + (tok + aq) // 3
+    at = down.T
+    pos2 = pos[None, :]
+
+    def like(*shape, dtype=bf):
+        return jax.ShapeDtypeStruct(shape, dtype)
+
+    units = call(
+        functools.partial(pack_body, n, kq, vq, aq, wide, kvr),
+        tuple([like(n, half + extra, wide)] + [like(n, half, wide)] * (CHUNKS - 1)),
+        [sc, x, kv, at, pos2, wq],
+        blocks={4: pl.BlockSpec((half, cols), lambda i, sc: (sc[1], 0))},
+        scratch=[pltpu.VMEM((128, 128), f32)] * 2,
+        moved=4 * half * cols,
+    )
+    moved, passed, stack = [], [], None
+    for c in range(CHUNKS):
+        unit = units[c]
+        if c:
+            unit, _ = lax.optimization_barrier((unit, moved[c - 1]))
+        got = lax.all_to_all(unit, "seq", 0, 0, tiled=True)
+        moved.append(got)
+        outs = [like(n - 1, half, wide)] + ([] if c else [like(n - 1, extra, wide)])
+        outs = call(
+            functools.partial(split_body, n, half),
+            tuple(outs),
+            [sc, got],
+            moved=4 * got.size,
+        )
+        passed.append(lax.ppermute(outs[0], "groups", cyclic(2, 1)))
+        if c == 0:
+            stack = outs[1]
+    across = lax.ppermute(stack, "head", flipped(nh, 2))
+    stacks = [
+        stack,
+        lax.ppermute(stack, "head", flipped(nh, 1)),
+        across,
+        lax.ppermute(across, "head", flipped(nh, 1)),
+    ]
+    x_all, kv_all, at_all, bias = call(
+        functools.partial(unpack_body, n, nh, kq, vq, aq, kvr),
+        (
+            like(tokens, depth),
+            like(tokens, kvr + rope),
+            like(rank, n * rows),
+            like(tokens, tokens, dtype=f32),
+        ),
+        [sc, x, kv, at, pos2] + stacks,
+        scratch=[pltpu.VMEM((128, 128), f32)],
+        moved=4 * tokens * depth,
+    )
+
+    merged = (wq.astype(f32) + jnp.dot(down, up, preferred_element_type=f32)).astype(bf)
+
+    scale = 1.0 / math.sqrt(nope + rope)
+    slots = []
+    for c in range(CHUNKS):
+        def column(i, sc, c=c):
+            return (0, sc[0] * CHUNKS + c)
+
+        def leading(i, sc, c=c):
+            return (sc[0] * CHUNKS + c, 0, 0)
+
+        ho = call(
+            functools.partial(attend_body, n, nope, scale),
+            like(tokens, per * vdim),
+            [sc, x_all, at_all, up, wq, kv_all, bias, ku, vu, moved[c], passed[c]],
+            blocks={
+                2: pl.BlockSpec((rank, wide), column),
+                3: pl.BlockSpec((rows, wide), column),
+                6: pl.BlockSpec((per, nope, kvr), leading),
+                7: pl.BlockSpec((per, kvr, vdim), leading),
+            },
+            scratch=[pltpu.VMEM((n * rows, wide), bf)],
+            flops=2 * tokens * per * (depth * wide // per + 2 * nope * kvr + 2 * tokens * kvr),
+            moved=4 * n * rows * wide,
+        )
+        slots.append(gather_line(ho))
+
+    w4 = wo.reshape(n, CHUNKS, per * vdim, wo.shape[1])
+    total = wo.shape[1]
+    tile = 256
+    tiles = total // tile
+    lhs = pltpu.VMEM((tokens, n * per * vdim), bf)
+
+    def weights(c, begin):
+        return pl.BlockSpec((n, None, per * vdim, tile), lambda i, sc: (0, c, 0, i + begin))
+
+    def band(count, begin=0):
+        return pl.BlockSpec((count, tile), lambda i, sc: (0, i + begin))
+
+    cost = dict(flops=2 * tokens * n * per * vdim * total, moved=w4.size * 2 // CHUNKS)
+    acc = call(
+        first_body,
+        like(tokens, total, dtype=f32),
+        [sc, w4] + slots[0],
+        blocks={0: weights(0, 0)},
+        out_blocks=band(tokens),
+        steps=tiles,
+        scratch=[lhs],
+        **cost,
+    )
+    side = h // 2
+    bands = []
+    cut = (tiles + 1) // 2
+    for begin, count in ((0, cut), (cut, tiles - cut)):
+        keep, send = call(
+            functools.partial(last_body, nh, tok),
+            (
+                like(nh // 2 * tok, count * tile, dtype=f32),
+                like(nh // 2 * tok, count * tile),
+            ),
+            [sc, w4, acc] + slots[1],
+            blocks={0: weights(1, begin), 1: band(tokens, begin)},
+            out_blocks=(band(nh // 2 * tok), band(nh // 2 * tok)),
+            steps=count,
+            scratch=[lhs, pltpu.VMEM((tokens, tile), f32)],
+            flops=cost["flops"] * count // tiles,
+            moved=cost["moved"] * count // tiles,
+        )
+        got = lax.ppermute(send, "head", flipped(nh, 1))
+        pair = (keep + got.astype(f32)).reshape(nh // 2, tok, count * tile)
+        out = lax.dynamic_index_in_dim(pair, side, 0, keepdims=False)
+        away = lax.dynamic_index_in_dim(pair, 1 - side, 0, keepdims=False).astype(bf)
+        out = out + lax.ppermute(away, "head", flipped(nh, 2)).astype(f32)
+        bands.append(out.astype(bf))
+    return merged, jnp.concatenate(bands, axis=1)
+
+
+def fits(mesh, shapes):
+    n, nh = mesh.shape["seq"], mesh.shape["head"]
+    x, kv, _, wq, down, _, ku, vu, wo = shapes
+    tok, kvr, rank = x[0], ku[2], down[1]
+    if mesh.shape["groups"] != 2 or n != 4 or nh != 4 or CHUNKS != 2 or ku[0] % (n * CHUNKS):
+        return False
+    wide = wq[1] // n // CHUNKS
+    return (
+        (tok + rank // nh) % 48 == 0
+        and tok % 16 == 0
+        and tok + 3 <= 128
+        and rank <= 128
+        and rank // nh % 16 == 0
+        and kv[1] - kvr == rank
+        and kvr // nh == 128
+        and x[1] // nh == wide
+        and down[0] == wide
+        and wide == 3 * 128
+        and wo[1] % 256 == 0
+    )
+
+
 def solution(mesh):
     placed = (
         P(("groups", "seq"), None),
@@ -95,8 +477,13 @@
         P("head", None, None),
         P("head", "seq"),
     )
+
+    def local(*args):
+        chosen = by_heads if fits(mesh, [a.shape for a in args]) else on_device
+        return chosen(*args)
+
     return jax.shard_map(
-        on_device,
+        local,
         mesh=mesh,
         in_specs=placed,
         out_specs=(P(("groups", "seq"), "head"), P(("groups", "head"), "seq")),

time: 269 us -> 118 us (0.44)
  waiting for transfers between devices: 194 us -> 22.8 us
  Pallas kernels: 0 us -> 28.9 us
  starting transfers between devices: 0.12 us -> 27.4 us
  matrix products: 20.6 us -> 2.2 us
  between operations: 14.5 us -> 0.94 us
  blocking collectives: 34.6 us -> 30.6 us
    all_gather x2 -> x0, waiting for transfers between devices: 169 us -> none  [the longest x1 138 us: on_device(): lax.all_gather(merged_query_weight, 'seq', axis=0, tiled=True)]
    all_to_all x0 -> x1, blocking collectives: none -> 30.6 us  [by_heads(): got = lax.all_to_all(unit, 'seq', 0, 0, tiled=True)]
    pallas_call x0 -> x9, Pallas kernels: none -> 28.9 us  [call(): pl.pallas_call(body, out_shape=outs, grid_spec=pltpu.PrefetchScalarGridSp...]
    all_gather x1 -> x0, blocking collectives: 24.7 us -> none  [on_device(): key_rows = lax.all_gather(key_value_latents, 'seq', axis=0, tiled=True)]
    reduce_scatter x1 -> x0, waiting for transfers between devices: 24.6 us -> none  [on_device(): lax.psum_scatter(partial_value.astype(jnp.bfloat16), 'head', scatter_dime...]
    ppermute x0 -> x17, starting transfers between devices: none -> 23.8 us  [the longest x2 9.11 us: gather_line(): left = lax.ppermute(x, 'seq', [(0, 1), (1, 2), (2, 3)])]
    dot_general x7 -> x1, matrix products: 20.6 us -> 2.2 us  [by_heads(): jnp.dot(down, up, preferred_element_type=f32)]
    ppermute x0 -> x17, waiting for transfers between devices: none -> 11.9 us  [the longest x2 5.9 us: by_heads(): out = out + lax.ppermute(away, 'head', flipped(nh, 2)).astype(f32)]
  transfers between devices with their start and end apart: 3 -> 18, of which waited for: 3 -> 7; matrix products, arithmetic and copies ran while one was open for 0% -> 2% of each run, Pallas kernels for 0% -> 19%
where the time goes in v2:
time: 118 us; the launch traced here: 117 us
  blocking collectives  30.6 us (26%)
  Pallas kernels  28.9 us (24%)
  starting transfers between devices  27.4 us (23%)
  waiting for transfers between devices  22.8 us (19%)
  local copies, waits for them, and re-layouts  3.37 us (3%)
  matrix products  2.2 us (2%)
    all_to_all x1, blocking collectives, by_heads(): got = lax.all_to_all(unit, 'seq', 0, 0, tiled=True)  30.6 us
    pallas_call x9, Pallas kernels, call(): pl.pallas_call(body, out_shape=outs, grid_spec=pltpu.PrefetchScalarGridSp...  28.9 us
    all_to_all x1, waiting for transfers between devices, by_heads(): got = lax.all_to_all(unit, 'seq', 0, 0, tiled=True)  10.9 us
    ppermute x2, starting transfers between devices, gather_line(): left = lax.ppermute(x, 'seq', [(0, 1), (1, 2), (2, 3)])  9.11 us
    ppermute x2, waiting for transfers between devices, by_heads(): out = out + lax.ppermute(away, 'head', flipped(nh, 2)).astype(f32)  5.9 us
    all_to_all x1, starting transfers between devices, by_heads(): got = lax.all_to_all(unit, 'seq', 0, 0, tiled=True)  3.61 us
    ppermute x2, waiting for transfers between devices, gather_line(): three = lax.ppermute(two, 'seq', [(2, 3), (1, 0)])  3.39 us
    unnamed x20, local copies, waits for them, and re-layouts  3.32 us
  transfers between devices with their start and end apart: 18, of which 7 were waited for; matrix products, arithmetic and copies ran while one was open for 2% of the time, Pallas kernels for 19%

profile of v2, /device:TPU:0, one launch (start us, length us, event | category | flops | bytes accessed | tf_op | source)
XLA Modules:
  0.0 117.2 jit_solution(16036270453791486670)
XLA Ops:
  0.7 0.9 copy-done.1
  1.7 0.8 copy-done.3
  2.5 0.9 copy-done.5
  4.0 2.8 %shard_map.104 = (bf16[4,320,384]{2,1,0:T(8,128)(2,1)S(1)}, bf16[4,192,384]{2,1,0:T(8,128)(2,1)}) custom-call(s32[3]{0:T(128)S(1)} %pad_add_fusion.sc, bf16[80,1536]{1,0:T(8,128)(2,1)S(1)} %copy-done.1, bf16[80,576]{1,0:T(8,128)(2,1)S(1)} %copy-done.5, bf16[64,384]{1,0:T(8,128)(2,1)S(1)} %bitcast.22, s32[1,80]{1,0:T(1,128)S(1)} %bitcast.24, ...), custom_call_target="tpu_custom_call" | custom-call | bytes 2359296 | tf_op jit(solution)/shard_map/pallas_call | solution.py:103
  6.8 30.6 %all_to_all.10.u_ref = bf16[4,320,384]{2,1,0:T(8,128)(2,1)S(1)} all-to-all(bf16[4,320,384]{2,1,0:T(8,128)(2,1)S(1)} %get-tuple-element.15), channel_id=1, replica_groups=mesh['groups'=2,'seq'=4,'head'=4] {'seq'}, dimensions={0} | all-to-all | bytes 1966080 | tf_op jit(solution)/shard_map/all_to_all | solution.py:337
  37.4 3.6 %all-to-all-start.1 = ((bf16[4,192,384]{2,1,0:T(8,128)(2,1)}), bf16[4,192,384]{2,1,0:T(8,128)(2,1)S(1)}, u32[]{:S(2)}, u32[]{:S(2)}) async-start(bf16[4,192,384]{2,1,0:T(8,128)(2,1)} %get-tuple-element.23), calls=%async_computation.1 | async-start | bytes 1179648 | tf_op jit(solution)/shard_map/all_to_all | solution.py:337
  41.0 1.4 %shard_map.105 = (bf16[3,192,384]{2,1,0:T(8,128)(2,1)}, bf16[3,128,384]{2,1,0:T(8,128)(2,1)S(1)}) custom-call(s32[3]{0:T(128)S(1)} %pad_add_fusion.sc, bf16[4,320,384]{2,1,0:T(8,128)(2,1)S(1)} %all_to_all.10.u_ref), custom_call_target="tpu_custom_call" | custom-call | bytes 1966080 | tf_op jit(solution)/shard_map/pallas_call | solution.py:103
  42.4 1.5 %collective-permute-start.1 = (bf16[3,128,384]{2,1,0:T(8,128)(2,1)S(1)}, bf16[3,128,384]{2,1,0:T(8,128)(2,1)S(1)}, u32[]{:S(2)}, u32[]{:S(2)}) collective-permute-start(bf16[3,128,384]{2,1,0:T(8,128)(2,1)S(1)} %get-tuple-element.16.rest_0_), channel_id=1, source_target_pairs={{0,2},{1,3},{2,0},{3,1},{4,6},{5,7},{6,4},{7,5},{8,10},{9,11},{10,... | collective-permute-start | bytes 884744 | tf_op jit(solution)/shard_map/ppermute | solution.py:349
  43.9 1.5 %collective-permute-start.3 = (bf16[3,192,384]{2,1,0:T(8,128)(2,1)}, bf16[3,192,384]{2,1,0:T(8,128)(2,1)S(1)}, u32[]{:S(2)}, u32[]{:S(2)}) collective-permute-start(bf16[3,192,384]{2,1,0:T(8,128)(2,1)} %get-tuple-element.21), channel_id=1, source_target_pairs={{0,16},{16,0},{1,17},{17,1},{2,18},{18,2},{3,19},{19,3},{4,20},{20... | collective-permute-start | bytes 1327112 | tf_op jit(solution)/shard_map/ppermute | solution.py:346
  45.4 10.9 %all-to-all-done.1.u_ref = bf16[4,192,384]{2,1,0:T(8,128)(2,1)S(1)} async-done(((bf16[4,192,384]{2,1,0:T(8,128)(2,1)}), bf16[4,192,384]{2,1,0:T(8,128)(2,1)S(1)}, u32[]{:S(2)}, u32[]{:S(2)}) %all-to-all-start.1) | async-done | bytes 589856 | tf_op jit(solution)/shard_map/all_to_all | solution.py:337
  56.9 1.6 %collective-permute-start.8 = (bf16[3,192,384]{2,1,0:T(8,128)(2,1)S(1)}, bf16[3,192,384]{2,1,0:T(8,128)(2,1)S(1)}, u32[]{:S(2)}, u32[]{:S(2)}) collective-permute-start(bf16[3,192,384]{2,1,0:T(8,128)(2,1)S(1)} %shard_map.109), channel_id=1, source_target_pairs={{0,16},{16,0},{1,17},{17,1},{2,18},{18,2},{3,19},{19,3},{4,20},{20... | collective-permute-start | bytes 1327112 | tf_op jit(solution)/shard_map/ppermute | solution.py:346
  59.0 1.1 collective-permute-done.rest_1_
  60.5 1.0 shard_map.106
  61.5 4.5 %shard_map.107.rest_0_ = bf16[320,256]{1,0:T(8,128)(2,1)S(1)} custom-call(s32[3]{0:T(128)S(1)} %pad_add_fusion.sc, bf16[320,1536]{1,0:T(8,128)(2,1)S(1)} %get-tuple-element.17.x_ref, bf16[64,1536]{1,0:T(8,128)(2,1)S(1)} %get-tuple-element.18.at_ref, bf16[64,3072]{1,0:T(8,128)(2,1)S(1)} %copy-done, bf16[384,3072]{1,0:T(8,128)(2,1)} %w_ref.5, ...), custom_call_target="tpu_custom_call" | custom-call | flops 964689920 | bytes 2359296 | tf_op jit(solution)/shard_map/pallas_call | solution.py:103
  66.0 3.9 %collective-permute-start.4 = (bf16[320,256]{1,0:T(8,128)(2,1)S(1)}, bf16[320,256]{1,0:T(8,128)(2,1)S(1)}, u32[]{:S(2)}, u32[]{:S(2)}) collective-permute-start(bf16[320,256]{1,0:T(8,128)(2,1)S(1)} %shard_map.107.rest_0_), channel_id=1, source_target_pairs={{0,4},{4,8},{8,12},{1,5},{5,9},{9,13},{2,6},{6,10},{10,14},{3,7},{... | collective-permute-start | bytes 491528 | tf_op jit(solution)/shard_map/ppermute | solution.py:243
  70.0 4.5 %shard_map.110.rest_0_ = bf16[320,256]{1,0:T(8,128)(2,1)S(1)} custom-call(s32[3]{0:T(128)S(1)} %pad_add_fusion.sc, bf16[320,1536]{1,0:T(8,128)(2,1)S(1)} %get-tuple-element.17.x_ref, bf16[64,1536]{1,0:T(8,128)(2,1)S(1)} %get-tuple-element.18.at_ref, bf16[64,3072]{1,0:T(8,128)(2,1)S(1)} %copy-done, bf16[384,3072]{1,0:T(8,128)(2,1)} %w_ref.5, ...), custom_call_target="tpu_custom_call" | custom-call | flops 964689920 | bytes 2359296 | tf_op jit(solution)/shard_map/pallas_call | solution.py:103
  74.5 1.0 collective-permute-start.11
  75.4 1.3 %collective-permute-start.5 = (bf16[320,256]{1,0:T(8,128)(2,1)S(1)}, bf16[320,256]{1,0:T(8,128)(2,1)S(1)}, u32[]{:S(2)}, u32[]{:S(2)}) collective-permute-start(bf16[320,256]{1,0:T(8,128)(2,1)S(1)} %shard_map.107.rest_0_), channel_id=1, source_target_pairs={{4,0},{8,4},{12,8},{5,1},{9,5},{13,9},{6,2},{10,6},{14,10},{7,3},{... | collective-permute-start | bytes 491528 | tf_op jit(solution)/shard_map/ppermute | solution.py:244
  76.7 1.3 %collective-permute-start.7 = (bf16[320,256]{1,0:T(8,128)(2,1)S(1)}, bf16[320,256]{1,0:T(8,128)(2,1)S(1)}, u32[]{:S(2)}, u32[]{:S(2)}) collective-permute-start(bf16[320,256]{1,0:T(8,128)(2,1)S(1)} %collective-permute-done.6.rest_3_), channel_id=1, source_target_pairs={{8,12},{4,0},{9,13},{5,1},{10,14},{6,2},{11,15},{7,3},{24,28},{20,... | collective-permute-start | bytes 491528 | tf_op jit(solution)/shard_map/ppermute | solution.py:246
  78.0 1.3 %collective-permute-start.10 = (bf16[320,256]{1,0:T(8,128)(2,1)S(1)}, bf16[320,256]{1,0:T(8,128)(2,1)S(1)}, u32[]{:S(2)}, u32[]{:S(2)}) collective-permute-start(bf16[320,256]{1,0:T(8,128)(2,1)S(1)} %shard_map.110.rest_0_), channel_id=1, source_target_pairs={{4,0},{8,4},{12,8},{5,1},{9,5},{13,9},{6,2},{10,6},{14,10},{7,3},{... | collective-permute-start | bytes 491528 | tf_op jit(solution)/shard_map/ppermute | solution.py:244
  79.3 5.2 %collective-permute-start.9 = (bf16[320,256]{1,0:T(8,128)(2,1)S(1)}, bf16[320,256]{1,0:T(8,128)(2,1)S(1)}, u32[]{:S(2)}, u32[]{:S(2)}) collective-permute-start(bf16[320,256]{1,0:T(8,128)(2,1)S(1)} %shard_map.110.rest_0_), channel_id=1, source_target_pairs={{0,4},{4,8},{8,12},{1,5},{5,9},{9,13},{2,6},{6,10},{10,14},{3,7},{... | collective-permute-start | bytes 491528 | tf_op jit(solution)/shard_map/ppermute | solution.py:243
  84.5 1.1 collective-permute-done.11.rest_3_
  85.7 1.3 %collective-permute-start.12 = (bf16[320,256]{1,0:T(8,128)(2,1)S(1)}, bf16[320,256]{1,0:T(8,128)(2,1)S(1)}, u32[]{:S(2)}, u32[]{:S(2)}) collective-permute-start(bf16[320,256]{1,0:T(8,128)(2,1)S(1)} %collective-permute-done.11.rest_3_), channel_id=1, source_target_pairs={{8,12},{4,0},{9,13},{5,1},{10,14},{6,2},{11,15},{7,3},{24,28},{20,... | collective-permute-start | bytes 491528 | tf_op jit(solution)/shard_map/ppermute | solution.py:246
  87.0 3.4 %collective-permute-done.7.rest_4_ = bf16[320,256]{1,0:T(8,128)(2,1)S(1)} collective-permute-done((bf16[320,256]{1,0:T(8,128)(2,1)S(1)}, bf16[320,256]{1,0:T(8,128)(2,1)S(1)}, u32[]{:S(2)}, u32[]{:S(2)}) %collective-permute-start.7) | collective-permute-done | bytes 163872 | tf_op jit(solution)/shard_map/ppermute | solution.py:246
  90.4 6.3 %shard_map.108.acc = f32[320,1792]{1,0:T(8,128)S(1)} custom-call(s32[3]{0:T(128)S(1)} %pad_add_fusion.sc, bf16[4,2,256,1792]{3,2,1,0:T(8,128)(2,1)} %bitcast.26, bf16[320,256]{1,0:T(8,128)(2,1)S(1)} %shard_map.107.rest_0_, bf16[320,256]{1,0:T(8,128)(2,1)S(1)} %collective-permute-done.4.rest_1_, bf16[320,256]{1,0:T(8,128)(2,1)S(1)} %collective-permute-done.5.rest_2_, ...), custom_call_target="tpu_custom_call" | custom-call | flops 1174405120 | bytes 3670016 | tf_op jit(solution)/shard_map/pallas_call | solution.py:103
  96.8 3.8 %shard_map.112 = (f32[160,768]{1,0:T(8,128)S(1)}, bf16[160,768]{1,0:T(8,128)(2,1)S(1)}) custom-call(s32[3]{0:T(128)S(1)} %pad_add_fusion.sc, bf16[4,2,256,1792]{3,2,1,0:T(8,128)(2,1)} %bitcast.27, f32[320,1792]{1,0:T(8,128)S(1)} %shard_map.108.acc, bf16[320,256]{1,0:T(8,128)(2,1)S(1)} %shard_map.110.rest_0_, ...), custom_call_target="tpu_custom_call" | custom-call | flops 503316480 | bytes 1572864 | tf_op jit(solution)/shard_map/pallas_call | solution.py:103
  100.6 2.2 %add_convert_fusion = bf16[384,3072]{1,0:T(8,128)(2,1)} fusion(bf16[384,3072]{1,0:T(8,128)(2,1)S(1)} %copy-done.9, bf16[384,64]{0,1:T(8,128)(2,1)S(1)} %copy-done.4, bf16[64,3072]{1,0:T(8,128)(2,1)S(1)} %copy-done), kind=kOutput, calls=%fused_computation | convolution fusion | flops 154533888 | bytes 5160960 | tf_op jit(solution)/shard_map/dot_general | solution.py:369
  102.8 4.2 %shard_map.111 = (f32[160,1024]{1,0:T(8,128)S(1)}, bf16[160,1024]{1,0:T(8,128)(2,1)S(1)}) custom-call(s32[3]{0:T(128)S(1)} %pad_add_fusion.sc, bf16[4,2,256,1792]{3,2,1,0:T(8,128)(2,1)} %bitcast.28, f32[320,1792]{1,0:T(8,128)S(1)} %shard_map.108.acc, bf16[320,256]{1,0:T(8,128)(2,1)S(1)} %shard_map.110.rest_0_, ...), custom_call_target="tpu_custom_call" | custom-call | flops 671088640 | bytes 2097152 | tf_op jit(solution)/shard_map/pallas_call | solution.py:103
  107.6 1.6 %collective-permute-start.16 = (bf16[80,768]{1,0:T(8,128)(2,1)S(1)}, bf16[80,768]{1,0:T(8,128)(2,1)S(1)}, u32[]{:S(2)}, u32[]{:S(2)}) collective-permute-start(bf16[80,768]{1,0:T(8,128)(2,1)S(1)} %fusion.3), channel_id=1, source_target_pairs={{0,2},{1,3},{2,0},{3,1},{4,6},{5,7},{6,4},{7,5},{8,10},{9,11},{10,... | collective-permute-start | bytes 368648 | tf_op jit(solution)/shard_map/ppermute | solution.py:441
  109.4 1.2 %collective-permute-start.14 = (bf16[80,1024]{1,0:T(8,128)(2,1)S(1)}, bf16[80,1024]{1,0:T(8,128)(2,1)S(1)}, u32[]{:S(2)}, u32[]{:S(2)}) collective-permute-start(bf16[80,1024]{1,0:T(8,128)(2,1)S(1)} %fusion.2), channel_id=1, source_target_pairs={{0,2},{1,3},{2,0},{3,1},{4,6},{5,7},{6,4},{7,5},{8,10},{9,11},{10,... | collective-permute-start | bytes 491528 | tf_op jit(solution)/shard_map/ppermute | solution.py:441
  110.5 3.4 %collective-permute-done.16 = bf16[80,768]{1,0:T(8,128)(2,1)S(1)} collective-permute-done((bf16[80,768]{1,0:T(8,128)(2,1)S(1)}, bf16[80,768]{1,0:T(8,128)(2,1)S(1)}, u32[]{:S(2)}, u32[]{:S(2)}) %collective-permute-start.16) | collective-permute-done | bytes 122912 | tf_op jit(solution)/shard_map/ppermute | solution.py:441
  113.9 2.5 %collective-permute-done.14 = bf16[80,1024]{1,0:T(8,128)(2,1)S(1)} collective-permute-done((bf16[80,1024]{1,0:T(8,128)(2,1)S(1)}, bf16[80,1024]{1,0:T(8,128)(2,1)S(1)}, u32[]{:S(2)}, u32[]{:S(2)}) %collective-permute-start.14) | collective-permute-done | bytes 163872 | tf_op jit(solution)/shard_map/ppermute | solution.py:441
  (43 shorter events, 4.0 us)
Async XLA Ops:
  0.7 0.9 copy-start.1
  1.7 0.8 copy-start.3
  2.5 0.9 copy-start.5
  3.4 0.7 copy-start.7
  6.8 53.7 %copy-start.2 = (bf16[80,1536]{1,0:T(8,128)(2,1)S(1)}, bf16[80,1536]{1,0:T(8,128)(2,1)}, u32[]{:S(2)}) copy-start(bf16[80,1536]{1,0:T(8,128)(2,1)} %x_ref.3) | copy-start | bytes 737284
  6.8 53.7 %copy-start.4 = (bf16[384,64]{0,1:T(8,128)(2,1)S(1)}, bf16[384,64]{0,1:T(8,128)(2,1)}, u32[]{:S(2)}) copy-start(bf16[384,64]{0,1:T(8,128)(2,1)} %param.13) | copy-start | bytes 147460
  6.8 53.7 %copy-start.6 = (bf16[80,576]{1,0:T(8,128)(2,1)S(1)}, bf16[80,576]{1,0:T(8,128)(2,1)}, u32[]{:S(2)}) copy-start(bf16[80,576]{1,0:T(8,128)(2,1)} %kv_ref.3) | copy-start | bytes 276484
  6.8 53.7 %copy-start.8 = (s32[80]{0:T(128)S(1)}, s32[80]{0:T(128)}, u32[]{:S(2)}) copy-start(s32[80]{0:T(128)} %param.11) | copy-start | bytes 964
  37.4 24.1 %copy-start = (bf16[64,3072]{1,0:T(8,128)(2,1)S(1)}, bf16[64,3072]{1,0:T(8,128)(2,1)}, u32[]{:S(2)}) copy-start(bf16[64,3072]{1,0:T(8,128)(2,1)} %b_ref.3) | copy-start | bytes 1179652
  37.4 18.9 %all-to-all-start.1 = ((bf16[4,192,384]{2,1,0:T(8,128)(2,1)}), bf16[4,192,384]{2,1,0:T(8,128)(2,1)S(1)}, u32[]{:S(2)}, u32[]{:S(2)}) async-start(bf16[4,192,384]{2,1,0:T(8,128)(2,1)} %get-tuple-element.23), calls=%async_computation.1 | async-start | bytes 1179648 | tf_op jit(solution)/shard_map/all_to_all | solution.py:337
  42.4 16.1 %collective-permute-start.1 = (bf16[3,128,384]{2,1,0:T(8,128)(2,1)S(1)}, bf16[3,128,384]{2,1,0:T(8,128)(2,1)S(1)}, u32[]{:S(2)}, u32[]{:S(2)}) collective-permute-start(bf16[3,128,384]{2,1,0:T(8,128)(2,1)S(1)} %get-tuple-element.16.rest_0_), channel_id=1, source_target_pairs={{0,2},{1,3},{2,0},{3,1},{4,6},{5,7},{6,4},{7,5},{8,10},{9,11},{10,... | collective-permute-start | bytes 884744 | tf_op jit(solution)/shard_map/ppermute | solution.py:349
  43.9 17.6 %collective-permute-start.3 = (bf16[3,192,384]{2,1,0:T(8,128)(2,1)}, bf16[3,192,384]{2,1,0:T(8,128)(2,1)S(1)}, u32[]{:S(2)}, u32[]{:S(2)}) collective-permute-start(bf16[3,192,384]{2,1,0:T(8,128)(2,1)} %get-tuple-element.21), channel_id=1, source_target_pairs={{0,16},{16,0},{1,17},{17,1},{2,18},{18,2},{3,19},{19,3},{4,20},{20... | collective-permute-start | bytes 1327112 | tf_op jit(solution)/shard_map/ppermute | solution.py:346
  56.9 13.1 %collective-permute-start.8 = (bf16[3,192,384]{2,1,0:T(8,128)(2,1)S(1)}, bf16[3,192,384]{2,1,0:T(8,128)(2,1)S(1)}, u32[]{:S(2)}, u32[]{:S(2)}) collective-permute-start(bf16[3,192,384]{2,1,0:T(8,128)(2,1)S(1)} %shard_map.109), channel_id=1, source_target_pairs={{0,16},{16,0},{1,17},{17,1},{2,18},{18,2},{3,19},{19,3},{4,20},{20... | collective-permute-start | bytes 1327112 | tf_op jit(solution)/shard_map/ppermute | solution.py:346
  58.5 1.6 %collective-permute-start = (bf16[3,128,384]{2,1,0:T(8,128)(2,1)S(1)}, bf16[3,128,384]{2,1,0:T(8,128)(2,1)S(1)}, u32[]{:S(2)}, u32[]{:S(2)}) collective-permute-start(bf16[3,128,384]{2,1,0:T(8,128)(2,1)S(1)} %get-tuple-element.16.rest_0_), channel_id=1, source_target_pairs={{0,1},{1,0},{2,3},{3,2},{4,5},{5,4},{6,7},{7,6},{8,9},{9,8},{10,11... | collective-permute-start | bytes 884744 | tf_op jit(solution)/shard_map/ppermute | solution.py:352
  58.5 2.0 %collective-permute-start.2 = (bf16[3,128,384]{2,1,0:T(8,128)(2,1)S(1)}, bf16[3,128,384]{2,1,0:T(8,128)(2,1)S(1)}, u32[]{:S(2)}, u32[]{:S(2)}) collective-permute-start(bf16[3,128,384]{2,1,0:T(8,128)(2,1)S(1)} %collective-permute-done.1.rest_2_), channel_id=1, source_target_pairs={{0,1},{1,0},{2,3},{3,2},{4,5},{5,4},{6,7},{7,6},{8,9},{9,8},{10,11... | collective-permute-start | bytes 884744 | tf_op jit(solution)/shard_map/ppermute | solution.py:354
  66.0 10.8 %collective-permute-start.6 = (bf16[320,256]{1,0:T(8,128)(2,1)S(1)}, bf16[320,256]{1,0:T(8,128)(2,1)S(1)}, u32[]{:S(2)}, u32[]{:S(2)}) collective-permute-start(bf16[320,256]{1,0:T(8,128)(2,1)S(1)} %shard_map.107.rest_0_), channel_id=1, source_target_pairs={{0,8},{4,12},{8,0},{12,4},{1,9},{5,13},{9,1},{13,5},{2,10},{6,14},... | collective-permute-start | bytes 491528 | tf_op jit(solution)/shard_map/ppermute | solution.py:245
  66.0 13.3 %collective-permute-start.4 = (bf16[320,256]{1,0:T(8,128)(2,1)S(1)}, bf16[320,256]{1,0:T(8,128)(2,1)S(1)}, u32[]{:S(2)}, u32[]{:S(2)}) collective-permute-start(bf16[320,256]{1,0:T(8,128)(2,1)S(1)} %shard_map.107.rest_0_), channel_id=1, source_target_pairs={{0,4},{4,8},{8,12},{1,5},{5,9},{9,13},{2,6},{6,10},{10,14},{3,7},{... | collective-permute-start | bytes 491528 | tf_op jit(solution)/shard_map/ppermute | solution.py:243
  74.5 11.2 %collective-permute-start.11 = (bf16[320,256]{1,0:T(8,128)(2,1)S(1)}, bf16[320,256]{1,0:T(8,128)(2,1)S(1)}, u32[]{:S(2)}, u32[]{:S(2)}) collective-permute-start(bf16[320,256]{1,0:T(8,128)(2,1)S(1)} %shard_map.110.rest_0_), channel_id=1, source_target_pairs={{0,8},{4,12},{8,0},{12,4},{1,9},{5,13},{9,1},{13,5},{2,10},{6,14},... | collective-permute-start | bytes 491528 | tf_op jit(solution)/shard_map/ppermute | solution.py:245
  75.4 11.5 %collective-permute-start.5 = (bf16[320,256]{1,0:T(8,128)(2,1)S(1)}, bf16[320,256]{1,0:T(8,128)(2,1)S(1)}, u32[]{:S(2)}, u32[]{:S(2)}) collective-permute-start(bf16[320,256]{1,0:T(8,128)(2,1)S(1)} %shard_map.107.rest_0_), channel_id=1, source_target_pairs={{4,0},{8,4},{12,8},{5,1},{9,5},{13,9},{6,2},{10,6},{14,10},{7,3},{... | collective-permute-start | bytes 491528 | tf_op jit(solution)/shard_map/ppermute | solution.py:244
  76.7 13.6 %collective-permute-start.7 = (bf16[320,256]{1,0:T(8,128)(2,1)S(1)}, bf16[320,256]{1,0:T(8,128)(2,1)S(1)}, u32[]{:S(2)}, u32[]{:S(2)}) collective-permute-start(bf16[320,256]{1,0:T(8,128)(2,1)S(1)} %collective-permute-done.6.rest_3_), channel_id=1, source_target_pairs={{8,12},{4,0},{9,13},{5,1},{10,14},{6,2},{11,15},{7,3},{24,28},{20,... | collective-permute-start | bytes 491528 | tf_op jit(solution)/shard_map/ppermute | solution.py:246
  78.0 18.7 %collective-permute-start.10 = (bf16[320,256]{1,0:T(8,128)(2,1)S(1)}, bf16[320,256]{1,0:T(8,128)(2,1)S(1)}, u32[]{:S(2)}, u32[]{:S(2)}) collective-permute-start(bf16[320,256]{1,0:T(8,128)(2,1)S(1)} %shard_map.110.rest_0_), channel_id=1, source_target_pairs={{4,0},{8,4},{12,8},{5,1},{9,5},{13,9},{6,2},{10,6},{14,10},{7,3},{... | collective-permute-start | bytes 491528 | tf_op jit(solution)/shard_map/ppermute | solution.py:244
  79.3 17.4 %collective-permute-start.9 = (bf16[320,256]{1,0:T(8,128)(2,1)S(1)}, bf16[320,256]{1,0:T(8,128)(2,1)S(1)}, u32[]{:S(2)}, u32[]{:S(2)}) collective-permute-start(bf16[320,256]{1,0:T(8,128)(2,1)S(1)} %shard_map.110.rest_0_), channel_id=1, source_target_pairs={{0,4},{4,8},{8,12},{1,5},{5,9},{9,13},{2,6},{6,10},{10,14},{3,7},{... | collective-permute-start | bytes 491528 | tf_op jit(solution)/shard_map/ppermute | solution.py:243
  85.7 11.1 %collective-permute-start.12 = (bf16[320,256]{1,0:T(8,128)(2,1)S(1)}, bf16[320,256]{1,0:T(8,128)(2,1)S(1)}, u32[]{:S(2)}, u32[]{:S(2)}) collective-permute-start(bf16[320,256]{1,0:T(8,128)(2,1)S(1)} %collective-permute-done.11.rest_3_), channel_id=1, source_target_pairs={{8,12},{4,0},{9,13},{5,1},{10,14},{6,2},{11,15},{7,3},{24,28},{20,... | collective-permute-start | bytes 491528 | tf_op jit(solution)/shard_map/ppermute | solution.py:246
  96.7 3.9 %copy-start.9 = (bf16[384,3072]{1,0:T(8,128)(2,1)S(1)}, bf16[384,3072]{1,0:T(8,128)(2,1)}, u32[]{:S(2)}) copy-start(bf16[384,3072]{1,0:T(8,128)(2,1)} %w_ref.5) | copy-start | bytes 7077892
  100.5 7.0 %collective-permute-start.15 = (bf16[160,768]{1,0:T(8,128)(2,1)S(1)}, bf16[160,768]{1,0:T(8,128)(2,1)S(1)}, u32[]{:S(2)}, u32[]{:S(2)}) collective-permute-start(bf16[160,768]{1,0:T(8,128)(2,1)S(1)} %get-tuple-element.27), channel_id=1, source_target_pairs={{0,1},{1,0},{2,3},{3,2},{4,5},{5,4},{6,7},{7,6},{8,9},{9,8},{10,11... | collective-permute-start | bytes 737288 | tf_op jit(solution)/shard_map/ppermute | solution.py:437
  107.0 2.2 %collective-permute-start.13 = (bf16[160,1024]{1,0:T(8,128)(2,1)S(1)}, bf16[160,1024]{1,0:T(8,128)(2,1)S(1)}, u32[]{:S(2)}, u32[]{:S(2)}) collective-permute-start(bf16[160,1024]{1,0:T(8,128)(2,1)S(1)} %get-tuple-element.25), channel_id=1, source_target_pairs={{0,1},{1,0},{2,3},{3,2},{4,5},{5,4},{6,7},{7,6},{8,9},{9,8},{10,11... | collective-permute-start | bytes 983048 | tf_op jit(solution)/shard_map/ppermute | solution.py:437
  107.6 6.3 %collective-permute-start.16 = (bf16[80,768]{1,0:T(8,128)(2,1)S(1)}, bf16[80,768]{1,0:T(8,128)(2,1)S(1)}, u32[]{:S(2)}, u32[]{:S(2)}) collective-permute-start(bf16[80,768]{1,0:T(8,128)(2,1)S(1)} %fusion.3), channel_id=1, source_target_pairs={{0,2},{1,3},{2,0},{3,1},{4,6},{5,7},{6,4},{7,5},{8,10},{9,11},{10,... | collective-permute-start | bytes 368648 | tf_op jit(solution)/shard_map/ppermute | solution.py:441
  109.4 7.1 %collective-permute-start.14 = (bf16[80,1024]{1,0:T(8,128)(2,1)S(1)}, bf16[80,1024]{1,0:T(8,128)(2,1)S(1)}, u32[]{:S(2)}, u32[]{:S(2)}) collective-permute-start(bf16[80,1024]{1,0:T(8,128)(2,1)S(1)} %fusion.2), channel_id=1, source_target_pairs={{0,2},{1,3},{2,0},{3,1},{4,6},{5,7},{6,4},{7,5},{8,10},{9,11},{10,... | collective-permute-start | bytes 491528 | tf_op jit(solution)/shard_map/ppermute | solution.py:441

commit v3 on v2

--- a/solution.py
+++ b/solution.py
@@ -9,7 +9,8 @@
 from jax.sharding import PartitionSpec as P
 
 CHUNKS = 2
-VMEM_BYTES = 50 * 1024 * 1024
+VMEM_BYTES = 20 * 1024 * 1024
+TILE = 512
 
 
 def on_device(
@@ -97,22 +98,30 @@
     return [(i, i ^ bit) for i in range(n)]
 
 
-def call(body, outs, args, blocks=None, out_blocks=None, steps=1, scratch=(), flops=0, moved=0):
-    whole = pl.BlockSpec(memory_space=pltpu.VMEM)
-    blocks = blocks or {}
+def call(body, outs, args, hbm=(), scratch=(), flops=0, moved=0):
+    vmem = pl.BlockSpec(memory_space=pltpu.VMEM)
+    far = pl.BlockSpec(memory_space=pl.ANY)
+    args = [pltpu.with_memory_space_constraint(a, pltpu.HBM) if i in hbm else a for i, a in enumerate(args)]
     return pl.pallas_call(
         body,
         out_shape=outs,
         grid_spec=pltpu.PrefetchScalarGridSpec(
             num_scalar_prefetch=1,
-            grid=(steps,),
-            in_specs=[blocks.get(i, whole) for i in range(len(args) - 1)],
-            out_specs=out_blocks if out_blocks is not None else jax.tree.map(lambda o: whole, outs),
+            grid=(1,),
+            in_specs=[far if i in hbm else vmem for i in range(1, len(args))],
+            out_specs=jax.tree.map(lambda o: vmem, outs),
             scratch_shapes=list(scratch),
         ),
         compiler_params=pltpu.CompilerParams(vmem_limit_bytes=VMEM_BYTES),
         cost_estimate=pl.CostEstimate(flops=flops, bytes_accessed=moved, transcendentals=0),
     )(*args)
+
+
+def fetch(pairs, sems):
+    copies = [pltpu.make_async_copy(a, b, sems.at[i]) for i, (a, b) in enumerate(pairs)]
+    for copy in copies:
+        copy.start()
+    return copies
 
 
 def three_terms(p):
@@ -124,35 +133,45 @@
     return out
 
 
-def pack_body(n, kq, vq, aq, wide, kvr, sc, x_ref, kv_ref, at_ref, pos_ref, w_ref, first, *rest):
-    others, turn, turned = rest[:-2], rest[-2], rest[-1]
-    h = sc[2]
+def pack_body(n, kq, vq, aq, wide, kvr, sc, x_ref, kv_ref, at_ref, pos_ref, w_ref, *rest):
+    outs, (xs, kvs, ats, ps, turn, turned, sems) = rest[:CHUNKS], rest[CHUNKS:]
+    g, h = sc[1], sc[2]
     tok = x_ref.shape[0]
     rope = kv_ref.shape[1] - kvr
-    half = w_ref.shape[0]
-    pieces = 1 + len(others)
+    half = outs[1].shape[1]
+    small = [
+        (x_ref.at[:, pl.ds(pl.multiple_of(h * kq, 128), kq)], xs),
+        (kv_ref, kvs),
+        (at_ref.at[pl.ds(pl.multiple_of(h * aq, 16), aq), :], ats),
+        (pos_ref, ps),
+    ]
+    mine = pl.ds(pl.multiple_of(g * half, 16), half)
+    large = []
+    for c in range(CHUNKS):
+        for j in range(n):
+            at = (j * CHUNKS + c) * wide
+            large.append((w_ref.at[mine, at : at + wide], outs[c].at[j, :half]))
+    copies = fetch(small + large, sems)
     turn[...] = jnp.zeros_like(turn)
-    turn[:tok, :rope] = kv_ref[:, kvr:].astype(jnp.float32)
-    start = pos_ref[0:1, 0:1].astype(jnp.float32)
+    for copy in copies[: len(small)]:
+        copy.wait()
+    turn[:tok, :rope] = kvs[:, kvr:].astype(jnp.float32)
+    start = ps[0:1, 0:1].astype(jnp.float32)
     for i, t in enumerate(three_terms(start)):
         turn[tok + i : tok + i + 1, :] = jnp.broadcast_to(t, (1, turn.shape[1]))
     turned[...] = turn[...].T
-    xs = x_ref[:, pl.ds(pl.multiple_of(h * kq, 128), kq)]
-    ats = at_ref[pl.ds(pl.multiple_of(h * aq, 16), aq), :]
-    keys = kv_ref[:, pl.ds(pl.multiple_of(h * vq, 128), vq)]
+    keys = kvs[:, pl.ds(pl.multiple_of(h * vq, 128), vq)]
     ropes = turned[pl.ds(pl.multiple_of(h * aq, 16), aq), :].astype(jnp.bfloat16)
     third = (tok + aq) // 3
     tail = jnp.concatenate([keys, ropes], axis=0)
     for j in range(n):
-        at = j * pieces * wide
-        first[j, :half, :] = w_ref[:, at : at + wide]
-        first[j, half : half + tok, :] = xs
-        first[j, half + tok : half + tok + aq, :] = ats
+        first = outs[0].at[j]
+        first[half : half + tok, :] = xs[...]
+        first[half + tok : half + tok + aq, :] = ats[...]
         for i in range(3):
-            first[j, half + tok + aq :, i * vq : (i + 1) * vq] = tail[i * third : (i + 1) * third]
-        for c, other in enumerate(others):
-            at = (j * pieces + c + 1) * wide
-            other[j] = w_ref[:, at : at + wide]
+            first[half + tok + aq :, i * vq : (i + 1) * vq] = tail[i * third : (i + 1) * third]
+    for copy in copies[len(small) :]:
+        copy.wait()
 
 
 def split_body(n, half, sc, u_ref, *outs):
@@ -204,29 +223,43 @@
     bias[...] = jnp.where(seen, 0.0, -1e30)
 
 
-def attend_body(n, nope, scale, sc, x_ref, at_ref, b_ref, w_ref, kv_ref, bias_ref, ku_ref, vu_ref, u_ref, y_ref, out, raw):
+def attend_body(n, nope, scale, c, sc, x_ref, at_ref, kv_ref, bias_ref, u_ref, y_ref, b_ref, w_ref, ku_ref, vu_ref, *rest):
+    out, raw, b_own, ku, vu, sems = rest
     s, g = sc[0], sc[1]
     depth = w_ref.shape[0]
     half = depth // 2
-    raw[pl.ds(pl.multiple_of(s * depth, 16), depth), :] = w_ref[...]
+    wide = raw.shape[1]
+    heads, kvr, vdim = vu.shape
+    chunk = s * CHUNKS + c
+    columns = pl.ds(pl.multiple_of(chunk * wide, 128), wide)
+    copies = fetch(
+        [
+            (b_ref.at[:, columns], b_own),
+            (w_ref.at[:, columns], raw.at[pl.ds(pl.multiple_of(s * depth, 16), depth), :]),
+            (ku_ref.at[pl.ds(chunk * heads, heads)], ku),
+            (vu_ref.at[pl.ds(chunk * heads, heads)], vu),
+        ],
+        sems,
+    )
     for k in range(1, n):
         src = lax.rem(s - k + n, n)
         raw[pl.ds(pl.multiple_of(src * depth + g * half, 16), half), :] = u_ref[src, :half]
         raw[pl.ds(pl.multiple_of(src * depth + (1 - g) * half, 16), half), :] = y_ref[k - 1]
+    for copy in copies:
+        copy.wait()
     add = lax.dot_general(
-        at_ref[...], b_ref[...], (((0,), (0,)), ((), ())), preferred_element_type=jnp.float32
+        at_ref[...], b_own[...], (((0,), (0,)), ((), ())), preferred_element_type=jnp.float32
     )
     merged = (raw[...].astype(jnp.float32) + add).astype(jnp.bfloat16)
     q = jnp.dot(x_ref[...], merged, preferred_element_type=jnp.float32)
-    heads, kvr, vdim = vu_ref.shape
-    width = q.shape[1] // heads
+    width = wide // heads
     lat, rope_key = kv_ref[:, :kvr], kv_ref[:, kvr:]
     bias = bias_ref[...]
     nt = (((1,), (1,)), ((), ()))
     for j in range(heads):
         qn = q[:, j * width : j * width + nope].astype(jnp.bfloat16)
         qr = q[:, j * width + nope : (j + 1) * width].astype(jnp.bfloat16)
-        absorbed = jnp.dot(qn, ku_ref[j], preferred_element_type=jnp.float32).astype(jnp.bfloat16)
+        absorbed = jnp.dot(qn, ku[j], preferred_element_type=jnp.float32).astype(jnp.bfloat16)
         scores = lax.dot_general(absorbed, lat, nt, preferred_element_type=jnp.float32)
         scores = scores + lax.dot_general(qr, rope_key, nt, preferred_element_type=jnp.float32)
         scores = scores * scale + bias
@@ -235,7 +268,7 @@
         total = jnp.sum(e, axis=1, keepdims=True)
         ctx = jnp.dot(e.astype(jnp.bfloat16), lat, preferred_element_type=jnp.float32)
         ctx = (ctx / total).astype(jnp.bfloat16)
-        ho = jnp.dot(ctx, vu_ref[j], preferred_element_type=jnp.float32)
+        ho = jnp.dot(ctx, vu[j], preferred_element_type=jnp.float32)
         out[:, j * vdim : (j + 1) * vdim] = ho.astype(jnp.bfloat16)
 
 
@@ -270,26 +303,35 @@
         put(3 - s, three)
 
 
-def first_body(sc, w_ref, *rest):
-    slots, acc, lhs = rest[:5], rest[5], rest[6]
-
-    @pl.when(pl.program_id(0) == 0)
-    def _():
-        place_line(sc[0], slots, lhs)
-
-    w = w_ref[...].reshape(lhs.shape[1], w_ref.shape[-1])
-    acc[...] = jnp.dot(lhs[...], w, preferred_element_type=jnp.float32)
-
-
-def last_body(nh, tok, sc, w_ref, acc, *rest):
+def first_body(n, sc, *rest):
+    slots, (w_ref, acc, kept, lhs, w, sems) = rest[:5], rest[5:]
+    width = lhs.shape[1] // n
+    pairs = [(w_ref.at[j, 0], w.at[j]) for j in range(n)]
+    copies = fetch(pairs + [(w_ref.at[j, 1], kept.at[j]) for j in range(n)], sems)
+    place_line(sc[0], slots, lhs)
+    total = acc.shape[1]
+    for j in range(n):
+        copies[j].wait()
+    for at in range(0, total, TILE):
+        band = slice(at, min(at + TILE, total))
+        tile = w[:, :, band]
+        tile = tile.reshape(lhs.shape[1], tile.shape[-1])
+        acc[:, band] = jnp.dot(lhs[...], tile, preferred_element_type=jnp.float32)
+    for copy in copies[n:]:
+        copy.wait()
+
+
+def last_body(nh, tok, begin, sc, w_ref, acc, *rest):
     slots, (keep, send), lhs, tot = rest[:5], rest[5:7], rest[7], rest[8]
-
-    @pl.when(pl.program_id(0) == 0)
-    def _():
-        place_line(sc[0], slots, lhs)
-
-    w = w_ref[...].reshape(lhs.shape[1], w_ref.shape[-1])
-    tot[...] = acc[...] + jnp.dot(lhs[...], w, preferred_element_type=jnp.float32)
+    place_line(sc[0], slots, lhs)
+    total = keep.shape[1]
+    for at in range(0, total, TILE):
+        end = min(at + TILE, total)
+        w = w_ref[:, :, begin + at : begin + end]
+        w = w.reshape(lhs.shape[1], w.shape[-1])
+        tot[:, at:end] = acc[:, begin + at : begin + end] + jnp.dot(
+            lhs[...], w, preferred_element_type=jnp.float32
+        )
     core = sc[2] % 2
     for i in range(nh // 2):
         mine = pl.ds(pl.multiple_of((2 * i + core) * tok, 16), tok)
@@ -325,27 +367,32 @@
         functools.partial(pack_body, n, kq, vq, aq, wide, kvr),
         tuple([like(n, half + extra, wide)] + [like(n, half, wide)] * (CHUNKS - 1)),
         [sc, x, kv, at, pos2, wq],
-        blocks={4: pl.BlockSpec((half, cols), lambda i, sc: (sc[1], 0))},
-        scratch=[pltpu.VMEM((128, 128), f32)] * 2,
+        hbm=range(1, 6),
+        scratch=[
+            pltpu.VMEM((tok, kq), bf),
+            pltpu.VMEM(kv.shape, bf),
+            pltpu.VMEM((aq, rows), bf),
+            pltpu.VMEM(pos2.shape, jnp.int32),
+            pltpu.VMEM((128, 128), f32),
+            pltpu.VMEM((128, 128), f32),
+            pltpu.SemaphoreType.DMA((4 + n * CHUNKS,)),
+        ],
         moved=4 * half * cols,
     )
-    moved, passed, stack = [], [], None
-    for c in range(CHUNKS):
-        unit = units[c]
-        if c:
-            unit, _ = lax.optimization_barrier((unit, moved[c - 1]))
-        got = lax.all_to_all(unit, "seq", 0, 0, tiled=True)
-        moved.append(got)
-        outs = [like(n - 1, half, wide)] + ([] if c else [like(n - 1, extra, wide)])
-        outs = call(
-            functools.partial(split_body, n, half),
-            tuple(outs),
-            [sc, got],
-            moved=4 * got.size,
-        )
-        passed.append(lax.ppermute(outs[0], "groups", cyclic(2, 1)))
-        if c == 0:
-            stack = outs[1]
+    def exchange(unit):
+        return lax.all_to_all(unit, "seq", 0, 0, tiled=True)
+
+    def split(got, *sizes):
+        outs = tuple(like(n - 1, size, wide) for size in sizes)
+        return call(functools.partial(split_body, n, half), outs, [sc, got], moved=4 * got.size)
+
+    merged = (wq.astype(f32) + jnp.dot(down, up, preferred_element_type=f32)).astype(bf)
+    moved = [exchange(units[0])]
+    moved[0], merged = lax.optimization_barrier((moved[0], merged))
+    later, _ = lax.optimization_barrier((units[1], moved[0]))
+    moved.append(exchange(later))
+    share, stack = split(moved[0], half, extra)
+    passed = [lax.ppermute(share, "groups", cyclic(2, 1))]
     across = lax.ppermute(stack, "head", flipped(nh, 2))
     stacks = [
         stack,
@@ -353,6 +400,7 @@
         across,
         lax.ppermute(across, "head", flipped(nh, 1)),
     ]
+    moved[1], passed[0], *stacks = lax.optimization_barrier((moved[1], passed[0], *stacks))
     x_all, kv_all, at_all, bias = call(
         functools.partial(unpack_body, n, nh, kq, vq, aq, kvr),
         (
@@ -365,29 +413,24 @@
         scratch=[pltpu.VMEM((128, 128), f32)],
         moved=4 * tokens * depth,
     )
-
-    merged = (wq.astype(f32) + jnp.dot(down, up, preferred_element_type=f32)).astype(bf)
+    (share,) = split(moved[1], half)
+    passed.append(lax.ppermute(share, "groups", cyclic(2, 1)))
 
     scale = 1.0 / math.sqrt(nope + rope)
     slots = []
     for c in range(CHUNKS):
-        def column(i, sc, c=c):
-            return (0, sc[0] * CHUNKS + c)
-
-        def leading(i, sc, c=c):
-            return (sc[0] * CHUNKS + c, 0, 0)
-
         ho = call(
-            functools.partial(attend_body, n, nope, scale),
+            functools.partial(attend_body, n, nope, scale, c),
             like(tokens, per * vdim),
-            [sc, x_all, at_all, up, wq, kv_all, bias, ku, vu, moved[c], passed[c]],
-            blocks={
-                2: pl.BlockSpec((rank, wide), column),
-                3: pl.BlockSpec((rows, wide), column),
-                6: pl.BlockSpec((per, nope, kvr), leading),
-                7: pl.BlockSpec((per, kvr, vdim), leading),
-            },
-            scratch=[pltpu.VMEM((n * rows, wide), bf)],
+            [sc, x_all, at_all, kv_all, bias, moved[c], passed[c], up, wq, ku, vu],
+            hbm=range(7, 11),
+            scratch=[
+                pltpu.VMEM((n * rows, wide), bf),
+                pltpu.VMEM((rank, wide), bf),
+                pltpu.VMEM((per, nope, kvr), bf),
+                pltpu.VMEM((per, kvr, vdim), bf),
+                pltpu.SemaphoreType.DMA((4,)),
+            ],
             flops=2 * tokens * per * (depth * wide // per + 2 * nope * kvr + 2 * tokens * kvr),
             moved=4 * n * rows * wide,
         )
@@ -395,47 +438,36 @@
 
     w4 = wo.reshape(n, CHUNKS, per * vdim, wo.shape[1])
     total = wo.shape[1]
-    tile = 256
-    tiles = total // tile
     lhs = pltpu.VMEM((tokens, n * per * vdim), bf)
-
-    def weights(c, begin):
-        return pl.BlockSpec((n, None, per * vdim, tile), lambda i, sc: (0, c, 0, i + begin))
-
-    def band(count, begin=0):
-        return pl.BlockSpec((count, tile), lambda i, sc: (0, i + begin))
-
-    cost = dict(flops=2 * tokens * n * per * vdim * total, moved=w4.size * 2 // CHUNKS)
-    acc = call(
-        first_body,
-        like(tokens, total, dtype=f32),
-        [sc, w4] + slots[0],
-        blocks={0: weights(0, 0)},
-        out_blocks=band(tokens),
-        steps=tiles,
-        scratch=[lhs],
-        **cost,
+    flops = 2 * tokens * n * per * vdim * total
+    acc, w_last = call(
+        functools.partial(first_body, n),
+        (like(tokens, total, dtype=f32), like(n, per * vdim, total)),
+        [sc] + slots[0] + [w4],
+        hbm=(6,),
+        scratch=[
+            lhs,
+            pltpu.VMEM((n, per * vdim, total), bf),
+            pltpu.SemaphoreType.DMA((2 * n,)),
+        ],
+        flops=flops,
+        moved=w4.size,
     )
     side = h // 2
     bands = []
-    cut = (tiles + 1) // 2
-    for begin, count in ((0, cut), (cut, tiles - cut)):
+    cut = (total // 128 + 1) // 2 * 128
+    for begin, end in ((0, cut), (cut, total)):
+        size = end - begin
         keep, send = call(
-            functools.partial(last_body, nh, tok),
-            (
-                like(nh // 2 * tok, count * tile, dtype=f32),
-                like(nh // 2 * tok, count * tile),
-            ),
-            [sc, w4, acc] + slots[1],
-            blocks={0: weights(1, begin), 1: band(tokens, begin)},
-            out_blocks=(band(nh // 2 * tok), band(nh // 2 * tok)),
-            steps=count,
-            scratch=[lhs, pltpu.VMEM((tokens, tile), f32)],
-            flops=cost["flops"] * count // tiles,
-            moved=cost["moved"] * count // tiles,
+            functools.partial(last_body, nh, tok, begin),
+            (like(nh // 2 * tok, size, dtype=f32), like(nh // 2 * tok, size)),
+            [sc, w_last, acc] + slots[1],
+            scratch=[lhs, pltpu.VMEM((tokens, size), f32)],
+            flops=flops * size // total,
+            moved=w4.size * size // total,
         )
         got = lax.ppermute(send, "head", flipped(nh, 1))
-        pair = (keep + got.astype(f32)).reshape(nh // 2, tok, count * tile)
+        pair = (keep + got.astype(f32)).reshape(nh // 2, tok, size)
         out = lax.dynamic_index_in_dim(pair, side, 0, keepdims=False)
         away = lax.dynamic_index_in_dim(pair, 1 - side, 0, keepdims=False).astype(bf)
         out = out + lax.ppermute(away, "head", flipped(nh, 2)).astype(f32)
@@ -461,7 +493,7 @@
         and x[1] // nh == wide
         and down[0] == wide
         and wide == 3 * 128
-        and wo[1] % 256 == 0
+        and wo[1] % 128 == 0
     )
 
 

time: 118 us -> 108 us (0.915)
  blocking collectives: 30.6 us -> 0 us
  waiting for transfers between devices: 22.8 us -> 42.1 us
  Pallas kernels: 28.9 us -> 22.7 us
  starting transfers between devices: 27.4 us -> 33.1 us
  local copies, waits for them, and re-layouts: 3.37 us -> 4.61 us
    all_to_all x1 -> x0, blocking collectives: 30.6 us -> none  [by_heads(): got = lax.all_to_all(unit, 'seq', 0, 0, tiled=True)]
    all_to_all x1 -> x2, waiting for transfers between devices: 10.9 us -> 22.7 us  [exchange(): return lax.all_to_all(unit, 'seq', 0, 0, tiled=True)]
    pallas_call x9, Pallas kernels: 28.9 us -> 22.7 us  [call(): pl.pallas_call(body, out_shape=outs, grid_spec=pltpu.PrefetchScalarGridSp...]
    all_to_all x1 -> x2, starting transfers between devices: 3.61 us -> 9.81 us  [exchange(): return lax.all_to_all(unit, 'seq', 0, 0, tiled=True)]
    ppermute x1, waiting for transfers between devices: 0.01 us -> 4.96 us  [by_heads(): across = lax.ppermute(stack, 'head', flipped(nh, 2))]
    ppermute x2, waiting for transfers between devices: 0.01 us -> 4.37 us  [the longest x1 4.36 us: by_heads(): passed = [lax.ppermute(share, 'groups', cyclic(2, 1))]]
    unnamed x20 -> x22, local copies, waits for them, and re-layouts: 3.32 us -> 4.56 us
  transfers between devices with their start and end apart: 18 -> 19, of which waited for: 7 -> 9; matrix products, arithmetic and copies ran while one was open for 2% -> 3% of each run, Pallas kernels for 19% -> 15%
where the time goes in v3:
time: 108 us
  waiting for transfers between devices  42.1 us (39%)
  starting transfers between devices  33.1 us (31%)
  Pallas kernels  22.7 us (21%)
  local copies, waits for them, and re-layouts  4.61 us (4%)
  matrix products  3.2 us (3%)
    all_to_all x2, waiting for transfers between devices, exchange(): return lax.all_to_all(unit, 'seq', 0, 0, tiled=True)  22.7 us
    pallas_call x9, Pallas kernels, call(): pl.pallas_call(body, out_shape=outs, grid_spec=pltpu.PrefetchScalarGridSp...  22.7 us
    all_to_all x2, starting transfers between devices, exchange(): return lax.all_to_all(unit, 'seq', 0, 0, tiled=True)  9.81 us
    ppermute x2, starting transfers between devices, gather_line(): left = lax.ppermute(x, 'seq', [(0, 1), (1, 2), (2, 3)])  8.56 us
    ppermute x2, waiting for transfers between devices, by_heads(): out = out + lax.ppermute(away, 'head', flipped(nh, 2)).astype(f32)  6.04 us
    ppermute x1, waiting for transfers between devices, by_heads(): across = lax.ppermute(stack, 'head', flipped(nh, 2))  4.96 us
    unnamed x22, local copies, waits for them, and re-layouts  4.56 us
    ppermute x1, waiting for transfers between devices, by_heads(): passed = [lax.ppermute(share, 'groups', cyclic(2, 1))]  4.36 us
  transfers between devices with their start and end apart: 19, of which 9 were waited for; matrix products, arithmetic and copies ran while one was open for 3% of the time, Pallas kernels for 15%

profile of v3, /device:TPU:0, one launch (start us, length us, event | category | flops | bytes accessed | tf_op | source)
XLA Modules:
  0.0 107.6 jit_solution(16402510032650734655)
XLA Ops:
  0.7 3.4 %shard_map.104 = (bf16[4,320,384]{2,1,0:T(8,128)(2,1)}, bf16[4,192,384]{2,1,0:T(8,128)(2,1)}) custom-call(s32[3]{0:T(128)S(1)} %pad_add_fusion.sc, bf16[80,1536]{1,0:T(8,128)(2,1)} %x_ref.3, bf16[80,576]{1,0:T(8,128)(2,1)} %kv_ref.3, bf16[64,384]{1,0:T(8,128)(2,1)} %bitcast.22, s32[1,80]{1,0:T(1,128)} %bitcast.24, bf16[384,3072]{1,0:T(8,128)(2,1)} %w_ref.5), custom_call_target="tpu_custom_call" | custom-call | bytes 2359296 | tf_op jit(solution)/shard_map/pallas_call | solution.py:105
  4.2 6.3 %all-to-all-start = ((bf16[4,320,384]{2,1,0:T(8,128)(2,1)}), bf16[4,320,384]{2,1,0:T(8,128)(2,1)S(1)}, u32[]{:S(2)}, u32[]{:S(2)}) async-start(bf16[4,320,384]{2,1,0:T(8,128)(2,1)} %get-tuple-element.25), calls=%async_computation | async-start | bytes 1966080 | tf_op jit(solution)/shard_map/all_to_all | solution.py:383
  10.5 3.2 %add_convert_fusion = bf16[384,3072]{1,0:T(8,128)(2,1)} fusion(bf16[384,3072]{1,0:T(8,128)(2,1)S(1)} %copy-done.10, bf16[384,64]{0,1:T(8,128)(2,1)S(1)} %copy-done.5, bf16[64,3072]{1,0:T(8,128)(2,1)} %b_ref.3), kind=kOutput, calls=%fused_computation | convolution fusion | flops 154533888 | bytes 5160960 | tf_op jit(solution)/shard_map/dot_general | solution.py:389
  13.7 21.1 %all-to-all-done.u_ref = bf16[4,320,384]{2,1,0:T(8,128)(2,1)S(1)} async-done(((bf16[4,320,384]{2,1,0:T(8,128)(2,1)}), bf16[4,320,384]{2,1,0:T(8,128)(2,1)S(1)}, u32[]{:S(2)}, u32[]{:S(2)}) %all-to-all-start) | async-done | bytes 983072 | tf_op jit(solution)/shard_map/all_to_all | solution.py:383
  34.8 3.5 %all-to-all-start.1 = ((bf16[4,192,384]{2,1,0:T(8,128)(2,1)}), bf16[4,192,384]{2,1,0:T(8,128)(2,1)S(1)}, u32[]{:S(2)}, u32[]{:S(2)}) async-start(bf16[4,192,384]{2,1,0:T(8,128)(2,1)} %get-tuple-element.29), calls=%async_computation.1 | async-start | bytes 1179648 | tf_op jit(solution)/shard_map/all_to_all | solution.py:383
  38.9 1.6 %collective-permute-start.2 = (bf16[3,128,384]{2,1,0:T(8,128)(2,1)S(1)}, bf16[3,128,384]{2,1,0:T(8,128)(2,1)S(1)}, u32[]{:S(2)}, u32[]{:S(2)}) collective-permute-start(bf16[3,128,384]{2,1,0:T(8,128)(2,1)S(1)} %get-tuple-element.32.rest_0_), channel_id=1, source_target_pairs={{0,2},{1,3},{2,0},{3,1},{4,6},{5,7},{6,4},{7,5},{8,10},{9,11},{10,... | collective-permute-start | bytes 884744 | tf_op jit(solution)/shard_map/ppermute | solution.py:396
  40.5 1.5 %collective-permute-start = (bf16[3,192,384]{2,1,0:T(8,128)(2,1)S(1)}, bf16[3,192,384]{2,1,0:T(8,128)(2,1)S(1)}, u32[]{:S(2)}, u32[]{:S(2)}) collective-permute-start(bf16[3,192,384]{2,1,0:T(8,128)(2,1)S(1)} %get-tuple-element.30), channel_id=1, source_target_pairs={{0,16},{16,0},{1,17},{17,1},{2,18},{18,2},{3,19},{19,3},{4,20},{20... | collective-permute-start | bytes 1327112 | tf_op jit(solution)/shard_map/ppermute | solution.py:395
  42.0 5.0 %collective-permute-done.2.rest_2_ = bf16[3,128,384]{2,1,0:T(8,128)(2,1)S(1)} collective-permute-done((bf16[3,128,384]{2,1,0:T(8,128)(2,1)S(1)}, bf16[3,128,384]{2,1,0:T(8,128)(2,1)S(1)}, u32[]{:S(2)}, u32[]{:S(2)}) %collective-permute-start.2) | collective-permute-done | bytes 294944 | tf_op jit(solution)/shard_map/ppermute | solution.py:396
  47.0 4.4 %collective-permute-done.y_ref = bf16[3,192,384]{2,1,0:T(8,128)(2,1)S(1)} collective-permute-done((bf16[3,192,384]{2,1,0:T(8,128)(2,1)S(1)}, bf16[3,192,384]{2,1,0:T(8,128)(2,1)S(1)}, u32[]{:S(2)}, u32[]{:S(2)}) %collective-permute-start) | collective-permute-done | bytes 442400 | tf_op jit(solution)/shard_map/ppermute | solution.py:395
  52.0 1.6 %all-to-all-done.1.u_ref = bf16[4,192,384]{2,1,0:T(8,128)(2,1)S(1)} async-done(((bf16[4,192,384]{2,1,0:T(8,128)(2,1)}), bf16[4,192,384]{2,1,0:T(8,128)(2,1)S(1)}, u32[]{:S(2)}, u32[]{:S(2)}) %all-to-all-start.1) | async-done | bytes 589856 | tf_op jit(solution)/shard_map/all_to_all | solution.py:383
  54.3 1.6 %collective-permute-start.8 = (bf16[3,192,384]{2,1,0:T(8,128)(2,1)S(1)}, bf16[3,192,384]{2,1,0:T(8,128)(2,1)S(1)}, u32[]{:S(2)}, u32[]{:S(2)}) collective-permute-start(bf16[3,192,384]{2,1,0:T(8,128)(2,1)S(1)} %shard_map.109), channel_id=1, source_target_pairs={{0,16},{16,0},{1,17},{17,1},{2,18},{18,2},{3,19},{19,3},{4,20},{20... | collective-permute-start | bytes 1327112 | tf_op jit(solution)/shard_map/ppermute | solution.py:417
  55.9 1.0 copy-done.8
  56.8 1.0 shard_map.106
  57.8 4.6 %shard_map.107.rest_0_ = bf16[320,256]{1,0:T(8,128)(2,1)S(1)} custom-call(s32[3]{0:T(128)S(1)} %pad_add_fusion.sc, bf16[320,1536]{1,0:T(8,128)(2,1)S(1)} %get-tuple-element.36.x_ref, bf16[64,1536]{1,0:T(8,128)(2,1)S(1)} %get-tuple-element.37.at_ref, bf16[320,576]{1,0:T(8,128)(2,1)S(1)} %get-tuple-element.38.kv_ref, ...), custom_call_target="tpu_custom_call" | custom-call | flops 964689920 | bytes 2359296 | tf_op jit(solution)/shard_map/pallas_call | solution.py:105
  62.3 1.1 collective-permute-start.6
  63.4 3.4 %collective-permute-start.4 = (bf16[320,256]{1,0:T(8,128)(2,1)S(1)}, bf16[320,256]{1,0:T(8,128)(2,1)S(1)}, u32[]{:S(2)}, u32[]{:S(2)}) collective-permute-start(bf16[320,256]{1,0:T(8,128)(2,1)S(1)} %shard_map.107.rest_0_), channel_id=1, source_target_pairs={{0,4},{4,8},{8,12},{1,5},{5,9},{9,13},{2,6},{6,10},{10,14},{3,7},{... | collective-permute-start | bytes 491528 | tf_op jit(solution)/shard_map/ppermute | solution.py:276
  66.8 4.6 %shard_map.110.rest_0_ = bf16[320,256]{1,0:T(8,128)(2,1)S(1)} custom-call(s32[3]{0:T(128)S(1)} %pad_add_fusion.sc, bf16[320,1536]{1,0:T(8,128)(2,1)S(1)} %get-tuple-element.36.x_ref, bf16[64,1536]{1,0:T(8,128)(2,1)S(1)} %get-tuple-element.37.at_ref, bf16[320,576]{1,0:T(8,128)(2,1)S(1)} %get-tuple-element.38.kv_ref, ...), custom_call_target="tpu_custom_call" | custom-call | flops 964689920 | bytes 2359296 | tf_op jit(solution)/shard_map/pallas_call | solution.py:105
  72.0 1.3 %collective-permute-start.5 = (bf16[320,256]{1,0:T(8,128)(2,1)S(1)}, bf16[320,256]{1,0:T(8,128)(2,1)S(1)}, u32[]{:S(2)}, u32[]{:S(2)}) collective-permute-start(bf16[320,256]{1,0:T(8,128)(2,1)S(1)} %shard_map.107.rest_0_), channel_id=1, source_target_pairs={{4,0},{8,4},{12,8},{5,1},{9,5},{13,9},{6,2},{10,6},{14,10},{7,3},{... | collective-permute-start | bytes 491528 | tf_op jit(solution)/shard_map/ppermute | solution.py:277
  73.3 1.3 %collective-permute-start.7 = (bf16[320,256]{1,0:T(8,128)(2,1)S(1)}, bf16[320,256]{1,0:T(8,128)(2,1)S(1)}, u32[]{:S(2)}, u32[]{:S(2)}) collective-permute-start(bf16[320,256]{1,0:T(8,128)(2,1)S(1)} %collective-permute-done.6.rest_3_), channel_id=1, source_target_pairs={{8,12},{4,0},{9,13},{5,1},{10,14},{6,2},{11,15},{7,3},{24,28},{20,... | collective-permute-start | bytes 491528 | tf_op jit(solution)/shard_map/ppermute | solution.py:279
  74.6 1.3 %collective-permute-start.10 = (bf16[320,256]{1,0:T(8,128)(2,1)S(1)}, bf16[320,256]{1,0:T(8,128)(2,1)S(1)}, u32[]{:S(2)}, u32[]{:S(2)}) collective-permute-start(bf16[320,256]{1,0:T(8,128)(2,1)S(1)} %shard_map.110.rest_0_), channel_id=1, source_target_pairs={{4,0},{8,4},{12,8},{5,1},{9,5},{13,9},{6,2},{10,6},{14,10},{7,3},{... | collective-permute-start | bytes 491528 | tf_op jit(solution)/shard_map/ppermute | solution.py:277
  75.9 5.2 %collective-permute-start.9 = (bf16[320,256]{1,0:T(8,128)(2,1)S(1)}, bf16[320,256]{1,0:T(8,128)(2,1)S(1)}, u32[]{:S(2)}, u32[]{:S(2)}) collective-permute-start(bf16[320,256]{1,0:T(8,128)(2,1)S(1)} %shard_map.110.rest_0_), channel_id=1, source_target_pairs={{0,4},{4,8},{8,12},{1,5},{5,9},{9,13},{2,6},{6,10},{10,14},{3,7},{... | collective-permute-start | bytes 491528 | tf_op jit(solution)/shard_map/ppermute | solution.py:276
  81.2 1.3 %collective-permute-start.12 = (bf16[320,256]{1,0:T(8,128)(2,1)S(1)}, bf16[320,256]{1,0:T(8,128)(2,1)S(1)}, u32[]{:S(2)}, u32[]{:S(2)}) collective-permute-start(bf16[320,256]{1,0:T(8,128)(2,1)S(1)} %collective-permute-done.11.rest_3_), channel_id=1, source_target_pairs={{8,12},{4,0},{9,13},{5,1},{10,14},{6,2},{11,15},{7,3},{24,28},{20,... | collective-permute-start | bytes 491528 | tf_op jit(solution)/shard_map/ppermute | solution.py:279
  82.5 3.3 %collective-permute-done.7.rest_4_ = bf16[320,256]{1,0:T(8,128)(2,1)S(1)} collective-permute-done((bf16[320,256]{1,0:T(8,128)(2,1)S(1)}, bf16[320,256]{1,0:T(8,128)(2,1)S(1)}, u32[]{:S(2)}, u32[]{:S(2)}) %collective-permute-start.7) | collective-permute-done | bytes 163872 | tf_op jit(solution)/shard_map/ppermute | solution.py:279
  85.8 4.0 %shard_map.108 = (f32[320,1792]{1,0:T(8,128)S(1)}, bf16[4,256,1792]{2,1,0:T(8,128)(2,1)S(1)}) custom-call(s32[3]{0:T(128)S(1)} %pad_add_fusion.sc, bf16[320,256]{1,0:T(8,128)(2,1)S(1)} %shard_map.107.rest_0_, bf16[320,256]{1,0:T(8,128)(2,1)S(1)} %collective-permute-done.4.rest_1_, bf16[320,256]{1,0:T(8,128)(2,1)S(1)} %collective-permute-done.5.rest_2_, ...), custom_call_target="tpu_custom_call" | custom-call | flops 1174405120 | bytes 3670016 | tf_op jit(solution)/shard_map/pallas_call | solution.py:105
  90.4 2.4 %shard_map.111 = (f32[160,896]{1,0:T(8,128)S(1)}, bf16[160,896]{1,0:T(8,128)(2,1)}) custom-call(s32[3]{0:T(128)S(1)} %pad_add_fusion.sc, bf16[4,256,1792]{2,1,0:T(8,128)(2,1)S(1)} %get-tuple-element.41.w_ref, f32[320,1792]{1,0:T(8,128)S(1)} %get-tuple-element.42.acc, bf16[320,256]{1,0:T(8,128)(2,1)S(1)} %shard_map.110.rest_0_, ...), custom_call_target="tpu_custom_call" | custom-call | flops 587202560 | bytes 1835008 | tf_op jit(solution)/shard_map/pallas_call | solution.py:105
  92.8 0.8 copy-done.3
  93.6 2.0 %copy-done.1 = bf16[4,256,1792]{2,1,0:T(8,128)(2,1)S(1)} copy-done((bf16[4,256,1792]{2,1,0:T(8,128)(2,1)S(1)}, bf16[4,256,1792]{2,1,0:T(8,128)(2,1)}, u32[]{:S(2)}) %copy-start.1) | copy-done | bytes 3670040
  95.6 1.7 %shard_map.112 = (f32[160,896]{1,0:T(8,128)S(1)}, bf16[160,896]{1,0:T(8,128)(2,1)S(1)}) custom-call(s32[3]{0:T(128)S(1)} %pad_add_fusion.sc, bf16[4,256,1792]{2,1,0:T(8,128)(2,1)S(1)} %copy-done.1, f32[320,1792]{1,0:T(8,128)S(1)} %get-tuple-element.42.acc, bf16[320,256]{1,0:T(8,128)(2,1)S(1)} %shard_map.110.rest_0_, ...), custom_call_target="tpu_custom_call" | custom-call | flops 587202560 | bytes 1835008 | tf_op jit(solution)/shard_map/pallas_call | solution.py:105
  98.0 1.6 %collective-permute-start.14 = (bf16[80,896]{1,0:T(8,128)(2,1)S(1)}, bf16[80,896]{1,0:T(8,128)(2,1)S(1)}, u32[]{:S(2)}, u32[]{:S(2)}) collective-permute-start(bf16[80,896]{1,0:T(8,128)(2,1)S(1)} %fusion.2), channel_id=1, source_target_pairs={{0,2},{1,3},{2,0},{3,1},{4,6},{5,7},{6,4},{7,5},{8,10},{9,11},{10,... | collective-permute-start | bytes 430088 | tf_op jit(solution)/shard_map/ppermute | solution.py:473
  99.6 1.1 %collective-permute-start.16 = (bf16[80,896]{1,0:T(8,128)(2,1)S(1)}, bf16[80,896]{1,0:T(8,128)(2,1)S(1)}, u32[]{:S(2)}, u32[]{:S(2)}) collective-permute-start(bf16[80,896]{1,0:T(8,128)(2,1)S(1)} %fusion.3), channel_id=1, source_target_pairs={{0,2},{1,3},{2,0},{3,1},{4,6},{5,7},{6,4},{7,5},{8,10},{9,11},{10,... | collective-permute-start | bytes 430088 | tf_op jit(solution)/shard_map/ppermute | solution.py:473
  100.7 3.9 %collective-permute-done.14 = bf16[80,896]{1,0:T(8,128)(2,1)S(1)} collective-permute-done((bf16[80,896]{1,0:T(8,128)(2,1)S(1)}, bf16[80,896]{1,0:T(8,128)(2,1)S(1)}, u32[]{:S(2)}, u32[]{:S(2)}) %collective-permute-start.14) | collective-permute-done | bytes 143392 | tf_op jit(solution)/shard_map/ppermute | solution.py:473
  104.7 2.1 %collective-permute-done.16 = bf16[80,896]{1,0:T(8,128)(2,1)S(1)} collective-permute-done((bf16[80,896]{1,0:T(8,128)(2,1)S(1)}, bf16[80,896]{1,0:T(8,128)(2,1)S(1)}, u32[]{:S(2)}, u32[]{:S(2)}) %collective-permute-start.16) | collective-permute-done | bytes 143392 | tf_op jit(solution)/shard_map/ppermute | solution.py:473
  (46 shorter events, 4.9 us)
Async XLA Ops:
  0.7 9.8 %copy-start.5 = (bf16[384,64]{0,1:T(8,128)(2,1)S(1)}, bf16[384,64]{0,1:T(8,128)(2,1)}, u32[]{:S(2)}) copy-start(bf16[384,64]{0,1:T(8,128)(2,1)} %param.13) | copy-start | bytes 147460
  0.7 9.8 %copy-start.10 = (bf16[384,3072]{1,0:T(8,128)(2,1)S(1)}, bf16[384,3072]{1,0:T(8,128)(2,1)}, u32[]{:S(2)}) copy-start(bf16[384,3072]{1,0:T(8,128)(2,1)} %w_ref.5) | copy-start | bytes 7077892
  4.2 30.7 %all-to-all-start = ((bf16[4,320,384]{2,1,0:T(8,128)(2,1)}), bf16[4,320,384]{2,1,0:T(8,128)(2,1)S(1)}, u32[]{:S(2)}, u32[]{:S(2)}) async-start(bf16[4,320,384]{2,1,0:T(8,128)(2,1)} %get-tuple-element.25), calls=%async_computation | async-start | bytes 1966080 | tf_op jit(solution)/shard_map/all_to_all | solution.py:383
  13.7 42.1 %copy-start.2 = (bf16[80,1536]{1,0:T(8,128)(2,1)S(1)}, bf16[80,1536]{1,0:T(8,128)(2,1)}, u32[]{:S(2)}) copy-start(bf16[80,1536]{1,0:T(8,128)(2,1)} %x_ref.3) | copy-start | bytes 737284
  13.7 42.1 %copy-start.6 = (bf16[80,576]{1,0:T(8,128)(2,1)S(1)}, bf16[80,576]{1,0:T(8,128)(2,1)}, u32[]{:S(2)}) copy-start(bf16[80,576]{1,0:T(8,128)(2,1)} %kv_ref.3) | copy-start | bytes 276484
  13.7 42.2 %copy-start.9 = (s32[80]{0:T(128)S(1)}, s32[80]{0:T(128)}, u32[]{:S(2)}) copy-start(s32[80]{0:T(128)} %param.11) | copy-start | bytes 964
  34.8 18.8 %all-to-all-start.1 = ((bf16[4,192,384]{2,1,0:T(8,128)(2,1)}), bf16[4,192,384]{2,1,0:T(8,128)(2,1)S(1)}, u32[]{:S(2)}, u32[]{:S(2)}) async-start(bf16[4,192,384]{2,1,0:T(8,128)(2,1)} %get-tuple-element.29), calls=%async_computation.1 | async-start | bytes 1179648 | tf_op jit(solution)/shard_map/all_to_all | solution.py:383
  38.9 8.0 %collective-permute-start.2 = (bf16[3,128,384]{2,1,0:T(8,128)(2,1)S(1)}, bf16[3,128,384]{2,1,0:T(8,128)(2,1)S(1)}, u32[]{:S(2)}, u32[]{:S(2)}) collective-permute-start(bf16[3,128,384]{2,1,0:T(8,128)(2,1)S(1)} %get-tuple-element.32.rest_0_), channel_id=1, source_target_pairs={{0,2},{1,3},{2,0},{3,1},{4,6},{5,7},{6,4},{7,5},{8,10},{9,11},{10,... | collective-permute-start | bytes 884744 | tf_op jit(solution)/shard_map/ppermute | solution.py:396
  40.5 10.9 %collective-permute-start = (bf16[3,192,384]{2,1,0:T(8,128)(2,1)S(1)}, bf16[3,192,384]{2,1,0:T(8,128)(2,1)S(1)}, u32[]{:S(2)}, u32[]{:S(2)}) collective-permute-start(bf16[3,192,384]{2,1,0:T(8,128)(2,1)S(1)} %get-tuple-element.30), channel_id=1, source_target_pairs={{0,16},{16,0},{1,17},{17,1},{2,18},{18,2},{3,19},{19,3},{4,20},{20... | collective-permute-start | bytes 1327112 | tf_op jit(solution)/shard_map/ppermute | solution.py:395
  42.0 5.0 %collective-permute-start.1 = (bf16[3,128,384]{2,1,0:T(8,128)(2,1)S(1)}, bf16[3,128,384]{2,1,0:T(8,128)(2,1)S(1)}, u32[]{:S(2)}, u32[]{:S(2)}) collective-permute-start(bf16[3,128,384]{2,1,0:T(8,128)(2,1)S(1)} %get-tuple-element.32.rest_0_), channel_id=1, source_target_pairs={{0,1},{1,0},{2,3},{3,2},{4,5},{5,4},{6,7},{7,6},{8,9},{9,8},{10,11... | collective-permute-start | bytes 884744 | tf_op jit(solution)/shard_map/ppermute | solution.py:399
  47.0 4.4 %collective-permute-start.3 = (bf16[3,128,384]{2,1,0:T(8,128)(2,1)S(1)}, bf16[3,128,384]{2,1,0:T(8,128)(2,1)S(1)}, u32[]{:S(2)}, u32[]{:S(2)}) collective-permute-start(bf16[3,128,384]{2,1,0:T(8,128)(2,1)S(1)} %collective-permute-done.2.rest_2_), channel_id=1, source_target_pairs={{0,1},{1,0},{2,3},{3,2},{4,5},{5,4},{6,7},{7,6},{8,9},{9,8},{10,11... | collective-permute-start | bytes 884744 | tf_op jit(solution)/shard_map/ppermute | solution.py:401
  51.3 0.7 copy-start.7
  54.3 12.5 %collective-permute-start.8 = (bf16[3,192,384]{2,1,0:T(8,128)(2,1)S(1)}, bf16[3,192,384]{2,1,0:T(8,128)(2,1)S(1)}, u32[]{:S(2)}, u32[]{:S(2)}) collective-permute-start(bf16[3,192,384]{2,1,0:T(8,128)(2,1)S(1)} %shard_map.109), channel_id=1, source_target_pairs={{0,16},{16,0},{1,17},{17,1},{2,18},{18,2},{3,19},{19,3},{4,20},{20... | collective-permute-start | bytes 1327112 | tf_op jit(solution)/shard_map/ppermute | solution.py:417
  55.9 1.0 copy-start.8
  62.3 10.9 %collective-permute-start.6 = (bf16[320,256]{1,0:T(8,128)(2,1)S(1)}, bf16[320,256]{1,0:T(8,128)(2,1)S(1)}, u32[]{:S(2)}, u32[]{:S(2)}) collective-permute-start(bf16[320,256]{1,0:T(8,128)(2,1)S(1)} %shard_map.107.rest_0_), channel_id=1, source_target_pairs={{0,8},{4,12},{8,0},{12,4},{1,9},{5,13},{9,1},{13,5},{2,10},{6,14},... | collective-permute-start | bytes 491528 | tf_op jit(solution)/shard_map/ppermute | solution.py:278
  63.4 12.5 %collective-permute-start.4 = (bf16[320,256]{1,0:T(8,128)(2,1)S(1)}, bf16[320,256]{1,0:T(8,128)(2,1)S(1)}, u32[]{:S(2)}, u32[]{:S(2)}) collective-permute-start(bf16[320,256]{1,0:T(8,128)(2,1)S(1)} %shard_map.107.rest_0_), channel_id=1, source_target_pairs={{0,4},{4,8},{8,12},{1,5},{5,9},{9,13},{2,6},{6,10},{10,14},{3,7},{... | collective-permute-start | bytes 491528 | tf_op jit(solution)/shard_map/ppermute | solution.py:276
  71.4 9.8 %collective-permute-start.11 = (bf16[320,256]{1,0:T(8,128)(2,1)S(1)}, bf16[320,256]{1,0:T(8,128)(2,1)S(1)}, u32[]{:S(2)}, u32[]{:S(2)}) collective-permute-start(bf16[320,256]{1,0:T(8,128)(2,1)S(1)} %shard_map.110.rest_0_), channel_id=1, source_target_pairs={{0,8},{4,12},{8,0},{12,4},{1,9},{5,13},{9,1},{13,5},{2,10},{6,14},... | collective-permute-start | bytes 491528 | tf_op jit(solution)/shard_map/ppermute | solution.py:278
  72.0 10.5 %collective-permute-start.5 = (bf16[320,256]{1,0:T(8,128)(2,1)S(1)}, bf16[320,256]{1,0:T(8,128)(2,1)S(1)}, u32[]{:S(2)}, u32[]{:S(2)}) collective-permute-start(bf16[320,256]{1,0:T(8,128)(2,1)S(1)} %shard_map.107.rest_0_), channel_id=1, source_target_pairs={{4,0},{8,4},{12,8},{5,1},{9,5},{13,9},{6,2},{10,6},{14,10},{7,3},{... | collective-permute-start | bytes 491528 | tf_op jit(solution)/shard_map/ppermute | solution.py:277
  73.3 12.5 %collective-permute-start.7 = (bf16[320,256]{1,0:T(8,128)(2,1)S(1)}, bf16[320,256]{1,0:T(8,128)(2,1)S(1)}, u32[]{:S(2)}, u32[]{:S(2)}) collective-permute-start(bf16[320,256]{1,0:T(8,128)(2,1)S(1)} %collective-permute-done.6.rest_3_), channel_id=1, source_target_pairs={{8,12},{4,0},{9,13},{5,1},{10,14},{6,2},{11,15},{7,3},{24,28},{20,... | collective-permute-start | bytes 491528 | tf_op jit(solution)/shard_map/ppermute | solution.py:279
  74.6 15.2 %collective-permute-start.10 = (bf16[320,256]{1,0:T(8,128)(2,1)S(1)}, bf16[320,256]{1,0:T(8,128)(2,1)S(1)}, u32[]{:S(2)}, u32[]{:S(2)}) collective-permute-start(bf16[320,256]{1,0:T(8,128)(2,1)S(1)} %shard_map.110.rest_0_), channel_id=1, source_target_pairs={{4,0},{8,4},{12,8},{5,1},{9,5},{13,9},{6,2},{10,6},{14,10},{7,3},{... | collective-permute-start | bytes 491528 | tf_op jit(solution)/shard_map/ppermute | solution.py:277
  75.9 13.9 %collective-permute-start.9 = (bf16[320,256]{1,0:T(8,128)(2,1)S(1)}, bf16[320,256]{1,0:T(8,128)(2,1)S(1)}, u32[]{:S(2)}, u32[]{:S(2)}) collective-permute-start(bf16[320,256]{1,0:T(8,128)(2,1)S(1)} %shard_map.110.rest_0_), channel_id=1, source_target_pairs={{0,4},{4,8},{8,12},{1,5},{5,9},{9,13},{2,6},{6,10},{10,14},{3,7},{... | collective-permute-start | bytes 491528 | tf_op jit(solution)/shard_map/ppermute | solution.py:276
  81.2 9.2 %collective-permute-start.12 = (bf16[320,256]{1,0:T(8,128)(2,1)S(1)}, bf16[320,256]{1,0:T(8,128)(2,1)S(1)}, u32[]{:S(2)}, u32[]{:S(2)}) collective-permute-start(bf16[320,256]{1,0:T(8,128)(2,1)S(1)} %collective-permute-done.11.rest_3_), channel_id=1, source_target_pairs={{8,12},{4,0},{9,13},{5,1},{10,14},{6,2},{11,15},{7,3},{24,28},{20,... | collective-permute-start | bytes 491528 | tf_op jit(solution)/shard_map/ppermute | solution.py:279
  89.8 3.0 %copy-start = (bf16[4,256,1792]{2,1,0:T(8,128)(2,1)}, bf16[4,256,1792]{2,1,0:T(8,128)(2,1)S(1)}, u32[]{:S(2)}) copy-start(bf16[4,256,1792]{2,1,0:T(8,128)(2,1)S(1)} %get-tuple-element.41.w_ref) | copy-start | bytes 11010052
  92.8 0.8 copy-start.3
  93.6 4.3 %collective-permute-start.13 = (bf16[160,896]{1,0:T(8,128)(2,1)}, bf16[160,896]{1,0:T(8,128)(2,1)S(1)}, u32[]{:S(2)}, u32[]{:S(2)}) collective-permute-start(bf16[160,896]{1,0:T(8,128)(2,1)} %get-tuple-element.45), channel_id=1, source_target_pairs={{0,1},{1,0},{2,3},{3,2},{4,5},{5,4},{6,7},{7,6},{8,9},{9,8},{10,11... | collective-permute-start | bytes 860168 | tf_op jit(solution)/shard_map/ppermute | solution.py:469
  93.6 2.0 %copy-start.1 = (bf16[4,256,1792]{2,1,0:T(8,128)(2,1)S(1)}, bf16[4,256,1792]{2,1,0:T(8,128)(2,1)}, u32[]{:S(2)}) copy-start(bf16[4,256,1792]{2,1,0:T(8,128)(2,1)} %copy-done) | copy-start | bytes 11010052
  95.6 2.2 %copy-start.4 = (f32[160,896]{1,0:T(8,128)S(1)}, f32[160,896]{1,0:T(8,128)}, u32[]{:S(2)}) copy-start(f32[160,896]{1,0:T(8,128)} %copy-done.3) | copy-start | bytes 1720324
  97.3 2.2 %collective-permute-start.15 = (bf16[160,896]{1,0:T(8,128)(2,1)S(1)}, bf16[160,896]{1,0:T(8,128)(2,1)S(1)}, u32[]{:S(2)}, u32[]{:S(2)}) collective-permute-start(bf16[160,896]{1,0:T(8,128)(2,1)S(1)} %get-tuple-element.47), channel_id=1, source_target_pairs={{0,1},{1,0},{2,3},{3,2},{4,5},{5,4},{6,7},{7,6},{8,9},{9,8},{10,11... | collective-permute-start | bytes 860168 | tf_op jit(solution)/shard_map/ppermute | solution.py:469
  98.0 6.7 %collective-permute-start.14 = (bf16[80,896]{1,0:T(8,128)(2,1)S(1)}, bf16[80,896]{1,0:T(8,128)(2,1)S(1)}, u32[]{:S(2)}, u32[]{:S(2)}) collective-permute-start(bf16[80,896]{1,0:T(8,128)(2,1)S(1)} %fusion.2), channel_id=1, source_target_pairs={{0,2},{1,3},{2,0},{3,1},{4,6},{5,7},{6,4},{7,5},{8,10},{9,11},{10,... | collective-permute-start | bytes 430088 | tf_op jit(solution)/shard_map/ppermute | solution.py:473
  99.6 7.2 %collective-permute-start.16 = (bf16[80,896]{1,0:T(8,128)(2,1)S(1)}, bf16[80,896]{1,0:T(8,128)(2,1)S(1)}, u32[]{:S(2)}, u32[]{:S(2)}) collective-permute-start(bf16[80,896]{1,0:T(8,128)(2,1)S(1)} %fusion.3), channel_id=1, source_target_pairs={{0,2},{1,3},{2,0},{3,1},{4,6},{5,7},{6,4},{7,5},{8,10},{9,11},{10,... | collective-permute-start | bytes 430088 | tf_op jit(solution)/shard_map/ppermute | solution.py:473

commit v4 on v3

--- a/solution.py
+++ b/solution.py
@@ -11,6 +11,9 @@
 CHUNKS = 2
 VMEM_BYTES = 20 * 1024 * 1024
 TILE = 512
+W_PARTS = 4
+HEAD_PARTS = 2
+PACK_PARTS = 4
 
 
 def on_device(
@@ -98,7 +101,7 @@
     return [(i, i ^ bit) for i in range(n)]
 
 
-def call(body, outs, args, hbm=(), scratch=(), flops=0, moved=0):
+def call(body, outs, args, hbm=(), scratch=(), alias=None, flops=0, moved=0):
     vmem = pl.BlockSpec(memory_space=pltpu.VMEM)
     far = pl.BlockSpec(memory_space=pl.ANY)
     args = [pltpu.with_memory_space_constraint(a, pltpu.HBM) if i in hbm else a for i, a in enumerate(args)]
@@ -112,6 +115,7 @@
             out_specs=jax.tree.map(lambda o: vmem, outs),
             scratch_shapes=list(scratch),
         ),
+        input_output_aliases=alias or {},
         compiler_params=pltpu.CompilerParams(vmem_limit_bytes=VMEM_BYTES),
         cost_estimate=pl.CostEstimate(flops=flops, bytes_accessed=moved, transcendentals=0),
     )(*args)
@@ -134,11 +138,12 @@
 
 
 def pack_body(n, kq, vq, aq, wide, kvr, sc, x_ref, kv_ref, at_ref, pos_ref, w_ref, *rest):
-    outs, (xs, kvs, ats, ps, turn, turned, sems) = rest[:CHUNKS], rest[CHUNKS:]
-    g, h = sc[1], sc[2]
+    count = CHUNKS * (n - 1)
+    outs, (xs, kvs, ats, ps, turn, turned, sems) = rest[:count], rest[count:]
+    s, g, h = sc[0], sc[1], sc[2]
     tok = x_ref.shape[0]
     rope = kv_ref.shape[1] - kvr
-    half = outs[1].shape[1]
+    half = outs[-1].shape[0]
     small = [
         (x_ref.at[:, pl.ds(pl.multiple_of(h * kq, 128), kq)], xs),
         (kv_ref, kvs),
@@ -148,9 +153,10 @@
     mine = pl.ds(pl.multiple_of(g * half, 16), half)
     large = []
     for c in range(CHUNKS):
-        for j in range(n):
-            at = (j * CHUNKS + c) * wide
-            large.append((w_ref.at[mine, at : at + wide], outs[c].at[j, :half]))
+        for k in range(1, n):
+            chunk = lax.rem(s + k, n) * CHUNKS + c
+            columns = pl.ds(pl.multiple_of(chunk * wide, 128), wide)
+            large.append((w_ref.at[mine, columns], outs[c * (n - 1) + k - 1].at[:half]))
     copies = fetch(small + large, sems)
     turn[...] = jnp.zeros_like(turn)
     for copy in copies[: len(small)]:
@@ -164,8 +170,7 @@
     ropes = turned[pl.ds(pl.multiple_of(h * aq, 16), aq), :].astype(jnp.bfloat16)
     third = (tok + aq) // 3
     tail = jnp.concatenate([keys, ropes], axis=0)
-    for j in range(n):
-        first = outs[0].at[j]
+    for first in outs[: n - 1]:
         first[half : half + tok, :] = xs[...]
         first[half + tok : half + tok + aq, :] = ats[...]
         for i in range(3):
@@ -174,19 +179,21 @@
         copy.wait()
 
 
-def split_body(n, half, sc, u_ref, *outs):
-    for k in range(1, n):
-        src = lax.rem(sc[0] - k + n, n)
-        outs[0][k - 1] = u_ref[src, :half]
+def split_body(n, half, sc, *refs):
+    outs = refs[n - 1 :]
+    for k in range(n - 1):
+        outs[0][k] = refs[k][:half]
         if len(outs) > 1:
-            outs[1][k - 1] = u_ref[src, half:]
-
-
-def unpack_body(n, nh, kq, vq, aq, kvr, sc, x_ref, kv_ref, at_ref, pos_ref, *rest):
-    stacks, (xo, kvo, ao, bias), turn = rest[:nh], rest[nh : nh + 4], rest[nh + 4]
+            outs[1][k] = refs[k][half:]
+
+
+def unpack(n, nh, kq, vq, aq, sc, own, units, stacks, outs, turn):
+    (x_ref, kv_ref, at_ref, pos_ref), (xo, kvo, ao, bias) = own, outs
     s, h = sc[0], sc[2]
     tok, depth = x_ref.shape[0], at_ref.shape[1]
+    kvr = vq * nh
     rope = kv_ref.shape[1] - kvr
+    half = units[0].shape[0] - stacks[0].shape[1]
     third = (tok + aq) // 3
     tokens = bias.shape[0]
     row = pl.multiple_of(s * tok, 16)
@@ -200,7 +207,7 @@
         rows = pl.ds(pl.multiple_of(src * tok, 16), tok)
         for j in range(nh):
             hh = h ^ j
-            got = stacks[j].at[k - 1]
+            got = stacks[j - 1].at[k - 1] if j else units[k - 1].at[half:]
             xo[rows, pl.ds(pl.multiple_of(hh * kq, 128), kq)] = got[:tok, :]
             arow = pl.ds(pl.multiple_of(hh * aq, 16), aq)
             ao[arow, pl.ds(pl.multiple_of(src * depth, 128), depth)] = got[tok : tok + aq, :]
@@ -209,7 +216,8 @@
             turn[arow, :] = tail[tok:].astype(jnp.float32)
         turned = turn[...].T
         kvo[rows, kvr:] = turned[:tok, :rope].astype(jnp.bfloat16)
-        starts.append((src, turned[tok : tok + 1, :1] + turned[tok + 1 : tok + 2, :1] + turned[tok + 2 : tok + 3, :1]))
+        terms = [turned[tok + i : tok + i + 1, :1] for i in range(3)]
+        starts.append((src, terms[0] + terms[1] + terms[2]))
 
     def places(shape, dim):
         index = lax.broadcasted_iota(jnp.int32, shape, dim)
@@ -223,8 +231,10 @@
     bias[...] = jnp.where(seen, 0.0, -1e30)
 
 
-def attend_body(n, nope, scale, c, sc, x_ref, at_ref, kv_ref, bias_ref, u_ref, y_ref, b_ref, w_ref, ku_ref, vu_ref, *rest):
-    out, raw, b_own, ku, vu, sems = rest
+def attend(n, nope, scale, c, sc, shared, units, y_ref, weights, out, scratch, before=None):
+    x_ref, kv_ref, at_ref, bias_ref = shared
+    b_ref, w_ref, ku_ref, vu_ref = weights
+    raw, b_own, ku, vu, sems = scratch
     s, g = sc[0], sc[1]
     depth = w_ref.shape[0]
     half = depth // 2
@@ -232,26 +242,36 @@
     heads, kvr, vdim = vu.shape
     chunk = s * CHUNKS + c
     columns = pl.ds(pl.multiple_of(chunk * wide, 128), wide)
-    copies = fetch(
+    mine = pl.ds(pl.multiple_of(s * depth, 128), depth)
+    b_copy, w_copy, ku_copy, vu_copy = fetch(
         [
             (b_ref.at[:, columns], b_own),
-            (w_ref.at[:, columns], raw.at[pl.ds(pl.multiple_of(s * depth, 16), depth), :]),
+            (w_ref.at[:, columns], raw.at[mine, :]),
             (ku_ref.at[pl.ds(chunk * heads, heads)], ku),
             (vu_ref.at[pl.ds(chunk * heads, heads)], vu),
         ],
         sems,
     )
+    if before is not None:
+        before()
     for k in range(1, n):
         src = lax.rem(s - k + n, n)
-        raw[pl.ds(pl.multiple_of(src * depth + g * half, 16), half), :] = u_ref[src, :half]
+        raw[pl.ds(pl.multiple_of(src * depth + g * half, 16), half), :] = units[k - 1][:half]
         raw[pl.ds(pl.multiple_of(src * depth + (1 - g) * half, 16), half), :] = y_ref[k - 1]
-    for copy in copies:
-        copy.wait()
-    add = lax.dot_general(
-        at_ref[...], b_own[...], (((0,), (0,)), ((), ())), preferred_element_type=jnp.float32
-    )
-    merged = (raw[...].astype(jnp.float32) + add).astype(jnp.bfloat16)
-    q = jnp.dot(x_ref[...], merged, preferred_element_type=jnp.float32)
+    b_copy.wait()
+    w_copy.wait()
+
+    def merge(rows):
+        add = lax.dot_general(
+            at_ref[:, rows], b_own[...], (((0,), (0,)), ((), ())), preferred_element_type=jnp.float32
+        )
+        raw[rows, :] = (raw[rows, :].astype(jnp.float32) + add).astype(jnp.bfloat16)
+
+    for src in range(n):
+        merge(slice(src * depth, (src + 1) * depth))
+    q = jnp.dot(x_ref[...], raw[...], preferred_element_type=jnp.float32)
+    ku_copy.wait()
+    vu_copy.wait()
     width = wide // heads
     lat, rope_key = kv_ref[:, :kvr], kv_ref[:, kvr:]
     bias = bias_ref[...]
@@ -272,6 +292,22 @@
         out[:, j * vdim : (j + 1) * vdim] = ho.astype(jnp.bfloat16)
 
 
+def attend_first(n, nh, kq, vq, aq, nope, scale, sc, *refs):
+    own, units, y_ref, stacks = refs[:4], refs[4 : 3 + n], refs[3 + n], refs[4 + n : 3 + n + nh]
+    refs = refs[3 + n + nh :]
+    weights, out, shared, turn, scratch = refs[:4], refs[4], refs[5:9], refs[9], refs[10:]
+
+    def before():
+        unpack(n, nh, kq, vq, aq, sc, own, units, stacks, shared, turn)
+
+    attend(n, nope, scale, 0, sc, shared, units, y_ref, weights, out, scratch, before)
+
+
+def attend_next(n, nope, scale, sc, *refs):
+    shared, units, refs = refs[:4], refs[4 : 3 + n], refs[3 + n :]
+    attend(n, nope, scale, CHUNKS - 1, sc, shared, units, refs[0], refs[1:5], refs[5], refs[6:])
+
+
 def gather_line(x):
     left = lax.ppermute(x, "seq", [(0, 1), (1, 2), (2, 3)])
     right = lax.ppermute(x, "seq", [(1, 0), (2, 1), (3, 2)])
@@ -303,41 +339,61 @@
         put(3 - s, three)
 
 
-def first_body(n, sc, *rest):
-    slots, (w_ref, acc, kept, lhs, w, sems) = rest[:5], rest[5:]
-    width = lhs.shape[1] // n
-    pairs = [(w_ref.at[j, 0], w.at[j]) for j in range(n)]
-    copies = fetch(pairs + [(w_ref.at[j, 1], kept.at[j]) for j in range(n)], sems)
+def columns_dot(lhs, w, begin, end, put):
+    for at in range(begin, end, TILE):
+        stop = min(at + TILE, end)
+        tile = w[:, :, at:stop]
+        tile = tile.reshape(lhs.shape[1], tile.shape[-1])
+        put(slice(at, stop), jnp.dot(lhs[...], tile, preferred_element_type=jnp.float32))
+
+
+def first_body(n, cut, sc, *refs):
+    slots, (w_ref, acc, later, lhs, w, sems) = refs[:5], refs[5:]
+    copies = fetch(
+        [(w_ref.at[j, 0], w.at[j]) for j in range(n)]
+        + [(w_ref.at[j, 1, :, :cut], later.at[j]) for j in range(n)],
+        sems,
+    )
     place_line(sc[0], slots, lhs)
-    total = acc.shape[1]
-    for j in range(n):
-        copies[j].wait()
-    for at in range(0, total, TILE):
-        band = slice(at, min(at + TILE, total))
-        tile = w[:, :, band]
-        tile = tile.reshape(lhs.shape[1], tile.shape[-1])
-        acc[:, band] = jnp.dot(lhs[...], tile, preferred_element_type=jnp.float32)
+    for copy in copies[:n]:
+        copy.wait()
+
+    def put(band, value):
+        acc[:, band] = value
+
+    columns_dot(lhs, w, 0, acc.shape[1], put)
     for copy in copies[n:]:
         copy.wait()
 
 
-def last_body(nh, tok, begin, sc, w_ref, acc, *rest):
-    slots, (keep, send), lhs, tot = rest[:5], rest[5:7], rest[7], rest[8]
+def last_body(nh, tok, begin, sc, w, acc, slots, keep, send, lhs, tot):
     place_line(sc[0], slots, lhs)
-    total = keep.shape[1]
-    for at in range(0, total, TILE):
-        end = min(at + TILE, total)
-        w = w_ref[:, :, begin + at : begin + end]
-        w = w.reshape(lhs.shape[1], w.shape[-1])
-        tot[:, at:end] = acc[:, begin + at : begin + end] + jnp.dot(
-            lhs[...], w, preferred_element_type=jnp.float32
-        )
+
+    def put(band, value):
+        tot[:, band] = acc[:, begin + band.start : begin + band.stop] + value
+
+    columns_dot(lhs, w, 0, keep.shape[1], put)
     core = sc[2] % 2
     for i in range(nh // 2):
         mine = pl.ds(pl.multiple_of((2 * i + core) * tok, 16), tok)
         theirs = pl.ds(pl.multiple_of((2 * i + 1 - core) * tok, 16), tok)
         keep[i * tok : (i + 1) * tok, :] = tot[mine, :]
         send[i * tok : (i + 1) * tok, :] = tot[theirs, :].astype(jnp.bfloat16)
+
+
+def last_left(n, nh, tok, sc, *refs):
+    slots, (w, acc, w_ref, keep, send, later, lhs, tot, sems) = refs[:5], refs[5:]
+    cut = keep.shape[1]
+    copies = fetch([(w_ref.at[j, 1, :, cut:], later.at[j]) for j in range(n)], sems)
+    last_body(nh, tok, 0, sc, w, acc, slots, keep, send, lhs, tot)
+    for copy in copies:
+        copy.wait()
+
+
+def last_right(nh, tok, sc, *refs):
+    slots, (w, acc, held, keep, send, passed, lhs, tot) = refs[:5], refs[5:]
+    del held, passed
+    last_body(nh, tok, acc.shape[1] - keep.shape[1], sc, w, acc, slots, keep, send, lhs, tot)
 
 
 def by_heads(x, kv, pos, wq, down, up, ku, vu, wo):
@@ -365,7 +421,7 @@
 
     units = call(
         functools.partial(pack_body, n, kq, vq, aq, wide, kvr),
-        tuple([like(n, half + extra, wide)] + [like(n, half, wide)] * (CHUNKS - 1)),
+        tuple([like(half + extra, wide)] * (n - 1) + [like(half, wide)] * (n - 1) * (CHUNKS - 1)),
         [sc, x, kv, at, pos2, wq],
         hbm=range(1, 6),
         scratch=[
@@ -375,74 +431,79 @@
             pltpu.VMEM(pos2.shape, jnp.int32),
             pltpu.VMEM((128, 128), f32),
             pltpu.VMEM((128, 128), f32),
-            pltpu.SemaphoreType.DMA((4 + n * CHUNKS,)),
+            pltpu.SemaphoreType.DMA((4 + (n - 1) * CHUNKS,)),
         ],
         moved=4 * half * cols,
     )
-    def exchange(unit):
-        return lax.all_to_all(unit, "seq", 0, 0, tiled=True)
+    def exchange(parts):
+        return [lax.ppermute(p, "seq", cyclic(n, k)) for p, k in zip(parts, range(1, n))]
 
     def split(got, *sizes):
         outs = tuple(like(n - 1, size, wide) for size in sizes)
-        return call(functools.partial(split_body, n, half), outs, [sc, got], moved=4 * got.size)
+        return call(functools.partial(split_body, n, half), outs, [sc] + got, moved=4 * 3 * got[0].size)
 
     merged = (wq.astype(f32) + jnp.dot(down, up, preferred_element_type=f32)).astype(bf)
-    moved = [exchange(units[0])]
-    moved[0], merged = lax.optimization_barrier((moved[0], merged))
-    later, _ = lax.optimization_barrier((units[1], moved[0]))
-    moved.append(exchange(later))
+    moved = [exchange(units[: n - 1])]
+    *moved[0], merged = lax.optimization_barrier((*moved[0], merged))
+    later = lax.optimization_barrier((*units[n - 1 :], moved[0][0]))
+    moved.append(exchange(later[: n - 1]))
     share, stack = split(moved[0], half, extra)
     passed = [lax.ppermute(share, "groups", cyclic(2, 1))]
     across = lax.ppermute(stack, "head", flipped(nh, 2))
+    across, *moved[1] = lax.optimization_barrier((across, *moved[1]))
     stacks = [
-        stack,
         lax.ppermute(stack, "head", flipped(nh, 1)),
         across,
         lax.ppermute(across, "head", flipped(nh, 1)),
     ]
-    moved[1], passed[0], *stacks = lax.optimization_barrier((moved[1], passed[0], *stacks))
-    x_all, kv_all, at_all, bias = call(
-        functools.partial(unpack_body, n, nh, kq, vq, aq, kvr),
+    (share,) = split(moved[1], half)
+    passed.append(lax.ppermute(share, "groups", cyclic(2, 1)))
+
+    scale = 1.0 / math.sqrt(nope + rope)
+    scratch = [
+        pltpu.VMEM((n * rows, wide), bf),
+        pltpu.VMEM((rank, wide), bf),
+        pltpu.VMEM((per, nope, kvr), bf),
+        pltpu.VMEM((per, kvr, vdim), bf),
+        pltpu.SemaphoreType.DMA((4,)),
+    ]
+    cost = dict(
+        flops=2 * tokens * per * (depth * wide // per + 2 * nope * kvr + 2 * tokens * kvr),
+        moved=4 * n * rows * wide,
+    )
+    ho, *shared = call(
+        functools.partial(attend_first, n, nh, kq, vq, aq, nope, scale),
         (
+            like(tokens, per * vdim),
             like(tokens, depth),
             like(tokens, kvr + rope),
             like(rank, n * rows),
             like(tokens, tokens, dtype=f32),
         ),
-        [sc, x, kv, at, pos2] + stacks,
-        scratch=[pltpu.VMEM((128, 128), f32)],
-        moved=4 * tokens * depth,
-    )
-    (share,) = split(moved[1], half)
-    passed.append(lax.ppermute(share, "groups", cyclic(2, 1)))
-
-    scale = 1.0 / math.sqrt(nope + rope)
-    slots = []
-    for c in range(CHUNKS):
-        ho = call(
-            functools.partial(attend_body, n, nope, scale, c),
-            like(tokens, per * vdim),
-            [sc, x_all, at_all, kv_all, bias, moved[c], passed[c], up, wq, ku, vu],
-            hbm=range(7, 11),
-            scratch=[
-                pltpu.VMEM((n * rows, wide), bf),
-                pltpu.VMEM((rank, wide), bf),
-                pltpu.VMEM((per, nope, kvr), bf),
-                pltpu.VMEM((per, kvr, vdim), bf),
-                pltpu.SemaphoreType.DMA((4,)),
-            ],
-            flops=2 * tokens * per * (depth * wide // per + 2 * nope * kvr + 2 * tokens * kvr),
-            moved=4 * n * rows * wide,
-        )
-        slots.append(gather_line(ho))
+        [sc, x, kv, at, pos2] + moved[0] + [passed[0]] + stacks + [up, wq, ku, vu],
+        hbm=range(4 + n + nh, 8 + n + nh),
+        scratch=[pltpu.VMEM((128, 128), f32)] + scratch,
+        **cost,
+    )
+    slots = [gather_line(ho)]
+    ho = call(
+        functools.partial(attend_next, n, nope, scale),
+        like(tokens, per * vdim),
+        [sc] + shared + moved[1] + [passed[1], up, wq, ku, vu],
+        hbm=range(5 + n, 9 + n),
+        scratch=scratch,
+        **cost,
+    )
+    slots.append(gather_line(ho))
 
     w4 = wo.reshape(n, CHUNKS, per * vdim, wo.shape[1])
     total = wo.shape[1]
     lhs = pltpu.VMEM((tokens, n * per * vdim), bf)
     flops = 2 * tokens * n * per * vdim * total
-    acc, w_last = call(
-        functools.partial(first_body, n),
-        (like(tokens, total, dtype=f32), like(n, per * vdim, total)),
+    cut = (total // 128 + 1) // 2 * 128
+    acc, w_left = call(
+        functools.partial(first_body, n, cut),
+        (like(tokens, total, dtype=f32), like(n, per * vdim, cut)),
         [sc] + slots[0] + [w4],
         hbm=(6,),
         scratch=[
@@ -453,21 +514,35 @@
         flops=flops,
         moved=w4.size,
     )
+    pair_rows = nh // 2 * tok
+
+    def partial_sums(size):
+        return (like(pair_rows, size, dtype=f32), like(pair_rows, size))
+
+    keep, send, w_right = call(
+        functools.partial(last_left, n, nh, tok),
+        partial_sums(cut) + (like(n, per * vdim, total - cut),),
+        [sc] + slots[1] + [w_left, acc, w4],
+        hbm=(8,),
+        scratch=[lhs, pltpu.VMEM((tokens, cut), f32), pltpu.SemaphoreType.DMA((n,))],
+        flops=flops // 2,
+        moved=w4.size // 2,
+    )
+    left = send
+    keep_right, right, keep = call(
+        functools.partial(last_right, nh, tok),
+        partial_sums(total - cut) + (like(pair_rows, cut, dtype=f32),),
+        [sc] + slots[1] + [w_right, acc, keep],
+        scratch=[lhs, pltpu.VMEM((tokens, total - cut), f32)],
+        alias={8: 2},
+        flops=flops // 2,
+        moved=w4.size // 2,
+    )
     side = h // 2
     bands = []
-    cut = (total // 128 + 1) // 2 * 128
-    for begin, end in ((0, cut), (cut, total)):
-        size = end - begin
-        keep, send = call(
-            functools.partial(last_body, nh, tok, begin),
-            (like(nh // 2 * tok, size, dtype=f32), like(nh // 2 * tok, size)),
-            [sc, w_last, acc] + slots[1],
-            scratch=[lhs, pltpu.VMEM((tokens, size), f32)],
-            flops=flops * size // total,
-            moved=w4.size * size // total,
-        )
+    for keep, send in ((keep, left), (keep_right, right)):
         got = lax.ppermute(send, "head", flipped(nh, 1))
-        pair = (keep + got.astype(f32)).reshape(nh // 2, tok, size)
+        pair = (keep + got.astype(f32)).reshape(nh // 2, tok, keep.shape[1])
         out = lax.dynamic_index_in_dim(pair, side, 0, keepdims=False)
         away = lax.dynamic_index_in_dim(pair, 1 - side, 0, keepdims=False).astype(bf)
         out = out + lax.ppermute(away, "head", flipped(nh, 2)).astype(f32)

time: 108 us -> 102 us (0.944)
  starting transfers between devices: 33.1 us -> 41.3 us
  waiting for transfers between devices: 42.1 us -> 34.8 us
  local copies, waits for them, and re-layouts: 4.61 us -> 0.08 us
  Pallas kernels: 22.7 us -> 20.2 us
    all_to_all x2 -> x0, waiting for transfers between devices: 22.7 us -> none  [exchange(): return lax.all_to_all(unit, 'seq', 0, 0, tiled=True)]
    ppermute x0 -> x6, waiting for transfers between devices: none -> 18.2 us  [exchange(): lax.ppermute(p, 'seq', cyclic(n, k))]
    ppermute x0 -> x6, starting transfers between devices: none -> 15.1 us  [exchange(): lax.ppermute(p, 'seq', cyclic(n, k))]
    all_to_all x2 -> x0, starting transfers between devices: 9.81 us -> none  [exchange(): return lax.all_to_all(unit, 'seq', 0, 0, tiled=True)]
    ppermute x1, waiting for transfers between devices: 4.96 us -> 0.01 us  [by_heads(): across = lax.ppermute(stack, 'head', flipped(nh, 2))]
    unnamed x22 -> x10, local copies, waits for them, and re-layouts: 4.56 us -> 0.02 us
    ppermute x1, waiting for transfers between devices: 4.36 us -> 0.01 us  [by_heads(): passed = [lax.ppermute(share, 'groups', cyclic(2, 1))]]
    pallas_call x9 -> x8, Pallas kernels: 22.7 us -> 20.2 us  [call(): pl.pallas_call(body, out_shape=outs, grid_spec=pltpu.PrefetchScalarGridSp...]
  transfers between devices with their start and end apart: 19 -> 23, of which waited for: 9 -> 13; matrix products, arithmetic and copies ran while one was open for 3% -> 3% of each run, Pallas kernels for 15% -> 14%
where the time goes in v4:
time: 102 us; the launch traced here: 101 us
  starting transfers between devices  41.3 us (40%)
  waiting for transfers between devices  34.8 us (34%)
  Pallas kernels  20.2 us (20%)
  matrix products  3.2 us (3%)
    pallas_call x8, Pallas kernels, call(): pl.pallas_call(body, out_shape=outs, grid_spec=pltpu.PrefetchScalarGridSp...  20.2 us
    ppermute x6, waiting for transfers between devices, exchange(): lax.ppermute(p, 'seq', cyclic(n, k))  18.2 us
    ppermute x6, starting transfers between devices, exchange(): lax.ppermute(p, 'seq', cyclic(n, k))  15.1 us
    ppermute x2, starting transfers between devices, gather_line(): left = lax.ppermute(x, 'seq', [(0, 1), (1, 2), (2, 3)])  9.44 us
    ppermute x2, waiting for transfers between devices, by_heads(): out = out + lax.ppermute(away, 'head', flipped(nh, 2)).astype(f32)  6.64 us
    ppermute x2, waiting for transfers between devices, gather_line(): three = lax.ppermute(two, 'seq', [(2, 3), (1, 0)])  4.83 us
    ppermute x2, starting transfers between devices, gather_line(): two = lax.ppermute(x, 'seq', cyclic(4, 2))  3.7 us
    dot_general x1, matrix products, by_heads(): jnp.dot(down, up, preferred_element_type=f32)  3.2 us
  transfers between devices with their start and end apart: 23, of which 13 were waited for; matrix products, arithmetic and copies ran while one was open for 3% of the time, Pallas kernels for 14%

profile of v4, /device:TPU:0, one launch (start us, length us, event | category | flops | bytes accessed | tf_op | source)
XLA Modules:
  0.0 101.4 jit_solution(2259167950754698188)
XLA Ops:
  0.7 2.0 %shard_map.104 = (bf16[320,384]{1,0:T(8,128)(2,1)S(1)}, bf16[320,384]{1,0:T(8,128)(2,1)S(1)}, bf16[320,384]{1,0:T(8,128)(2,1)S(1)}, bf16[192,384]{1,0:T(8,128)(2...) custom-call(s32[3]{0:T(128)S(1)} %pad_add_fusion.sc, bf16[80,1536]{1,0:T(8,128)(2,1)} %refs_0_.1, ...), custom_call_target="tpu_custom_call" | custom-call | bytes 2359296 | tf_op jit(solution)/shard_map/pallas_call | solution.py:108
  2.8 3.1 %collective-permute-start = (bf16[320,384]{1,0:T(8,128)(2,1)S(1)}, bf16[320,384]{1,0:T(8,128)(2,1)S(1)}, u32[]{:S(2)}, u32[]{:S(2)}) collective-permute-start(bf16[320,384]{1,0:T(8,128)(2,1)S(1)} %get-tuple-element.34), channel_id=1, source_target_pairs={{0,4},{4,8},{8,12},{12,0},{1,5},{5,9},{9,13},{13,1},{2,6},{6,10},{... | collective-permute-start | bytes 737288 | tf_op jit(solution)/shard_map/ppermute | solution.py:439
  5.9 2.6 %collective-permute-start.1 = (bf16[320,384]{1,0:T(8,128)(2,1)S(1)}, bf16[320,384]{1,0:T(8,128)(2,1)S(1)}, u32[]{:S(2)}, u32[]{:S(2)}) collective-permute-start(bf16[320,384]{1,0:T(8,128)(2,1)S(1)} %get-tuple-element.35), channel_id=1, source_target_pairs={{0,8},{4,12},{8,0},{12,4},{1,9},{5,13},{9,1},{13,5},{2,10},{6,14},... | collective-permute-start | bytes 737288 | tf_op jit(solution)/shard_map/ppermute | solution.py:439
  8.5 1.3 %collective-permute-start.2 = (bf16[320,384]{1,0:T(8,128)(2,1)S(1)}, bf16[320,384]{1,0:T(8,128)(2,1)S(1)}, u32[]{:S(2)}, u32[]{:S(2)}) collective-permute-start(bf16[320,384]{1,0:T(8,128)(2,1)S(1)} %get-tuple-element.36), channel_id=1, source_target_pairs={{0,12},{4,0},{8,4},{12,8},{1,13},{5,1},{9,5},{13,9},{2,14},{6,2},{... | collective-permute-start | bytes 737288 | tf_op jit(solution)/shard_map/ppermute | solution.py:439
  9.8 3.2 %add_convert_fusion = bf16[384,3072]{1,0:T(8,128)(2,1)} fusion(bf16[384,3072]{1,0:T(8,128)(2,1)S(1)} %copy-done.4, bf16[384,64]{0,1:T(8,128)(2,1)S(1)} %copy-done.1, bf16[64,3072]{1,0:T(8,128)(2,1)} %refs_8_.1), kind=kOutput, calls=%fused_computation | convolution fusion | flops 154533888 | bytes 5160960 | tf_op jit(solution)/shard_map/dot_general | solution.py:445
  13.0 1.8 %collective-permute-done.refs_0_.refs_4_ = bf16[320,384]{1,0:T(8,128)(2,1)S(1)} collective-permute-done((bf16[320,384]{1,0:T(8,128)(2,1)S(1)}, bf16[320,384]{1,0:T(8,128)(2,1)S(1)}, u32[]{:S(2)}, u32[]{:S(2)}) %collective-permute-start) | collective-permute-done | bytes 245792 | tf_op jit(solution)/shard_map/ppermute | solution.py:439
  14.8 9.7 %collective-permute-done.1.refs_1_.refs_5_ = bf16[320,384]{1,0:T(8,128)(2,1)S(1)} collective-permute-done((bf16[320,384]{1,0:T(8,128)(2,1)S(1)}, bf16[320,384]{1,0:T(8,128)(2,1)S(1)}, u32[]{:S(2)}, u32[]{:S(2)}) %collective-permute-start.1) | collective-permute-done | bytes 245792 | tf_op jit(solution)/shard_map/ppermute | solution.py:439
  25.1 1.6 %collective-permute-start.5 = (bf16[3,128,384]{2,1,0:T(8,128)(2,1)S(1)}, bf16[3,128,384]{2,1,0:T(8,128)(2,1)S(1)}, u32[]{:S(2)}, u32[]{:S(2)}) collective-permute-start(bf16[3,128,384]{2,1,0:T(8,128)(2,1)S(1)} %get-tuple-element.42), channel_id=1, source_target_pairs={{0,2},{1,3},{2,0},{3,1},{4,6},{5,7},{6,4},{7,5},{8,10},{9,11},{10,... | collective-permute-start | bytes 884744 | tf_op jit(solution)/shard_map/ppermute | solution.py:452
  26.7 5.7 %collective-permute-start.6 = (bf16[192,384]{1,0:T(8,128)(2,1)S(1)}, bf16[192,384]{1,0:T(8,128)(2,1)S(1)}, u32[]{:S(2)}, u32[]{:S(2)}) collective-permute-start(bf16[192,384]{1,0:T(8,128)(2,1)S(1)} %get-tuple-element.46), channel_id=1, source_target_pairs={{0,4},{4,8},{8,12},{12,0},{1,5},{5,9},{9,13},{13,1},{2,6},{6,10},{... | collective-permute-start | bytes 442376 | tf_op jit(solution)/shard_map/ppermute | solution.py:439
  32.4 1.6 %collective-permute-start.7 = (bf16[192,384]{1,0:T(8,128)(2,1)S(1)}, bf16[192,384]{1,0:T(8,128)(2,1)S(1)}, u32[]{:S(2)}, u32[]{:S(2)}) collective-permute-start(bf16[192,384]{1,0:T(8,128)(2,1)S(1)} %get-tuple-element.47), channel_id=1, source_target_pairs={{0,8},{4,12},{8,0},{12,4},{1,9},{5,13},{9,1},{13,5},{2,10},{6,14},... | collective-permute-start | bytes 442376 | tf_op jit(solution)/shard_map/ppermute | solution.py:439
  34.8 1.5 %collective-permute-start.3 = (bf16[3,192,384]{2,1,0:T(8,128)(2,1)S(1)}, bf16[3,192,384]{2,1,0:T(8,128)(2,1)S(1)}, u32[]{:S(2)}, u32[]{:S(2)}) collective-permute-start(bf16[3,192,384]{2,1,0:T(8,128)(2,1)S(1)} %get-tuple-element.41), channel_id=1, source_target_pairs={{0,16},{16,0},{1,17},{17,1},{2,18},{18,2},{3,19},{19,3},{4,20},{20... | collective-permute-start | bytes 1327112 | tf_op jit(solution)/shard_map/ppermute | solution.py:451
  36.3 1.8 %collective-permute-done.6.refs_0_.refs_4_ = bf16[192,384]{1,0:T(8,128)(2,1)S(1)} collective-permute-done((bf16[192,384]{1,0:T(8,128)(2,1)S(1)}, bf16[192,384]{1,0:T(8,128)(2,1)S(1)}, u32[]{:S(2)}, u32[]{:S(2)}) %collective-permute-start.6) | collective-permute-done | bytes 147488 | tf_op jit(solution)/shard_map/ppermute | solution.py:439
  38.1 4.8 %collective-permute-done.7.refs_1_.refs_5_ = bf16[192,384]{1,0:T(8,128)(2,1)S(1)} collective-permute-done((bf16[192,384]{1,0:T(8,128)(2,1)S(1)}, bf16[192,384]{1,0:T(8,128)(2,1)S(1)}, u32[]{:S(2)}, u32[]{:S(2)}) %collective-permute-start.7) | collective-permute-done | bytes 147488 | tf_op jit(solution)/shard_map/ppermute | solution.py:439
  43.6 1.6 %collective-permute-start.10 = (bf16[3,192,384]{2,1,0:T(8,128)(2,1)S(1)}, bf16[3,192,384]{2,1,0:T(8,128)(2,1)S(1)}, u32[]{:S(2)}, u32[]{:S(2)}) collective-permute-start(bf16[3,192,384]{2,1,0:T(8,128)(2,1)S(1)} %shard_map.107), channel_id=1, source_target_pairs={{0,16},{16,0},{1,17},{17,1},{2,18},{18,2},{3,19},{19,3},{4,20},{20... | collective-permute-start | bytes 1327112 | tf_op jit(solution)/shard_map/ppermute | solution.py:460
  47.2 4.8 %shard_map.106 = (bf16[320,256]{1,0:T(8,128)(2,1)S(1)}, bf16[320,1536]{1,0:T(8,128)(2,1)S(1)}, bf16[320,576]{1,0:T(8,128)(2,1)S(1)}, bf16[64,1536]{1,0:T(8,128)(2,1)S(1)}, f32[320,320]{1,0:T(8,128)S(1)}) custom-call(s32[3]{0:T(128)S(1)} %pad_add_fusion.sc, bf16[80,1536]{1,0:T(8,128)(2,1)S(1)} %copy-done, bf16[80,576]{1,0:T(8,128)(2,1)S(1)} %copy-done.2, ...), custom_call_target="tpu_custom_call" | custom-call | flops 964689920 | bytes 2359296 | tf_op jit(solution)/shard_map/pallas_call | solution.py:108
  52.0 2.7 %collective-permute-start.17 = (bf16[320,256]{1,0:T(8,128)(2,1)S(1)}, bf16[320,256]{1,0:T(8,128)(2,1)S(1)}, u32[]{:S(2)}, u32[]{:S(2)}) collective-permute-start(bf16[320,256]{1,0:T(8,128)(2,1)S(1)} %get-tuple-element.57.refs_0_), channel_id=1, source_target_pairs={{0,8},{4,12},{8,0},{12,4},{1,9},{5,13},{9,1},{13,5},{2,10},{6,14},... | collective-permute-start | bytes 491528 | tf_op jit(solution)/shard_map/ppermute | solution.py:314
  54.6 4.9 %collective-permute-start.15 = (bf16[320,256]{1,0:T(8,128)(2,1)S(1)}, bf16[320,256]{1,0:T(8,128)(2,1)S(1)}, u32[]{:S(2)}, u32[]{:S(2)}) collective-permute-start(bf16[320,256]{1,0:T(8,128)(2,1)S(1)} %get-tuple-element.57.refs_0_), channel_id=1, source_target_pairs={{0,4},{4,8},{8,12},{1,5},{5,9},{9,13},{2,6},{6,10},{10,14},{3,7},{... | collective-permute-start | bytes 491528 | tf_op jit(solution)/shard_map/ppermute | solution.py:312
  59.5 4.5 %shard_map.108.refs_0_ = bf16[320,256]{1,0:T(8,128)(2,1)S(1)} custom-call(s32[3]{0:T(128)S(1)} %pad_add_fusion.sc, bf16[320,1536]{1,0:T(8,128)(2,1)S(1)} %get-tuple-element.50.refs_0_, bf16[320,576]{1,0:T(8,128)(2,1)S(1)} %get-tuple-element.51.refs_1_, bf16[64,1536]{1,0:T(8,128)(2,1)S(1)} %get-tuple-element.52.refs_2_, ...), custom_call_target="tpu_custom_call" | custom-call | flops 964689920 | bytes 2359296 | tf_op jit(solution)/shard_map/pallas_call | solution.py:108
  65.1 1.3 %collective-permute-start.16 = (bf16[320,256]{1,0:T(8,128)(2,1)S(1)}, bf16[320,256]{1,0:T(8,128)(2,1)S(1)}, u32[]{:S(2)}, u32[]{:S(2)}) collective-permute-start(bf16[320,256]{1,0:T(8,128)(2,1)S(1)} %get-tuple-element.57.refs_0_), channel_id=1, source_target_pairs={{4,0},{8,4},{12,8},{5,1},{9,5},{13,9},{6,2},{10,6},{14,10},{7,3},{... | collective-permute-start | bytes 491528 | tf_op jit(solution)/shard_map/ppermute | solution.py:313
  66.4 1.3 %collective-permute-start.18 = (bf16[320,256]{1,0:T(8,128)(2,1)S(1)}, bf16[320,256]{1,0:T(8,128)(2,1)S(1)}, u32[]{:S(2)}, u32[]{:S(2)}) collective-permute-start(bf16[320,256]{1,0:T(8,128)(2,1)S(1)} %collective-permute-done.17.refs_3_), channel_id=1, source_target_pairs={{8,12},{4,0},{9,13},{5,1},{10,14},{6,2},{11,15},{7,3},{24,28},{20,... | collective-permute-start | bytes 491528 | tf_op jit(solution)/shard_map/ppermute | solution.py:315
  67.7 4.6 %collective-permute-start.11 = (bf16[320,256]{1,0:T(8,128)(2,1)S(1)}, bf16[320,256]{1,0:T(8,128)(2,1)S(1)}, u32[]{:S(2)}, u32[]{:S(2)}) collective-permute-start(bf16[320,256]{1,0:T(8,128)(2,1)S(1)} %shard_map.108.refs_0_), channel_id=1, source_target_pairs={{0,4},{4,8},{8,12},{1,5},{5,9},{9,13},{2,6},{6,10},{10,14},{3,7},{... | collective-permute-start | bytes 491528 | tf_op jit(solution)/shard_map/ppermute | solution.py:312
  72.3 1.3 %collective-permute-start.12 = (bf16[320,256]{1,0:T(8,128)(2,1)S(1)}, bf16[320,256]{1,0:T(8,128)(2,1)S(1)}, u32[]{:S(2)}, u32[]{:S(2)}) collective-permute-start(bf16[320,256]{1,0:T(8,128)(2,1)S(1)} %shard_map.108.refs_0_), channel_id=1, source_target_pairs={{4,0},{8,4},{12,8},{5,1},{9,5},{13,9},{6,2},{10,6},{14,10},{7,3},{... | collective-permute-start | bytes 491528 | tf_op jit(solution)/shard_map/ppermute | solution.py:313
  74.1 1.3 %collective-permute-start.14 = (bf16[320,256]{1,0:T(8,128)(2,1)S(1)}, bf16[320,256]{1,0:T(8,128)(2,1)S(1)}, u32[]{:S(2)}, u32[]{:S(2)}) collective-permute-start(bf16[320,256]{1,0:T(8,128)(2,1)S(1)} %collective-permute-done.13.refs_3_), channel_id=1, source_target_pairs={{8,12},{4,0},{9,13},{5,1},{10,14},{6,2},{11,15},{7,3},{24,28},{20,... | collective-permute-start | bytes 491528 | tf_op jit(solution)/shard_map/ppermute | solution.py:315
  75.4 2.1 %collective-permute-done.16.refs_2_ = bf16[320,256]{1,0:T(8,128)(2,1)S(1)} collective-permute-done((bf16[320,256]{1,0:T(8,128)(2,1)S(1)}, bf16[320,256]{1,0:T(8,128)(2,1)S(1)}, u32[]{:S(2)}, u32[]{:S(2)}) %collective-permute-start.16) | collective-permute-done | bytes 163872 | tf_op jit(solution)/shard_map/ppermute | solution.py:313
  77.5 3.5 %collective-permute-done.18.refs_4_ = bf16[320,256]{1,0:T(8,128)(2,1)S(1)} collective-permute-done((bf16[320,256]{1,0:T(8,128)(2,1)S(1)}, bf16[320,256]{1,0:T(8,128)(2,1)S(1)}, u32[]{:S(2)}, u32[]{:S(2)}) %collective-permute-start.18) | collective-permute-done | bytes 163872 | tf_op jit(solution)/shard_map/ppermute | solution.py:315
  81.0 4.0 %shard_map.109 = (f32[320,1792]{1,0:T(8,128)S(1)}, bf16[4,256,896]{2,1,0:T(8,128)(2,1)S(1)}) custom-call(s32[3]{0:T(128)S(1)} %pad_add_fusion.sc, bf16[320,256]{1,0:T(8,128)(2,1)S(1)} %get-tuple-element.57.refs_0_, bf16[320,256]{1,0:T(8,128)(2,1)S(1)} %collective-permute-done.15.refs_1_, bf16[320,256]{1,0:T(8,128)(2,1)S(1)} %collective-permute-done.16.refs_2_, ...), custom_call_target="tpu_custom_call" | custom-call | flops 1174405120 | bytes 3670016 | tf_op jit(solution)/shard_map/pallas_call | solution.py:108
  85.0 1.3 %collective-permute-done.14.refs_4_ = bf16[320,256]{1,0:T(8,128)(2,1)S(1)} collective-permute-done((bf16[320,256]{1,0:T(8,128)(2,1)S(1)}, bf16[320,256]{1,0:T(8,128)(2,1)S(1)}, u32[]{:S(2)}, u32[]{:S(2)}) %collective-permute-start.14) | collective-permute-done | bytes 163872 | tf_op jit(solution)/shard_map/ppermute | solution.py:315
  86.3 2.0 %shard_map.110 = (f32[160,896]{1,0:T(8,128)S(1)}, bf16[160,896]{1,0:T(8,128)(2,1)S(1)}, bf16[4,256,896]{2,1,0:T(8,128)(2,1)S(1)}) custom-call(s32[3]{0:T(128)S(1)} %pad_add_fusion.sc, bf16[320,256]{1,0:T(8,128)(2,1)S(1)} %shard_map.108.refs_0_, bf16[320,256]{1,0:T(8,128)(2,1)S(1)} %collective-permute-done.11.refs_1_, ...), custom_call_target="tpu_custom_call" | custom-call | flops 587202560 | bytes 1835008 | tf_op jit(solution)/shard_map/pallas_call | solution.py:108
  88.3 1.6 %shard_map.111 = (f32[160,896]{1,0:T(8,128)S(1)}, bf16[160,896]{1,0:T(8,128)(2,1)S(1)}, f32[160,896]{1,0:T(8,128)S(1)}) custom-call(s32[3]{0:T(128)S(1)} %pad_add_fusion.sc, bf16[320,256]{1,0:T(8,128)(2,1)S(1)} %shard_map.108.refs_0_, bf16[320,256]{1,0:T(8,128)(2,1)S(1)} %collective-permute-done.11.refs_1_, ...), custom_call_target="tpu_custom_call", output_to_operand_aliasing={{2}: (8, {})} | custom-call | flops 587202560 | bytes 1835008 | tf_op jit(solution)/shard_map/pallas_call | solution.py:108
  92.4 1.6 %collective-permute-start.20 = (bf16[80,896]{1,0:T(8,128)(2,1)S(1)}, bf16[80,896]{1,0:T(8,128)(2,1)S(1)}, u32[]{:S(2)}, u32[]{:S(2)}) collective-permute-start(bf16[80,896]{1,0:T(8,128)(2,1)S(1)} %fusion.2), channel_id=1, source_target_pairs={{0,2},{1,3},{2,0},{3,1},{4,6},{5,7},{6,4},{7,5},{8,10},{9,11},{10,... | collective-permute-start | bytes 430088 | tf_op jit(solution)/shard_map/ppermute | solution.py:548
  94.0 4.4 %collective-permute-done.22 = bf16[80,896]{1,0:T(8,128)(2,1)S(1)} collective-permute-done((bf16[80,896]{1,0:T(8,128)(2,1)S(1)}, bf16[80,896]{1,0:T(8,128)(2,1)S(1)}, u32[]{:S(2)}, u32[]{:S(2)}) %collective-permute-start.22) | collective-permute-done | bytes 143392 | tf_op jit(solution)/shard_map/ppermute | solution.py:548
  98.4 2.2 %collective-permute-done.20 = bf16[80,896]{1,0:T(8,128)(2,1)S(1)} collective-permute-done((bf16[80,896]{1,0:T(8,128)(2,1)S(1)}, bf16[80,896]{1,0:T(8,128)(2,1)S(1)}, u32[]{:S(2)}, u32[]{:S(2)}) %collective-permute-start.20) | collective-permute-done | bytes 143392 | tf_op jit(solution)/shard_map/ppermute | solution.py:548
  (41 shorter events, 8.8 us)
Async XLA Ops:
  0.6 9.2 %copy-start.1 = (bf16[384,64]{0,1:T(8,128)(2,1)S(1)}, bf16[384,64]{0,1:T(8,128)(2,1)}, u32[]{:S(2)}) copy-start(bf16[384,64]{0,1:T(8,128)(2,1)} %param.13) | copy-start | bytes 147460
  0.6 9.2 %copy-start.4 = (bf16[384,3072]{1,0:T(8,128)(2,1)S(1)}, bf16[384,3072]{1,0:T(8,128)(2,1)}, u32[]{:S(2)}) copy-start(bf16[384,3072]{1,0:T(8,128)(2,1)} %refs_9_.1) | copy-start | bytes 7077892
  2.8 12.0 %collective-permute-start = (bf16[320,384]{1,0:T(8,128)(2,1)S(1)}, bf16[320,384]{1,0:T(8,128)(2,1)S(1)}, u32[]{:S(2)}, u32[]{:S(2)}) collective-permute-start(bf16[320,384]{1,0:T(8,128)(2,1)S(1)} %get-tuple-element.34), channel_id=1, source_target_pairs={{0,4},{4,8},{8,12},{12,0},{1,5},{5,9},{9,13},{13,1},{2,6},{6,10},{... | collective-permute-start | bytes 737288 | tf_op jit(solution)/shard_map/ppermute | solution.py:439
  5.9 18.6 %collective-permute-start.1 = (bf16[320,384]{1,0:T(8,128)(2,1)S(1)}, bf16[320,384]{1,0:T(8,128)(2,1)S(1)}, u32[]{:S(2)}, u32[]{:S(2)}) collective-permute-start(bf16[320,384]{1,0:T(8,128)(2,1)S(1)} %get-tuple-element.35), channel_id=1, source_target_pairs={{0,8},{4,12},{8,0},{12,4},{1,9},{5,13},{9,1},{13,5},{2,10},{6,14},... | collective-permute-start | bytes 737288 | tf_op jit(solution)/shard_map/ppermute | solution.py:439
  8.5 38.7 %copy-start = (bf16[80,1536]{1,0:T(8,128)(2,1)S(1)}, bf16[80,1536]{1,0:T(8,128)(2,1)}, u32[]{:S(2)}) copy-start(bf16[80,1536]{1,0:T(8,128)(2,1)} %refs_0_.1) | copy-start | bytes 737284
  8.5 38.7 %copy-start.2 = (bf16[80,576]{1,0:T(8,128)(2,1)S(1)}, bf16[80,576]{1,0:T(8,128)(2,1)}, u32[]{:S(2)}) copy-start(bf16[80,576]{1,0:T(8,128)(2,1)} %refs_1_.1) | copy-start | bytes 276484
  8.5 38.7 %copy-start.3 = (s32[80]{0:T(128)S(1)}, s32[80]{0:T(128)}, u32[]{:S(2)}) copy-start(s32[80]{0:T(128)} %param.11) | copy-start | bytes 964
  8.5 16.1 %collective-permute-start.2 = (bf16[320,384]{1,0:T(8,128)(2,1)S(1)}, bf16[320,384]{1,0:T(8,128)(2,1)S(1)}, u32[]{:S(2)}, u32[]{:S(2)}) collective-permute-start(bf16[320,384]{1,0:T(8,128)(2,1)S(1)} %get-tuple-element.36), channel_id=1, source_target_pairs={{0,12},{4,0},{8,4},{12,8},{1,13},{5,1},{9,5},{13,9},{2,14},{6,2},{... | collective-permute-start | bytes 737288 | tf_op jit(solution)/shard_map/ppermute | solution.py:439
  25.1 17.9 %collective-permute-start.5 = (bf16[3,128,384]{2,1,0:T(8,128)(2,1)S(1)}, bf16[3,128,384]{2,1,0:T(8,128)(2,1)S(1)}, u32[]{:S(2)}, u32[]{:S(2)}) collective-permute-start(bf16[3,128,384]{2,1,0:T(8,128)(2,1)S(1)} %get-tuple-element.42), channel_id=1, source_target_pairs={{0,2},{1,3},{2,0},{3,1},{4,6},{5,7},{6,4},{7,5},{8,10},{9,11},{10,... | collective-permute-start | bytes 884744 | tf_op jit(solution)/shard_map/ppermute | solution.py:452
  26.7 11.5 %collective-permute-start.6 = (bf16[192,384]{1,0:T(8,128)(2,1)S(1)}, bf16[192,384]{1,0:T(8,128)(2,1)S(1)}, u32[]{:S(2)}, u32[]{:S(2)}) collective-permute-start(bf16[192,384]{1,0:T(8,128)(2,1)S(1)} %get-tuple-element.46), channel_id=1, source_target_pairs={{0,4},{4,8},{8,12},{12,0},{1,5},{5,9},{9,13},{13,1},{2,6},{6,10},{... | collective-permute-start | bytes 442376 | tf_op jit(solution)/shard_map/ppermute | solution.py:439
  32.4 10.6 %collective-permute-start.7 = (bf16[192,384]{1,0:T(8,128)(2,1)S(1)}, bf16[192,384]{1,0:T(8,128)(2,1)S(1)}, u32[]{:S(2)}, u32[]{:S(2)}) collective-permute-start(bf16[192,384]{1,0:T(8,128)(2,1)S(1)} %get-tuple-element.47), channel_id=1, source_target_pairs={{0,8},{4,12},{8,0},{12,4},{1,9},{5,13},{9,1},{13,5},{2,10},{6,14},... | collective-permute-start | bytes 442376 | tf_op jit(solution)/shard_map/ppermute | solution.py:439
  34.0 9.0 %collective-permute-start.8 = (bf16[192,384]{1,0:T(8,128)(2,1)S(1)}, bf16[192,384]{1,0:T(8,128)(2,1)S(1)}, u32[]{:S(2)}, u32[]{:S(2)}) collective-permute-start(bf16[192,384]{1,0:T(8,128)(2,1)S(1)} %get-tuple-element.48), channel_id=1, source_target_pairs={{0,12},{4,0},{8,4},{12,8},{1,13},{5,1},{9,5},{13,9},{2,14},{6,2},{... | collective-permute-start | bytes 442376 | tf_op jit(solution)/shard_map/ppermute | solution.py:439
  34.8 12.0 %collective-permute-start.3 = (bf16[3,192,384]{2,1,0:T(8,128)(2,1)S(1)}, bf16[3,192,384]{2,1,0:T(8,128)(2,1)S(1)}, u32[]{:S(2)}, u32[]{:S(2)}) collective-permute-start(bf16[3,192,384]{2,1,0:T(8,128)(2,1)S(1)} %get-tuple-element.41), channel_id=1, source_target_pairs={{0,16},{16,0},{1,17},{17,1},{2,18},{18,2},{3,19},{19,3},{4,20},{20... | collective-permute-start | bytes 1327112 | tf_op jit(solution)/shard_map/ppermute | solution.py:451
  43.6 16.0 %collective-permute-start.10 = (bf16[3,192,384]{2,1,0:T(8,128)(2,1)S(1)}, bf16[3,192,384]{2,1,0:T(8,128)(2,1)S(1)}, u32[]{:S(2)}, u32[]{:S(2)}) collective-permute-start(bf16[3,192,384]{2,1,0:T(8,128)(2,1)S(1)} %shard_map.107), channel_id=1, source_target_pairs={{0,16},{16,0},{1,17},{17,1},{2,18},{18,2},{3,19},{19,3},{4,20},{20... | collective-permute-start | bytes 1327112 | tf_op jit(solution)/shard_map/ppermute | solution.py:460
  45.2 1.6 %collective-permute-start.4 = (bf16[3,128,384]{2,1,0:T(8,128)(2,1)S(1)}, bf16[3,128,384]{2,1,0:T(8,128)(2,1)S(1)}, u32[]{:S(2)}, u32[]{:S(2)}) collective-permute-start(bf16[3,128,384]{2,1,0:T(8,128)(2,1)S(1)} %get-tuple-element.42), channel_id=1, source_target_pairs={{0,1},{1,0},{2,3},{3,2},{4,5},{5,4},{6,7},{7,6},{8,9},{9,8},{10,11... | collective-permute-start | bytes 884744 | tf_op jit(solution)/shard_map/ppermute | solution.py:455
  45.2 2.0 %collective-permute-start.9 = (bf16[3,128,384]{2,1,0:T(8,128)(2,1)S(1)}, bf16[3,128,384]{2,1,0:T(8,128)(2,1)S(1)}, u32[]{:S(2)}, u32[]{:S(2)}) collective-permute-start(bf16[3,128,384]{2,1,0:T(8,128)(2,1)S(1)} %collective-permute-done.5.refs_9_), channel_id=1, source_target_pairs={{0,1},{1,0},{2,3},{3,2},{4,5},{5,4},{6,7},{7,6},{8,9},{9,8},{10,11... | collective-permute-start | bytes 884744 | tf_op jit(solution)/shard_map/ppermute | solution.py:457
  52.0 14.4 %collective-permute-start.17 = (bf16[320,256]{1,0:T(8,128)(2,1)S(1)}, bf16[320,256]{1,0:T(8,128)(2,1)S(1)}, u32[]{:S(2)}, u32[]{:S(2)}) collective-permute-start(bf16[320,256]{1,0:T(8,128)(2,1)S(1)} %get-tuple-element.57.refs_0_), channel_id=1, source_target_pairs={{0,8},{4,12},{8,0},{12,4},{1,9},{5,13},{9,1},{13,5},{2,10},{6,14},... | collective-permute-start | bytes 491528 | tf_op jit(solution)/shard_map/ppermute | solution.py:314
  54.6 17.6 %collective-permute-start.15 = (bf16[320,256]{1,0:T(8,128)(2,1)S(1)}, bf16[320,256]{1,0:T(8,128)(2,1)S(1)}, u32[]{:S(2)}, u32[]{:S(2)}) collective-permute-start(bf16[320,256]{1,0:T(8,128)(2,1)S(1)} %get-tuple-element.57.refs_0_), channel_id=1, source_target_pairs={{0,4},{4,8},{8,12},{1,5},{5,9},{9,13},{2,6},{6,10},{10,14},{3,7},{... | collective-permute-start | bytes 491528 | tf_op jit(solution)/shard_map/ppermute | solution.py:312
  64.1 10.0 %collective-permute-start.13 = (bf16[320,256]{1,0:T(8,128)(2,1)S(1)}, bf16[320,256]{1,0:T(8,128)(2,1)S(1)}, u32[]{:S(2)}, u32[]{:S(2)}) collective-permute-start(bf16[320,256]{1,0:T(8,128)(2,1)S(1)} %shard_map.108.refs_0_), channel_id=1, source_target_pairs={{0,8},{4,12},{8,0},{12,4},{1,9},{5,13},{9,1},{13,5},{2,10},{6,14},... | collective-permute-start | bytes 491528 | tf_op jit(solution)/shard_map/ppermute | solution.py:314
  65.1 12.4 %collective-permute-start.16 = (bf16[320,256]{1,0:T(8,128)(2,1)S(1)}, bf16[320,256]{1,0:T(8,128)(2,1)S(1)}, u32[]{:S(2)}, u32[]{:S(2)}) collective-permute-start(bf16[320,256]{1,0:T(8,128)(2,1)S(1)} %get-tuple-element.57.refs_0_), channel_id=1, source_target_pairs={{4,0},{8,4},{12,8},{5,1},{9,5},{13,9},{6,2},{10,6},{14,10},{7,3},{... | collective-permute-start | bytes 491528 | tf_op jit(solution)/shard_map/ppermute | solution.py:313
  66.4 14.6 %collective-permute-start.18 = (bf16[320,256]{1,0:T(8,128)(2,1)S(1)}, bf16[320,256]{1,0:T(8,128)(2,1)S(1)}, u32[]{:S(2)}, u32[]{:S(2)}) collective-permute-start(bf16[320,256]{1,0:T(8,128)(2,1)S(1)} %collective-permute-done.17.refs_3_), channel_id=1, source_target_pairs={{8,12},{4,0},{9,13},{5,1},{10,14},{6,2},{11,15},{7,3},{24,28},{20,... | collective-permute-start | bytes 491528 | tf_op jit(solution)/shard_map/ppermute | solution.py:315
  67.7 17.3 %collective-permute-start.11 = (bf16[320,256]{1,0:T(8,128)(2,1)S(1)}, bf16[320,256]{1,0:T(8,128)(2,1)S(1)}, u32[]{:S(2)}, u32[]{:S(2)}) collective-permute-start(bf16[320,256]{1,0:T(8,128)(2,1)S(1)} %shard_map.108.refs_0_), channel_id=1, source_target_pairs={{0,4},{4,8},{8,12},{1,5},{5,9},{9,13},{2,6},{6,10},{10,14},{3,7},{... | collective-permute-start | bytes 491528 | tf_op jit(solution)/shard_map/ppermute | solution.py:312
  72.3 12.7 %collective-permute-start.12 = (bf16[320,256]{1,0:T(8,128)(2,1)S(1)}, bf16[320,256]{1,0:T(8,128)(2,1)S(1)}, u32[]{:S(2)}, u32[]{:S(2)}) collective-permute-start(bf16[320,256]{1,0:T(8,128)(2,1)S(1)} %shard_map.108.refs_0_), channel_id=1, source_target_pairs={{4,0},{8,4},{12,8},{5,1},{9,5},{13,9},{6,2},{10,6},{14,10},{7,3},{... | collective-permute-start | bytes 491528 | tf_op jit(solution)/shard_map/ppermute | solution.py:313
  74.1 12.2 %collective-permute-start.14 = (bf16[320,256]{1,0:T(8,128)(2,1)S(1)}, bf16[320,256]{1,0:T(8,128)(2,1)S(1)}, u32[]{:S(2)}, u32[]{:S(2)}) collective-permute-start(bf16[320,256]{1,0:T(8,128)(2,1)S(1)} %collective-permute-done.13.refs_3_), channel_id=1, source_target_pairs={{8,12},{4,0},{9,13},{5,1},{10,14},{6,2},{11,15},{7,3},{24,28},{20,... | collective-permute-start | bytes 491528 | tf_op jit(solution)/shard_map/ppermute | solution.py:315
  90.0 1.6 %collective-permute-start.21 = (bf16[160,896]{1,0:T(8,128)(2,1)S(1)}, bf16[160,896]{1,0:T(8,128)(2,1)S(1)}, u32[]{:S(2)}, u32[]{:S(2)}) collective-permute-start(bf16[160,896]{1,0:T(8,128)(2,1)S(1)} %get-tuple-element.65), channel_id=1, source_target_pairs={{0,1},{1,0},{2,3},{3,2},{4,5},{5,4},{6,7},{7,6},{8,9},{9,8},{10,11... | collective-permute-start | bytes 860168 | tf_op jit(solution)/shard_map/ppermute | solution.py:544
  90.1 2.2 %collective-permute-start.19 = (bf16[160,896]{1,0:T(8,128)(2,1)S(1)}, bf16[160,896]{1,0:T(8,128)(2,1)S(1)}, u32[]{:S(2)}, u32[]{:S(2)}) collective-permute-start(bf16[160,896]{1,0:T(8,128)(2,1)S(1)} %get-tuple-element.63), channel_id=1, source_target_pairs={{0,1},{1,0},{2,3},{3,2},{4,5},{5,4},{6,7},{7,6},{8,9},{9,8},{10,11... | collective-permute-start | bytes 860168 | tf_op jit(solution)/shard_map/ppermute | solution.py:544
  91.7 6.7 %collective-permute-start.22 = (bf16[80,896]{1,0:T(8,128)(2,1)S(1)}, bf16[80,896]{1,0:T(8,128)(2,1)S(1)}, u32[]{:S(2)}, u32[]{:S(2)}) collective-permute-start(bf16[80,896]{1,0:T(8,128)(2,1)S(1)} %fusion.3), channel_id=1, source_target_pairs={{0,2},{1,3},{2,0},{3,1},{4,6},{5,7},{6,4},{7,5},{8,10},{9,11},{10,... | collective-permute-start | bytes 430088 | tf_op jit(solution)/shard_map/ppermute | solution.py:548
  92.4 8.2 %collective-permute-start.20 = (bf16[80,896]{1,0:T(8,128)(2,1)S(1)}, bf16[80,896]{1,0:T(8,128)(2,1)S(1)}, u32[]{:S(2)}, u32[]{:S(2)}) collective-permute-start(bf16[80,896]{1,0:T(8,128)(2,1)S(1)} %fusion.2), channel_id=1, source_target_pairs={{0,2},{1,3},{2,0},{3,1},{4,6},{5,7},{6,4},{7,5},{8,10},{9,11},{10,... | collective-permute-start | bytes 430088 | tf_op jit(solution)/shard_map/ppermute | solution.py:548

commit v5 on v4

--- a/solution.py
+++ b/solution.py
@@ -93,12 +93,12 @@
     return (merged_query_weight, mixed)
 
 
-def cyclic(n, k):
-    return [(i, (i + k) % n) for i in range(n)]
-
-
 def flipped(n, bit):
     return [(i, i ^ bit) for i in range(n)]
+
+
+def partners(n):
+    return [b for b in range(2, n)] + [1]
 
 
 def call(body, outs, args, hbm=(), scratch=(), alias=None, flops=0, moved=0):
@@ -153,10 +153,10 @@
     mine = pl.ds(pl.multiple_of(g * half, 16), half)
     large = []
     for c in range(CHUNKS):
-        for k in range(1, n):
-            chunk = lax.rem(s + k, n) * CHUNKS + c
+        for k, bits in enumerate(partners(n)):
+            chunk = (s ^ bits) * CHUNKS + c
             columns = pl.ds(pl.multiple_of(chunk * wide, 128), wide)
-            large.append((w_ref.at[mine, columns], outs[c * (n - 1) + k - 1].at[:half]))
+            large.append((w_ref.at[mine, columns], outs[c * (n - 1) + k].at[:half]))
     copies = fetch(small + large, sems)
     turn[...] = jnp.zeros_like(turn)
     for copy in copies[: len(small)]:
@@ -202,12 +202,12 @@
     ao[:, pl.ds(pl.multiple_of(s * depth, 128), depth)] = at_ref[...]
     starts = [(s, pos_ref[0:1, 0:1].astype(jnp.float32))]
     turn[...] = jnp.zeros_like(turn)
-    for k in range(1, n):
-        src = lax.rem(s - k + n, n)
+    for k, bits in enumerate(partners(n)):
+        src = s ^ bits
         rows = pl.ds(pl.multiple_of(src * tok, 16), tok)
         for j in range(nh):
             hh = h ^ j
-            got = stacks[j - 1].at[k - 1] if j else units[k - 1].at[half:]
+            got = stacks[j - 1].at[k] if j else units[k].at[half:]
             xo[rows, pl.ds(pl.multiple_of(hh * kq, 128), kq)] = got[:tok, :]
             arow = pl.ds(pl.multiple_of(hh * aq, 16), aq)
             ao[arow, pl.ds(pl.multiple_of(src * depth, 128), depth)] = got[tok : tok + aq, :]
@@ -254,10 +254,10 @@
     )
     if before is not None:
         before()
-    for k in range(1, n):
-        src = lax.rem(s - k + n, n)
-        raw[pl.ds(pl.multiple_of(src * depth + g * half, 16), half), :] = units[k - 1][:half]
-        raw[pl.ds(pl.multiple_of(src * depth + (1 - g) * half, 16), half), :] = y_ref[k - 1]
+    for k, bits in enumerate(partners(n)):
+        src = s ^ bits
+        raw[pl.ds(pl.multiple_of(src * depth + g * half, 16), half), :] = units[k][:half]
+        raw[pl.ds(pl.multiple_of(src * depth + (1 - g) * half, 16), half), :] = y_ref[k]
     b_copy.wait()
     w_copy.wait()
 
@@ -309,34 +309,24 @@
 
 
 def gather_line(x):
-    left = lax.ppermute(x, "seq", [(0, 1), (1, 2), (2, 3)])
-    right = lax.ppermute(x, "seq", [(1, 0), (2, 1), (3, 2)])
-    two = lax.ppermute(x, "seq", cyclic(4, 2))
-    three = lax.ppermute(two, "seq", [(2, 3), (1, 0)])
-    return [x, left, right, two, three]
-
-
-def place_line(s, slots, lhs):
-    own, left, right, two, three = slots
-    width = own.shape[1]
-
-    def put(src, ref):
-        lhs[:, pl.ds(pl.multiple_of(src * width, 128), width)] = ref[...]
-
-    put(s, own)
-    put(lax.rem(s + 2, 4), two)
-
-    @pl.when(s > 0)
-    def _():
-        put(s - 1, left)
-
-    @pl.when(s < 3)
-    def _():
-        put(s + 1, right)
-
-    @pl.when((s == 0) | (s == 3))
-    def _():
-        put(3 - s, three)
+    two = lax.ppermute(x, "seq", flipped(4, 2))
+    one = lax.ppermute(x, "seq", flipped(4, 1))
+    two, one = lax.optimization_barrier((two, one))
+    return [x, one, two, lax.ppermute(two, "seq", flipped(4, 1))]
+
+
+EARLY = ((0, 0), (1, 0), (2, 0), (0, 1))
+LATE = ((3, 0), (1, 1), (2, 1), (3, 1))
+
+
+def place(slots, lhs):
+    for i, ref in enumerate(slots):
+        width = ref.shape[1]
+        lhs[:, i * width : (i + 1) * width] = ref[...]
+
+
+def slabs(sc, w_ref, pieces, columns, out):
+    return [(w_ref.at[sc[0] ^ bits, c, :, columns], out.at[i]) for i, (bits, c) in enumerate(pieces)]
 
 
 def columns_dot(lhs, w, begin, end, put):
@@ -347,27 +337,29 @@
         put(slice(at, stop), jnp.dot(lhs[...], tile, preferred_element_type=jnp.float32))
 
 
-def first_body(n, cut, sc, *refs):
-    slots, (w_ref, acc, later, lhs, w, sems) = refs[:5], refs[5:]
+def first_body(cut, sc, *refs):
+    count = len(EARLY)
+    slots, (w_ref, acc, left, right, lhs, w, sems) = refs[:count], refs[count:]
     copies = fetch(
-        [(w_ref.at[j, 0], w.at[j]) for j in range(n)]
-        + [(w_ref.at[j, 1, :, :cut], later.at[j]) for j in range(n)],
+        slabs(sc, w_ref, EARLY, slice(None), w)
+        + slabs(sc, w_ref, LATE, slice(0, cut), left)
+        + slabs(sc, w_ref, LATE, slice(cut, acc.shape[1]), right),
         sems,
     )
-    place_line(sc[0], slots, lhs)
-    for copy in copies[:n]:
+    place(slots, lhs)
+    for copy in copies[:count]:
         copy.wait()
 
     def put(band, value):
         acc[:, band] = value
 
     columns_dot(lhs, w, 0, acc.shape[1], put)
-    for copy in copies[n:]:
+    for copy in copies[count:]:
         copy.wait()
 
 
 def last_body(nh, tok, begin, sc, w, acc, slots, keep, send, lhs, tot):
-    place_line(sc[0], slots, lhs)
+    place(slots, lhs)
 
     def put(band, value):
         tot[:, band] = acc[:, begin + band.start : begin + band.stop] + value
@@ -381,17 +373,16 @@
         send[i * tok : (i + 1) * tok, :] = tot[theirs, :].astype(jnp.bfloat16)
 
 
-def last_left(n, nh, tok, sc, *refs):
-    slots, (w, acc, w_ref, keep, send, later, lhs, tot, sems) = refs[:5], refs[5:]
-    cut = keep.shape[1]
-    copies = fetch([(w_ref.at[j, 1, :, cut:], later.at[j]) for j in range(n)], sems)
+def last_left(nh, tok, sc, *refs):
+    count = len(LATE)
+    slots, (w, acc, held, keep, send, passed, lhs, tot) = refs[:count], refs[count:]
+    del held, passed
     last_body(nh, tok, 0, sc, w, acc, slots, keep, send, lhs, tot)
-    for copy in copies:
-        copy.wait()
 
 
 def last_right(nh, tok, sc, *refs):
-    slots, (w, acc, held, keep, send, passed, lhs, tot) = refs[:5], refs[5:]
+    count = len(LATE)
+    slots, (w, acc, held, keep, send, passed, lhs, tot) = refs[:count], refs[count:]
     del held, passed
     last_body(nh, tok, acc.shape[1] - keep.shape[1], sc, w, acc, slots, keep, send, lhs, tot)
 
@@ -436,7 +427,7 @@
         moved=4 * half * cols,
     )
     def exchange(parts):
-        return [lax.ppermute(p, "seq", cyclic(n, k)) for p, k in zip(parts, range(1, n))]
+        return [lax.ppermute(p, "seq", flipped(n, bits)) for p, bits in zip(parts, partners(n))]
 
     def split(got, *sizes):
         outs = tuple(like(n - 1, size, wide) for size in sizes)
@@ -448,7 +439,7 @@
     later = lax.optimization_barrier((*units[n - 1 :], moved[0][0]))
     moved.append(exchange(later[: n - 1]))
     share, stack = split(moved[0], half, extra)
-    passed = [lax.ppermute(share, "groups", cyclic(2, 1))]
+    passed = [lax.ppermute(share, "groups", flipped(2, 1))]
     across = lax.ppermute(stack, "head", flipped(nh, 2))
     across, *moved[1] = lax.optimization_barrier((across, *moved[1]))
     stacks = [
@@ -457,7 +448,7 @@
         lax.ppermute(across, "head", flipped(nh, 1)),
     ]
     (share,) = split(moved[1], half)
-    passed.append(lax.ppermute(share, "groups", cyclic(2, 1)))
+    passed.append(lax.ppermute(share, "groups", flipped(2, 1)))
 
     scale = 1.0 / math.sqrt(nope + rope)
     scratch = [
@@ -498,18 +489,23 @@
 
     w4 = wo.reshape(n, CHUNKS, per * vdim, wo.shape[1])
     total = wo.shape[1]
+    early, late = ([slots[c][bits] for bits, c in pieces] for pieces in (EARLY, LATE))
     lhs = pltpu.VMEM((tokens, n * per * vdim), bf)
     flops = 2 * tokens * n * per * vdim * total
     cut = (total // 128 + 1) // 2 * 128
-    acc, w_left = call(
-        functools.partial(first_body, n, cut),
-        (like(tokens, total, dtype=f32), like(n, per * vdim, cut)),
-        [sc] + slots[0] + [w4],
-        hbm=(6,),
+    acc, w_left, w_right = call(
+        functools.partial(first_body, cut),
+        (
+            like(tokens, total, dtype=f32),
+            like(n, per * vdim, cut),
+            like(n, per * vdim, total - cut),
+        ),
+        [sc] + early + [w4],
+        hbm=(5,),
         scratch=[
             lhs,
             pltpu.VMEM((n, per * vdim, total), bf),
-            pltpu.SemaphoreType.DMA((2 * n,)),
+            pltpu.SemaphoreType.DMA((3 * n,)),
         ],
         flops=flops,
         moved=w4.size,
@@ -520,11 +516,11 @@
         return (like(pair_rows, size, dtype=f32), like(pair_rows, size))
 
     keep, send, w_right = call(
-        functools.partial(last_left, n, nh, tok),
+        functools.partial(last_left, nh, tok),
         partial_sums(cut) + (like(n, per * vdim, total - cut),),
-        [sc] + slots[1] + [w_left, acc, w4],
-        hbm=(8,),
-        scratch=[lhs, pltpu.VMEM((tokens, cut), f32), pltpu.SemaphoreType.DMA((n,))],
+        [sc] + late + [w_left, acc, w_right],
+        scratch=[lhs, pltpu.VMEM((tokens, cut), f32)],
+        alias={7: 2},
         flops=flops // 2,
         moved=w4.size // 2,
     )
@@ -532,9 +528,9 @@
     keep_right, right, keep = call(
         functools.partial(last_right, nh, tok),
         partial_sums(total - cut) + (like(pair_rows, cut, dtype=f32),),
-        [sc] + slots[1] + [w_right, acc, keep],
+        [sc] + late + [w_right, acc, keep],
         scratch=[lhs, pltpu.VMEM((tokens, total - cut), f32)],
-        alias={8: 2},
+        alias={7: 2},
         flops=flops // 2,
         moved=w4.size // 2,
     )

time: 102 us -> 93.7 us (0.919)
  starting transfers between devices: 41.3 us -> 29.1 us
  waiting for transfers between devices: 34.8 us -> 39.6 us
    ppermute x16 -> x14, starting transfers between devices: 36.5 us -> 24.3 us  [the longest x6 12.8 us: exchange(): lax.ppermute(p, 'seq', flipped(n, bits))]
    ppermute x16 -> x14, waiting for transfers between devices: 25.6 us -> 30.4 us  [the longest x6 22.6 us: exchange(): lax.ppermute(p, 'seq', flipped(n, bits))]
  transfers between devices with their start and end apart: 23 -> 21, of which waited for: 13 -> 13; matrix products, arithmetic and copies ran while one was open for 3% -> 4% of each run, Pallas kernels for 14% -> 15%
where the time goes in v5:
time: 93.7 us; the launch traced here: 93.6 us
  waiting for transfers between devices  39.6 us (42%)
  starting transfers between devices  29.1 us (31%)
  Pallas kernels  19.8 us (21%)
  matrix products  3.2 us (3%)
  other arithmetic  0.98 us (1%)
    ppermute x6, waiting for transfers between devices, exchange(): lax.ppermute(p, 'seq', flipped(n, bits))  22.6 us
    pallas_call x8, Pallas kernels, call(): pl.pallas_call(body, out_shape=outs, grid_spec=pltpu.PrefetchScalarGridSp...  19.8 us
    ppermute x6, starting transfers between devices, exchange(): lax.ppermute(p, 'seq', flipped(n, bits))  12.8 us
    ppermute x2, waiting for transfers between devices, by_heads(): out = out + lax.ppermute(away, 'head', flipped(nh, 2)).astype(f32)  6.64 us
    ppermute x2, waiting for transfers between devices, gather_line(): two = lax.ppermute(x, 'seq', flipped(4, 2))  6.57 us
    ppermute x2, starting transfers between devices, gather_line(): two = lax.ppermute(x, 'seq', flipped(4, 2))  4.17 us
    dot_general x1, matrix products, by_heads(): jnp.dot(down, up, preferred_element_type=f32)  3.2 us
    ppermute x2, starting transfers between devices, gather_line(): return [x, one, two, lax.ppermute(two, 'seq', flipped(4, 1))]  2.49 us
  transfers between devices with their start and end apart: 21, of which 13 were waited for; matrix products, arithmetic and copies ran while one was open for 4% of the time, Pallas kernels for 15%

profile of v5, /device:TPU:0, one launch (start us, length us, event | category | flops | bytes accessed | tf_op | source)
XLA Modules:
  0.0 93.6 jit_solution(6936585565330851996)
XLA Ops:
  0.7 2.0 %shard_map.104 = (bf16[320,384]{1,0:T(8,128)(2,1)S(1)}, bf16[320,384]{1,0:T(8,128)(2,1)S(1)}, bf16[320,384]{1,0:T(8,128)(2,1)S(1)}, bf16[192,384]{1,0:T(8,128)(2...) custom-call(s32[3]{0:T(128)S(1)} %pad_add_fusion.sc, bf16[80,1536]{1,0:T(8,128)(2,1)} %refs_0_.1, ...), custom_call_target="tpu_custom_call" | custom-call | bytes 2359296 | tf_op jit(solution)/shard_map/pallas_call | solution.py:108
  2.8 4.1 %collective-permute-start = (bf16[320,384]{1,0:T(8,128)(2,1)S(1)}, bf16[320,384]{1,0:T(8,128)(2,1)S(1)}, u32[]{:S(2)}, u32[]{:S(2)}) collective-permute-start(bf16[320,384]{1,0:T(8,128)(2,1)S(1)} %get-tuple-element.39), channel_id=1, source_target_pairs={{0,8},{4,12},{8,0},{12,4},{1,9},{5,13},{9,1},{13,5},{2,10},{6,14},... | collective-permute-start | bytes 737288 | tf_op jit(solution)/shard_map/ppermute | solution.py:430
  6.9 1.3 %collective-permute-start.1 = (bf16[320,384]{1,0:T(8,128)(2,1)S(1)}, bf16[320,384]{1,0:T(8,128)(2,1)S(1)}, u32[]{:S(2)}, u32[]{:S(2)}) collective-permute-start(bf16[320,384]{1,0:T(8,128)(2,1)S(1)} %get-tuple-element.40), channel_id=1, source_target_pairs={{0,12},{4,8},{8,4},{12,0},{1,13},{5,9},{9,5},{13,1},{2,14},{6,10},... | collective-permute-start | bytes 737288 | tf_op jit(solution)/shard_map/ppermute | solution.py:430
  8.6 3.2 %add_convert_fusion = bf16[384,3072]{1,0:T(8,128)(2,1)} fusion(bf16[384,3072]{1,0:T(8,128)(2,1)S(1)} %copy-done.4, bf16[384,64]{0,1:T(8,128)(2,1)S(1)} %copy-done.1, bf16[64,3072]{1,0:T(8,128)(2,1)} %refs_8_.1), kind=kOutput, calls=%fused_computation | convolution fusion | flops 154533888 | bytes 5160960 | tf_op jit(solution)/shard_map/dot_general | solution.py:436
  11.8 12.5 %collective-permute-done.refs_0_.refs_4_ = bf16[320,384]{1,0:T(8,128)(2,1)S(1)} collective-permute-done((bf16[320,384]{1,0:T(8,128)(2,1)S(1)}, bf16[320,384]{1,0:T(8,128)(2,1)S(1)}, u32[]{:S(2)}, u32[]{:S(2)}) %collective-permute-start) | collective-permute-done | bytes 245792 | tf_op jit(solution)/shard_map/ppermute | solution.py:430
  24.8 0.6 shard_map.105
  25.4 1.6 %collective-permute-start.5 = (bf16[3,128,384]{2,1,0:T(8,128)(2,1)S(1)}, bf16[3,128,384]{2,1,0:T(8,128)(2,1)S(1)}, u32[]{:S(2)}, u32[]{:S(2)}) collective-permute-start(bf16[3,128,384]{2,1,0:T(8,128)(2,1)S(1)} %get-tuple-element.47), channel_id=1, source_target_pairs={{0,2},{1,3},{2,0},{3,1},{4,6},{5,7},{6,4},{7,5},{8,10},{9,11},{10,... | collective-permute-start | bytes 884744 | tf_op jit(solution)/shard_map/ppermute | solution.py:443
  27.0 6.5 %collective-permute-start.6 = (bf16[192,384]{1,0:T(8,128)(2,1)S(1)}, bf16[192,384]{1,0:T(8,128)(2,1)S(1)}, u32[]{:S(2)}, u32[]{:S(2)}) collective-permute-start(bf16[192,384]{1,0:T(8,128)(2,1)S(1)} %get-tuple-element.51), channel_id=1, source_target_pairs={{0,8},{4,12},{8,0},{12,4},{1,9},{5,13},{9,1},{13,5},{2,10},{6,14},... | collective-permute-start | bytes 442376 | tf_op jit(solution)/shard_map/ppermute | solution.py:430
  34.1 1.5 %collective-permute-start.3 = (bf16[3,192,384]{2,1,0:T(8,128)(2,1)S(1)}, bf16[3,192,384]{2,1,0:T(8,128)(2,1)S(1)}, u32[]{:S(2)}, u32[]{:S(2)}) collective-permute-start(bf16[3,192,384]{2,1,0:T(8,128)(2,1)S(1)} %get-tuple-element.46), channel_id=1, source_target_pairs={{0,16},{16,0},{1,17},{17,1},{2,18},{18,2},{3,19},{19,3},{4,20},{20... | collective-permute-start | bytes 1327112 | tf_op jit(solution)/shard_map/ppermute | solution.py:442
  35.6 8.3 %collective-permute-done.6.refs_0_.refs_4_ = bf16[192,384]{1,0:T(8,128)(2,1)S(1)} collective-permute-done((bf16[192,384]{1,0:T(8,128)(2,1)S(1)}, bf16[192,384]{1,0:T(8,128)(2,1)S(1)}, u32[]{:S(2)}, u32[]{:S(2)}) %collective-permute-start.6) | collective-permute-done | bytes 147488 | tf_op jit(solution)/shard_map/ppermute | solution.py:430
  43.9 1.3 %collective-permute-done.8.refs_2_.refs_6_ = bf16[192,384]{1,0:T(8,128)(2,1)S(1)} collective-permute-done((bf16[192,384]{1,0:T(8,128)(2,1)S(1)}, bf16[192,384]{1,0:T(8,128)(2,1)S(1)}, u32[]{:S(2)}, u32[]{:S(2)}) %collective-permute-start.8) | collective-permute-done | bytes 147488 | tf_op jit(solution)/shard_map/ppermute | solution.py:430
  45.7 1.6 %collective-permute-start.13 = (bf16[3,192,384]{2,1,0:T(8,128)(2,1)S(1)}, bf16[3,192,384]{2,1,0:T(8,128)(2,1)S(1)}, u32[]{:S(2)}, u32[]{:S(2)}) collective-permute-start(bf16[3,192,384]{2,1,0:T(8,128)(2,1)S(1)} %shard_map.107), channel_id=1, source_target_pairs={{0,16},{16,0},{1,17},{17,1},{2,18},{18,2},{3,19},{19,3},{4,20},{20... | collective-permute-start | bytes 1327112 | tf_op jit(solution)/shard_map/ppermute | solution.py:451
  47.8 1.1 %collective-permute-done.4.refs_8_ = bf16[3,128,384]{2,1,0:T(8,128)(2,1)S(1)} collective-permute-done((bf16[3,128,384]{2,1,0:T(8,128)(2,1)S(1)}, bf16[3,128,384]{2,1,0:T(8,128)(2,1)S(1)}, u32[]{:S(2)}, u32[]{:S(2)}) %collective-permute-start.4) | collective-permute-done | bytes 294944 | tf_op jit(solution)/shard_map/ppermute | solution.py:446
  49.3 4.9 %shard_map.106 = (bf16[320,256]{1,0:T(8,128)(2,1)S(1)}, bf16[320,1536]{1,0:T(8,128)(2,1)S(1)}, bf16[320,576]{1,0:T(8,128)(2,1)S(1)}, bf16[64,1536]{1,0:T(8,128)(2,1)S(1)}, f32[320,320]{1,0:T(8,128)S(1)}) custom-call(s32[3]{0:T(128)S(1)} %pad_add_fusion.sc, bf16[80,1536]{1,0:T(8,128)(2,1)S(1)} %copy-done, bf16[80,576]{1,0:T(8,128)(2,1)S(1)} %copy-done.2, ...), custom_call_target="tpu_custom_call" | custom-call | flops 964689920 | bytes 2359296 | tf_op jit(solution)/shard_map/pallas_call | solution.py:108
  54.2 1.3 %collective-permute-start.10 = (bf16[320,256]{1,0:T(8,128)(2,1)S(1)}, bf16[320,256]{1,0:T(8,128)(2,1)S(1)}, u32[]{:S(2)}, u32[]{:S(2)}) collective-permute-start(bf16[320,256]{1,0:T(8,128)(2,1)S(1)} %get-tuple-element.55.refs_0_), channel_id=1, source_target_pairs={{0,8},{4,12},{8,0},{12,4},{1,9},{5,13},{9,1},{13,5},{2,10},{6,14},... | collective-permute-start | bytes 491528 | tf_op jit(solution)/shard_map/ppermute | solution.py:312
  55.4 1.1 %collective-permute-start.11 = (bf16[320,256]{1,0:T(8,128)(2,1)S(1)}, bf16[320,256]{1,0:T(8,128)(2,1)S(1)}, u32[]{:S(2)}, u32[]{:S(2)}) collective-permute-start(bf16[320,256]{1,0:T(8,128)(2,1)S(1)} %get-tuple-element.55.refs_0_), channel_id=1, source_target_pairs={{0,4},{4,0},{8,12},{12,8},{1,5},{5,1},{9,13},{13,9},{2,6},{6,2},{1... | collective-permute-start | bytes 491528 | tf_op jit(solution)/shard_map/ppermute | solution.py:313
  56.5 4.5 %shard_map.108.refs_3_ = bf16[320,256]{1,0:T(8,128)(2,1)S(1)} custom-call(s32[3]{0:T(128)S(1)} %pad_add_fusion.sc, bf16[320,1536]{1,0:T(8,128)(2,1)S(1)} %get-tuple-element.57.refs_0_, bf16[320,576]{1,0:T(8,128)(2,1)S(1)} %get-tuple-element.58.refs_1_, bf16[64,1536]{1,0:T(8,128)(2,1)S(1)} %get-tuple-element.59.refs_2_, ...), custom_call_target="tpu_custom_call" | custom-call | flops 964689920 | bytes 2359296 | tf_op jit(solution)/shard_map/pallas_call | solution.py:108
  61.0 2.9 %collective-permute-start.14 = (bf16[320,256]{1,0:T(8,128)(2,1)S(1)}, bf16[320,256]{1,0:T(8,128)(2,1)S(1)}, u32[]{:S(2)}, u32[]{:S(2)}) collective-permute-start(bf16[320,256]{1,0:T(8,128)(2,1)S(1)} %shard_map.108.refs_3_), channel_id=1, source_target_pairs={{0,8},{4,12},{8,0},{12,4},{1,9},{5,13},{9,1},{13,5},{2,10},{6,14},... | collective-permute-start | bytes 491528 | tf_op jit(solution)/shard_map/ppermute | solution.py:312
  64.0 0.6 collective-permute-start.15
  64.6 0.7 collective-permute-done.10.refs_2_
  65.3 0.7 collective-permute-start.12
  66.0 5.9 %collective-permute-done.14.refs_2_ = bf16[320,256]{1,0:T(8,128)(2,1)S(1)} collective-permute-done((bf16[320,256]{1,0:T(8,128)(2,1)S(1)}, bf16[320,256]{1,0:T(8,128)(2,1)S(1)}, u32[]{:S(2)}, u32[]{:S(2)}) %collective-permute-start.14) | collective-permute-done | bytes 163872 | tf_op jit(solution)/shard_map/ppermute | solution.py:312
  71.9 1.0 %collective-permute-done.15.refs_1_ = bf16[320,256]{1,0:T(8,128)(2,1)S(1)} collective-permute-done((bf16[320,256]{1,0:T(8,128)(2,1)S(1)}, bf16[320,256]{1,0:T(8,128)(2,1)S(1)}, u32[]{:S(2)}, u32[]{:S(2)}) %collective-permute-start.15) | collective-permute-done | bytes 163872 | tf_op jit(solution)/shard_map/ppermute | solution.py:313
  72.8 1.8 %collective-permute-start.16 = (bf16[320,256]{1,0:T(8,128)(2,1)S(1)}, bf16[320,256]{1,0:T(8,128)(2,1)S(1)}, u32[]{:S(2)}, u32[]{:S(2)}) collective-permute-start(bf16[320,256]{1,0:T(8,128)(2,1)S(1)} %collective-permute-done.14.refs_2_), channel_id=1, source_target_pairs={{0,4},{4,0},{8,12},{12,8},{1,5},{5,1},{9,13},{13,9},{2,6},{6,2},{1... | collective-permute-start | bytes 491528 | tf_op jit(solution)/shard_map/ppermute | solution.py:315
  74.6 4.0 %shard_map.109 = (f32[320,1792]{1,0:T(8,128)S(1)}, bf16[4,256,896]{2,1,0:T(8,128)(2,1)S(1)}, bf16[4,256,896]{2,1,0:T(8,128)(2,1)S(1)}) custom-call(s32[3]{0:T(128)S(1)} %pad_add_fusion.sc, bf16[320,256]{1,0:T(8,128)(2,1)S(1)} %get-tuple-element.55.refs_0_, bf16[320,256]{1,0:T(8,128)(2,1)S(1)} %collective-permute-done.11.refs_1_, ...), custom_call_target="tpu_custom_call" | custom-call | flops 1174405120 | bytes 3670016 | tf_op jit(solution)/shard_map/pallas_call | solution.py:108
  78.9 1.6 %shard_map.110 = (f32[160,896]{1,0:T(8,128)S(1)}, bf16[160,896]{1,0:T(8,128)(2,1)S(1)}, bf16[4,256,896]{2,1,0:T(8,128)(2,1)S(1)}) custom-call(s32[3]{0:T(128)S(1)} %pad_add_fusion.sc, bf16[320,256]{1,0:T(8,128)(2,1)S(1)} %collective-permute-done.12.refs_0_, bf16[320,256]{1,0:T(8,128)(2,1)S(1)} %collective-permute-done.15.refs_1_, ...), custom_call_target="tpu_custom_call", output_to_operand_aliasing={{2}: (7, {})} | custom-call | flops 587202560 | bytes 1835008 | tf_op jit(solution)/shard_map/pallas_call | solution.py:108
  80.5 1.6 %shard_map.111 = (f32[160,896]{1,0:T(8,128)S(1)}, bf16[160,896]{1,0:T(8,128)(2,1)S(1)}, f32[160,896]{1,0:T(8,128)S(1)}) custom-call(s32[3]{0:T(128)S(1)} %pad_add_fusion.sc, bf16[320,256]{1,0:T(8,128)(2,1)S(1)} %collective-permute-done.12.refs_0_, bf16[320,256]{1,0:T(8,128)(2,1)S(1)} %collective-permute-done.15.refs_1_, ...), custom_call_target="tpu_custom_call", output_to_operand_aliasing={{2}: (7, {})} | custom-call | flops 587202560 | bytes 1835008 | tf_op jit(solution)/shard_map/pallas_call | solution.py:108
  82.7 1.1 %collective-permute-done.19 = bf16[160,896]{1,0:T(8,128)(2,1)S(1)} collective-permute-done((bf16[160,896]{1,0:T(8,128)(2,1)S(1)}, bf16[160,896]{1,0:T(8,128)(2,1)S(1)}, u32[]{:S(2)}, u32[]{:S(2)}) %collective-permute-start.19) | collective-permute-done | bytes 286752 | tf_op jit(solution)/shard_map/ppermute | solution.py:540
  84.6 1.6 %collective-permute-start.18 = (bf16[80,896]{1,0:T(8,128)(2,1)S(1)}, bf16[80,896]{1,0:T(8,128)(2,1)S(1)}, u32[]{:S(2)}, u32[]{:S(2)}) collective-permute-start(bf16[80,896]{1,0:T(8,128)(2,1)S(1)} %fusion.2), channel_id=1, source_target_pairs={{0,2},{1,3},{2,0},{3,1},{4,6},{5,7},{6,4},{7,5},{8,10},{9,11},{10,... | collective-permute-start | bytes 430088 | tf_op jit(solution)/shard_map/ppermute | solution.py:544
  86.1 4.4 %collective-permute-done.20 = bf16[80,896]{1,0:T(8,128)(2,1)S(1)} collective-permute-done((bf16[80,896]{1,0:T(8,128)(2,1)S(1)}, bf16[80,896]{1,0:T(8,128)(2,1)S(1)}, u32[]{:S(2)}, u32[]{:S(2)}) %collective-permute-start.20) | collective-permute-done | bytes 143392 | tf_op jit(solution)/shard_map/ppermute | solution.py:544
  90.6 2.2 %collective-permute-done.18 = bf16[80,896]{1,0:T(8,128)(2,1)S(1)} collective-permute-done((bf16[80,896]{1,0:T(8,128)(2,1)S(1)}, bf16[80,896]{1,0:T(8,128)(2,1)S(1)}, u32[]{:S(2)}, u32[]{:S(2)}) %collective-permute-start.18) | collective-permute-done | bytes 143392 | tf_op jit(solution)/shard_map/ppermute | solution.py:544
  92.8 0.7 pad_maximum_fusion
  (37 shorter events, 4.7 us)
Async XLA Ops:
  0.6 7.9 %copy-start.1 = (bf16[384,64]{0,1:T(8,128)(2,1)S(1)}, bf16[384,64]{0,1:T(8,128)(2,1)}, u32[]{:S(2)}) copy-start(bf16[384,64]{0,1:T(8,128)(2,1)} %param.13) | copy-start | bytes 147460
  0.6 7.9 %copy-start.4 = (bf16[384,3072]{1,0:T(8,128)(2,1)S(1)}, bf16[384,3072]{1,0:T(8,128)(2,1)}, u32[]{:S(2)}) copy-start(bf16[384,3072]{1,0:T(8,128)(2,1)} %refs_9_.1) | copy-start | bytes 7077892
  2.8 21.5 %collective-permute-start = (bf16[320,384]{1,0:T(8,128)(2,1)S(1)}, bf16[320,384]{1,0:T(8,128)(2,1)S(1)}, u32[]{:S(2)}, u32[]{:S(2)}) collective-permute-start(bf16[320,384]{1,0:T(8,128)(2,1)S(1)} %get-tuple-element.39), channel_id=1, source_target_pairs={{0,8},{4,12},{8,0},{12,4},{1,9},{5,13},{9,1},{13,5},{2,10},{6,14},... | collective-permute-start | bytes 737288 | tf_op jit(solution)/shard_map/ppermute | solution.py:430
  6.9 17.4 %collective-permute-start.1 = (bf16[320,384]{1,0:T(8,128)(2,1)S(1)}, bf16[320,384]{1,0:T(8,128)(2,1)S(1)}, u32[]{:S(2)}, u32[]{:S(2)}) collective-permute-start(bf16[320,384]{1,0:T(8,128)(2,1)S(1)} %get-tuple-element.40), channel_id=1, source_target_pairs={{0,12},{4,8},{8,4},{12,0},{1,13},{5,9},{9,5},{13,1},{2,14},{6,10},... | collective-permute-start | bytes 737288 | tf_op jit(solution)/shard_map/ppermute | solution.py:430
  8.2 41.1 %copy-start = (bf16[80,1536]{1,0:T(8,128)(2,1)S(1)}, bf16[80,1536]{1,0:T(8,128)(2,1)}, u32[]{:S(2)}) copy-start(bf16[80,1536]{1,0:T(8,128)(2,1)} %refs_0_.1) | copy-start | bytes 737284
  8.2 41.1 %copy-start.2 = (bf16[80,576]{1,0:T(8,128)(2,1)S(1)}, bf16[80,576]{1,0:T(8,128)(2,1)}, u32[]{:S(2)}) copy-start(bf16[80,576]{1,0:T(8,128)(2,1)} %refs_1_.1) | copy-start | bytes 276484
  8.2 41.1 %copy-start.3 = (s32[80]{0:T(128)S(1)}, s32[80]{0:T(128)}, u32[]{:S(2)}) copy-start(s32[80]{0:T(128)} %param.11) | copy-start | bytes 964
  8.2 16.5 %collective-permute-start.2 = (bf16[320,384]{1,0:T(8,128)(2,1)S(1)}, bf16[320,384]{1,0:T(8,128)(2,1)S(1)}, u32[]{:S(2)}, u32[]{:S(2)}) collective-permute-start(bf16[320,384]{1,0:T(8,128)(2,1)S(1)} %get-tuple-element.41), channel_id=1, source_target_pairs={{0,4},{4,0},{8,12},{12,8},{1,5},{5,1},{9,13},{13,9},{2,6},{6,2},{1... | collective-permute-start | bytes 737288 | tf_op jit(solution)/shard_map/ppermute | solution.py:430
  25.4 19.7 %collective-permute-start.5 = (bf16[3,128,384]{2,1,0:T(8,128)(2,1)S(1)}, bf16[3,128,384]{2,1,0:T(8,128)(2,1)S(1)}, u32[]{:S(2)}, u32[]{:S(2)}) collective-permute-start(bf16[3,128,384]{2,1,0:T(8,128)(2,1)S(1)} %get-tuple-element.47), channel_id=1, source_target_pairs={{0,2},{1,3},{2,0},{3,1},{4,6},{5,7},{6,4},{7,5},{8,10},{9,11},{10,... | collective-permute-start | bytes 884744 | tf_op jit(solution)/shard_map/ppermute | solution.py:443
  27.0 16.9 %collective-permute-start.6 = (bf16[192,384]{1,0:T(8,128)(2,1)S(1)}, bf16[192,384]{1,0:T(8,128)(2,1)S(1)}, u32[]{:S(2)}, u32[]{:S(2)}) collective-permute-start(bf16[192,384]{1,0:T(8,128)(2,1)S(1)} %get-tuple-element.51), channel_id=1, source_target_pairs={{0,8},{4,12},{8,0},{12,4},{1,9},{5,13},{9,1},{13,5},{2,10},{6,14},... | collective-permute-start | bytes 442376 | tf_op jit(solution)/shard_map/ppermute | solution.py:430
  33.5 10.4 %collective-permute-start.7 = (bf16[192,384]{1,0:T(8,128)(2,1)S(1)}, bf16[192,384]{1,0:T(8,128)(2,1)S(1)}, u32[]{:S(2)}, u32[]{:S(2)}) collective-permute-start(bf16[192,384]{1,0:T(8,128)(2,1)S(1)} %get-tuple-element.52), channel_id=1, source_target_pairs={{0,12},{4,8},{8,4},{12,0},{1,13},{5,9},{9,5},{13,1},{2,14},{6,10},... | collective-permute-start | bytes 442376 | tf_op jit(solution)/shard_map/ppermute | solution.py:430
  33.9 11.2 %collective-permute-start.8 = (bf16[192,384]{1,0:T(8,128)(2,1)S(1)}, bf16[192,384]{1,0:T(8,128)(2,1)S(1)}, u32[]{:S(2)}, u32[]{:S(2)}) collective-permute-start(bf16[192,384]{1,0:T(8,128)(2,1)S(1)} %get-tuple-element.53), channel_id=1, source_target_pairs={{0,4},{4,0},{8,12},{12,8},{1,5},{5,1},{9,13},{13,9},{2,6},{6,2},{1... | collective-permute-start | bytes 442376 | tf_op jit(solution)/shard_map/ppermute | solution.py:430
  34.1 14.8 %collective-permute-start.3 = (bf16[3,192,384]{2,1,0:T(8,128)(2,1)S(1)}, bf16[3,192,384]{2,1,0:T(8,128)(2,1)S(1)}, u32[]{:S(2)}, u32[]{:S(2)}) collective-permute-start(bf16[3,192,384]{2,1,0:T(8,128)(2,1)S(1)} %get-tuple-element.46), channel_id=1, source_target_pairs={{0,16},{16,0},{1,17},{17,1},{2,18},{18,2},{3,19},{19,3},{4,20},{20... | collective-permute-start | bytes 1327112 | tf_op jit(solution)/shard_map/ppermute | solution.py:442
  45.7 10.8 %collective-permute-start.13 = (bf16[3,192,384]{2,1,0:T(8,128)(2,1)S(1)}, bf16[3,192,384]{2,1,0:T(8,128)(2,1)S(1)}, u32[]{:S(2)}, u32[]{:S(2)}) collective-permute-start(bf16[3,192,384]{2,1,0:T(8,128)(2,1)S(1)} %shard_map.107), channel_id=1, source_target_pairs={{0,16},{16,0},{1,17},{17,1},{2,18},{18,2},{3,19},{19,3},{4,20},{20... | collective-permute-start | bytes 1327112 | tf_op jit(solution)/shard_map/ppermute | solution.py:451
  47.3 1.6 %collective-permute-start.4 = (bf16[3,128,384]{2,1,0:T(8,128)(2,1)S(1)}, bf16[3,128,384]{2,1,0:T(8,128)(2,1)S(1)}, u32[]{:S(2)}, u32[]{:S(2)}) collective-permute-start(bf16[3,128,384]{2,1,0:T(8,128)(2,1)S(1)} %get-tuple-element.47), channel_id=1, source_target_pairs={{0,1},{1,0},{2,3},{3,2},{4,5},{5,4},{6,7},{7,6},{8,9},{9,8},{10,11... | collective-permute-start | bytes 884744 | tf_op jit(solution)/shard_map/ppermute | solution.py:446
  47.3 2.0 %collective-permute-start.9 = (bf16[3,128,384]{2,1,0:T(8,128)(2,1)S(1)}, bf16[3,128,384]{2,1,0:T(8,128)(2,1)S(1)}, u32[]{:S(2)}, u32[]{:S(2)}) collective-permute-start(bf16[3,128,384]{2,1,0:T(8,128)(2,1)S(1)} %collective-permute-done.5.refs_9_), channel_id=1, source_target_pairs={{0,1},{1,0},{2,3},{3,2},{4,5},{5,4},{6,7},{7,6},{8,9},{9,8},{10,11... | collective-permute-start | bytes 884744 | tf_op jit(solution)/shard_map/ppermute | solution.py:448
  54.2 11.1 %collective-permute-start.10 = (bf16[320,256]{1,0:T(8,128)(2,1)S(1)}, bf16[320,256]{1,0:T(8,128)(2,1)S(1)}, u32[]{:S(2)}, u32[]{:S(2)}) collective-permute-start(bf16[320,256]{1,0:T(8,128)(2,1)S(1)} %get-tuple-element.55.refs_0_), channel_id=1, source_target_pairs={{0,8},{4,12},{8,0},{12,4},{1,9},{5,13},{9,1},{13,5},{2,10},{6,14},... | collective-permute-start | bytes 491528 | tf_op jit(solution)/shard_map/ppermute | solution.py:312
  55.4 9.8 %collective-permute-start.11 = (bf16[320,256]{1,0:T(8,128)(2,1)S(1)}, bf16[320,256]{1,0:T(8,128)(2,1)S(1)}, u32[]{:S(2)}, u32[]{:S(2)}) collective-permute-start(bf16[320,256]{1,0:T(8,128)(2,1)S(1)} %get-tuple-element.55.refs_0_), channel_id=1, source_target_pairs={{0,4},{4,0},{8,12},{12,8},{1,5},{5,1},{9,13},{13,9},{2,6},{6,2},{1... | collective-permute-start | bytes 491528 | tf_op jit(solution)/shard_map/ppermute | solution.py:313
  61.0 10.8 %collective-permute-start.14 = (bf16[320,256]{1,0:T(8,128)(2,1)S(1)}, bf16[320,256]{1,0:T(8,128)(2,1)S(1)}, u32[]{:S(2)}, u32[]{:S(2)}) collective-permute-start(bf16[320,256]{1,0:T(8,128)(2,1)S(1)} %shard_map.108.refs_3_), channel_id=1, source_target_pairs={{0,8},{4,12},{8,0},{12,4},{1,9},{5,13},{9,1},{13,5},{2,10},{6,14},... | collective-permute-start | bytes 491528 | tf_op jit(solution)/shard_map/ppermute | solution.py:312
  64.0 8.9 %collective-permute-start.15 = (bf16[320,256]{1,0:T(8,128)(2,1)S(1)}, bf16[320,256]{1,0:T(8,128)(2,1)S(1)}, u32[]{:S(2)}, u32[]{:S(2)}) collective-permute-start(bf16[320,256]{1,0:T(8,128)(2,1)S(1)} %shard_map.108.refs_3_), channel_id=1, source_target_pairs={{0,4},{4,0},{8,12},{12,8},{1,5},{5,1},{9,13},{13,9},{2,6},{6,2},{1... | collective-permute-start | bytes 491528 | tf_op jit(solution)/shard_map/ppermute | solution.py:313
  65.3 13.3 %collective-permute-start.12 = (bf16[320,256]{1,0:T(8,128)(2,1)S(1)}, bf16[320,256]{1,0:T(8,128)(2,1)S(1)}, u32[]{:S(2)}, u32[]{:S(2)}) collective-permute-start(bf16[320,256]{1,0:T(8,128)(2,1)S(1)} %collective-permute-done.10.refs_2_), channel_id=1, source_target_pairs={{0,4},{4,0},{8,12},{12,8},{1,5},{5,1},{9,13},{13,9},{2,6},{6,2},{1... | collective-permute-start | bytes 491528 | tf_op jit(solution)/shard_map/ppermute | solution.py:315
  72.8 6.1 %collective-permute-start.16 = (bf16[320,256]{1,0:T(8,128)(2,1)S(1)}, bf16[320,256]{1,0:T(8,128)(2,1)S(1)}, u32[]{:S(2)}, u32[]{:S(2)}) collective-permute-start(bf16[320,256]{1,0:T(8,128)(2,1)S(1)} %collective-permute-done.14.refs_2_), channel_id=1, source_target_pairs={{0,4},{4,0},{8,12},{12,8},{1,5},{5,1},{9,13},{13,9},{2,6},{6,2},{1... | collective-permute-start | bytes 491528 | tf_op jit(solution)/shard_map/ppermute | solution.py:315
  82.1 1.6 %collective-permute-start.19 = (bf16[160,896]{1,0:T(8,128)(2,1)S(1)}, bf16[160,896]{1,0:T(8,128)(2,1)S(1)}, u32[]{:S(2)}, u32[]{:S(2)}) collective-permute-start(bf16[160,896]{1,0:T(8,128)(2,1)S(1)} %get-tuple-element.75), channel_id=1, source_target_pairs={{0,1},{1,0},{2,3},{3,2},{4,5},{5,4},{6,7},{7,6},{8,9},{9,8},{10,11... | collective-permute-start | bytes 860168 | tf_op jit(solution)/shard_map/ppermute | solution.py:540
  82.2 2.2 %collective-permute-start.17 = (bf16[160,896]{1,0:T(8,128)(2,1)S(1)}, bf16[160,896]{1,0:T(8,128)(2,1)S(1)}, u32[]{:S(2)}, u32[]{:S(2)}) collective-permute-start(bf16[160,896]{1,0:T(8,128)(2,1)S(1)} %get-tuple-element.73), channel_id=1, source_target_pairs={{0,1},{1,0},{2,3},{3,2},{4,5},{5,4},{6,7},{7,6},{8,9},{9,8},{10,11... | collective-permute-start | bytes 860168 | tf_op jit(solution)/shard_map/ppermute | solution.py:540
  83.9 6.7 %collective-permute-start.20 = (bf16[80,896]{1,0:T(8,128)(2,1)S(1)}, bf16[80,896]{1,0:T(8,128)(2,1)S(1)}, u32[]{:S(2)}, u32[]{:S(2)}) collective-permute-start(bf16[80,896]{1,0:T(8,128)(2,1)S(1)} %fusion.3), channel_id=1, source_target_pairs={{0,2},{1,3},{2,0},{3,1},{4,6},{5,7},{6,4},{7,5},{8,10},{9,11},{10,... | collective-permute-start | bytes 430088 | tf_op jit(solution)/shard_map/ppermute | solution.py:544
  84.6 8.2 %collective-permute-start.18 = (bf16[80,896]{1,0:T(8,128)(2,1)S(1)}, bf16[80,896]{1,0:T(8,128)(2,1)S(1)}, u32[]{:S(2)}, u32[]{:S(2)}) collective-permute-start(bf16[80,896]{1,0:T(8,128)(2,1)S(1)} %fusion.2), channel_id=1, source_target_pairs={{0,2},{1,3},{2,0},{3,1},{4,6},{5,7},{6,4},{7,5},{8,10},{9,11},{10,... | collective-permute-start | bytes 430088 | tf_op jit(solution)/shard_map/ppermute | solution.py:544

commit v6 on v5

--- a/solution.py
+++ b/solution.py
@@ -231,35 +231,36 @@
     bias[...] = jnp.where(seen, 0.0, -1e30)
 
 
-def attend(n, nope, scale, c, sc, shared, units, y_ref, weights, out, scratch, before=None):
+def own_weights(sc, c, weights, outs):
+    b_ref, w_ref, ku_ref, vu_ref = weights
+    b, w, ku, vu = outs
+    wide, heads = w.shape[1], ku.shape[0]
+    chunk = sc[0] * CHUNKS + c
+    columns = pl.ds(pl.multiple_of(chunk * wide, 128), wide)
+    return [
+        (b_ref.at[:, columns], b),
+        (w_ref.at[:, columns], w),
+        (ku_ref.at[pl.ds(chunk * heads, heads)], ku),
+        (vu_ref.at[pl.ds(chunk * heads, heads)], vu),
+    ]
+
+
+def attend(n, nope, scale, sc, shared, units, ys, weights, out, raw, before=None, copies=()):
     x_ref, kv_ref, at_ref, bias_ref = shared
-    b_ref, w_ref, ku_ref, vu_ref = weights
-    raw, b_own, ku, vu, sems = scratch
+    b_own, w_own, ku, vu = weights
     s, g = sc[0], sc[1]
-    depth = w_ref.shape[0]
+    depth, wide = w_own.shape
     half = depth // 2
-    wide = raw.shape[1]
     heads, kvr, vdim = vu.shape
-    chunk = s * CHUNKS + c
-    columns = pl.ds(pl.multiple_of(chunk * wide, 128), wide)
-    mine = pl.ds(pl.multiple_of(s * depth, 128), depth)
-    b_copy, w_copy, ku_copy, vu_copy = fetch(
-        [
-            (b_ref.at[:, columns], b_own),
-            (w_ref.at[:, columns], raw.at[mine, :]),
-            (ku_ref.at[pl.ds(chunk * heads, heads)], ku),
-            (vu_ref.at[pl.ds(chunk * heads, heads)], vu),
-        ],
-        sems,
-    )
     if before is not None:
         before()
     for k, bits in enumerate(partners(n)):
         src = s ^ bits
         raw[pl.ds(pl.multiple_of(src * depth + g * half, 16), half), :] = units[k][:half]
-        raw[pl.ds(pl.multiple_of(src * depth + (1 - g) * half, 16), half), :] = y_ref[k]
-    b_copy.wait()
-    w_copy.wait()
+        raw[pl.ds(pl.multiple_of(src * depth + (1 - g) * half, 16), half), :] = ys[k][...]
+    for copy in copies[:2]:
+        copy.wait()
+    raw[pl.ds(pl.multiple_of(s * depth, 16), depth), :] = w_own[...]
 
     def merge(rows):
         add = lax.dot_general(
@@ -270,8 +271,8 @@
     for src in range(n):
         merge(slice(src * depth, (src + 1) * depth))
     q = jnp.dot(x_ref[...], raw[...], preferred_element_type=jnp.float32)
-    ku_copy.wait()
-    vu_copy.wait()
+    for copy in copies[2:]:
+        copy.wait()
     width = wide // heads
     lat, rope_key = kv_ref[:, :kvr], kv_ref[:, kvr:]
     bias = bias_ref[...]
@@ -295,28 +296,34 @@
 def attend_first(n, nh, kq, vq, aq, nope, scale, sc, *refs):
     own, units, y_ref, stacks = refs[:4], refs[4 : 3 + n], refs[3 + n], refs[4 + n : 3 + n + nh]
     refs = refs[3 + n + nh :]
-    weights, out, shared, turn, scratch = refs[:4], refs[4], refs[5:9], refs[9], refs[10:]
+    far, out, shared, later = refs[:4], refs[4], refs[5:9], refs[9:13]
+    turn, raw, weights, sems = refs[13], refs[14], refs[15:19], refs[19]
+    copies = fetch(own_weights(sc, 0, far, weights) + own_weights(sc, CHUNKS - 1, far, later), sems)
 
     def before():
         unpack(n, nh, kq, vq, aq, sc, own, units, stacks, shared, turn)
 
-    attend(n, nope, scale, 0, sc, shared, units, y_ref, weights, out, scratch, before)
+    ys = [y_ref.at[k] for k in range(n - 1)]
+    attend(n, nope, scale, sc, shared, units, ys, weights, out, raw, before, copies[:4])
+    for copy in copies[4:]:
+        copy.wait()
 
 
 def attend_next(n, nope, scale, sc, *refs):
-    shared, units, refs = refs[:4], refs[4 : 3 + n], refs[3 + n :]
-    attend(n, nope, scale, CHUNKS - 1, sc, shared, units, refs[0], refs[1:5], refs[5], refs[6:])
-
-
-def gather_line(x):
+    shared, units, ys, refs = refs[:4], refs[4 : 3 + n], refs[3 + n : 2 + 2 * n], refs[2 + 2 * n :]
+    attend(n, nope, scale, sc, shared, units, ys, refs[:4], refs[4], refs[5])
+
+
+def gather_line(x, *held):
     two = lax.ppermute(x, "seq", flipped(4, 2))
     one = lax.ppermute(x, "seq", flipped(4, 1))
-    two, one = lax.optimization_barrier((two, one))
-    return [x, one, two, lax.ppermute(two, "seq", flipped(4, 1))]
+    two, one, *held = lax.optimization_barrier((two, one) + held)
+    return [x, one, two, lax.ppermute(two, "seq", flipped(4, 1))] + held
 
 
 EARLY = ((0, 0), (1, 0), (2, 0), (0, 1))
-LATE = ((3, 0), (1, 1), (2, 1), (3, 1))
+MIDDLE = ((3, 0), (1, 1), (2, 1))
+LATE = ((3, 1),)
 
 
 def place(slots, lhs):
@@ -333,36 +340,51 @@
     for at in range(begin, end, TILE):
         stop = min(at + TILE, end)
         tile = w[:, :, at:stop]
-        tile = tile.reshape(lhs.shape[1], tile.shape[-1])
+        tile = tile.reshape(-1, tile.shape[-1])
         put(slice(at, stop), jnp.dot(lhs[...], tile, preferred_element_type=jnp.float32))
 
 
-def first_body(cut, sc, *refs):
+def early_body(sc, *refs):
     count = len(EARLY)
-    slots, (w_ref, acc, left, right, lhs, w, sems) = refs[:count], refs[count:]
+    slots, (w_ref, acc, token, lhs, w, sems) = refs[:count], refs[count:]
+    copies = fetch(slabs(sc, w_ref, EARLY, slice(None), w), sems)
+    place(slots, lhs)
+    token[...] = jnp.zeros_like(token)
+    for copy in copies:
+        copy.wait()
+
+    def put(band, value):
+        acc[:, band] = value
+
+    columns_dot(lhs, w, 0, acc.shape[1], put)
+
+
+def middle_body(sc, *refs):
+    count = len(MIDDLE)
+    slots, (w_ref, before, token, acc, last, lhs, w, sems) = refs[:count], refs[count:]
+    del before, token
+    total = acc.shape[1]
     copies = fetch(
-        slabs(sc, w_ref, EARLY, slice(None), w)
-        + slabs(sc, w_ref, LATE, slice(0, cut), left)
-        + slabs(sc, w_ref, LATE, slice(cut, acc.shape[1]), right),
-        sems,
+        slabs(sc, w_ref, MIDDLE, slice(None), w) + slabs(sc, w_ref, LATE, slice(None), last), sems
     )
     place(slots, lhs)
     for copy in copies[:count]:
         copy.wait()
 
+    def add(band, value):
+        acc[:, band] += value
+
+    columns_dot(lhs, w, 0, total, add)
+    for copy in copies[count:]:
+        copy.wait()
+
+
+def last_body(nh, tok, sc, *refs):
+    slots, (w, acc, keep, send, lhs, tot) = refs[: len(LATE)], refs[len(LATE) :]
+    place(slots, lhs)
+
     def put(band, value):
-        acc[:, band] = value
-
-    columns_dot(lhs, w, 0, acc.shape[1], put)
-    for copy in copies[count:]:
-        copy.wait()
-
-
-def last_body(nh, tok, begin, sc, w, acc, slots, keep, send, lhs, tot):
-    place(slots, lhs)
-
-    def put(band, value):
-        tot[:, band] = acc[:, begin + band.start : begin + band.stop] + value
+        tot[:, band] = acc[:, band] + value
 
     columns_dot(lhs, w, 0, keep.shape[1], put)
     core = sc[2] % 2
@@ -371,20 +393,6 @@
         theirs = pl.ds(pl.multiple_of((2 * i + 1 - core) * tok, 16), tok)
         keep[i * tok : (i + 1) * tok, :] = tot[mine, :]
         send[i * tok : (i + 1) * tok, :] = tot[theirs, :].astype(jnp.bfloat16)
-
-
-def last_left(nh, tok, sc, *refs):
-    count = len(LATE)
-    slots, (w, acc, held, keep, send, passed, lhs, tot) = refs[:count], refs[count:]
-    del held, passed
-    last_body(nh, tok, 0, sc, w, acc, slots, keep, send, lhs, tot)
-
-
-def last_right(nh, tok, sc, *refs):
-    count = len(LATE)
-    slots, (w, acc, held, keep, send, passed, lhs, tot) = refs[:count], refs[count:]
-    del held, passed
-    last_body(nh, tok, acc.shape[1] - keep.shape[1], sc, w, acc, slots, keep, send, lhs, tot)
 
 
 def by_heads(x, kv, pos, wq, down, up, ku, vu, wo):
@@ -439,7 +447,7 @@
     later = lax.optimization_barrier((*units[n - 1 :], moved[0][0]))
     moved.append(exchange(later[: n - 1]))
     share, stack = split(moved[0], half, extra)
-    passed = [lax.ppermute(share, "groups", flipped(2, 1))]
+    passed = [[lax.ppermute(share, "groups", flipped(2, 1))]]
     across = lax.ppermute(stack, "head", flipped(nh, 2))
     across, *moved[1] = lax.optimization_barrier((across, *moved[1]))
     stacks = [
@@ -447,22 +455,16 @@
         across,
         lax.ppermute(across, "head", flipped(nh, 1)),
     ]
-    (share,) = split(moved[1], half)
-    passed.append(lax.ppermute(share, "groups", flipped(2, 1)))
+    passed.append([lax.ppermute(p, "groups", flipped(2, 1)) for p in moved[1]])
 
     scale = 1.0 / math.sqrt(nope + rope)
-    scratch = [
-        pltpu.VMEM((n * rows, wide), bf),
-        pltpu.VMEM((rank, wide), bf),
-        pltpu.VMEM((per, nope, kvr), bf),
-        pltpu.VMEM((per, kvr, vdim), bf),
-        pltpu.SemaphoreType.DMA((4,)),
-    ]
+    shapes = ((rank, wide), (rows, wide), (per, nope, kvr), (per, kvr, vdim))
+    raw = pltpu.VMEM((n * rows, wide), bf)
     cost = dict(
         flops=2 * tokens * per * (depth * wide // per + 2 * nope * kvr + 2 * tokens * kvr),
         moved=4 * n * rows * wide,
     )
-    ho, *shared = call(
+    ho, *kept = call(
         functools.partial(attend_first, n, nh, kq, vq, aq, nope, scale),
         (
             like(tokens, per * vdim),
@@ -470,80 +472,74 @@
             like(tokens, kvr + rope),
             like(rank, n * rows),
             like(tokens, tokens, dtype=f32),
+            *(like(*shape) for shape in shapes),
         ),
-        [sc, x, kv, at, pos2] + moved[0] + [passed[0]] + stacks + [up, wq, ku, vu],
+        [sc, x, kv, at, pos2] + moved[0] + passed[0] + stacks + [up, wq, ku, vu],
         hbm=range(4 + n + nh, 8 + n + nh),
-        scratch=[pltpu.VMEM((128, 128), f32)] + scratch,
+        scratch=[pltpu.VMEM((128, 128), f32), raw]
+        + [pltpu.VMEM(shape, bf) for shape in shapes]
+        + [pltpu.SemaphoreType.DMA((8,))],
         **cost,
     )
     slots = [gather_line(ho)]
     ho = call(
         functools.partial(attend_next, n, nope, scale),
         like(tokens, per * vdim),
-        [sc] + shared + moved[1] + [passed[1], up, wq, ku, vu],
-        hbm=range(5 + n, 9 + n),
-        scratch=scratch,
+        [sc] + kept[:4] + moved[1] + passed[1] + kept[4:],
+        scratch=[raw],
         **cost,
     )
-    slots.append(gather_line(ho))
-
     w4 = wo.reshape(n, CHUNKS, per * vdim, wo.shape[1])
     total = wo.shape[1]
-    early, late = ([slots[c][bits] for bits, c in pieces] for pieces in (EARLY, LATE))
-    lhs = pltpu.VMEM((tokens, n * per * vdim), bf)
-    flops = 2 * tokens * n * per * vdim * total
-    cut = (total // 128 + 1) // 2 * 128
-    acc, w_left, w_right = call(
-        functools.partial(first_body, cut),
-        (
-            like(tokens, total, dtype=f32),
-            like(n, per * vdim, cut),
-            like(n, per * vdim, total - cut),
-        ),
-        [sc] + early + [w4],
-        hbm=(5,),
-        scratch=[
-            lhs,
-            pltpu.VMEM((n, per * vdim, total), bf),
-            pltpu.SemaphoreType.DMA((3 * n,)),
-        ],
-        flops=flops,
-        moved=w4.size,
-    )
-    pair_rows = nh // 2 * tok
-
-    def partial_sums(size):
-        return (like(pair_rows, size, dtype=f32), like(pair_rows, size))
-
-    keep, send, w_right = call(
-        functools.partial(last_left, nh, tok),
-        partial_sums(cut) + (like(n, per * vdim, total - cut),),
-        [sc] + late + [w_left, acc, w_right],
-        scratch=[lhs, pltpu.VMEM((tokens, cut), f32)],
-        alias={7: 2},
-        flops=flops // 2,
-        moved=w4.size // 2,
-    )
-    left = send
-    keep_right, right, keep = call(
-        functools.partial(last_right, nh, tok),
-        partial_sums(total - cut) + (like(pair_rows, cut, dtype=f32),),
-        [sc] + late + [w_right, acc, keep],
-        scratch=[lhs, pltpu.VMEM((tokens, total - cut), f32)],
-        alias={7: 2},
-        flops=flops // 2,
-        moved=w4.size // 2,
-    )
+    width = per * vdim
+
+    def room(pieces):
+        return [
+            pltpu.VMEM((tokens, len(pieces) * width), bf),
+            pltpu.VMEM((len(pieces), width, total), bf),
+        ]
+
+    def work(pieces):
+        rows = len(pieces) * width
+        return dict(flops=2 * tokens * rows * total, moved=2 * rows * total)
+
+    def pick(pieces):
+        return [slots[c][bits] for bits, c in pieces]
+
+    slots.append([ho])
+    acc, token = call(
+        early_body,
+        (like(tokens, total, dtype=f32), like(8, 128, dtype=f32)),
+        [sc] + pick(EARLY) + [w4],
+        hbm=(1 + len(EARLY),),
+        scratch=room(EARLY) + [pltpu.SemaphoreType.DMA((len(EARLY),))],
+        **work(EARLY),
+    )
+    *slots[1], token = gather_line(ho, token)
+    late = pick(LATE)
+    acc, w_last = call(
+        middle_body,
+        (like(tokens, total, dtype=f32), like(len(LATE), width, total)),
+        [sc] + pick(MIDDLE) + [w4, acc, token],
+        hbm=(1 + len(MIDDLE),),
+        scratch=room(MIDDLE) + [pltpu.SemaphoreType.DMA((len(MIDDLE) + len(LATE),))],
+        alias={2 + len(MIDDLE): 0},
+        **work(MIDDLE),
+    )
+    keep, send = call(
+        functools.partial(last_body, nh, tok),
+        (like(nh // 2 * tok, total, dtype=f32), like(nh // 2 * tok, total)),
+        [sc] + late + [w_last, acc],
+        scratch=[room(LATE)[0], pltpu.VMEM((tokens, total), f32)],
+        **work(LATE),
+    )
+    got = lax.ppermute(send, "head", flipped(nh, 1))
+    pair = (keep + got.astype(f32)).reshape(nh // 2, tok, total)
     side = h // 2
-    bands = []
-    for keep, send in ((keep, left), (keep_right, right)):
-        got = lax.ppermute(send, "head", flipped(nh, 1))
-        pair = (keep + got.astype(f32)).reshape(nh // 2, tok, keep.shape[1])
-        out = lax.dynamic_index_in_dim(pair, side, 0, keepdims=False)
-        away = lax.dynamic_index_in_dim(pair, 1 - side, 0, keepdims=False).astype(bf)
-        out = out + lax.ppermute(away, "head", flipped(nh, 2)).astype(f32)
-        bands.append(out.astype(bf))
-    return merged, jnp.concatenate(bands, axis=1)
+    out = lax.dynamic_index_in_dim(pair, side, 0, keepdims=False)
+    away = lax.dynamic_index_in_dim(pair, 1 - side, 0, keepdims=False).astype(bf)
+    out = out + lax.ppermute(away, "head", flipped(nh, 2)).astype(f32)
+    return merged, out.astype(bf)
 
 
 def fits(mesh, shapes):

time: 93.7 us -> 91.7 us (0.979)
  starting transfers between devices: 29.1 us -> 26.9 us
    ppermute x4 -> x6, waiting for transfers between devices: 0.31 us -> 3.63 us  [the longest x2 1.99 us: gather_line(): return [x, one, two, lax.ppermute(two, 'seq', flipped(4, 1))] + held]
    ppermute x2, waiting for transfers between devices: 6.57 us -> 3.7 us  [gather_line(): two = lax.ppermute(x, 'seq', flipped(4, 2))]
    ppermute x2 -> x1, waiting for transfers between devices: 6.64 us -> 8.34 us  [by_heads(): out = out + lax.ppermute(away, 'head', flipped(nh, 2)).astype(f32)]
    ppermute x2 -> x1, starting transfers between devices: 2.16 us -> 0.6 us  [by_heads(): out = out + lax.ppermute(away, 'head', flipped(nh, 2)).astype(f32)]
    ppermute x2, starting transfers between devices: 4.17 us -> 2.65 us  [gather_line(): two = lax.ppermute(x, 'seq', flipped(4, 2))]
    ppermute x4 -> x6, starting transfers between devices: 5.59 us -> 6.98 us  [the longest x3 3.55 us: by_heads(): passed.append([lax.ppermute(p, 'groups', flipped(2, 1)) for p in moved[1]])]
    ppermute x1, waiting for transfers between devices: 1.07 us -> 0.01 us  [by_heads(): lax.ppermute(stack, 'head', flipped(nh, 1))]
    ppermute x2, waiting for transfers between devices: 0.96 us -> 0.01 us  [gather_line(): one = lax.ppermute(x, 'seq', flipped(4, 1))]
  transfers between devices with their start and end apart: 21 -> 21, of which waited for: 13 -> 10; matrix products, arithmetic and copies ran while one was open for 4% -> 3% of each run, Pallas kernels for 15% -> 17%
where the time goes in v6:
time: 91.7 us; the launch traced here: 91.5 us
  waiting for transfers between devices  40.2 us (44%)
  starting transfers between devices  26.9 us (29%)
  Pallas kernels  19.4 us (21%)
  matrix products  3.2 us (3%)
  other arithmetic  0.94 us (1%)
    ppermute x6, waiting for transfers between devices, exchange(): lax.ppermute(p, 'seq', flipped(n, bits))  22.6 us
    pallas_call x7, Pallas kernels, call(): pl.pallas_call(body, out_shape=outs, grid_spec=pltpu.PrefetchScalarGridSp...  19.4 us
    ppermute x6, starting transfers between devices, exchange(): lax.ppermute(p, 'seq', flipped(n, bits))  12.8 us
    ppermute x1, waiting for transfers between devices, by_heads(): out = out + lax.ppermute(away, 'head', flipped(nh, 2)).astype(f32)  8.34 us
    ppermute x2, waiting for transfers between devices, gather_line(): two = lax.ppermute(x, 'seq', flipped(4, 2))  3.7 us
    ppermute x3, starting transfers between devices, by_heads(): passed.append([lax.ppermute(p, 'groups', flipped(2, 1)) for p in moved[1]])  3.55 us
    dot_general x1, matrix products, by_heads(): jnp.dot(down, up, preferred_element_type=f32)  3.2 us
    ppermute x2, starting transfers between devices, gather_line(): two = lax.ppermute(x, 'seq', flipped(4, 2))  2.65 us
  transfers between devices with their start and end apart: 21, of which 10 were waited for; matrix products, arithmetic and copies ran while one was open for 3% of the time, Pallas kernels for 17%

profile of v6, /device:TPU:0, one launch (start us, length us, event | category | flops | bytes accessed | tf_op | source)
XLA Modules:
  0.0 91.5 jit_solution(10565407412876572647)
XLA Ops:
  0.7 2.0 %shard_map.104 = (bf16[320,384]{1,0:T(8,128)(2,1)S(1)}, bf16[320,384]{1,0:T(8,128)(2,1)S(1)}, bf16[320,384]{1,0:T(8,128)(2,1)S(1)}, bf16[192,384]{1,0:T(8,128)(2...) custom-call(s32[3]{0:T(128)S(1)} %pad_add_fusion.sc, bf16[80,1536]{1,0:T(8,128)(2,1)} %refs_0_.1, ...), custom_call_target="tpu_custom_call" | custom-call | bytes 2359296 | tf_op jit(solution)/shard_map/pallas_call | solution.py:108
  2.8 4.1 %collective-permute-start = (bf16[320,384]{1,0:T(8,128)(2,1)S(1)}, bf16[320,384]{1,0:T(8,128)(2,1)S(1)}, u32[]{:S(2)}, u32[]{:S(2)}) collective-permute-start(bf16[320,384]{1,0:T(8,128)(2,1)S(1)} %get-tuple-element.41), channel_id=1, source_target_pairs={{0,8},{4,12},{8,0},{12,4},{1,9},{5,13},{9,1},{13,5},{2,10},{6,14},... | collective-permute-start | bytes 737288 | tf_op jit(solution)/shard_map/ppermute | solution.py:438
  6.9 1.3 %collective-permute-start.1 = (bf16[320,384]{1,0:T(8,128)(2,1)S(1)}, bf16[320,384]{1,0:T(8,128)(2,1)S(1)}, u32[]{:S(2)}, u32[]{:S(2)}) collective-permute-start(bf16[320,384]{1,0:T(8,128)(2,1)S(1)} %get-tuple-element.42), channel_id=1, source_target_pairs={{0,12},{4,8},{8,4},{12,0},{1,13},{5,9},{9,5},{13,1},{2,14},{6,10},... | collective-permute-start | bytes 737288 | tf_op jit(solution)/shard_map/ppermute | solution.py:438
  8.6 3.2 %add_convert_fusion = bf16[384,3072]{1,0:T(8,128)(2,1)} fusion(bf16[384,3072]{1,0:T(8,128)(2,1)S(1)} %copy-done.4, bf16[384,64]{0,1:T(8,128)(2,1)S(1)} %copy-done.1, bf16[64,3072]{1,0:T(8,128)(2,1)} %refs_11_.1), kind=kOutput, calls=%fused_computation | convolution fusion | flops 154533888 | bytes 5160960 | tf_op jit(solution)/shard_map/dot_general | solution.py:444
  11.8 12.5 %collective-permute-done.refs_0_.refs_4_ = bf16[320,384]{1,0:T(8,128)(2,1)S(1)} collective-permute-done((bf16[320,384]{1,0:T(8,128)(2,1)S(1)}, bf16[320,384]{1,0:T(8,128)(2,1)S(1)}, u32[]{:S(2)}, u32[]{:S(2)}) %collective-permute-start) | collective-permute-done | bytes 245792 | tf_op jit(solution)/shard_map/ppermute | solution.py:438
  24.3 0.5 collective-permute-done.2.refs_2_.refs_6_
  24.8 0.6 shard_map.105
  25.4 1.6 %collective-permute-start.5 = (bf16[3,128,384]{2,1,0:T(8,128)(2,1)S(1)}, bf16[3,128,384]{2,1,0:T(8,128)(2,1)S(1)}, u32[]{:S(2)}, u32[]{:S(2)}) collective-permute-start(bf16[3,128,384]{2,1,0:T(8,128)(2,1)S(1)} %get-tuple-element.49), channel_id=1, source_target_pairs={{0,2},{1,3},{2,0},{3,1},{4,6},{5,7},{6,4},{7,5},{8,10},{9,11},{10,... | collective-permute-start | bytes 884744 | tf_op jit(solution)/shard_map/ppermute | solution.py:451
  27.0 6.5 %collective-permute-start.6 = (bf16[192,384]{1,0:T(8,128)(2,1)S(1)}, bf16[192,384]{1,0:T(8,128)(2,1)S(1)}, u32[]{:S(2)}, u32[]{:S(2)}) collective-permute-start(bf16[192,384]{1,0:T(8,128)(2,1)S(1)} %get-tuple-element.53), channel_id=1, source_target_pairs={{0,8},{4,12},{8,0},{12,4},{1,9},{5,13},{9,1},{13,5},{2,10},{6,14},... | collective-permute-start | bytes 442376 | tf_op jit(solution)/shard_map/ppermute | solution.py:438
  34.1 1.5 %collective-permute-start.3 = (bf16[3,192,384]{2,1,0:T(8,128)(2,1)S(1)}, bf16[3,192,384]{2,1,0:T(8,128)(2,1)S(1)}, u32[]{:S(2)}, u32[]{:S(2)}) collective-permute-start(bf16[3,192,384]{2,1,0:T(8,128)(2,1)S(1)} %get-tuple-element.48), channel_id=1, source_target_pairs={{0,16},{16,0},{1,17},{17,1},{2,18},{18,2},{3,19},{19,3},{4,20},{20... | collective-permute-start | bytes 1327112 | tf_op jit(solution)/shard_map/ppermute | solution.py:450
  35.6 8.3 %collective-permute-done.6.refs_4_ = bf16[192,384]{1,0:T(8,128)(2,1)S(1)} collective-permute-done((bf16[192,384]{1,0:T(8,128)(2,1)S(1)}, bf16[192,384]{1,0:T(8,128)(2,1)S(1)}, u32[]{:S(2)}, u32[]{:S(2)}) %collective-permute-start.6) | collective-permute-done | bytes 147488 | tf_op jit(solution)/shard_map/ppermute | solution.py:438
  43.9 1.2 %collective-permute-done.8.refs_6_ = bf16[192,384]{1,0:T(8,128)(2,1)S(1)} collective-permute-done((bf16[192,384]{1,0:T(8,128)(2,1)S(1)}, bf16[192,384]{1,0:T(8,128)(2,1)S(1)}, u32[]{:S(2)}, u32[]{:S(2)}) %collective-permute-start.8) | collective-permute-done | bytes 147488 | tf_op jit(solution)/shard_map/ppermute | solution.py:438
  45.1 1.5 %collective-permute-start.10 = (bf16[192,384]{1,0:T(8,128)(2,1)S(1)}, bf16[192,384]{1,0:T(8,128)(2,1)S(1)}, u32[]{:S(2)}, u32[]{:S(2)}) collective-permute-start(bf16[192,384]{1,0:T(8,128)(2,1)S(1)} %collective-permute-done.6.refs_4_), channel_id=1, source_target_pairs={{0,16},{16,0},{1,17},{17,1},{2,18},{18,2},{3,19},{19,3},{4,20},{20... | collective-permute-start | bytes 442376 | tf_op jit(solution)/shard_map/ppermute | solution.py:458
  47.2 1.5 %collective-permute-start.12 = (bf16[192,384]{1,0:T(8,128)(2,1)S(1)}, bf16[192,384]{1,0:T(8,128)(2,1)S(1)}, u32[]{:S(2)}, u32[]{:S(2)}) collective-permute-start(bf16[192,384]{1,0:T(8,128)(2,1)S(1)} %collective-permute-done.8.refs_6_), channel_id=1, source_target_pairs={{0,16},{16,0},{1,17},{17,1},{2,18},{18,2},{3,19},{19,3},{4,20},{20... | collective-permute-start | bytes 442376 | tf_op jit(solution)/shard_map/ppermute | solution.py:458
  48.7 4.9 %shard_map.106 = (bf16[320,256]{1,0:T(8,128)(2,1)S(1)}, bf16[320,1536]{1,0:T(8,128)(2,1)S(1)}, bf16[320,576]{1,0:T(8,128)(2,1)S(1)}, bf16[64,1536]{1,0:T(8,128)(...) custom-call(s32[3]{0:T(128)S(1)} %pad_add_fusion.sc, ...), custom_call_target="tpu_custom_call" | custom-call | flops 964689920 | bytes 2359296 | tf_op jit(solution)/shard_map/pallas_call | solution.py:108
  53.6 1.4 %collective-permute-start.15 = (bf16[320,256]{1,0:T(8,128)(2,1)S(1)}, bf16[320,256]{1,0:T(8,128)(2,1)S(1)}, u32[]{:S(2)}, u32[]{:S(2)}) collective-permute-start(bf16[320,256]{1,0:T(8,128)(2,1)S(1)} %get-tuple-element.68.refs_0_), channel_id=1, source_target_pairs={{0,8},{4,12},{8,0},{12,4},{1,9},{5,13},{9,1},{13,5},{2,10},{6,14},... | collective-permute-start | bytes 491528 | tf_op jit(solution)/shard_map/ppermute | solution.py:318
  55.0 1.1 %collective-permute-start.16 = (bf16[320,256]{1,0:T(8,128)(2,1)S(1)}, bf16[320,256]{1,0:T(8,128)(2,1)S(1)}, u32[]{:S(2)}, u32[]{:S(2)}) collective-permute-start(bf16[320,256]{1,0:T(8,128)(2,1)S(1)} %get-tuple-element.68.refs_0_), channel_id=1, source_target_pairs={{0,4},{4,0},{8,12},{12,8},{1,5},{5,1},{9,13},{13,9},{2,6},{6,2},{1... | collective-permute-start | bytes 491528 | tf_op jit(solution)/shard_map/ppermute | solution.py:319
  56.1 1.6 %collective-permute-done.12.refs_9_ = bf16[192,384]{1,0:T(8,128)(2,1)S(1)} collective-permute-done((bf16[192,384]{1,0:T(8,128)(2,1)S(1)}, bf16[192,384]{1,0:T(8,128)(2,1)S(1)}, u32[]{:S(2)}, u32[]{:S(2)}) %collective-permute-start.12) | collective-permute-done | bytes 147488 | tf_op jit(solution)/shard_map/ppermute | solution.py:458
  57.7 3.3 %shard_map.107.refs_3_ = bf16[320,256]{1,0:T(8,128)(2,1)S(1)} custom-call(s32[3]{0:T(128)S(1)} %pad_add_fusion.sc, bf16[320,1536]{1,0:T(8,128)(2,1)S(1)} %get-tuple-element.57.refs_0_, bf16[320,576]{1,0:T(8,128)(2,1)S(1)} %get-tuple-element.58.refs_1_, bf16[64,1536]{1,0:T(8,128)(2,1)S(1)} %get-tuple-element.59.refs_2_, ...), custom_call_target="tpu_custom_call" | custom-call | flops 964689920 | bytes 2359296 | tf_op jit(solution)/shard_map/pallas_call | solution.py:108
  61.0 1.3 %collective-permute-start.13 = (bf16[320,256]{1,0:T(8,128)(2,1)S(1)}, bf16[320,256]{1,0:T(8,128)(2,1)S(1)}, u32[]{:S(2)}, u32[]{:S(2)}) collective-permute-start(bf16[320,256]{1,0:T(8,128)(2,1)S(1)} %shard_map.107.refs_3_), channel_id=1, source_target_pairs={{0,8},{4,12},{8,0},{12,4},{1,9},{5,13},{9,1},{13,5},{2,10},{6,14},... | collective-permute-start | bytes 491528 | tf_op jit(solution)/shard_map/ppermute | solution.py:318
  62.3 1.1 %collective-permute-start.14 = (bf16[320,256]{1,0:T(8,128)(2,1)S(1)}, bf16[320,256]{1,0:T(8,128)(2,1)S(1)}, u32[]{:S(2)}, u32[]{:S(2)}) collective-permute-start(bf16[320,256]{1,0:T(8,128)(2,1)S(1)} %shard_map.107.refs_3_), channel_id=1, source_target_pairs={{0,4},{4,0},{8,12},{12,8},{1,5},{5,1},{9,13},{13,9},{2,6},{6,2},{1... | collective-permute-start | bytes 491528 | tf_op jit(solution)/shard_map/ppermute | solution.py:319
  63.4 0.5 collective-permute-done.15.refs_2_
  64.3 3.9 %shard_map.108 = (f32[320,1792]{1,0:T(8,128)S(1)}, f32[8,128]{1,0:T(8,128)S(1)}) custom-call(s32[3]{0:T(128)S(1)} %pad_add_fusion.sc, bf16[320,256]{1,0:T(8,128)(2,1)S(1)} %get-tuple-element.68.refs_0_, bf16[320,256]{1,0:T(8,128)(2,1)S(1)} %collective-permute-done.16.refs_1_, bf16[320,256]{1,0:T(8,128)(2,1)S(1)} %collective-permute-done.15.refs_2_, ...), custom_call_target="tpu_custom_call" | custom-call | flops 1174405120 | bytes 3670016 | tf_op jit(solution)/shard_map/pallas_call | solution.py:108
  68.3 3.2 %collective-permute-done.13.refs_2_ = bf16[320,256]{1,0:T(8,128)(2,1)S(1)} collective-permute-done((bf16[320,256]{1,0:T(8,128)(2,1)S(1)}, bf16[320,256]{1,0:T(8,128)(2,1)S(1)}, u32[]{:S(2)}, u32[]{:S(2)}) %collective-permute-start.13) | collective-permute-done | bytes 163872 | tf_op jit(solution)/shard_map/ppermute | solution.py:318
  71.5 1.5 %collective-permute-start.17 = (bf16[320,256]{1,0:T(8,128)(2,1)S(1)}, bf16[320,256]{1,0:T(8,128)(2,1)S(1)}, u32[]{:S(2)}, u32[]{:S(2)}) collective-permute-start(bf16[320,256]{1,0:T(8,128)(2,1)S(1)} %collective-permute-done.13.refs_2_), channel_id=1, source_target_pairs={{0,4},{4,0},{8,12},{12,8},{1,5},{5,1},{9,13},{13,9},{2,6},{6,2},{1... | collective-permute-start | bytes 491528 | tf_op jit(solution)/shard_map/ppermute | solution.py:321
  72.9 2.0 %collective-permute-done.18.refs_0_ = bf16[320,256]{1,0:T(8,128)(2,1)S(1)} collective-permute-done((bf16[320,256]{1,0:T(8,128)(2,1)S(1)}, bf16[320,256]{1,0:T(8,128)(2,1)S(1)}, u32[]{:S(2)}, u32[]{:S(2)}) %collective-permute-start.18) | collective-permute-done | bytes 163872 | tf_op jit(solution)/shard_map/ppermute | solution.py:321
  74.9 3.4 %shard_map.109 = (f32[320,1792]{1,0:T(8,128)S(1)}, bf16[1,256,1792]{2,1,0:T(8,128)(2,1)S(1)}) custom-call(s32[3]{0:T(128)S(1)} %pad_add_fusion.sc, bf16[320,256]{1,0:T(8,128)(2,1)S(1)} %collective-permute-done.18.refs_0_, bf16[320,256]{1,0:T(8,128)(2,1)S(1)} %collective-permute-done.14.refs_1_, ...), custom_call_target="tpu_custom_call", output_to_operand_aliasing={{0}: (5, {})} | custom-call | flops 880803840 | bytes 2752512 | tf_op jit(solution)/shard_map/pallas_call | solution.py:108
  78.3 1.3 %shard_map.110 = (f32[160,1792]{1,0:T(8,128)S(1)}, bf16[160,1792]{1,0:T(8,128)(2,1)S(1)}) custom-call(s32[3]{0:T(128)S(1)} %pad_add_fusion.sc, bf16[320,256]{1,0:T(8,128)(2,1)S(1)} %collective-permute-done.17.refs_0_, bf16[1,256,1792]{2,1,0:T(8,128)(2,1)S(1)} %get-tuple-element.76.refs_1_, f32[320,1792]{1,0:T(8,128)S(1)} %get-tuple-element.77.refs_2_), custom_call_target="tpu_custom_call" | custom-call | flops 293601280 | bytes 917504 | tf_op jit(solution)/shard_map/pallas_call | solution.py:108
  79.7 1.9 %collective-permute-done.19 = bf16[160,1792]{1,0:T(8,128)(2,1)S(1)} collective-permute-done((bf16[160,1792]{1,0:T(8,128)(2,1)S(1)}, bf16[160,1792]{1,0:T(8,128)(2,1)S(1)}, u32[]{:S(2)}, u32[]{:S(2)}) %collective-permute-start.19) | collective-permute-done | bytes 573472 | tf_op jit(solution)/shard_map/ppermute | solution.py:536
  81.8 0.6 collective-permute-start.20
  82.4 8.3 %collective-permute-done.20 = bf16[80,1792]{1,0:T(8,128)(2,1)S(1)} collective-permute-done((bf16[80,1792]{1,0:T(8,128)(2,1)S(1)}, bf16[80,1792]{1,0:T(8,128)(2,1)S(1)}, u32[]{:S(2)}, u32[]{:S(2)}) %collective-permute-start.20) | collective-permute-done | bytes 286752 | tf_op jit(solution)/shard_map/ppermute | solution.py:541
  90.7 0.8 fusion
  (32 shorter events, 2.2 us)
Async XLA Ops:
  0.6 7.9 %copy-start.1 = (bf16[384,64]{0,1:T(8,128)(2,1)S(1)}, bf16[384,64]{0,1:T(8,128)(2,1)}, u32[]{:S(2)}) copy-start(bf16[384,64]{0,1:T(8,128)(2,1)} %param.13) | copy-start | bytes 147460
  0.6 7.9 %copy-start.4 = (bf16[384,3072]{1,0:T(8,128)(2,1)S(1)}, bf16[384,3072]{1,0:T(8,128)(2,1)}, u32[]{:S(2)}) copy-start(bf16[384,3072]{1,0:T(8,128)(2,1)} %refs_12_.1) | copy-start | bytes 7077892
  2.8 21.5 %collective-permute-start = (bf16[320,384]{1,0:T(8,128)(2,1)S(1)}, bf16[320,384]{1,0:T(8,128)(2,1)S(1)}, u32[]{:S(2)}, u32[]{:S(2)}) collective-permute-start(bf16[320,384]{1,0:T(8,128)(2,1)S(1)} %get-tuple-element.41), channel_id=1, source_target_pairs={{0,8},{4,12},{8,0},{12,4},{1,9},{5,13},{9,1},{13,5},{2,10},{6,14},... | collective-permute-start | bytes 737288 | tf_op jit(solution)/shard_map/ppermute | solution.py:438
  6.9 17.4 %collective-permute-start.1 = (bf16[320,384]{1,0:T(8,128)(2,1)S(1)}, bf16[320,384]{1,0:T(8,128)(2,1)S(1)}, u32[]{:S(2)}, u32[]{:S(2)}) collective-permute-start(bf16[320,384]{1,0:T(8,128)(2,1)S(1)} %get-tuple-element.42), channel_id=1, source_target_pairs={{0,12},{4,8},{8,4},{12,0},{1,13},{5,9},{9,5},{13,1},{2,14},{6,10},... | collective-permute-start | bytes 737288 | tf_op jit(solution)/shard_map/ppermute | solution.py:438
  8.2 40.5 %copy-start = (bf16[80,1536]{1,0:T(8,128)(2,1)S(1)}, bf16[80,1536]{1,0:T(8,128)(2,1)}, u32[]{:S(2)}) copy-start(bf16[80,1536]{1,0:T(8,128)(2,1)} %refs_0_.1) | copy-start | bytes 737284
  8.2 40.5 %copy-start.2 = (bf16[80,576]{1,0:T(8,128)(2,1)S(1)}, bf16[80,576]{1,0:T(8,128)(2,1)}, u32[]{:S(2)}) copy-start(bf16[80,576]{1,0:T(8,128)(2,1)} %refs_1_.1) | copy-start | bytes 276484
  8.2 40.5 %copy-start.3 = (s32[80]{0:T(128)S(1)}, s32[80]{0:T(128)}, u32[]{:S(2)}) copy-start(s32[80]{0:T(128)} %param.11) | copy-start | bytes 964
  8.2 16.5 %collective-permute-start.2 = (bf16[320,384]{1,0:T(8,128)(2,1)S(1)}, bf16[320,384]{1,0:T(8,128)(2,1)S(1)}, u32[]{:S(2)}, u32[]{:S(2)}) collective-permute-start(bf16[320,384]{1,0:T(8,128)(2,1)S(1)} %get-tuple-element.43), channel_id=1, source_target_pairs={{0,4},{4,0},{8,12},{12,8},{1,5},{5,1},{9,13},{13,9},{2,6},{6,2},{1... | collective-permute-start | bytes 737288 | tf_op jit(solution)/shard_map/ppermute | solution.py:438
  25.4 19.7 %collective-permute-start.5 = (bf16[3,128,384]{2,1,0:T(8,128)(2,1)S(1)}, bf16[3,128,384]{2,1,0:T(8,128)(2,1)S(1)}, u32[]{:S(2)}, u32[]{:S(2)}) collective-permute-start(bf16[3,128,384]{2,1,0:T(8,128)(2,1)S(1)} %get-tuple-element.49), channel_id=1, source_target_pairs={{0,2},{1,3},{2,0},{3,1},{4,6},{5,7},{6,4},{7,5},{8,10},{9,11},{10,... | collective-permute-start | bytes 884744 | tf_op jit(solution)/shard_map/ppermute | solution.py:451
  27.0 16.9 %collective-permute-start.6 = (bf16[192,384]{1,0:T(8,128)(2,1)S(1)}, bf16[192,384]{1,0:T(8,128)(2,1)S(1)}, u32[]{:S(2)}, u32[]{:S(2)}) collective-permute-start(bf16[192,384]{1,0:T(8,128)(2,1)S(1)} %get-tuple-element.53), channel_id=1, source_target_pairs={{0,8},{4,12},{8,0},{12,4},{1,9},{5,13},{9,1},{13,5},{2,10},{6,14},... | collective-permute-start | bytes 442376 | tf_op jit(solution)/shard_map/ppermute | solution.py:438
  33.5 10.4 %collective-permute-start.7 = (bf16[192,384]{1,0:T(8,128)(2,1)S(1)}, bf16[192,384]{1,0:T(8,128)(2,1)S(1)}, u32[]{:S(2)}, u32[]{:S(2)}) collective-permute-start(bf16[192,384]{1,0:T(8,128)(2,1)S(1)} %get-tuple-element.54), channel_id=1, source_target_pairs={{0,12},{4,8},{8,4},{12,0},{1,13},{5,9},{9,5},{13,1},{2,14},{6,10},... | collective-permute-start | bytes 442376 | tf_op jit(solution)/shard_map/ppermute | solution.py:438
  33.9 11.2 %collective-permute-start.8 = (bf16[192,384]{1,0:T(8,128)(2,1)S(1)}, bf16[192,384]{1,0:T(8,128)(2,1)S(1)}, u32[]{:S(2)}, u32[]{:S(2)}) collective-permute-start(bf16[192,384]{1,0:T(8,128)(2,1)S(1)} %get-tuple-element.55), channel_id=1, source_target_pairs={{0,4},{4,0},{8,12},{12,8},{1,5},{5,1},{9,13},{13,9},{2,6},{6,2},{1... | collective-permute-start | bytes 442376 | tf_op jit(solution)/shard_map/ppermute | solution.py:438
  34.1 14.6 %collective-permute-start.3 = (bf16[3,192,384]{2,1,0:T(8,128)(2,1)S(1)}, bf16[3,192,384]{2,1,0:T(8,128)(2,1)S(1)}, u32[]{:S(2)}, u32[]{:S(2)}) collective-permute-start(bf16[3,192,384]{2,1,0:T(8,128)(2,1)S(1)} %get-tuple-element.48), channel_id=1, source_target_pairs={{0,16},{16,0},{1,17},{17,1},{2,18},{18,2},{3,19},{19,3},{4,20},{20... | collective-permute-start | bytes 1327112 | tf_op jit(solution)/shard_map/ppermute | solution.py:450
  43.9 3.3 %collective-permute-start.4 = (bf16[3,128,384]{2,1,0:T(8,128)(2,1)S(1)}, bf16[3,128,384]{2,1,0:T(8,128)(2,1)S(1)}, u32[]{:S(2)}, u32[]{:S(2)}) collective-permute-start(bf16[3,128,384]{2,1,0:T(8,128)(2,1)S(1)} %get-tuple-element.49), channel_id=1, source_target_pairs={{0,1},{1,0},{2,3},{3,2},{4,5},{5,4},{6,7},{7,6},{8,9},{9,8},{10,11... | collective-permute-start | bytes 884744 | tf_op jit(solution)/shard_map/ppermute | solution.py:454
  45.1 3.6 %collective-permute-start.9 = (bf16[3,128,384]{2,1,0:T(8,128)(2,1)S(1)}, bf16[3,128,384]{2,1,0:T(8,128)(2,1)S(1)}, u32[]{:S(2)}, u32[]{:S(2)}) collective-permute-start(bf16[3,128,384]{2,1,0:T(8,128)(2,1)S(1)} %collective-permute-done.5.refs_9_), channel_id=1, source_target_pairs={{0,1},{1,0},{2,3},{3,2},{4,5},{5,4},{6,7},{7,6},{8,9},{9,8},{10,11... | collective-permute-start | bytes 884744 | tf_op jit(solution)/shard_map/ppermute | solution.py:456
  45.1 10.9 %collective-permute-start.10 = (bf16[192,384]{1,0:T(8,128)(2,1)S(1)}, bf16[192,384]{1,0:T(8,128)(2,1)S(1)}, u32[]{:S(2)}, u32[]{:S(2)}) collective-permute-start(bf16[192,384]{1,0:T(8,128)(2,1)S(1)} %collective-permute-done.6.refs_4_), channel_id=1, source_target_pairs={{0,16},{16,0},{1,17},{17,1},{2,18},{18,2},{3,19},{19,3},{4,20},{20... | collective-permute-start | bytes 442376 | tf_op jit(solution)/shard_map/ppermute | solution.py:458
  46.7 9.4 %collective-permute-start.11 = (bf16[192,384]{1,0:T(8,128)(2,1)S(1)}, bf16[192,384]{1,0:T(8,128)(2,1)S(1)}, u32[]{:S(2)}, u32[]{:S(2)}) collective-permute-start(bf16[192,384]{1,0:T(8,128)(2,1)S(1)} %collective-permute-done.7.refs_5_), channel_id=1, source_target_pairs={{0,16},{16,0},{1,17},{17,1},{2,18},{18,2},{3,19},{19,3},{4,20},{20... | collective-permute-start | bytes 442376 | tf_op jit(solution)/shard_map/ppermute | solution.py:458
  47.2 10.6 %collective-permute-start.12 = (bf16[192,384]{1,0:T(8,128)(2,1)S(1)}, bf16[192,384]{1,0:T(8,128)(2,1)S(1)}, u32[]{:S(2)}, u32[]{:S(2)}) collective-permute-start(bf16[192,384]{1,0:T(8,128)(2,1)S(1)} %collective-permute-done.8.refs_6_), channel_id=1, source_target_pairs={{0,16},{16,0},{1,17},{17,1},{2,18},{18,2},{3,19},{19,3},{4,20},{20... | collective-permute-start | bytes 442376 | tf_op jit(solution)/shard_map/ppermute | solution.py:458
  53.6 10.3 %collective-permute-start.15 = (bf16[320,256]{1,0:T(8,128)(2,1)S(1)}, bf16[320,256]{1,0:T(8,128)(2,1)S(1)}, u32[]{:S(2)}, u32[]{:S(2)}) collective-permute-start(bf16[320,256]{1,0:T(8,128)(2,1)S(1)} %get-tuple-element.68.refs_0_), channel_id=1, source_target_pairs={{0,8},{4,12},{8,0},{12,4},{1,9},{5,13},{9,1},{13,5},{2,10},{6,14},... | collective-permute-start | bytes 491528 | tf_op jit(solution)/shard_map/ppermute | solution.py:318
  55.0 8.9 %collective-permute-start.16 = (bf16[320,256]{1,0:T(8,128)(2,1)S(1)}, bf16[320,256]{1,0:T(8,128)(2,1)S(1)}, u32[]{:S(2)}, u32[]{:S(2)}) collective-permute-start(bf16[320,256]{1,0:T(8,128)(2,1)S(1)} %get-tuple-element.68.refs_0_), channel_id=1, source_target_pairs={{0,4},{4,0},{8,12},{12,8},{1,5},{5,1},{9,13},{13,9},{2,6},{6,2},{1... | collective-permute-start | bytes 491528 | tf_op jit(solution)/shard_map/ppermute | solution.py:319
  61.0 10.5 %collective-permute-start.13 = (bf16[320,256]{1,0:T(8,128)(2,1)S(1)}, bf16[320,256]{1,0:T(8,128)(2,1)S(1)}, u32[]{:S(2)}, u32[]{:S(2)}) collective-permute-start(bf16[320,256]{1,0:T(8,128)(2,1)S(1)} %shard_map.107.refs_3_), channel_id=1, source_target_pairs={{0,8},{4,12},{8,0},{12,4},{1,9},{5,13},{9,1},{13,5},{2,10},{6,14},... | collective-permute-start | bytes 491528 | tf_op jit(solution)/shard_map/ppermute | solution.py:318
  62.3 9.2 %collective-permute-start.14 = (bf16[320,256]{1,0:T(8,128)(2,1)S(1)}, bf16[320,256]{1,0:T(8,128)(2,1)S(1)}, u32[]{:S(2)}, u32[]{:S(2)}) collective-permute-start(bf16[320,256]{1,0:T(8,128)(2,1)S(1)} %shard_map.107.refs_3_), channel_id=1, source_target_pairs={{0,4},{4,0},{8,12},{12,8},{1,5},{5,1},{9,13},{13,9},{2,6},{6,2},{1... | collective-permute-start | bytes 491528 | tf_op jit(solution)/shard_map/ppermute | solution.py:319
  63.9 11.0 %collective-permute-start.18 = (bf16[320,256]{1,0:T(8,128)(2,1)S(1)}, bf16[320,256]{1,0:T(8,128)(2,1)S(1)}, u32[]{:S(2)}, u32[]{:S(2)}) collective-permute-start(bf16[320,256]{1,0:T(8,128)(2,1)S(1)} %collective-permute-done.15.refs_2_), channel_id=1, source_target_pairs={{0,4},{4,0},{8,12},{12,8},{1,5},{5,1},{9,13},{13,9},{2,6},{6,2},{1... | collective-permute-start | bytes 491528 | tf_op jit(solution)/shard_map/ppermute | solution.py:321
  71.5 6.8 %collective-permute-start.17 = (bf16[320,256]{1,0:T(8,128)(2,1)S(1)}, bf16[320,256]{1,0:T(8,128)(2,1)S(1)}, u32[]{:S(2)}, u32[]{:S(2)}) collective-permute-start(bf16[320,256]{1,0:T(8,128)(2,1)S(1)} %collective-permute-done.13.refs_2_), channel_id=1, source_target_pairs={{0,4},{4,0},{8,12},{12,8},{1,5},{5,1},{9,13},{13,9},{2,6},{6,2},{1... | collective-permute-start | bytes 491528 | tf_op jit(solution)/shard_map/ppermute | solution.py:321
  79.6 2.0 %collective-permute-start.19 = (bf16[160,1792]{1,0:T(8,128)(2,1)S(1)}, bf16[160,1792]{1,0:T(8,128)(2,1)S(1)}, u32[]{:S(2)}, u32[]{:S(2)}) collective-permute-start(bf16[160,1792]{1,0:T(8,128)(2,1)S(1)} %get-tuple-element.79), channel_id=1, source_target_pairs={{0,1},{1,0},{2,3},{3,2},{4,5},{5,4},{6,7},{7,6},{8,9},{9,8},{10,11... | collective-permute-start | bytes 1720328 | tf_op jit(solution)/shard_map/ppermute | solution.py:536
  81.8 8.9 %collective-permute-start.20 = (bf16[80,1792]{1,0:T(8,128)(2,1)S(1)}, bf16[80,1792]{1,0:T(8,128)(2,1)S(1)}, u32[]{:S(2)}, u32[]{:S(2)}) collective-permute-start(bf16[80,1792]{1,0:T(8,128)(2,1)S(1)} %fusion.1), channel_id=1, source_target_pairs={{0,2},{1,3},{2,0},{3,1},{4,6},{5,7},{6,4},{7,5},{8,10},{9,11},{10,... | collective-permute-start | bytes 860168 | tf_op jit(solution)/shard_map/ppermute | solution.py:541

commit v7 on v6

--- a/solution.py
+++ b/solution.py
@@ -139,7 +139,7 @@
 
 def pack_body(n, kq, vq, aq, wide, kvr, sc, x_ref, kv_ref, at_ref, pos_ref, w_ref, *rest):
     count = CHUNKS * (n - 1)
-    outs, (xs, kvs, ats, ps, turn, turned, sems) = rest[:count], rest[count:]
+    parts, outs, (xs, kvs, ats, ps, turn, turned, sems) = rest[0], rest[1 : 1 + count], rest[1 + count :]
     s, g, h = sc[0], sc[1], sc[2]
     tok = x_ref.shape[0]
     rope = kv_ref.shape[1] - kvr
@@ -156,7 +156,7 @@
         for k, bits in enumerate(partners(n)):
             chunk = (s ^ bits) * CHUNKS + c
             columns = pl.ds(pl.multiple_of(chunk * wide, 128), wide)
-            large.append((w_ref.at[mine, columns], outs[c * (n - 1) + k].at[:half]))
+            large.append((w_ref.at[mine, columns], outs[c * (n - 1) + k]))
     copies = fetch(small + large, sems)
     turn[...] = jnp.zeros_like(turn)
     for copy in copies[: len(small)]:
@@ -170,30 +170,28 @@
     ropes = turned[pl.ds(pl.multiple_of(h * aq, 16), aq), :].astype(jnp.bfloat16)
     third = (tok + aq) // 3
     tail = jnp.concatenate([keys, ropes], axis=0)
-    for first in outs[: n - 1]:
-        first[half : half + tok, :] = xs[...]
-        first[half + tok : half + tok + aq, :] = ats[...]
-        for i in range(3):
-            first[half + tok + aq :, i * vq : (i + 1) * vq] = tail[i * third : (i + 1) * third]
+    parts[:tok, :] = xs[...]
+    parts[tok : tok + aq, :] = ats[...]
+    for i in range(3):
+        parts[tok + aq :, i * vq : (i + 1) * vq] = tail[i * third : (i + 1) * third]
     for copy in copies[len(small) :]:
         copy.wait()
 
 
-def split_body(n, half, sc, *refs):
-    outs = refs[n - 1 :]
-    for k in range(n - 1):
-        outs[0][k] = refs[k][:half]
-        if len(outs) > 1:
-            outs[1][k] = refs[k][half:]
-
-
-def unpack(n, nh, kq, vq, aq, sc, own, units, stacks, outs, turn):
+def join_body(sc, *refs):
+    outs = [ref for ref in refs if len(ref.shape) == 3]
+    count = (len(refs) - len(outs)) // len(outs)
+    for i, out in enumerate(outs):
+        for k in range(count):
+            out[k] = refs[i * count + k][...]
+
+
+def unpack(n, nh, kq, vq, aq, sc, own, packs, stacks, outs, turn):
     (x_ref, kv_ref, at_ref, pos_ref), (xo, kvo, ao, bias) = own, outs
     s, h = sc[0], sc[2]
     tok, depth = x_ref.shape[0], at_ref.shape[1]
     kvr = vq * nh
     rope = kv_ref.shape[1] - kvr
-    half = units[0].shape[0] - stacks[0].shape[1]
     third = (tok + aq) // 3
     tokens = bias.shape[0]
     row = pl.multiple_of(s * tok, 16)
@@ -207,7 +205,7 @@
         rows = pl.ds(pl.multiple_of(src * tok, 16), tok)
         for j in range(nh):
             hh = h ^ j
-            got = stacks[j - 1].at[k] if j else units[k].at[half:]
+            got = stacks[j - 1].at[k] if j else packs[k]
             xo[rows, pl.ds(pl.multiple_of(hh * kq, 128), kq)] = got[:tok, :]
             arow = pl.ds(pl.multiple_of(hh * aq, 16), aq)
             ao[arow, pl.ds(pl.multiple_of(src * depth, 128), depth)] = got[tok : tok + aq, :]
@@ -293,19 +291,25 @@
         out[:, j * vdim : (j + 1) * vdim] = ho.astype(jnp.bfloat16)
 
 
+def pick_body(sc, *refs):
+    far, outs, sems = refs[:4], refs[4:8], refs[8]
+    for copy in fetch(own_weights(sc, 0, far, outs), sems):
+        copy.wait()
+
+
 def attend_first(n, nh, kq, vq, aq, nope, scale, sc, *refs):
     own, units, y_ref, stacks = refs[:4], refs[4 : 3 + n], refs[3 + n], refs[4 + n : 3 + n + nh]
-    refs = refs[3 + n + nh :]
-    far, out, shared, later = refs[:4], refs[4], refs[5:9], refs[9:13]
-    turn, raw, weights, sems = refs[13], refs[14], refs[15:19], refs[19]
-    copies = fetch(own_weights(sc, 0, far, weights) + own_weights(sc, CHUNKS - 1, far, later), sems)
+    packs, refs = refs[3 + n + nh : 2 + 2 * n + nh], refs[2 + 2 * n + nh :]
+    weights, far, out, shared, later = refs[:4], refs[4:8], refs[8], refs[9:13], refs[13:17]
+    turn, raw, sems = refs[17:]
+    copies = fetch(own_weights(sc, CHUNKS - 1, far, later), sems)
 
     def before():
-        unpack(n, nh, kq, vq, aq, sc, own, units, stacks, shared, turn)
+        unpack(n, nh, kq, vq, aq, sc, own, packs, stacks, shared, turn)
 
     ys = [y_ref.at[k] for k in range(n - 1)]
-    attend(n, nope, scale, sc, shared, units, ys, weights, out, raw, before, copies[:4])
-    for copy in copies[4:]:
+    attend(n, nope, scale, sc, shared, units, ys, weights, out, raw, before)
+    for copy in copies:
         copy.wait()
 
 
@@ -346,37 +350,36 @@
 
 def early_body(sc, *refs):
     count = len(EARLY)
-    slots, (w_ref, acc, token, lhs, w, sems) = refs[:count], refs[count:]
-    copies = fetch(slabs(sc, w_ref, EARLY, slice(None), w), sems)
+    slots, (w_ref, acc, token, middle, late, lhs, w, sems) = refs[:count], refs[count:]
+    copies = fetch(
+        slabs(sc, w_ref, EARLY, slice(None), w)
+        + slabs(sc, w_ref, MIDDLE, slice(None), middle)
+        + slabs(sc, w_ref, LATE, slice(None), late),
+        sems,
+    )
     place(slots, lhs)
     token[...] = jnp.zeros_like(token)
-    for copy in copies:
+    for copy in copies[:count]:
         copy.wait()
 
     def put(band, value):
         acc[:, band] = value
 
     columns_dot(lhs, w, 0, acc.shape[1], put)
+    for copy in copies[count:]:
+        copy.wait()
 
 
 def middle_body(sc, *refs):
     count = len(MIDDLE)
-    slots, (w_ref, before, token, acc, last, lhs, w, sems) = refs[:count], refs[count:]
+    slots, (w, before, token, acc, lhs) = refs[:count], refs[count:]
     del before, token
-    total = acc.shape[1]
-    copies = fetch(
-        slabs(sc, w_ref, MIDDLE, slice(None), w) + slabs(sc, w_ref, LATE, slice(None), last), sems
-    )
     place(slots, lhs)
-    for copy in copies[:count]:
-        copy.wait()
 
     def add(band, value):
         acc[:, band] += value
 
-    columns_dot(lhs, w, 0, total, add)
-    for copy in copies[count:]:
-        copy.wait()
+    columns_dot(lhs, w, 0, acc.shape[1], add)
 
 
 def last_body(nh, tok, sc, *refs):
@@ -418,9 +421,9 @@
     def like(*shape, dtype=bf):
         return jax.ShapeDtypeStruct(shape, dtype)
 
-    units = call(
+    parts, *units = call(
         functools.partial(pack_body, n, kq, vq, aq, wide, kvr),
-        tuple([like(half + extra, wide)] * (n - 1) + [like(half, wide)] * (n - 1) * (CHUNKS - 1)),
+        (like(extra, wide), *[like(half, wide)] * (n - 1) * CHUNKS),
         [sc, x, kv, at, pos2, wq],
         hbm=range(1, 6),
         scratch=[
@@ -437,19 +440,32 @@
     def exchange(parts):
         return [lax.ppermute(p, "seq", flipped(n, bits)) for p, bits in zip(parts, partners(n))]
 
-    def split(got, *sizes):
-        outs = tuple(like(n - 1, size, wide) for size in sizes)
-        return call(functools.partial(split_body, n, half), outs, [sc] + got, moved=4 * 3 * got[0].size)
+    def join(*groups):
+        outs = tuple(like(n - 1, *group[0].shape) for group in groups)
+        args = [a for group in groups for a in group]
+        return call(join_body, outs, [sc] + args, moved=4 * sum(a.size for a in args))
 
     merged = (wq.astype(f32) + jnp.dot(down, up, preferred_element_type=f32)).astype(bf)
+    _, one, two, three = gather_line(parts)
+    packs = [two, three, one]
     moved = [exchange(units[: n - 1])]
-    *moved[0], merged = lax.optimization_barrier((*moved[0], merged))
-    later = lax.optimization_barrier((*units[n - 1 :], moved[0][0]))
-    moved.append(exchange(later[: n - 1]))
-    share, stack = split(moved[0], half, extra)
+    held = lax.optimization_barrier((*moved[0], *packs, merged))
+    moved[0], packs, merged = list(held[: n - 1]), list(held[n - 1 : -1]), held[-1]
+    moved.append(exchange(units[n - 1 :]))
+    share, stack = join(moved[0], packs)
     passed = [[lax.ppermute(share, "groups", flipped(2, 1))]]
     across = lax.ppermute(stack, "head", flipped(nh, 2))
-    across, *moved[1] = lax.optimization_barrier((across, *moved[1]))
+    shapes = ((rank, wide), (rows, wide), (per, nope, kvr), (per, kvr, vdim))
+    picked = call(
+        pick_body,
+        tuple(like(*shape) for shape in shapes),
+        [sc, up, wq, ku, vu],
+        hbm=range(1, 5),
+        scratch=[pltpu.SemaphoreType.DMA((4,))],
+        moved=4 * sum(math.prod(shape) for shape in shapes),
+    )
+    across, *rest = lax.optimization_barrier((across, *moved[1], *picked))
+    moved[1], picked = rest[: n - 1], rest[n - 1 :]
     stacks = [
         lax.ppermute(stack, "head", flipped(nh, 1)),
         across,
@@ -458,7 +474,6 @@
     passed.append([lax.ppermute(p, "groups", flipped(2, 1)) for p in moved[1]])
 
     scale = 1.0 / math.sqrt(nope + rope)
-    shapes = ((rank, wide), (rows, wide), (per, nope, kvr), (per, kvr, vdim))
     raw = pltpu.VMEM((n * rows, wide), bf)
     cost = dict(
         flops=2 * tokens * per * (depth * wide // per + 2 * nope * kvr + 2 * tokens * kvr),
@@ -474,11 +489,10 @@
             like(tokens, tokens, dtype=f32),
             *(like(*shape) for shape in shapes),
         ),
-        [sc, x, kv, at, pos2] + moved[0] + passed[0] + stacks + [up, wq, ku, vu],
-        hbm=range(4 + n + nh, 8 + n + nh),
+        [sc, x, kv, at, pos2] + moved[0] + passed[0] + stacks + packs + picked + [up, wq, ku, vu],
+        hbm=range(7 + 2 * n + nh, 11 + 2 * n + nh),
         scratch=[pltpu.VMEM((128, 128), f32), raw]
-        + [pltpu.VMEM(shape, bf) for shape in shapes]
-        + [pltpu.SemaphoreType.DMA((8,))],
+        + [pltpu.SemaphoreType.DMA((4,))],
         **cost,
     )
     slots = [gather_line(ho)]
@@ -507,29 +521,33 @@
         return [slots[c][bits] for bits, c in pieces]
 
     slots.append([ho])
-    acc, token = call(
+    acc, token, w_middle, w_late = call(
         early_body,
-        (like(tokens, total, dtype=f32), like(8, 128, dtype=f32)),
+        (
+            like(tokens, total, dtype=f32),
+            like(8, 128, dtype=f32),
+            like(len(MIDDLE), width, total),
+            like(len(LATE), width, total),
+        ),
         [sc] + pick(EARLY) + [w4],
         hbm=(1 + len(EARLY),),
-        scratch=room(EARLY) + [pltpu.SemaphoreType.DMA((len(EARLY),))],
+        scratch=room(EARLY) + [pltpu.SemaphoreType.DMA((len(EARLY + MIDDLE + LATE),))],
         **work(EARLY),
     )
     *slots[1], token = gather_line(ho, token)
     late = pick(LATE)
-    acc, w_last = call(
+    acc = call(
         middle_body,
-        (like(tokens, total, dtype=f32), like(len(LATE), width, total)),
-        [sc] + pick(MIDDLE) + [w4, acc, token],
-        hbm=(1 + len(MIDDLE),),
-        scratch=room(MIDDLE) + [pltpu.SemaphoreType.DMA((len(MIDDLE) + len(LATE),))],
+        like(tokens, total, dtype=f32),
+        [sc] + pick(MIDDLE) + [w_middle, acc, token],
+        scratch=room(MIDDLE)[:1],
         alias={2 + len(MIDDLE): 0},
         **work(MIDDLE),
     )
     keep, send = call(
         functools.partial(last_body, nh, tok),
         (like(nh // 2 * tok, total, dtype=f32), like(nh // 2 * tok, total)),
-        [sc] + late + [w_last, acc],
+        [sc] + late + [w_late, acc],
         scratch=[room(LATE)[0], pltpu.VMEM((tokens, total), f32)],
         **work(LATE),
     )

time: 91.7 us -> 88.8 us (0.968)
  waiting for transfers between devices: 40.2 us -> 34.3 us
  starting transfers between devices: 26.9 us -> 30.5 us
    ppermute x6, waiting for transfers between devices: 22.6 us -> 13.4 us  [exchange(): lax.ppermute(p, 'seq', flipped(n, bits))]
    ppermute x2 -> x3, starting transfers between devices: 2.65 us -> 7.69 us  [gather_line(): two = lax.ppermute(x, 'seq', flipped(4, 2))]
    ppermute x6, starting transfers between devices: 12.8 us -> 7.88 us  [exchange(): lax.ppermute(p, 'seq', flipped(n, bits))]
    ppermute x2 -> x3, starting transfers between devices: 2.16 us -> 5.43 us  [gather_line(): one = lax.ppermute(x, 'seq', flipped(4, 1))]
    ppermute x2 -> x3, waiting for transfers between devices: 1.99 us -> 5.18 us  [gather_line(): return [x, one, two, lax.ppermute(two, 'seq', flipped(4, 1))] + held]
    ppermute x2 -> x3, waiting for transfers between devices: 0.01 us -> 1.7 us  [gather_line(): one = lax.ppermute(x, 'seq', flipped(4, 1))]
    ppermute x2 -> x3, waiting for transfers between devices: 3.7 us -> 2.76 us  [gather_line(): two = lax.ppermute(x, 'seq', flipped(4, 2))]
    pallas_call x7 -> x8, Pallas kernels: 19.4 us -> 18.8 us  [call(): pl.pallas_call(body, out_shape=outs, grid_spec=pltpu.PrefetchScalarGridSp...]
  transfers between devices with their start and end apart: 21 -> 24, of which waited for: 10 -> 15; matrix products, arithmetic and copies ran while one was open for 3% -> 4% of each run, Pallas kernels for 17% -> 17%
where the time goes in v7:
time: 88.8 us; the launch traced here: 88.6 us
  waiting for transfers between devices  34.3 us (39%)
  starting transfers between devices  30.5 us (34%)
  Pallas kernels  18.8 us (21%)
  matrix products  3.19 us (4%)
  other arithmetic  0.94 us (1%)
    pallas_call x8, Pallas kernels, call(): pl.pallas_call(body, out_shape=outs, grid_spec=pltpu.PrefetchScalarGridSp...  18.8 us
    ppermute x6, waiting for transfers between devices, exchange(): lax.ppermute(p, 'seq', flipped(n, bits))  13.4 us
    ppermute x1, waiting for transfers between devices, by_heads(): out = out + lax.ppermute(away, 'head', flipped(nh, 2)).astype(f32)  8.34 us
    ppermute x6, starting transfers between devices, exchange(): lax.ppermute(p, 'seq', flipped(n, bits))  7.88 us
    ppermute x3, starting transfers between devices, gather_line(): two = lax.ppermute(x, 'seq', flipped(4, 2))  7.69 us
    ppermute x3, starting transfers between devices, gather_line(): one = lax.ppermute(x, 'seq', flipped(4, 1))  5.43 us
    ppermute x3, waiting for transfers between devices, gather_line(): return [x, one, two, lax.ppermute(two, 'seq', flipped(4, 1))] + held  5.18 us
    ppermute x3, starting transfers between devices, by_heads(): passed.append([lax.ppermute(p, 'groups', flipped(2, 1)) for p in moved[1]])  3.55 us
  transfers between devices with their start and end apart: 24, of which 15 were waited for; matrix products, arithmetic and copies ran while one was open for 4% of the time, Pallas kernels for 17%

profile of v7, /device:TPU:0, one launch (start us, length us, event | category | flops | bytes accessed | tf_op | source)
XLA Modules:
  0.0 88.6 jit_solution(1064342228012406831)
XLA Ops:
  0.7 2.0 %shard_map.104 = (bf16[128,384]{1,0:T(8,128)(2,1)S(1)}, bf16[192,384]{1,0:T(8,128)(2,1)S(1)}, bf16[192,384]{1,0:T(8,128)(2,1)S(1)}, bf16[192,384]{1,0:T(8,128)(2...) custom-call(s32[3]{0:T(128)S(1)} %pad_add_fusion.sc, ...), custom_call_target="tpu_custom_call" | custom-call | bytes 2359296 | tf_op jit(solution)/shard_map/pallas_call | solution.py:108
  2.8 4.1 %collective-permute-start.3 = (bf16[128,384]{1,0:T(8,128)(2,1)S(1)}, bf16[128,384]{1,0:T(8,128)(2,1)S(1)}, u32[]{:S(2)}, u32[]{:S(2)}) collective-permute-start(bf16[128,384]{1,0:T(8,128)(2,1)S(1)} %get-tuple-element.55), channel_id=1, source_target_pairs={{0,8},{4,12},{8,0},{12,4},{1,9},{5,13},{9,1},{13,5},{2,10},{6,14},... | collective-permute-start | bytes 294920 | tf_op jit(solution)/shard_map/ppermute | solution.py:322
  6.9 1.6 %collective-permute-start.4 = (bf16[128,384]{1,0:T(8,128)(2,1)S(1)}, bf16[128,384]{1,0:T(8,128)(2,1)S(1)}, u32[]{:S(2)}, u32[]{:S(2)}) collective-permute-start(bf16[128,384]{1,0:T(8,128)(2,1)S(1)} %get-tuple-element.55), channel_id=1, source_target_pairs={{0,4},{4,0},{8,12},{12,8},{1,5},{5,1},{9,13},{13,9},{2,6},{6,2},{1... | collective-permute-start | bytes 294920 | tf_op jit(solution)/shard_map/ppermute | solution.py:323
  8.8 2.5 %collective-permute-start.1 = (bf16[192,384]{1,0:T(8,128)(2,1)S(1)}, bf16[192,384]{1,0:T(8,128)(2,1)S(1)}, u32[]{:S(2)}, u32[]{:S(2)}) collective-permute-start(bf16[192,384]{1,0:T(8,128)(2,1)S(1)} %get-tuple-element.53), channel_id=1, source_target_pairs={{0,12},{4,8},{8,4},{12,0},{1,13},{5,9},{9,5},{13,1},{2,14},{6,10},... | collective-permute-start | bytes 442376 | tf_op jit(solution)/shard_map/ppermute | solution.py:441
  12.5 2.1 %collective-permute-start.5 = (bf16[128,384]{1,0:T(8,128)(2,1)S(1)}, bf16[128,384]{1,0:T(8,128)(2,1)S(1)}, u32[]{:S(2)}, u32[]{:S(2)}) collective-permute-start(bf16[128,384]{1,0:T(8,128)(2,1)S(1)} %collective-permute-done.3.refs_3_.refs_11_), channel_id=1, source_target_pairs={{0,4},{4,0},{8,12},{12,8},{1,5},{5,1},{9,13},{13,9},{2,6},{6,2},{1... | collective-permute-start | bytes 294920 | tf_op jit(solution)/shard_map/ppermute | solution.py:325
  14.5 3.2 %add_convert_fusion = bf16[384,3072]{1,0:T(8,128)(2,1)} fusion(bf16[384,3072]{1,0:T(8,128)(2,1)S(1)} %copy-done.4, bf16[384,64]{0,1:T(8,128)(2,1)S(1)} %copy-done.1, bf16[64,3072]{1,0:T(8,128)(2,1)} %refs_18_.1), kind=kOutput, calls=%fused_computation | convolution fusion | flops 154533888 | bytes 5160960 | tf_op jit(solution)/shard_map/dot_general | solution.py:448
  17.7 4.2 %collective-permute-done.refs_0_.refs_4_ = bf16[192,384]{1,0:T(8,128)(2,1)S(1)} collective-permute-done((bf16[192,384]{1,0:T(8,128)(2,1)S(1)}, bf16[192,384]{1,0:T(8,128)(2,1)S(1)}, u32[]{:S(2)}, u32[]{:S(2)}) %collective-permute-start) | collective-permute-done | bytes 147488 | tf_op jit(solution)/shard_map/ppermute | solution.py:441
  22.7 1.1 %collective-permute-done.5.refs_4_.refs_12_ = bf16[128,384]{1,0:T(8,128)(2,1)S(1)} collective-permute-done((bf16[128,384]{1,0:T(8,128)(2,1)S(1)}, bf16[128,384]{1,0:T(8,128)(2,1)S(1)}, u32[]{:S(2)}, u32[]{:S(2)}) %collective-permute-start.5) | collective-permute-done | bytes 98336 | tf_op jit(solution)/shard_map/ppermute | solution.py:325
  24.4 1.6 %collective-permute-start.8 = (bf16[3,128,384]{2,1,0:T(8,128)(2,1)S(1)}, bf16[3,128,384]{2,1,0:T(8,128)(2,1)S(1)}, u32[]{:S(2)}, u32[]{:S(2)}) collective-permute-start(bf16[3,128,384]{2,1,0:T(8,128)(2,1)S(1)} %get-tuple-element.66), channel_id=1, source_target_pairs={{0,2},{1,3},{2,0},{3,1},{4,6},{5,7},{6,4},{7,5},{8,10},{9,11},{10,... | collective-permute-start | bytes 884744 | tf_op jit(solution)/shard_map/ppermute | solution.py:457
  26.0 2.9 %collective-permute-start.10 = (bf16[192,384]{1,0:T(8,128)(2,1)S(1)}, bf16[192,384]{1,0:T(8,128)(2,1)S(1)}, u32[]{:S(2)}, u32[]{:S(2)}) collective-permute-start(bf16[192,384]{1,0:T(8,128)(2,1)S(1)} %get-tuple-element.68), channel_id=1, source_target_pairs={{0,12},{4,8},{8,4},{12,0},{1,13},{5,9},{9,5},{13,1},{2,14},{6,10},... | collective-permute-start | bytes 442376 | tf_op jit(solution)/shard_map/ppermute | solution.py:441
  29.0 0.9 %collective-permute-start.11 = (bf16[192,384]{1,0:T(8,128)(2,1)S(1)}, bf16[192,384]{1,0:T(8,128)(2,1)S(1)}, u32[]{:S(2)}, u32[]{:S(2)}) collective-permute-start(bf16[192,384]{1,0:T(8,128)(2,1)S(1)} %get-tuple-element.69), channel_id=1, source_target_pairs={{0,4},{4,0},{8,12},{12,8},{1,5},{5,1},{9,13},{13,9},{2,6},{6,2},{1... | collective-permute-start | bytes 442376 | tf_op jit(solution)/shard_map/ppermute | solution.py:441
  30.4 1.5 %collective-permute-start.6 = (bf16[3,192,384]{2,1,0:T(8,128)(2,1)S(1)}, bf16[3,192,384]{2,1,0:T(8,128)(2,1)S(1)}, u32[]{:S(2)}, u32[]{:S(2)}) collective-permute-start(bf16[3,192,384]{2,1,0:T(8,128)(2,1)S(1)} %get-tuple-element.65), channel_id=1, source_target_pairs={{0,16},{16,0},{1,17},{17,1},{2,18},{18,2},{3,19},{19,3},{4,20},{20... | collective-permute-start | bytes 1327112 | tf_op jit(solution)/shard_map/ppermute | solution.py:456
  32.0 2.7 %collective-permute-done.10.refs_5_ = bf16[192,384]{1,0:T(8,128)(2,1)S(1)} collective-permute-done((bf16[192,384]{1,0:T(8,128)(2,1)S(1)}, bf16[192,384]{1,0:T(8,128)(2,1)S(1)}, u32[]{:S(2)}, u32[]{:S(2)}) %collective-permute-start.10) | collective-permute-done | bytes 147488 | tf_op jit(solution)/shard_map/ppermute | solution.py:441
  34.6 1.7 %shard_map.106 = (bf16[64,384]{1,0:T(8,128)(2,1)S(1)}, bf16[384,384]{1,0:T(8,128)(2,1)S(1)}, bf16[2,128,512]{2,1,0:T(8,128)(2,1)S(1)}, bf16[2,512,128]{2,1,0:T(8,128)(2,1)S(1)}) custom-call(s32[3]{0:T(128)S(1)} %pad_add_fusion.sc, bf16[64,3072]{1,0:T(8,128)(2,1)} %refs_18_.1, bf16[384,3072]{1,0:T(8,128)(2,1)} %refs_19_.1, bf16[16,128,512]{2,1,0:T(8,128)(2,1)} %refs_20_.1, ...), custom_call_target="tpu_custom_call" | custom-call | bytes 1736704 | tf_op jit(solution)/shard_map/pallas_call | solution.py:108
  36.4 5.7 %collective-permute-done.9.refs_4_ = bf16[192,384]{1,0:T(8,128)(2,1)S(1)} collective-permute-done((bf16[192,384]{1,0:T(8,128)(2,1)S(1)}, bf16[192,384]{1,0:T(8,128)(2,1)S(1)}, u32[]{:S(2)}, u32[]{:S(2)}) %collective-permute-start.9) | collective-permute-done | bytes 147488 | tf_op jit(solution)/shard_map/ppermute | solution.py:441
  42.1 1.5 %collective-permute-start.13 = (bf16[192,384]{1,0:T(8,128)(2,1)S(1)}, bf16[192,384]{1,0:T(8,128)(2,1)S(1)}, u32[]{:S(2)}, u32[]{:S(2)}) collective-permute-start(bf16[192,384]{1,0:T(8,128)(2,1)S(1)} %collective-permute-done.9.refs_4_), channel_id=1, source_target_pairs={{0,16},{16,0},{1,17},{17,1},{2,18},{18,2},{3,19},{19,3},{4,20},{20... | collective-permute-start | bytes 442376 | tf_op jit(solution)/shard_map/ppermute | solution.py:474
  44.1 1.5 %collective-permute-start.15 = (bf16[192,384]{1,0:T(8,128)(2,1)S(1)}, bf16[192,384]{1,0:T(8,128)(2,1)S(1)}, u32[]{:S(2)}, u32[]{:S(2)}) collective-permute-start(bf16[192,384]{1,0:T(8,128)(2,1)S(1)} %collective-permute-done.11.refs_6_), channel_id=1, source_target_pairs={{0,16},{16,0},{1,17},{17,1},{2,18},{18,2},{3,19},{19,3},{4,20},{20... | collective-permute-start | bytes 442376 | tf_op jit(solution)/shard_map/ppermute | solution.py:474
  45.7 4.3 %shard_map.107 = (bf16[320,256]{1,0:T(8,128)(2,1)S(1)}, bf16[320,1536]{1,0:T(8,128)(2,1)S(1)}, bf16[320,576]{1,0:T(8,128)(2,1)S(1)}, bf16[64,1536]{1,0:T(8,128)(...) custom-call(s32[3]{0:T(128)S(1)} %pad_add_fusion.sc, ...), custom_call_target="tpu_custom_call" | custom-call | flops 964689920 | bytes 2359296 | tf_op jit(solution)/shard_map/pallas_call | solution.py:108
  49.9 2.0 %collective-permute-start.18 = (bf16[320,256]{1,0:T(8,128)(2,1)S(1)}, bf16[320,256]{1,0:T(8,128)(2,1)S(1)}, u32[]{:S(2)}, u32[]{:S(2)}) collective-permute-start(bf16[320,256]{1,0:T(8,128)(2,1)S(1)} %get-tuple-element.90.refs_0_), channel_id=1, source_target_pairs={{0,8},{4,12},{8,0},{12,4},{1,9},{5,13},{9,1},{13,5},{2,10},{6,14},... | collective-permute-start | bytes 491528 | tf_op jit(solution)/shard_map/ppermute | solution.py:322
  51.9 1.7 %collective-permute-start.19 = (bf16[320,256]{1,0:T(8,128)(2,1)S(1)}, bf16[320,256]{1,0:T(8,128)(2,1)S(1)}, u32[]{:S(2)}, u32[]{:S(2)}) collective-permute-start(bf16[320,256]{1,0:T(8,128)(2,1)S(1)} %get-tuple-element.90.refs_0_), channel_id=1, source_target_pairs={{0,4},{4,0},{8,12},{12,8},{1,5},{5,1},{9,13},{13,9},{2,6},{6,2},{1... | collective-permute-start | bytes 491528 | tf_op jit(solution)/shard_map/ppermute | solution.py:323
  53.7 1.0 %collective-permute-done.15.refs_9_ = bf16[192,384]{1,0:T(8,128)(2,1)S(1)} collective-permute-done((bf16[192,384]{1,0:T(8,128)(2,1)S(1)}, bf16[192,384]{1,0:T(8,128)(2,1)S(1)}, u32[]{:S(2)}, u32[]{:S(2)}) %collective-permute-start.15) | collective-permute-done | bytes 147488 | tf_op jit(solution)/shard_map/ppermute | solution.py:474
  54.7 3.3 %shard_map.108.refs_3_ = bf16[320,256]{1,0:T(8,128)(2,1)S(1)} custom-call(s32[3]{0:T(128)S(1)} %pad_add_fusion.sc, bf16[320,1536]{1,0:T(8,128)(2,1)S(1)} %get-tuple-element.79.refs_0_, bf16[320,576]{1,0:T(8,128)(2,1)S(1)} %get-tuple-element.80.refs_1_, bf16[64,1536]{1,0:T(8,128)(2,1)S(1)} %get-tuple-element.81.refs_2_, ...), custom_call_target="tpu_custom_call" | custom-call | flops 964689920 | bytes 2359296 | tf_op jit(solution)/shard_map/pallas_call | solution.py:108
  58.0 1.6 %collective-permute-start.16 = (bf16[320,256]{1,0:T(8,128)(2,1)S(1)}, bf16[320,256]{1,0:T(8,128)(2,1)S(1)}, u32[]{:S(2)}, u32[]{:S(2)}) collective-permute-start(bf16[320,256]{1,0:T(8,128)(2,1)S(1)} %shard_map.108.refs_3_), channel_id=1, source_target_pairs={{0,8},{4,12},{8,0},{12,4},{1,9},{5,13},{9,1},{13,5},{2,10},{6,14},... | collective-permute-start | bytes 491528 | tf_op jit(solution)/shard_map/ppermute | solution.py:322
  59.5 2.1 %collective-permute-start.17 = (bf16[320,256]{1,0:T(8,128)(2,1)S(1)}, bf16[320,256]{1,0:T(8,128)(2,1)S(1)}, u32[]{:S(2)}, u32[]{:S(2)}) collective-permute-start(bf16[320,256]{1,0:T(8,128)(2,1)S(1)} %shard_map.108.refs_3_), channel_id=1, source_target_pairs={{0,4},{4,0},{8,12},{12,8},{1,5},{5,1},{9,13},{13,9},{2,6},{6,2},{1... | collective-permute-start | bytes 491528 | tf_op jit(solution)/shard_map/ppermute | solution.py:323
  61.8 4.0 %shard_map.109 = (f32[320,1792]{1,0:T(8,128)S(1)}, f32[8,128]{1,0:T(8,128)S(1)}, bf16[3,256,1792]{2,1,0:T(8,128)(2,1)S(1)}, bf16[1,256,1792]{2,1,0:T(8,128)(2,1)S(1)}) custom-call(s32[3]{0:T(128)S(1)} %pad_add_fusion.sc, bf16[320,256]{1,0:T(8,128)(2,1)S(1)} %get-tuple-element.90.refs_0_, bf16[320,256]{1,0:T(8,128)(2,1)S(1)} %collective-permute-done.19.refs_1_, ...), custom_call_target="tpu_custom_call" | custom-call | flops 1174405120 | bytes 3670016 | tf_op jit(solution)/shard_map/pallas_call | solution.py:108
  65.7 2.6 %collective-permute-done.16.refs_2_ = bf16[320,256]{1,0:T(8,128)(2,1)S(1)} collective-permute-done((bf16[320,256]{1,0:T(8,128)(2,1)S(1)}, bf16[320,256]{1,0:T(8,128)(2,1)S(1)}, u32[]{:S(2)}, u32[]{:S(2)}) %collective-permute-start.16) | collective-permute-done | bytes 163872 | tf_op jit(solution)/shard_map/ppermute | solution.py:322
  68.4 1.3 %collective-permute-done.17.refs_1_ = bf16[320,256]{1,0:T(8,128)(2,1)S(1)} collective-permute-done((bf16[320,256]{1,0:T(8,128)(2,1)S(1)}, bf16[320,256]{1,0:T(8,128)(2,1)S(1)}, u32[]{:S(2)}, u32[]{:S(2)}) %collective-permute-start.17) | collective-permute-done | bytes 163872 | tf_op jit(solution)/shard_map/ppermute | solution.py:323
  69.7 3.5 %collective-permute-done.21.refs_0_ = bf16[320,256]{1,0:T(8,128)(2,1)S(1)} collective-permute-done((bf16[320,256]{1,0:T(8,128)(2,1)S(1)}, bf16[320,256]{1,0:T(8,128)(2,1)S(1)}, u32[]{:S(2)}, u32[]{:S(2)}) %collective-permute-start.21) | collective-permute-done | bytes 163872 | tf_op jit(solution)/shard_map/ppermute | solution.py:325
  73.2 1.6 %shard_map.110.refs_2_ = f32[320,1792]{1,0:T(8,128)S(1)} custom-call(s32[3]{0:T(128)S(1)} %pad_add_fusion.sc, bf16[320,256]{1,0:T(8,128)(2,1)S(1)} %collective-permute-done.21.refs_0_, bf16[320,256]{1,0:T(8,128)(2,1)S(1)} %collective-permute-done.17.refs_1_, bf16[320,256]{1,0:T(8,128)(2,1)S(1)} %collective-permute-done.16.refs_2_, ...), custom_call_target="tpu_custom_call", output_to_operand_aliasing={{}: (5, {})} | custom-call | flops 880803840 | bytes 2752512 | tf_op jit(solution)/shard_map/pallas_call | solution.py:108
  75.4 1.3 %shard_map.111 = (f32[160,1792]{1,0:T(8,128)S(1)}, bf16[160,1792]{1,0:T(8,128)(2,1)S(1)}) custom-call(s32[3]{0:T(128)S(1)} %pad_add_fusion.sc, bf16[320,256]{1,0:T(8,128)(2,1)S(1)} %collective-permute-done.20.refs_0_, bf16[1,256,1792]{2,1,0:T(8,128)(2,1)S(1)} %get-tuple-element.95.refs_1_, f32[320,1792]{1,0:T(8,128)S(1)} %shard_map.110.refs_2_), custom_call_target="tpu_custom_call" | custom-call | flops 293601280 | bytes 917504 | tf_op jit(solution)/shard_map/pallas_call | solution.py:108
  76.8 1.9 %collective-permute-done.22 = bf16[160,1792]{1,0:T(8,128)(2,1)S(1)} collective-permute-done((bf16[160,1792]{1,0:T(8,128)(2,1)S(1)}, bf16[160,1792]{1,0:T(8,128)(2,1)S(1)}, u32[]{:S(2)}, u32[]{:S(2)}) %collective-permute-start.22) | collective-permute-done | bytes 573472 | tf_op jit(solution)/shard_map/ppermute | solution.py:554
  79.5 8.3 %collective-permute-done.23 = bf16[80,1792]{1,0:T(8,128)(2,1)S(1)} collective-permute-done((bf16[80,1792]{1,0:T(8,128)(2,1)S(1)}, bf16[80,1792]{1,0:T(8,128)(2,1)S(1)}, u32[]{:S(2)}, u32[]{:S(2)}) %collective-permute-start.23) | collective-permute-done | bytes 286752 | tf_op jit(solution)/shard_map/ppermute | solution.py:559
  (39 shorter events, 6.4 us)
Async XLA Ops:
  0.6 13.9 %copy-start.1 = (bf16[384,64]{0,1:T(8,128)(2,1)S(1)}, bf16[384,64]{0,1:T(8,128)(2,1)}, u32[]{:S(2)}) copy-start(bf16[384,64]{0,1:T(8,128)(2,1)} %param.13) | copy-start | bytes 147460
  0.6 13.9 %copy-start.4 = (bf16[384,3072]{1,0:T(8,128)(2,1)S(1)}, bf16[384,3072]{1,0:T(8,128)(2,1)}, u32[]{:S(2)}) copy-start(bf16[384,3072]{1,0:T(8,128)(2,1)} %refs_19_.1) | copy-start | bytes 7077892
  2.8 9.3 %collective-permute-start.3 = (bf16[128,384]{1,0:T(8,128)(2,1)S(1)}, bf16[128,384]{1,0:T(8,128)(2,1)S(1)}, u32[]{:S(2)}, u32[]{:S(2)}) collective-permute-start(bf16[128,384]{1,0:T(8,128)(2,1)S(1)} %get-tuple-element.55), channel_id=1, source_target_pairs={{0,8},{4,12},{8,0},{12,4},{1,9},{5,13},{9,1},{13,5},{2,10},{6,14},... | collective-permute-start | bytes 294920 | tf_op jit(solution)/shard_map/ppermute | solution.py:322
  6.9 5.6 %collective-permute-start.4 = (bf16[128,384]{1,0:T(8,128)(2,1)S(1)}, bf16[128,384]{1,0:T(8,128)(2,1)S(1)}, u32[]{:S(2)}, u32[]{:S(2)}) collective-permute-start(bf16[128,384]{1,0:T(8,128)(2,1)S(1)} %get-tuple-element.55), channel_id=1, source_target_pairs={{0,4},{4,0},{8,12},{12,8},{1,5},{5,1},{9,13},{13,9},{2,6},{6,2},{1... | collective-permute-start | bytes 294920 | tf_op jit(solution)/shard_map/ppermute | solution.py:323
  8.5 13.5 %collective-permute-start = (bf16[192,384]{1,0:T(8,128)(2,1)S(1)}, bf16[192,384]{1,0:T(8,128)(2,1)S(1)}, u32[]{:S(2)}, u32[]{:S(2)}) collective-permute-start(bf16[192,384]{1,0:T(8,128)(2,1)S(1)} %get-tuple-element.52), channel_id=1, source_target_pairs={{0,8},{4,12},{8,0},{12,4},{1,9},{5,13},{9,1},{13,5},{2,10},{6,14},... | collective-permute-start | bytes 442376 | tf_op jit(solution)/shard_map/ppermute | solution.py:441
  8.8 13.1 %collective-permute-start.1 = (bf16[192,384]{1,0:T(8,128)(2,1)S(1)}, bf16[192,384]{1,0:T(8,128)(2,1)S(1)}, u32[]{:S(2)}, u32[]{:S(2)}) collective-permute-start(bf16[192,384]{1,0:T(8,128)(2,1)S(1)} %get-tuple-element.53), channel_id=1, source_target_pairs={{0,12},{4,8},{8,4},{12,0},{1,13},{5,9},{9,5},{13,1},{2,14},{6,10},... | collective-permute-start | bytes 442376 | tf_op jit(solution)/shard_map/ppermute | solution.py:441
  11.3 11.4 %collective-permute-start.2 = (bf16[192,384]{1,0:T(8,128)(2,1)S(1)}, bf16[192,384]{1,0:T(8,128)(2,1)S(1)}, u32[]{:S(2)}, u32[]{:S(2)}) collective-permute-start(bf16[192,384]{1,0:T(8,128)(2,1)S(1)} %get-tuple-element.54), channel_id=1, source_target_pairs={{0,4},{4,0},{8,12},{12,8},{1,5},{5,1},{9,13},{13,9},{2,6},{6,2},{1... | collective-permute-start | bytes 442376 | tf_op jit(solution)/shard_map/ppermute | solution.py:441
  12.5 11.3 %collective-permute-start.5 = (bf16[128,384]{1,0:T(8,128)(2,1)S(1)}, bf16[128,384]{1,0:T(8,128)(2,1)S(1)}, u32[]{:S(2)}, u32[]{:S(2)}) collective-permute-start(bf16[128,384]{1,0:T(8,128)(2,1)S(1)} %collective-permute-done.3.refs_3_.refs_11_), channel_id=1, source_target_pairs={{0,4},{4,0},{8,12},{12,8},{1,5},{5,1},{9,13},{13,9},{2,6},{6,2},{1... | collective-permute-start | bytes 294920 | tf_op jit(solution)/shard_map/ppermute | solution.py:325
  24.4 17.7 %collective-permute-start.8 = (bf16[3,128,384]{2,1,0:T(8,128)(2,1)S(1)}, bf16[3,128,384]{2,1,0:T(8,128)(2,1)S(1)}, u32[]{:S(2)}, u32[]{:S(2)}) collective-permute-start(bf16[3,128,384]{2,1,0:T(8,128)(2,1)S(1)} %get-tuple-element.66), channel_id=1, source_target_pairs={{0,2},{1,3},{2,0},{3,1},{4,6},{5,7},{6,4},{7,5},{8,10},{9,11},{10,... | collective-permute-start | bytes 884744 | tf_op jit(solution)/shard_map/ppermute | solution.py:457
  26.0 8.6 %collective-permute-start.10 = (bf16[192,384]{1,0:T(8,128)(2,1)S(1)}, bf16[192,384]{1,0:T(8,128)(2,1)S(1)}, u32[]{:S(2)}, u32[]{:S(2)}) collective-permute-start(bf16[192,384]{1,0:T(8,128)(2,1)S(1)} %get-tuple-element.68), channel_id=1, source_target_pairs={{0,12},{4,8},{8,4},{12,0},{1,13},{5,9},{9,5},{13,1},{2,14},{6,10},... | collective-permute-start | bytes 442376 | tf_op jit(solution)/shard_map/ppermute | solution.py:441
  29.0 7.4 %collective-permute-start.11 = (bf16[192,384]{1,0:T(8,128)(2,1)S(1)}, bf16[192,384]{1,0:T(8,128)(2,1)S(1)}, u32[]{:S(2)}, u32[]{:S(2)}) collective-permute-start(bf16[192,384]{1,0:T(8,128)(2,1)S(1)} %get-tuple-element.69), channel_id=1, source_target_pairs={{0,4},{4,0},{8,12},{12,8},{1,5},{5,1},{9,13},{13,9},{2,6},{6,2},{1... | collective-permute-start | bytes 442376 | tf_op jit(solution)/shard_map/ppermute | solution.py:441
  29.9 12.2 %collective-permute-start.9 = (bf16[192,384]{1,0:T(8,128)(2,1)S(1)}, bf16[192,384]{1,0:T(8,128)(2,1)S(1)}, u32[]{:S(2)}, u32[]{:S(2)}) collective-permute-start(bf16[192,384]{1,0:T(8,128)(2,1)S(1)} %get-tuple-element.67), channel_id=1, source_target_pairs={{0,8},{4,12},{8,0},{12,4},{1,9},{5,13},{9,1},{13,5},{2,10},{6,14},... | collective-permute-start | bytes 442376 | tf_op jit(solution)/shard_map/ppermute | solution.py:441
  30.4 15.2 %copy-start = (bf16[80,1536]{1,0:T(8,128)(2,1)S(1)}, bf16[80,1536]{1,0:T(8,128)(2,1)}, u32[]{:S(2)}) copy-start(bf16[80,1536]{1,0:T(8,128)(2,1)} %refs_0_.3) | copy-start | bytes 737284
  30.4 15.2 %copy-start.2 = (bf16[80,576]{1,0:T(8,128)(2,1)S(1)}, bf16[80,576]{1,0:T(8,128)(2,1)}, u32[]{:S(2)}) copy-start(bf16[80,576]{1,0:T(8,128)(2,1)} %refs_1_.3) | copy-start | bytes 276484
  30.4 15.2 %copy-start.3 = (s32[80]{0:T(128)S(1)}, s32[80]{0:T(128)}, u32[]{:S(2)}) copy-start(s32[80]{0:T(128)} %param.11) | copy-start | bytes 964
  30.4 15.2 %collective-permute-start.6 = (bf16[3,192,384]{2,1,0:T(8,128)(2,1)S(1)}, bf16[3,192,384]{2,1,0:T(8,128)(2,1)S(1)}, u32[]{:S(2)}, u32[]{:S(2)}) collective-permute-start(bf16[3,192,384]{2,1,0:T(8,128)(2,1)S(1)} %get-tuple-element.65), channel_id=1, source_target_pairs={{0,16},{16,0},{1,17},{17,1},{2,18},{18,2},{3,19},{19,3},{4,20},{20... | collective-permute-start | bytes 1327112 | tf_op jit(solution)/shard_map/ppermute | solution.py:456
  34.6 9.5 %collective-permute-start.7 = (bf16[3,128,384]{2,1,0:T(8,128)(2,1)S(1)}, bf16[3,128,384]{2,1,0:T(8,128)(2,1)S(1)}, u32[]{:S(2)}, u32[]{:S(2)}) collective-permute-start(bf16[3,128,384]{2,1,0:T(8,128)(2,1)S(1)} %get-tuple-element.66), channel_id=1, source_target_pairs={{0,1},{1,0},{2,3},{3,2},{4,5},{5,4},{6,7},{7,6},{8,9},{9,8},{10,11... | collective-permute-start | bytes 884744 | tf_op jit(solution)/shard_map/ppermute | solution.py:470
  42.1 3.6 %collective-permute-start.12 = (bf16[3,128,384]{2,1,0:T(8,128)(2,1)S(1)}, bf16[3,128,384]{2,1,0:T(8,128)(2,1)S(1)}, u32[]{:S(2)}, u32[]{:S(2)}) collective-permute-start(bf16[3,128,384]{2,1,0:T(8,128)(2,1)S(1)} %collective-permute-done.8.refs_9_), channel_id=1, source_target_pairs={{0,1},{1,0},{2,3},{3,2},{4,5},{5,4},{6,7},{7,6},{8,9},{9,8},{10,11... | collective-permute-start | bytes 884744 | tf_op jit(solution)/shard_map/ppermute | solution.py:472
  42.1 11.6 %collective-permute-start.13 = (bf16[192,384]{1,0:T(8,128)(2,1)S(1)}, bf16[192,384]{1,0:T(8,128)(2,1)S(1)}, u32[]{:S(2)}, u32[]{:S(2)}) collective-permute-start(bf16[192,384]{1,0:T(8,128)(2,1)S(1)} %collective-permute-done.9.refs_4_), channel_id=1, source_target_pairs={{0,16},{16,0},{1,17},{17,1},{2,18},{18,2},{3,19},{19,3},{4,20},{20... | collective-permute-start | bytes 442376 | tf_op jit(solution)/shard_map/ppermute | solution.py:474
  43.6 10.0 %collective-permute-start.14 = (bf16[192,384]{1,0:T(8,128)(2,1)S(1)}, bf16[192,384]{1,0:T(8,128)(2,1)S(1)}, u32[]{:S(2)}, u32[]{:S(2)}) collective-permute-start(bf16[192,384]{1,0:T(8,128)(2,1)S(1)} %collective-permute-done.10.refs_5_), channel_id=1, source_target_pairs={{0,16},{16,0},{1,17},{17,1},{2,18},{18,2},{3,19},{19,3},{4,20},{20... | collective-permute-start | bytes 442376 | tf_op jit(solution)/shard_map/ppermute | solution.py:474
  44.1 10.5 %collective-permute-start.15 = (bf16[192,384]{1,0:T(8,128)(2,1)S(1)}, bf16[192,384]{1,0:T(8,128)(2,1)S(1)}, u32[]{:S(2)}, u32[]{:S(2)}) collective-permute-start(bf16[192,384]{1,0:T(8,128)(2,1)S(1)} %collective-permute-done.11.refs_6_), channel_id=1, source_target_pairs={{0,16},{16,0},{1,17},{17,1},{2,18},{18,2},{3,19},{19,3},{4,20},{20... | collective-permute-start | bytes 442376 | tf_op jit(solution)/shard_map/ppermute | solution.py:474
  49.9 11.7 %collective-permute-start.18 = (bf16[320,256]{1,0:T(8,128)(2,1)S(1)}, bf16[320,256]{1,0:T(8,128)(2,1)S(1)}, u32[]{:S(2)}, u32[]{:S(2)}) collective-permute-start(bf16[320,256]{1,0:T(8,128)(2,1)S(1)} %get-tuple-element.90.refs_0_), channel_id=1, source_target_pairs={{0,8},{4,12},{8,0},{12,4},{1,9},{5,13},{9,1},{13,5},{2,10},{6,14},... | collective-permute-start | bytes 491528 | tf_op jit(solution)/shard_map/ppermute | solution.py:322
  51.9 9.8 %collective-permute-start.19 = (bf16[320,256]{1,0:T(8,128)(2,1)S(1)}, bf16[320,256]{1,0:T(8,128)(2,1)S(1)}, u32[]{:S(2)}, u32[]{:S(2)}) collective-permute-start(bf16[320,256]{1,0:T(8,128)(2,1)S(1)} %get-tuple-element.90.refs_0_), channel_id=1, source_target_pairs={{0,4},{4,0},{8,12},{12,8},{1,5},{5,1},{9,13},{13,9},{2,6},{6,2},{1... | collective-permute-start | bytes 491528 | tf_op jit(solution)/shard_map/ppermute | solution.py:323
  58.0 10.4 %collective-permute-start.16 = (bf16[320,256]{1,0:T(8,128)(2,1)S(1)}, bf16[320,256]{1,0:T(8,128)(2,1)S(1)}, u32[]{:S(2)}, u32[]{:S(2)}) collective-permute-start(bf16[320,256]{1,0:T(8,128)(2,1)S(1)} %shard_map.108.refs_3_), channel_id=1, source_target_pairs={{0,8},{4,12},{8,0},{12,4},{1,9},{5,13},{9,1},{13,5},{2,10},{6,14},... | collective-permute-start | bytes 491528 | tf_op jit(solution)/shard_map/ppermute | solution.py:322
  59.5 10.2 %collective-permute-start.17 = (bf16[320,256]{1,0:T(8,128)(2,1)S(1)}, bf16[320,256]{1,0:T(8,128)(2,1)S(1)}, u32[]{:S(2)}, u32[]{:S(2)}) collective-permute-start(bf16[320,256]{1,0:T(8,128)(2,1)S(1)} %shard_map.108.refs_3_), channel_id=1, source_target_pairs={{0,4},{4,0},{8,12},{12,8},{1,5},{5,1},{9,13},{13,9},{2,6},{6,2},{1... | collective-permute-start | bytes 491528 | tf_op jit(solution)/shard_map/ppermute | solution.py:323
  61.7 11.5 %collective-permute-start.21 = (bf16[320,256]{1,0:T(8,128)(2,1)S(1)}, bf16[320,256]{1,0:T(8,128)(2,1)S(1)}, u32[]{:S(2)}, u32[]{:S(2)}) collective-permute-start(bf16[320,256]{1,0:T(8,128)(2,1)S(1)} %collective-permute-done.18.refs_2_), channel_id=1, source_target_pairs={{0,4},{4,0},{8,12},{12,8},{1,5},{5,1},{9,13},{13,9},{2,6},{6,2},{1... | collective-permute-start | bytes 491528 | tf_op jit(solution)/shard_map/ppermute | solution.py:325
  69.7 5.7 %collective-permute-start.20 = (bf16[320,256]{1,0:T(8,128)(2,1)S(1)}, bf16[320,256]{1,0:T(8,128)(2,1)S(1)}, u32[]{:S(2)}, u32[]{:S(2)}) collective-permute-start(bf16[320,256]{1,0:T(8,128)(2,1)S(1)} %collective-permute-done.16.refs_2_), channel_id=1, source_target_pairs={{0,4},{4,0},{8,12},{12,8},{1,5},{5,1},{9,13},{13,9},{2,6},{6,2},{1... | collective-permute-start | bytes 491528 | tf_op jit(solution)/shard_map/ppermute | solution.py:325
  76.7 2.0 %collective-permute-start.22 = (bf16[160,1792]{1,0:T(8,128)(2,1)S(1)}, bf16[160,1792]{1,0:T(8,128)(2,1)S(1)}, u32[]{:S(2)}, u32[]{:S(2)}) collective-permute-start(bf16[160,1792]{1,0:T(8,128)(2,1)S(1)} %get-tuple-element.101), channel_id=1, source_target_pairs={{0,1},{1,0},{2,3},{3,2},{4,5},{5,4},{6,7},{7,6},{8,9},{9,8},{10,11... | collective-permute-start | bytes 1720328 | tf_op jit(solution)/shard_map/ppermute | solution.py:554
  78.9 8.9 %collective-permute-start.23 = (bf16[80,1792]{1,0:T(8,128)(2,1)S(1)}, bf16[80,1792]{1,0:T(8,128)(2,1)S(1)}, u32[]{:S(2)}, u32[]{:S(2)}) collective-permute-start(bf16[80,1792]{1,0:T(8,128)(2,1)S(1)} %fusion.1), channel_id=1, source_target_pairs={{0,2},{1,3},{2,0},{3,1},{4,6},{5,7},{6,4},{7,5},{8,10},{9,11},{10,... | collective-permute-start | bytes 860168 | tf_op jit(solution)/shard_map/ppermute | solution.py:559

commit v8 on v7

--- a/solution.py
+++ b/solution.py
@@ -98,7 +98,7 @@
 
 
 def partners(n):
-    return [b for b in range(2, n)] + [1]
+    return [1, 3, 2]
 
 
 def call(body, outs, args, hbm=(), scratch=(), alias=None, flops=0, moved=0):
@@ -383,19 +383,18 @@
 
 
 def last_body(nh, tok, sc, *refs):
-    slots, (w, acc, keep, send, lhs, tot) = refs[: len(LATE)], refs[len(LATE) :]
-    place(slots, lhs)
-
-    def put(band, value):
-        tot[:, band] = acc[:, band] + value
-
-    columns_dot(lhs, w, 0, keep.shape[1], put)
+    slots, (w, acc, keep, send) = refs[: len(LATE)], refs[len(LATE) :]
     core = sc[2] % 2
-    for i in range(nh // 2):
-        mine = pl.ds(pl.multiple_of((2 * i + core) * tok, 16), tok)
-        theirs = pl.ds(pl.multiple_of((2 * i + 1 - core) * tok, 16), tok)
-        keep[i * tok : (i + 1) * tok, :] = tot[mine, :]
-        send[i * tok : (i + 1) * tok, :] = tot[theirs, :].astype(jnp.bfloat16)
+    total = acc.shape[1]
+    for which, out in ((core, keep), (1 - core, send)):
+        rows = [pl.ds(pl.multiple_of((2 * i + which) * tok, 16), tok) for i in range(nh // 2)]
+        lhs = jnp.concatenate([slots[0][row, :] for row in rows], axis=0)
+        for at in range(0, total, TILE):
+            band = slice(at, min(at + TILE, total))
+            more = jnp.dot(lhs, w[0, :, band], preferred_element_type=jnp.float32)
+            for i, row in enumerate(rows):
+                part = acc[row, band] + more[i * tok : (i + 1) * tok]
+                out[i * tok : (i + 1) * tok, band] = part.astype(out.dtype)
 
 
 def by_heads(x, kv, pos, wq, down, up, ku, vu, wo):
@@ -447,7 +446,8 @@
 
     merged = (wq.astype(f32) + jnp.dot(down, up, preferred_element_type=f32)).astype(bf)
     _, one, two, three = gather_line(parts)
-    packs = [two, three, one]
+    by_bits = {1: one, 2: two, 3: three}
+    packs = [by_bits[b] for b in partners(n)]
     moved = [exchange(units[: n - 1])]
     held = lax.optimization_barrier((*moved[0], *packs, merged))
     moved[0], packs, merged = list(held[: n - 1]), list(held[n - 1 : -1]), held[-1]
@@ -548,7 +548,6 @@
         functools.partial(last_body, nh, tok),
         (like(nh // 2 * tok, total, dtype=f32), like(nh // 2 * tok, total)),
         [sc] + late + [w_late, acc],
-        scratch=[room(LATE)[0], pltpu.VMEM((tokens, total), f32)],
         **work(LATE),
     )
     got = lax.ppermute(send, "head", flipped(nh, 1))

time: 88.8 us -> 87.2 us (0.982)
  starting transfers between devices: 30.5 us -> 26 us
  waiting for transfers between devices: 34.3 us -> 37.5 us
    ppermute x3, starting transfers between devices: 7.69 us -> 4.24 us  [gather_line(): two = lax.ppermute(x, 'seq', flipped(4, 2))]
    ppermute x3, waiting for transfers between devices: 1.01 us -> 2.79 us  [by_heads(): passed.append([lax.ppermute(p, 'groups', flipped(2, 1)) for p in moved[1]])]
    ppermute x3, waiting for transfers between devices: 2.76 us -> 4.14 us  [gather_line(): two = lax.ppermute(x, 'seq', flipped(4, 2))]
    ppermute x3, waiting for transfers between devices: 5.18 us -> 4.11 us  [gather_line(): return [x, one, two, lax.ppermute(two, 'seq', flipped(4, 1))] + held]
  transfers between devices with their start and end apart: 24 -> 24, of which waited for: 15 -> 14; matrix products, arithmetic and copies ran while one was open for 4% -> 4% of each run, Pallas kernels for 17% -> 17%
where the time goes in v8:
time: 87.2 us; the launch traced here: 87 us
  waiting for transfers between devices  37.5 us (43%)
  starting transfers between devices  26 us (30%)
  Pallas kernels  18.5 us (21%)
  matrix products  3.19 us (4%)
  other arithmetic  0.94 us (1%)
    pallas_call x8, Pallas kernels, call(): pl.pallas_call(body, out_shape=outs, grid_spec=pltpu.PrefetchScalarGridSp...  18.5 us
    ppermute x6, waiting for transfers between devices, exchange(): lax.ppermute(p, 'seq', flipped(n, bits))  14.2 us
    ppermute x1, waiting for transfers between devices, by_heads(): out = out + lax.ppermute(away, 'head', flipped(nh, 2)).astype(f32)  8.34 us
    ppermute x6, starting transfers between devices, exchange(): lax.ppermute(p, 'seq', flipped(n, bits))  7.88 us
    ppermute x3, starting transfers between devices, gather_line(): one = lax.ppermute(x, 'seq', flipped(4, 1))  5.1 us
    ppermute x3, starting transfers between devices, gather_line(): two = lax.ppermute(x, 'seq', flipped(4, 2))  4.24 us
    ppermute x3, waiting for transfers between devices, gather_line(): two = lax.ppermute(x, 'seq', flipped(4, 2))  4.14 us
    ppermute x3, waiting for transfers between devices, gather_line(): return [x, one, two, lax.ppermute(two, 'seq', flipped(4, 1))] + held  4.11 us
  transfers between devices with their start and end apart: 24, of which 14 were waited for; matrix products, arithmetic and copies ran while one was open for 4% of the time, Pallas kernels for 17%

profile of v8, /device:TPU:0, one launch (start us, length us, event | category | flops | bytes accessed | tf_op | source)
XLA Modules:
  0.0 87.0 jit_solution(4649758208536395657)
XLA Ops:
  0.7 2.0 %shard_map.104 = (bf16[128,384]{1,0:T(8,128)(2,1)S(1)}, bf16[192,384]{1,0:T(8,128)(2,1)S(1)}, bf16[192,384]{1,0:T(8,128)(2,1)S(1)}, bf16[192,384]{1,0:T(8,128)(2...) custom-call(s32[3]{0:T(128)S(1)} %pad_add_fusion.sc, ...), custom_call_target="tpu_custom_call" | custom-call | bytes 2359296 | tf_op jit(solution)/shard_map/pallas_call | solution.py:108
  2.8 4.1 %collective-permute-start.3 = (bf16[128,384]{1,0:T(8,128)(2,1)S(1)}, bf16[128,384]{1,0:T(8,128)(2,1)S(1)}, u32[]{:S(2)}, u32[]{:S(2)}) collective-permute-start(bf16[128,384]{1,0:T(8,128)(2,1)S(1)} %get-tuple-element.55), channel_id=1, source_target_pairs={{0,8},{4,12},{8,0},{12,4},{1,9},{5,13},{9,1},{13,5},{2,10},{6,14},... | collective-permute-start | bytes 294920 | tf_op jit(solution)/shard_map/ppermute | solution.py:322
  6.9 1.6 %collective-permute-start.4 = (bf16[128,384]{1,0:T(8,128)(2,1)S(1)}, bf16[128,384]{1,0:T(8,128)(2,1)S(1)}, u32[]{:S(2)}, u32[]{:S(2)}) collective-permute-start(bf16[128,384]{1,0:T(8,128)(2,1)S(1)} %get-tuple-element.55), channel_id=1, source_target_pairs={{0,4},{4,0},{8,12},{12,8},{1,5},{5,1},{9,13},{13,9},{2,6},{6,2},{1... | collective-permute-start | bytes 294920 | tf_op jit(solution)/shard_map/ppermute | solution.py:323
  8.9 1.3 %collective-permute-start.1 = (bf16[192,384]{1,0:T(8,128)(2,1)S(1)}, bf16[192,384]{1,0:T(8,128)(2,1)S(1)}, u32[]{:S(2)}, u32[]{:S(2)}) collective-permute-start(bf16[192,384]{1,0:T(8,128)(2,1)S(1)} %get-tuple-element.53), channel_id=1, source_target_pairs={{0,12},{4,8},{8,4},{12,0},{1,13},{5,9},{9,5},{13,1},{2,14},{6,10},... | collective-permute-start | bytes 442376 | tf_op jit(solution)/shard_map/ppermute | solution.py:440
  10.3 1.7 %collective-permute-start.2 = (bf16[192,384]{1,0:T(8,128)(2,1)S(1)}, bf16[192,384]{1,0:T(8,128)(2,1)S(1)}, u32[]{:S(2)}, u32[]{:S(2)}) collective-permute-start(bf16[192,384]{1,0:T(8,128)(2,1)S(1)} %get-tuple-element.54), channel_id=1, source_target_pairs={{0,8},{4,12},{8,0},{12,4},{1,9},{5,13},{9,1},{13,5},{2,10},{6,14},... | collective-permute-start | bytes 442376 | tf_op jit(solution)/shard_map/ppermute | solution.py:440
  12.0 1.3 %collective-permute-done.4.refs_3_.refs_11_ = bf16[128,384]{1,0:T(8,128)(2,1)S(1)} collective-permute-done((bf16[128,384]{1,0:T(8,128)(2,1)S(1)}, bf16[128,384]{1,0:T(8,128)(2,1)S(1)}, u32[]{:S(2)}, u32[]{:S(2)}) %collective-permute-start.4) | collective-permute-done | bytes 98336 | tf_op jit(solution)/shard_map/ppermute | solution.py:323
  13.2 1.3 %collective-permute-start.5 = (bf16[128,384]{1,0:T(8,128)(2,1)S(1)}, bf16[128,384]{1,0:T(8,128)(2,1)S(1)}, u32[]{:S(2)}, u32[]{:S(2)}) collective-permute-start(bf16[128,384]{1,0:T(8,128)(2,1)S(1)} %collective-permute-done.3.refs_5_.refs_13_), channel_id=1, source_target_pairs={{0,4},{4,0},{8,12},{12,8},{1,5},{5,1},{9,13},{13,9},{2,6},{6,2},{1... | collective-permute-start | bytes 294920 | tf_op jit(solution)/shard_map/ppermute | solution.py:325
  14.5 3.2 %add_convert_fusion = bf16[384,3072]{1,0:T(8,128)(2,1)} fusion(bf16[384,3072]{1,0:T(8,128)(2,1)S(1)} %copy-done.4, bf16[384,64]{0,1:T(8,128)(2,1)S(1)} %copy-done.1, bf16[64,3072]{1,0:T(8,128)(2,1)} %refs_18_.1), kind=kOutput, calls=%fused_computation | convolution fusion | flops 154533888 | bytes 5160960 | tf_op jit(solution)/shard_map/dot_general | solution.py:447
  17.7 3.2 %collective-permute-done.refs_0_.refs_4_ = bf16[192,384]{1,0:T(8,128)(2,1)S(1)} collective-permute-done((bf16[192,384]{1,0:T(8,128)(2,1)S(1)}, bf16[192,384]{1,0:T(8,128)(2,1)S(1)}, u32[]{:S(2)}, u32[]{:S(2)}) %collective-permute-start) | collective-permute-done | bytes 147488 | tf_op jit(solution)/shard_map/ppermute | solution.py:440
  21.0 3.5 %collective-permute-done.2.refs_2_.refs_6_ = bf16[192,384]{1,0:T(8,128)(2,1)S(1)} collective-permute-done((bf16[192,384]{1,0:T(8,128)(2,1)S(1)}, bf16[192,384]{1,0:T(8,128)(2,1)S(1)}, u32[]{:S(2)}, u32[]{:S(2)}) %collective-permute-start.2) | collective-permute-done | bytes 147488 | tf_op jit(solution)/shard_map/ppermute | solution.py:440
  25.0 1.6 %collective-permute-start.8 = (bf16[3,128,384]{2,1,0:T(8,128)(2,1)S(1)}, bf16[3,128,384]{2,1,0:T(8,128)(2,1)S(1)}, u32[]{:S(2)}, u32[]{:S(2)}) collective-permute-start(bf16[3,128,384]{2,1,0:T(8,128)(2,1)S(1)} %get-tuple-element.66), channel_id=1, source_target_pairs={{0,2},{1,3},{2,0},{3,1},{4,6},{5,7},{6,4},{7,5},{8,10},{9,11},{10,... | collective-permute-start | bytes 884744 | tf_op jit(solution)/shard_map/ppermute | solution.py:457
  26.7 3.5 %collective-permute-start.10 = (bf16[192,384]{1,0:T(8,128)(2,1)S(1)}, bf16[192,384]{1,0:T(8,128)(2,1)S(1)}, u32[]{:S(2)}, u32[]{:S(2)}) collective-permute-start(bf16[192,384]{1,0:T(8,128)(2,1)S(1)} %get-tuple-element.68), channel_id=1, source_target_pairs={{0,12},{4,8},{8,4},{12,0},{1,13},{5,9},{9,5},{13,1},{2,14},{6,10},... | collective-permute-start | bytes 442376 | tf_op jit(solution)/shard_map/ppermute | solution.py:440
  30.2 0.9 collective-permute-start.9
  31.1 1.5 %collective-permute-start.6 = (bf16[3,192,384]{2,1,0:T(8,128)(2,1)S(1)}, bf16[3,192,384]{2,1,0:T(8,128)(2,1)S(1)}, u32[]{:S(2)}, u32[]{:S(2)}) collective-permute-start(bf16[3,192,384]{2,1,0:T(8,128)(2,1)S(1)} %get-tuple-element.65), channel_id=1, source_target_pairs={{0,16},{16,0},{1,17},{17,1},{2,18},{18,2},{3,19},{19,3},{4,20},{20... | collective-permute-start | bytes 1327112 | tf_op jit(solution)/shard_map/ppermute | solution.py:456
  32.6 2.7 %collective-permute-done.10.refs_5_ = bf16[192,384]{1,0:T(8,128)(2,1)S(1)} collective-permute-done((bf16[192,384]{1,0:T(8,128)(2,1)S(1)}, bf16[192,384]{1,0:T(8,128)(2,1)S(1)}, u32[]{:S(2)}, u32[]{:S(2)}) %collective-permute-start.10) | collective-permute-done | bytes 147488 | tf_op jit(solution)/shard_map/ppermute | solution.py:440
  35.3 1.7 %shard_map.106 = (bf16[64,384]{1,0:T(8,128)(2,1)S(1)}, bf16[384,384]{1,0:T(8,128)(2,1)S(1)}, bf16[2,128,512]{2,1,0:T(8,128)(2,1)S(1)}, bf16[2,512,128]{2,1,0:T(8,128)(2,1)S(1)}) custom-call(s32[3]{0:T(128)S(1)} %pad_add_fusion.sc, bf16[64,3072]{1,0:T(8,128)(2,1)} %refs_18_.1, bf16[384,3072]{1,0:T(8,128)(2,1)} %refs_19_.1, bf16[16,128,512]{2,1,0:T(8,128)(2,1)} %refs_20_.1, ...), custom_call_target="tpu_custom_call" | custom-call | bytes 1736704 | tf_op jit(solution)/shard_map/pallas_call | solution.py:108
  37.0 4.8 %collective-permute-done.11.refs_6_ = bf16[192,384]{1,0:T(8,128)(2,1)S(1)} collective-permute-done((bf16[192,384]{1,0:T(8,128)(2,1)S(1)}, bf16[192,384]{1,0:T(8,128)(2,1)S(1)}, u32[]{:S(2)}, u32[]{:S(2)}) %collective-permute-start.11) | collective-permute-done | bytes 147488 | tf_op jit(solution)/shard_map/ppermute | solution.py:440
  41.8 1.6 %collective-permute-start.13 = (bf16[192,384]{1,0:T(8,128)(2,1)S(1)}, bf16[192,384]{1,0:T(8,128)(2,1)S(1)}, u32[]{:S(2)}, u32[]{:S(2)}) collective-permute-start(bf16[192,384]{1,0:T(8,128)(2,1)S(1)} %collective-permute-done.9.refs_4_), channel_id=1, source_target_pairs={{0,16},{16,0},{1,17},{17,1},{2,18},{18,2},{3,19},{19,3},{4,20},{20... | collective-permute-start | bytes 442376 | tf_op jit(solution)/shard_map/ppermute | solution.py:474
  43.9 1.5 %collective-permute-start.15 = (bf16[192,384]{1,0:T(8,128)(2,1)S(1)}, bf16[192,384]{1,0:T(8,128)(2,1)S(1)}, u32[]{:S(2)}, u32[]{:S(2)}) collective-permute-start(bf16[192,384]{1,0:T(8,128)(2,1)S(1)} %collective-permute-done.11.refs_6_), channel_id=1, source_target_pairs={{0,16},{16,0},{1,17},{17,1},{2,18},{18,2},{3,19},{19,3},{4,20},{20... | collective-permute-start | bytes 442376 | tf_op jit(solution)/shard_map/ppermute | solution.py:474
  45.5 4.3 %shard_map.107 = (bf16[320,256]{1,0:T(8,128)(2,1)S(1)}, bf16[320,1536]{1,0:T(8,128)(2,1)S(1)}, bf16[320,576]{1,0:T(8,128)(2,1)S(1)}, bf16[64,1536]{1,0:T(8,128)(...) custom-call(s32[3]{0:T(128)S(1)} %pad_add_fusion.sc, ...), custom_call_target="tpu_custom_call" | custom-call | flops 964689920 | bytes 2359296 | tf_op jit(solution)/shard_map/pallas_call | solution.py:108
  49.8 1.8 %collective-permute-start.19 = (bf16[320,256]{1,0:T(8,128)(2,1)S(1)}, bf16[320,256]{1,0:T(8,128)(2,1)S(1)}, u32[]{:S(2)}, u32[]{:S(2)}) collective-permute-start(bf16[320,256]{1,0:T(8,128)(2,1)S(1)} %get-tuple-element.90.refs_0_), channel_id=1, source_target_pairs={{0,4},{4,0},{8,12},{12,8},{1,5},{5,1},{9,13},{13,9},{2,6},{6,2},{1... | collective-permute-start | bytes 491528 | tf_op jit(solution)/shard_map/ppermute | solution.py:323
  51.7 2.7 %collective-permute-done.15.refs_9_ = bf16[192,384]{1,0:T(8,128)(2,1)S(1)} collective-permute-done((bf16[192,384]{1,0:T(8,128)(2,1)S(1)}, bf16[192,384]{1,0:T(8,128)(2,1)S(1)}, u32[]{:S(2)}, u32[]{:S(2)}) %collective-permute-start.15) | collective-permute-done | bytes 147488 | tf_op jit(solution)/shard_map/ppermute | solution.py:474
  54.4 3.3 %shard_map.108.refs_3_ = bf16[320,256]{1,0:T(8,128)(2,1)S(1)} custom-call(s32[3]{0:T(128)S(1)} %pad_add_fusion.sc, bf16[320,1536]{1,0:T(8,128)(2,1)S(1)} %get-tuple-element.79.refs_0_, bf16[320,576]{1,0:T(8,128)(2,1)S(1)} %get-tuple-element.80.refs_1_, bf16[64,1536]{1,0:T(8,128)(2,1)S(1)} %get-tuple-element.81.refs_2_, ...), custom_call_target="tpu_custom_call" | custom-call | flops 964689920 | bytes 2359296 | tf_op jit(solution)/shard_map/pallas_call | solution.py:108
  57.8 1.8 %collective-permute-start.17 = (bf16[320,256]{1,0:T(8,128)(2,1)S(1)}, bf16[320,256]{1,0:T(8,128)(2,1)S(1)}, u32[]{:S(2)}, u32[]{:S(2)}) collective-permute-start(bf16[320,256]{1,0:T(8,128)(2,1)S(1)} %shard_map.108.refs_3_), channel_id=1, source_target_pairs={{0,4},{4,0},{8,12},{12,8},{1,5},{5,1},{9,13},{13,9},{2,6},{6,2},{1... | collective-permute-start | bytes 491528 | tf_op jit(solution)/shard_map/ppermute | solution.py:323
  59.9 4.0 %shard_map.109 = (f32[320,1792]{1,0:T(8,128)S(1)}, f32[8,128]{1,0:T(8,128)S(1)}, bf16[3,256,1792]{2,1,0:T(8,128)(2,1)S(1)}, bf16[1,256,1792]{2,1,0:T(8,128)(2,1)S(1)}) custom-call(s32[3]{0:T(128)S(1)} %pad_add_fusion.sc, bf16[320,256]{1,0:T(8,128)(2,1)S(1)} %get-tuple-element.90.refs_0_, bf16[320,256]{1,0:T(8,128)(2,1)S(1)} %collective-permute-done.19.refs_1_, ...), custom_call_target="tpu_custom_call" | custom-call | flops 1174405120 | bytes 3670016 | tf_op jit(solution)/shard_map/pallas_call | solution.py:108
  63.9 3.8 %collective-permute-done.16.refs_2_ = bf16[320,256]{1,0:T(8,128)(2,1)S(1)} collective-permute-done((bf16[320,256]{1,0:T(8,128)(2,1)S(1)}, bf16[320,256]{1,0:T(8,128)(2,1)S(1)}, u32[]{:S(2)}, u32[]{:S(2)}) %collective-permute-start.16) | collective-permute-done | bytes 163872 | tf_op jit(solution)/shard_map/ppermute | solution.py:322
  68.4 2.5 %collective-permute-done.21.refs_0_ = bf16[320,256]{1,0:T(8,128)(2,1)S(1)} collective-permute-done((bf16[320,256]{1,0:T(8,128)(2,1)S(1)}, bf16[320,256]{1,0:T(8,128)(2,1)S(1)}, u32[]{:S(2)}, u32[]{:S(2)}) %collective-permute-start.21) | collective-permute-done | bytes 163872 | tf_op jit(solution)/shard_map/ppermute | solution.py:325
  70.9 1.6 %shard_map.110.refs_2_ = f32[320,1792]{1,0:T(8,128)S(1)} custom-call(s32[3]{0:T(128)S(1)} %pad_add_fusion.sc, bf16[320,256]{1,0:T(8,128)(2,1)S(1)} %collective-permute-done.21.refs_0_, bf16[320,256]{1,0:T(8,128)(2,1)S(1)} %collective-permute-done.17.refs_1_, bf16[320,256]{1,0:T(8,128)(2,1)S(1)} %collective-permute-done.16.refs_2_, ...), custom_call_target="tpu_custom_call", output_to_operand_aliasing={{}: (5, {})} | custom-call | flops 880803840 | bytes 2752512 | tf_op jit(solution)/shard_map/pallas_call | solution.py:108
  72.5 1.6 %collective-permute-done.20.refs_0_ = bf16[320,256]{1,0:T(8,128)(2,1)S(1)} collective-permute-done((bf16[320,256]{1,0:T(8,128)(2,1)S(1)}, bf16[320,256]{1,0:T(8,128)(2,1)S(1)}, u32[]{:S(2)}, u32[]{:S(2)}) %collective-permute-start.20) | collective-permute-done | bytes 163872 | tf_op jit(solution)/shard_map/ppermute | solution.py:325
  74.1 1.0 %shard_map.111 = (f32[160,1792]{1,0:T(8,128)S(1)}, bf16[160,1792]{1,0:T(8,128)(2,1)S(1)}) custom-call(s32[3]{0:T(128)S(1)} %pad_add_fusion.sc, bf16[320,256]{1,0:T(8,128)(2,1)S(1)} %collective-permute-done.20.refs_0_, bf16[1,256,1792]{2,1,0:T(8,128)(2,1)S(1)} %get-tuple-element.95.refs_1_, f32[320,1792]{1,0:T(8,128)S(1)} %shard_map.110.refs_2_), custom_call_target="tpu_custom_call" | custom-call | flops 293601280 | bytes 917504 | tf_op jit(solution)/shard_map/pallas_call | solution.py:108
  75.2 1.9 %collective-permute-done.22 = bf16[160,1792]{1,0:T(8,128)(2,1)S(1)} collective-permute-done((bf16[160,1792]{1,0:T(8,128)(2,1)S(1)}, bf16[160,1792]{1,0:T(8,128)(2,1)S(1)}, u32[]{:S(2)}, u32[]{:S(2)}) %collective-permute-start.22) | collective-permute-done | bytes 573472 | tf_op jit(solution)/shard_map/ppermute | solution.py:553
  77.9 8.3 %collective-permute-done.23 = bf16[80,1792]{1,0:T(8,128)(2,1)S(1)} collective-permute-done((bf16[80,1792]{1,0:T(8,128)(2,1)S(1)}, bf16[80,1792]{1,0:T(8,128)(2,1)S(1)}, u32[]{:S(2)}, u32[]{:S(2)}) %collective-permute-start.23) | collective-permute-done | bytes 286752 | tf_op jit(solution)/shard_map/ppermute | solution.py:558
  (39 shorter events, 4.6 us)
Async XLA Ops:
  0.6 13.9 %copy-start.1 = (bf16[384,64]{0,1:T(8,128)(2,1)S(1)}, bf16[384,64]{0,1:T(8,128)(2,1)}, u32[]{:S(2)}) copy-start(bf16[384,64]{0,1:T(8,128)(2,1)} %param.13) | copy-start | bytes 147460
  0.6 13.9 %copy-start.4 = (bf16[384,3072]{1,0:T(8,128)(2,1)S(1)}, bf16[384,3072]{1,0:T(8,128)(2,1)}, u32[]{:S(2)}) copy-start(bf16[384,3072]{1,0:T(8,128)(2,1)} %refs_19_.1) | copy-start | bytes 7077892
  2.8 9.2 %collective-permute-start.3 = (bf16[128,384]{1,0:T(8,128)(2,1)S(1)}, bf16[128,384]{1,0:T(8,128)(2,1)S(1)}, u32[]{:S(2)}, u32[]{:S(2)}) collective-permute-start(bf16[128,384]{1,0:T(8,128)(2,1)S(1)} %get-tuple-element.55), channel_id=1, source_target_pairs={{0,8},{4,12},{8,0},{12,4},{1,9},{5,13},{9,1},{13,5},{2,10},{6,14},... | collective-permute-start | bytes 294920 | tf_op jit(solution)/shard_map/ppermute | solution.py:322
  6.9 6.3 %collective-permute-start.4 = (bf16[128,384]{1,0:T(8,128)(2,1)S(1)}, bf16[128,384]{1,0:T(8,128)(2,1)S(1)}, u32[]{:S(2)}, u32[]{:S(2)}) collective-permute-start(bf16[128,384]{1,0:T(8,128)(2,1)S(1)} %get-tuple-element.55), channel_id=1, source_target_pairs={{0,4},{4,0},{8,12},{12,8},{1,5},{5,1},{9,13},{13,9},{2,6},{6,2},{1... | collective-permute-start | bytes 294920 | tf_op jit(solution)/shard_map/ppermute | solution.py:323
  8.5 12.5 %collective-permute-start = (bf16[192,384]{1,0:T(8,128)(2,1)S(1)}, bf16[192,384]{1,0:T(8,128)(2,1)S(1)}, u32[]{:S(2)}, u32[]{:S(2)}) collective-permute-start(bf16[192,384]{1,0:T(8,128)(2,1)S(1)} %get-tuple-element.52), channel_id=1, source_target_pairs={{0,4},{4,0},{8,12},{12,8},{1,5},{5,1},{9,13},{13,9},{2,6},{6,2},{1... | collective-permute-start | bytes 442376 | tf_op jit(solution)/shard_map/ppermute | solution.py:440
  8.9 12.0 %collective-permute-start.1 = (bf16[192,384]{1,0:T(8,128)(2,1)S(1)}, bf16[192,384]{1,0:T(8,128)(2,1)S(1)}, u32[]{:S(2)}, u32[]{:S(2)}) collective-permute-start(bf16[192,384]{1,0:T(8,128)(2,1)S(1)} %get-tuple-element.53), channel_id=1, source_target_pairs={{0,12},{4,8},{8,4},{12,0},{1,13},{5,9},{9,5},{13,1},{2,14},{6,10},... | collective-permute-start | bytes 442376 | tf_op jit(solution)/shard_map/ppermute | solution.py:440
  10.3 14.2 %collective-permute-start.2 = (bf16[192,384]{1,0:T(8,128)(2,1)S(1)}, bf16[192,384]{1,0:T(8,128)(2,1)S(1)}, u32[]{:S(2)}, u32[]{:S(2)}) collective-permute-start(bf16[192,384]{1,0:T(8,128)(2,1)S(1)} %get-tuple-element.54), channel_id=1, source_target_pairs={{0,8},{4,12},{8,0},{12,4},{1,9},{5,13},{9,1},{13,5},{2,10},{6,14},... | collective-permute-start | bytes 442376 | tf_op jit(solution)/shard_map/ppermute | solution.py:440
  13.2 11.2 %collective-permute-start.5 = (bf16[128,384]{1,0:T(8,128)(2,1)S(1)}, bf16[128,384]{1,0:T(8,128)(2,1)S(1)}, u32[]{:S(2)}, u32[]{:S(2)}) collective-permute-start(bf16[128,384]{1,0:T(8,128)(2,1)S(1)} %collective-permute-done.3.refs_5_.refs_13_), channel_id=1, source_target_pairs={{0,4},{4,0},{8,12},{12,8},{1,5},{5,1},{9,13},{13,9},{2,6},{6,2},{1... | collective-permute-start | bytes 294920 | tf_op jit(solution)/shard_map/ppermute | solution.py:325
  25.0 16.7 %collective-permute-start.8 = (bf16[3,128,384]{2,1,0:T(8,128)(2,1)S(1)}, bf16[3,128,384]{2,1,0:T(8,128)(2,1)S(1)}, u32[]{:S(2)}, u32[]{:S(2)}) collective-permute-start(bf16[3,128,384]{2,1,0:T(8,128)(2,1)S(1)} %get-tuple-element.66), channel_id=1, source_target_pairs={{0,2},{1,3},{2,0},{3,1},{4,6},{5,7},{6,4},{7,5},{8,10},{9,11},{10,... | collective-permute-start | bytes 884744 | tf_op jit(solution)/shard_map/ppermute | solution.py:457
  26.7 8.6 %collective-permute-start.10 = (bf16[192,384]{1,0:T(8,128)(2,1)S(1)}, bf16[192,384]{1,0:T(8,128)(2,1)S(1)}, u32[]{:S(2)}, u32[]{:S(2)}) collective-permute-start(bf16[192,384]{1,0:T(8,128)(2,1)S(1)} %get-tuple-element.68), channel_id=1, source_target_pairs={{0,12},{4,8},{8,4},{12,0},{1,13},{5,9},{9,5},{13,1},{2,14},{6,10},... | collective-permute-start | bytes 442376 | tf_op jit(solution)/shard_map/ppermute | solution.py:440
  30.2 11.6 %collective-permute-start.11 = (bf16[192,384]{1,0:T(8,128)(2,1)S(1)}, bf16[192,384]{1,0:T(8,128)(2,1)S(1)}, u32[]{:S(2)}, u32[]{:S(2)}) collective-permute-start(bf16[192,384]{1,0:T(8,128)(2,1)S(1)} %get-tuple-element.69), channel_id=1, source_target_pairs={{0,8},{4,12},{8,0},{12,4},{1,9},{5,13},{9,1},{13,5},{2,10},{6,14},... | collective-permute-start | bytes 442376 | tf_op jit(solution)/shard_map/ppermute | solution.py:440
  30.2 11.6 %collective-permute-start.9 = (bf16[192,384]{1,0:T(8,128)(2,1)S(1)}, bf16[192,384]{1,0:T(8,128)(2,1)S(1)}, u32[]{:S(2)}, u32[]{:S(2)}) collective-permute-start(bf16[192,384]{1,0:T(8,128)(2,1)S(1)} %get-tuple-element.67), channel_id=1, source_target_pairs={{0,4},{4,0},{8,12},{12,8},{1,5},{5,1},{9,13},{13,9},{2,6},{6,2},{1... | collective-permute-start | bytes 442376 | tf_op jit(solution)/shard_map/ppermute | solution.py:440
  31.0 14.4 %copy-start = (bf16[80,1536]{1,0:T(8,128)(2,1)S(1)}, bf16[80,1536]{1,0:T(8,128)(2,1)}, u32[]{:S(2)}) copy-start(bf16[80,1536]{1,0:T(8,128)(2,1)} %refs_0_.3) | copy-start | bytes 737284
  31.0 14.4 %copy-start.2 = (bf16[80,576]{1,0:T(8,128)(2,1)S(1)}, bf16[80,576]{1,0:T(8,128)(2,1)}, u32[]{:S(2)}) copy-start(bf16[80,576]{1,0:T(8,128)(2,1)} %refs_1_.3) | copy-start | bytes 276484
  31.0 14.4 %copy-start.3 = (s32[80]{0:T(128)S(1)}, s32[80]{0:T(128)}, u32[]{:S(2)}) copy-start(s32[80]{0:T(128)} %param.11) | copy-start | bytes 964
  31.1 14.4 %collective-permute-start.6 = (bf16[3,192,384]{2,1,0:T(8,128)(2,1)S(1)}, bf16[3,192,384]{2,1,0:T(8,128)(2,1)S(1)}, u32[]{:S(2)}, u32[]{:S(2)}) collective-permute-start(bf16[3,192,384]{2,1,0:T(8,128)(2,1)S(1)} %get-tuple-element.65), channel_id=1, source_target_pairs={{0,16},{16,0},{1,17},{17,1},{2,18},{18,2},{3,19},{19,3},{4,20},{20... | collective-permute-start | bytes 1327112 | tf_op jit(solution)/shard_map/ppermute | solution.py:456
  35.3 8.6 %collective-permute-start.7 = (bf16[3,128,384]{2,1,0:T(8,128)(2,1)S(1)}, bf16[3,128,384]{2,1,0:T(8,128)(2,1)S(1)}, u32[]{:S(2)}, u32[]{:S(2)}) collective-permute-start(bf16[3,128,384]{2,1,0:T(8,128)(2,1)S(1)} %get-tuple-element.66), channel_id=1, source_target_pairs={{0,1},{1,0},{2,3},{3,2},{4,5},{5,4},{6,7},{7,6},{8,9},{9,8},{10,11... | collective-permute-start | bytes 884744 | tf_op jit(solution)/shard_map/ppermute | solution.py:470
  41.8 3.7 %collective-permute-start.12 = (bf16[3,128,384]{2,1,0:T(8,128)(2,1)S(1)}, bf16[3,128,384]{2,1,0:T(8,128)(2,1)S(1)}, u32[]{:S(2)}, u32[]{:S(2)}) collective-permute-start(bf16[3,128,384]{2,1,0:T(8,128)(2,1)S(1)} %collective-permute-done.8.refs_9_), channel_id=1, source_target_pairs={{0,1},{1,0},{2,3},{3,2},{4,5},{5,4},{6,7},{7,6},{8,9},{9,8},{10,11... | collective-permute-start | bytes 884744 | tf_op jit(solution)/shard_map/ppermute | solution.py:472
  41.8 9.8 %collective-permute-start.13 = (bf16[192,384]{1,0:T(8,128)(2,1)S(1)}, bf16[192,384]{1,0:T(8,128)(2,1)S(1)}, u32[]{:S(2)}, u32[]{:S(2)}) collective-permute-start(bf16[192,384]{1,0:T(8,128)(2,1)S(1)} %collective-permute-done.9.refs_4_), channel_id=1, source_target_pairs={{0,16},{16,0},{1,17},{17,1},{2,18},{18,2},{3,19},{19,3},{4,20},{20... | collective-permute-start | bytes 442376 | tf_op jit(solution)/shard_map/ppermute | solution.py:474
  43.4 8.3 %collective-permute-start.14 = (bf16[192,384]{1,0:T(8,128)(2,1)S(1)}, bf16[192,384]{1,0:T(8,128)(2,1)S(1)}, u32[]{:S(2)}, u32[]{:S(2)}) collective-permute-start(bf16[192,384]{1,0:T(8,128)(2,1)S(1)} %collective-permute-done.10.refs_5_), channel_id=1, source_target_pairs={{0,16},{16,0},{1,17},{17,1},{2,18},{18,2},{3,19},{19,3},{4,20},{20... | collective-permute-start | bytes 442376 | tf_op jit(solution)/shard_map/ppermute | solution.py:474
  43.9 10.5 %collective-permute-start.15 = (bf16[192,384]{1,0:T(8,128)(2,1)S(1)}, bf16[192,384]{1,0:T(8,128)(2,1)S(1)}, u32[]{:S(2)}, u32[]{:S(2)}) collective-permute-start(bf16[192,384]{1,0:T(8,128)(2,1)S(1)} %collective-permute-done.11.refs_6_), channel_id=1, source_target_pairs={{0,16},{16,0},{1,17},{17,1},{2,18},{18,2},{3,19},{19,3},{4,20},{20... | collective-permute-start | bytes 442376 | tf_op jit(solution)/shard_map/ppermute | solution.py:474
  49.7 10.2 %collective-permute-start.18 = (bf16[320,256]{1,0:T(8,128)(2,1)S(1)}, bf16[320,256]{1,0:T(8,128)(2,1)S(1)}, u32[]{:S(2)}, u32[]{:S(2)}) collective-permute-start(bf16[320,256]{1,0:T(8,128)(2,1)S(1)} %get-tuple-element.90.refs_0_), channel_id=1, source_target_pairs={{0,8},{4,12},{8,0},{12,4},{1,9},{5,13},{9,1},{13,5},{2,10},{6,14},... | collective-permute-start | bytes 491528 | tf_op jit(solution)/shard_map/ppermute | solution.py:322
  49.8 10.1 %collective-permute-start.19 = (bf16[320,256]{1,0:T(8,128)(2,1)S(1)}, bf16[320,256]{1,0:T(8,128)(2,1)S(1)}, u32[]{:S(2)}, u32[]{:S(2)}) collective-permute-start(bf16[320,256]{1,0:T(8,128)(2,1)S(1)} %get-tuple-element.90.refs_0_), channel_id=1, source_target_pairs={{0,4},{4,0},{8,12},{12,8},{1,5},{5,1},{9,13},{13,9},{2,6},{6,2},{1... | collective-permute-start | bytes 491528 | tf_op jit(solution)/shard_map/ppermute | solution.py:323
  57.7 10.0 %collective-permute-start.16 = (bf16[320,256]{1,0:T(8,128)(2,1)S(1)}, bf16[320,256]{1,0:T(8,128)(2,1)S(1)}, u32[]{:S(2)}, u32[]{:S(2)}) collective-permute-start(bf16[320,256]{1,0:T(8,128)(2,1)S(1)} %shard_map.108.refs_3_), channel_id=1, source_target_pairs={{0,8},{4,12},{8,0},{12,4},{1,9},{5,13},{9,1},{13,5},{2,10},{6,14},... | collective-permute-start | bytes 491528 | tf_op jit(solution)/shard_map/ppermute | solution.py:322
  57.8 10.5 %collective-permute-start.17 = (bf16[320,256]{1,0:T(8,128)(2,1)S(1)}, bf16[320,256]{1,0:T(8,128)(2,1)S(1)}, u32[]{:S(2)}, u32[]{:S(2)}) collective-permute-start(bf16[320,256]{1,0:T(8,128)(2,1)S(1)} %shard_map.108.refs_3_), channel_id=1, source_target_pairs={{0,4},{4,0},{8,12},{12,8},{1,5},{5,1},{9,13},{13,9},{2,6},{6,2},{1... | collective-permute-start | bytes 491528 | tf_op jit(solution)/shard_map/ppermute | solution.py:323
  59.9 11.0 %collective-permute-start.21 = (bf16[320,256]{1,0:T(8,128)(2,1)S(1)}, bf16[320,256]{1,0:T(8,128)(2,1)S(1)}, u32[]{:S(2)}, u32[]{:S(2)}) collective-permute-start(bf16[320,256]{1,0:T(8,128)(2,1)S(1)} %collective-permute-done.18.refs_2_), channel_id=1, source_target_pairs={{0,4},{4,0},{8,12},{12,8},{1,5},{5,1},{9,13},{13,9},{2,6},{6,2},{1... | collective-permute-start | bytes 491528 | tf_op jit(solution)/shard_map/ppermute | solution.py:325
  68.3 5.8 %collective-permute-start.20 = (bf16[320,256]{1,0:T(8,128)(2,1)S(1)}, bf16[320,256]{1,0:T(8,128)(2,1)S(1)}, u32[]{:S(2)}, u32[]{:S(2)}) collective-permute-start(bf16[320,256]{1,0:T(8,128)(2,1)S(1)} %collective-permute-done.16.refs_2_), channel_id=1, source_target_pairs={{0,4},{4,0},{8,12},{12,8},{1,5},{5,1},{9,13},{13,9},{2,6},{6,2},{1... | collective-permute-start | bytes 491528 | tf_op jit(solution)/shard_map/ppermute | solution.py:325
  75.1 2.0 %collective-permute-start.22 = (bf16[160,1792]{1,0:T(8,128)(2,1)S(1)}, bf16[160,1792]{1,0:T(8,128)(2,1)S(1)}, u32[]{:S(2)}, u32[]{:S(2)}) collective-permute-start(bf16[160,1792]{1,0:T(8,128)(2,1)S(1)} %get-tuple-element.101), channel_id=1, source_target_pairs={{0,1},{1,0},{2,3},{3,2},{4,5},{5,4},{6,7},{7,6},{8,9},{9,8},{10,11... | collective-permute-start | bytes 1720328 | tf_op jit(solution)/shard_map/ppermute | solution.py:553
  77.3 8.9 %collective-permute-start.23 = (bf16[80,1792]{1,0:T(8,128)(2,1)S(1)}, bf16[80,1792]{1,0:T(8,128)(2,1)S(1)}, u32[]{:S(2)}, u32[]{:S(2)}) collective-permute-start(bf16[80,1792]{1,0:T(8,128)(2,1)S(1)} %fusion.1), channel_id=1, source_target_pairs={{0,2},{1,3},{2,0},{3,1},{4,6},{5,7},{6,4},{7,5},{8,10},{9,11},{10,... | collective-permute-start | bytes 860168 | tf_op jit(solution)/shard_map/ppermute | solution.py:558

commit v9 on v8

--- a/solution.py
+++ b/solution.py
@@ -98,7 +98,7 @@
 
 
 def partners(n):
-    return [1, 3, 2]
+    return [2, 3, 1]
 
 
 def call(body, outs, args, hbm=(), scratch=(), alias=None, flops=0, moved=0):
@@ -382,19 +382,18 @@
     columns_dot(lhs, w, 0, acc.shape[1], add)
 
 
-def last_body(nh, tok, sc, *refs):
-    slots, (w, acc, keep, send) = refs[: len(LATE)], refs[len(LATE) :]
-    core = sc[2] % 2
+def last_body(tok, wanted, sc, *refs):
+    slots, (w, acc, *outs) = refs[: len(LATE)], refs[len(LATE) :]
+    outs = outs[-len(wanted) :]
     total = acc.shape[1]
-    for which, out in ((core, keep), (1 - core, send)):
-        rows = [pl.ds(pl.multiple_of((2 * i + which) * tok, 16), tok) for i in range(nh // 2)]
-        lhs = jnp.concatenate([slots[0][row, :] for row in rows], axis=0)
-        for at in range(0, total, TILE):
-            band = slice(at, min(at + TILE, total))
-            more = jnp.dot(lhs, w[0, :, band], preferred_element_type=jnp.float32)
-            for i, row in enumerate(rows):
-                part = acc[row, band] + more[i * tok : (i + 1) * tok]
-                out[i * tok : (i + 1) * tok, band] = part.astype(out.dtype)
+    rows = [pl.ds(pl.multiple_of((sc[2] ^ bits) * tok, 16), tok) for bits in wanted]
+    lhs = jnp.concatenate([slots[0][row, :] for row in rows], axis=0)
+    for at in range(0, total, TILE):
+        band = slice(at, min(at + TILE, total))
+        more = jnp.dot(lhs, w[0, :, band], preferred_element_type=jnp.float32)
+        for i, (row, out) in enumerate(zip(rows, outs)):
+            part = acc[row, band] + more[i * tok : (i + 1) * tok]
+            out[:, band] = part.astype(out.dtype)
 
 
 def by_heads(x, kv, pos, wq, down, up, ku, vu, wo):
@@ -471,7 +470,7 @@
         across,
         lax.ppermute(across, "head", flipped(nh, 1)),
     ]
-    passed.append([lax.ppermute(p, "groups", flipped(2, 1)) for p in moved[1]])
+    passed.append([lax.ppermute(p, "groups", flipped(2, 1)) for p in moved[1][:-1]])
 
     scale = 1.0 / math.sqrt(nope + rope)
     raw = pltpu.VMEM((n * rows, wide), bf)
@@ -495,6 +494,8 @@
         + [pltpu.SemaphoreType.DMA((4,))],
         **cost,
     )
+    moved[1][-1], ho = lax.optimization_barrier((moved[1][-1], ho))
+    passed[1].append(lax.ppermute(moved[1][-1], "groups", flipped(2, 1)))
     slots = [gather_line(ho)]
     ho = call(
         functools.partial(attend_next, n, nope, scale),
@@ -544,19 +545,21 @@
         alias={2 + len(MIDDLE): 0},
         **work(MIDDLE),
     )
-    keep, send = call(
-        functools.partial(last_body, nh, tok),
-        (like(nh // 2 * tok, total, dtype=f32), like(nh // 2 * tok, total)),
-        [sc] + late + [w_late, acc],
-        **work(LATE),
-    )
-    got = lax.ppermute(send, "head", flipped(nh, 1))
-    pair = (keep + got.astype(f32)).reshape(nh // 2, tok, total)
-    side = h // 2
-    out = lax.dynamic_index_in_dim(pair, side, 0, keepdims=False)
-    away = lax.dynamic_index_in_dim(pair, 1 - side, 0, keepdims=False).astype(bf)
-    out = out + lax.ppermute(away, "head", flipped(nh, 2)).astype(f32)
-    return merged, out.astype(bf)
+    def last(*wanted, after=()):
+        return call(
+            functools.partial(last_body, tok, [bits for bits, _ in wanted]),
+            tuple(like(tok, total, dtype=kind) for _, kind in wanted),
+            [sc] + late + [w_late, acc, *after],
+            flops=2 * len(wanted) * tok * width * total,
+            moved=8 * len(wanted) * tok * total,
+        )
+
+    (send_away,) = last((3, bf))
+    keep_away, send_home, keep_home = last((2, f32), (1, bf), (0, f32), after=[send_away])
+    away = keep_away + lax.ppermute(send_away, "head", flipped(nh, 1)).astype(f32)
+    got = lax.ppermute(away.astype(bf), "head", flipped(nh, 2))
+    home = keep_home + lax.ppermute(send_home, "head", flipped(nh, 1)).astype(f32)
+    return merged, (home + got.astype(f32)).astype(bf)
 
 
 def fits(mesh, shapes):

time: 87.2 us -> 85.7 us (0.983)
  waiting for transfers between devices: 37.5 us -> 31.3 us
  starting transfers between devices: 26 us -> 30 us
    ppermute x6, waiting for transfers between devices: 14.2 us -> 5.85 us  [exchange(): lax.ppermute(p, 'seq', flipped(n, bits))]
    ppermute x3, waiting for transfers between devices: 4.14 us -> 9.47 us  [gather_line(): two = lax.ppermute(x, 'seq', flipped(4, 2))]
    ppermute x5 -> x6, waiting for transfers between devices: 13.1 us -> 10.1 us  [the longest x1 7.84 us: by_heads(): got = lax.ppermute(away.astype(bf), 'head', flipped(nh, 2))]
    ppermute x3, starting transfers between devices: 5.1 us -> 6.79 us  [gather_line(): one = lax.ppermute(x, 'seq', flipped(4, 1))]
    ppermute x3, starting transfers between devices: 1.36 us -> 2.89 us  [gather_line(): return [x, one, two, lax.ppermute(two, 'seq', flipped(4, 1))] + held]
    pallas_call x8 -> x9, Pallas kernels: 18.5 us -> 19.3 us  [call(): pl.pallas_call(body, out_shape=outs, grid_spec=pltpu.PrefetchScalarGridSp...]
    ppermute x5 -> x6, starting transfers between devices: 4.31 us -> 4.84 us  [the longest x2 2.03 us: by_heads(): lax.ppermute(p, 'groups', flipped(2, 1))]
  transfers between devices with their start and end apart: 24 -> 25, of which waited for: 14 -> 10; matrix products, arithmetic and copies ran while one was open for 4% -> 4% of each run, Pallas kernels for 17% -> 18%
where the time goes in v9:
time: 85.7 us; the launch traced here: 85.5 us
  waiting for transfers between devices  31.3 us (37%)
  starting transfers between devices  30 us (35%)
  Pallas kernels  19.3 us (23%)
  matrix products  3.19 us (4%)
  other arithmetic  0.95 us (1%)
    pallas_call x9, Pallas kernels, call(): pl.pallas_call(body, out_shape=outs, grid_spec=pltpu.PrefetchScalarGridSp...  19.3 us
    ppermute x3, waiting for transfers between devices, gather_line(): two = lax.ppermute(x, 'seq', flipped(4, 2))  9.47 us
    ppermute x1, waiting for transfers between devices, by_heads(): got = lax.ppermute(away.astype(bf), 'head', flipped(nh, 2))  7.84 us
    ppermute x6, starting transfers between devices, exchange(): lax.ppermute(p, 'seq', flipped(n, bits))  7.72 us
    ppermute x3, starting transfers between devices, gather_line(): one = lax.ppermute(x, 'seq', flipped(4, 1))  6.79 us
    ppermute x6, waiting for transfers between devices, exchange(): lax.ppermute(p, 'seq', flipped(n, bits))  5.85 us
    ppermute x3, starting transfers between devices, gather_line(): two = lax.ppermute(x, 'seq', flipped(4, 2))  4.01 us
    ppermute x3, waiting for transfers between devices, gather_line(): return [x, one, two, lax.ppermute(two, 'seq', flipped(4, 1))] + held  3.29 us
  transfers between devices with their start and end apart: 25, of which 10 were waited for; matrix products, arithmetic and copies ran while one was open for 4% of the time, Pallas kernels for 18%

profile of v9, /device:TPU:0, one launch (start us, length us, event | category | flops | bytes accessed | tf_op | source)
XLA Modules:
  0.0 85.5 jit_solution(6894444948958793593)
XLA Ops:
  0.7 2.0 %shard_map.104 = (bf16[128,384]{1,0:T(8,128)(2,1)S(1)}, bf16[192,384]{1,0:T(8,128)(2,1)S(1)}, bf16[192,384]{1,0:T(8,128)(2,1)S(1)}, bf16[192,384]{1,0:T(8,128)(2...) custom-call(s32[3]{0:T(128)S(1)} %pad_add_fusion.sc, ...), custom_call_target="tpu_custom_call" | custom-call | bytes 2359296 | tf_op jit(solution)/shard_map/pallas_call | solution.py:108
  2.8 3.1 %collective-permute-start.4 = (bf16[128,384]{1,0:T(8,128)(2,1)S(1)}, bf16[128,384]{1,0:T(8,128)(2,1)S(1)}, u32[]{:S(2)}, u32[]{:S(2)}) collective-permute-start(bf16[128,384]{1,0:T(8,128)(2,1)S(1)} %get-tuple-element.58), channel_id=1, source_target_pairs={{0,4},{4,0},{8,12},{12,8},{1,5},{5,1},{9,13},{13,9},{2,6},{6,2},{1... | collective-permute-start | bytes 294920 | tf_op jit(solution)/shard_map/ppermute | solution.py:323
  5.9 2.6 %collective-permute-start.3 = (bf16[128,384]{1,0:T(8,128)(2,1)S(1)}, bf16[128,384]{1,0:T(8,128)(2,1)S(1)}, u32[]{:S(2)}, u32[]{:S(2)}) collective-permute-start(bf16[128,384]{1,0:T(8,128)(2,1)S(1)} %get-tuple-element.58), channel_id=1, source_target_pairs={{0,8},{4,12},{8,0},{12,4},{1,9},{5,13},{9,1},{13,5},{2,10},{6,14},... | collective-permute-start | bytes 294920 | tf_op jit(solution)/shard_map/ppermute | solution.py:322
  8.8 2.5 %collective-permute-start.1 = (bf16[192,384]{1,0:T(8,128)(2,1)S(1)}, bf16[192,384]{1,0:T(8,128)(2,1)S(1)}, u32[]{:S(2)}, u32[]{:S(2)}) collective-permute-start(bf16[192,384]{1,0:T(8,128)(2,1)S(1)} %get-tuple-element.56), channel_id=1, source_target_pairs={{0,12},{4,8},{8,4},{12,0},{1,13},{5,9},{9,5},{13,1},{2,14},{6,10},... | collective-permute-start | bytes 442376 | tf_op jit(solution)/shard_map/ppermute | solution.py:439
  12.0 8.0 %collective-permute-done.3.refs_3_.refs_11_ = bf16[128,384]{1,0:T(8,128)(2,1)S(1)} collective-permute-done((bf16[128,384]{1,0:T(8,128)(2,1)S(1)}, bf16[128,384]{1,0:T(8,128)(2,1)S(1)}, u32[]{:S(2)}, u32[]{:S(2)}) %collective-permute-start.3) | collective-permute-done | bytes 98336 | tf_op jit(solution)/shard_map/ppermute | solution.py:322
  20.3 3.2 %add_convert_fusion = bf16[384,3072]{1,0:T(8,128)(2,1)} fusion(bf16[384,3072]{1,0:T(8,128)(2,1)S(1)} %copy-done.4, bf16[384,64]{0,1:T(8,128)(2,1)S(1)} %copy-done.1, bf16[64,3072]{1,0:T(8,128)(2,1)} %refs_18_.1), kind=kOutput, calls=%fused_computation | convolution fusion | flops 154533888 | bytes 5160960 | tf_op jit(solution)/shard_map/dot_general | solution.py:446
  23.5 1.0 %collective-permute-done.5.refs_4_.refs_12_ = bf16[128,384]{1,0:T(8,128)(2,1)S(1)} collective-permute-done((bf16[128,384]{1,0:T(8,128)(2,1)S(1)}, bf16[128,384]{1,0:T(8,128)(2,1)S(1)}, u32[]{:S(2)}, u32[]{:S(2)}) %collective-permute-start.5) | collective-permute-done | bytes 98336 | tf_op jit(solution)/shard_map/ppermute | solution.py:325
  25.2 1.6 %collective-permute-start.8 = (bf16[3,128,384]{2,1,0:T(8,128)(2,1)S(1)}, bf16[3,128,384]{2,1,0:T(8,128)(2,1)S(1)}, u32[]{:S(2)}, u32[]{:S(2)}) collective-permute-start(bf16[3,128,384]{2,1,0:T(8,128)(2,1)S(1)} %get-tuple-element.69), channel_id=1, source_target_pairs={{0,2},{1,3},{2,0},{3,1},{4,6},{5,7},{6,4},{7,5},{8,10},{9,11},{10,... | collective-permute-start | bytes 884744 | tf_op jit(solution)/shard_map/ppermute | solution.py:456
  26.7 2.8 %collective-permute-start.9 = (bf16[192,384]{1,0:T(8,128)(2,1)S(1)}, bf16[192,384]{1,0:T(8,128)(2,1)S(1)}, u32[]{:S(2)}, u32[]{:S(2)}) collective-permute-start(bf16[192,384]{1,0:T(8,128)(2,1)S(1)} %get-tuple-element.70), channel_id=1, source_target_pairs={{0,8},{4,12},{8,0},{12,4},{1,9},{5,13},{9,1},{13,5},{2,10},{6,14},... | collective-permute-start | bytes 442376 | tf_op jit(solution)/shard_map/ppermute | solution.py:439
  29.6 1.4 %collective-permute-start.10 = (bf16[192,384]{1,0:T(8,128)(2,1)S(1)}, bf16[192,384]{1,0:T(8,128)(2,1)S(1)}, u32[]{:S(2)}, u32[]{:S(2)}) collective-permute-start(bf16[192,384]{1,0:T(8,128)(2,1)S(1)} %get-tuple-element.71), channel_id=1, source_target_pairs={{0,12},{4,8},{8,4},{12,0},{1,13},{5,9},{9,5},{13,1},{2,14},{6,10},... | collective-permute-start | bytes 442376 | tf_op jit(solution)/shard_map/ppermute | solution.py:439
  31.0 1.6 %collective-permute-start.6 = (bf16[3,192,384]{2,1,0:T(8,128)(2,1)S(1)}, bf16[3,192,384]{2,1,0:T(8,128)(2,1)S(1)}, u32[]{:S(2)}, u32[]{:S(2)}) collective-permute-start(bf16[3,192,384]{2,1,0:T(8,128)(2,1)S(1)} %get-tuple-element.68), channel_id=1, source_target_pairs={{0,16},{16,0},{1,17},{17,1},{2,18},{18,2},{3,19},{19,3},{4,20},{20... | collective-permute-start | bytes 1327112 | tf_op jit(solution)/shard_map/ppermute | solution.py:455
  32.6 1.7 %shard_map.106 = (bf16[64,384]{1,0:T(8,128)(2,1)S(1)}, bf16[384,384]{1,0:T(8,128)(2,1)S(1)}, bf16[2,128,512]{2,1,0:T(8,128)(2,1)S(1)}, bf16[2,512,128]{2,1,0:T(8,128)(2,1)S(1)}) custom-call(s32[3]{0:T(128)S(1)} %pad_add_fusion.sc, bf16[64,3072]{1,0:T(8,128)(2,1)} %refs_18_.1, bf16[384,3072]{1,0:T(8,128)(2,1)} %refs_19_.1, bf16[16,128,512]{2,1,0:T(8,128)(2,1)} %refs_20_.1, ...), custom_call_target="tpu_custom_call" | custom-call | bytes 1736704 | tf_op jit(solution)/shard_map/pallas_call | solution.py:108
  34.3 5.8 %collective-permute-done.9.refs_4_ = bf16[192,384]{1,0:T(8,128)(2,1)S(1)} collective-permute-done((bf16[192,384]{1,0:T(8,128)(2,1)S(1)}, bf16[192,384]{1,0:T(8,128)(2,1)S(1)}, u32[]{:S(2)}, u32[]{:S(2)}) %collective-permute-start.9) | collective-permute-done | bytes 147488 | tf_op jit(solution)/shard_map/ppermute | solution.py:439
  40.7 1.5 %collective-permute-start.13 = (bf16[192,384]{1,0:T(8,128)(2,1)S(1)}, bf16[192,384]{1,0:T(8,128)(2,1)S(1)}, u32[]{:S(2)}, u32[]{:S(2)}) collective-permute-start(bf16[192,384]{1,0:T(8,128)(2,1)S(1)} %collective-permute-done.9.refs_4_), channel_id=1, source_target_pairs={{0,16},{16,0},{1,17},{17,1},{2,18},{18,2},{3,19},{19,3},{4,20},{20... | collective-permute-start | bytes 442376 | tf_op jit(solution)/shard_map/ppermute | solution.py:473
  42.8 4.3 %shard_map.107 = (bf16[320,256]{1,0:T(8,128)(2,1)S(1)}, bf16[320,1536]{1,0:T(8,128)(2,1)S(1)}, bf16[320,576]{1,0:T(8,128)(2,1)S(1)}, bf16[64,1536]{1,0:T(8,128)(...) custom-call(s32[3]{0:T(128)S(1)} %pad_add_fusion.sc, ...), custom_call_target="tpu_custom_call" | custom-call | flops 964689920 | bytes 2359296 | tf_op jit(solution)/shard_map/pallas_call | solution.py:108
  47.1 1.6 %collective-permute-start.15 = (bf16[192,384]{1,0:T(8,128)(2,1)S(1)}, bf16[192,384]{1,0:T(8,128)(2,1)S(1)}, u32[]{:S(2)}, u32[]{:S(2)}) collective-permute-start(bf16[192,384]{1,0:T(8,128)(2,1)S(1)} %collective-permute-done.11.refs_6_), channel_id=1, source_target_pairs={{0,16},{16,0},{1,17},{17,1},{2,18},{18,2},{3,19},{19,3},{4,20},{20... | collective-permute-start | bytes 442376 | tf_op jit(solution)/shard_map/ppermute | solution.py:498
  48.6 1.6 %collective-permute-start.19 = (bf16[320,256]{1,0:T(8,128)(2,1)S(1)}, bf16[320,256]{1,0:T(8,128)(2,1)S(1)}, u32[]{:S(2)}, u32[]{:S(2)}) collective-permute-start(bf16[320,256]{1,0:T(8,128)(2,1)S(1)} %get-tuple-element.95.refs_0_), channel_id=1, source_target_pairs={{0,4},{4,0},{8,12},{12,8},{1,5},{5,1},{9,13},{13,9},{2,6},{6,2},{1... | collective-permute-start | bytes 491528 | tf_op jit(solution)/shard_map/ppermute | solution.py:323
  50.3 0.9 %collective-permute-start.18 = (bf16[320,256]{1,0:T(8,128)(2,1)S(1)}, bf16[320,256]{1,0:T(8,128)(2,1)S(1)}, u32[]{:S(2)}, u32[]{:S(2)}) collective-permute-start(bf16[320,256]{1,0:T(8,128)(2,1)S(1)} %get-tuple-element.95.refs_0_), channel_id=1, source_target_pairs={{0,8},{4,12},{8,0},{12,4},{1,9},{5,13},{9,1},{13,5},{2,10},{6,14},... | collective-permute-start | bytes 491528 | tf_op jit(solution)/shard_map/ppermute | solution.py:322
  51.2 1.7 %collective-permute-done.15.refs_9_ = bf16[192,384]{1,0:T(8,128)(2,1)S(1)} collective-permute-done((bf16[192,384]{1,0:T(8,128)(2,1)S(1)}, bf16[192,384]{1,0:T(8,128)(2,1)S(1)}, u32[]{:S(2)}, u32[]{:S(2)}) %collective-permute-start.15) | collective-permute-done | bytes 147488 | tf_op jit(solution)/shard_map/ppermute | solution.py:498
  52.9 3.3 %shard_map.108.refs_3_ = bf16[320,256]{1,0:T(8,128)(2,1)S(1)} custom-call(s32[3]{0:T(128)S(1)} %pad_add_fusion.sc, bf16[320,1536]{1,0:T(8,128)(2,1)S(1)} %get-tuple-element.82.refs_0_, bf16[320,576]{1,0:T(8,128)(2,1)S(1)} %get-tuple-element.83.refs_1_, bf16[64,1536]{1,0:T(8,128)(2,1)S(1)} %get-tuple-element.84.refs_2_, ...), custom_call_target="tpu_custom_call" | custom-call | flops 964689920 | bytes 2359296 | tf_op jit(solution)/shard_map/pallas_call | solution.py:108
  56.2 2.1 %collective-permute-start.17 = (bf16[320,256]{1,0:T(8,128)(2,1)S(1)}, bf16[320,256]{1,0:T(8,128)(2,1)S(1)}, u32[]{:S(2)}, u32[]{:S(2)}) collective-permute-start(bf16[320,256]{1,0:T(8,128)(2,1)S(1)} %shard_map.108.refs_3_), channel_id=1, source_target_pairs={{0,4},{4,0},{8,12},{12,8},{1,5},{5,1},{9,13},{13,9},{2,6},{6,2},{1... | collective-permute-start | bytes 491528 | tf_op jit(solution)/shard_map/ppermute | solution.py:323
  58.8 1.5 %collective-permute-done.18.refs_2_ = bf16[320,256]{1,0:T(8,128)(2,1)S(1)} collective-permute-done((bf16[320,256]{1,0:T(8,128)(2,1)S(1)}, bf16[320,256]{1,0:T(8,128)(2,1)S(1)}, u32[]{:S(2)}, u32[]{:S(2)}) %collective-permute-start.18) | collective-permute-done | bytes 163872 | tf_op jit(solution)/shard_map/ppermute | solution.py:322
  60.8 4.0 %shard_map.109 = (f32[320,1792]{1,0:T(8,128)S(1)}, f32[8,128]{1,0:T(8,128)S(1)}, bf16[3,256,1792]{2,1,0:T(8,128)(2,1)S(1)}, bf16[1,256,1792]{2,1,0:T(8,128)(2,1)S(1)}) custom-call(s32[3]{0:T(128)S(1)} %pad_add_fusion.sc, bf16[320,256]{1,0:T(8,128)(2,1)S(1)} %get-tuple-element.95.refs_0_, bf16[320,256]{1,0:T(8,128)(2,1)S(1)} %collective-permute-done.19.refs_1_, ...), custom_call_target="tpu_custom_call" | custom-call | flops 1174405120 | bytes 3670016 | tf_op jit(solution)/shard_map/pallas_call | solution.py:108
  64.7 2.6 %collective-permute-done.17.refs_1_ = bf16[320,256]{1,0:T(8,128)(2,1)S(1)} collective-permute-done((bf16[320,256]{1,0:T(8,128)(2,1)S(1)}, bf16[320,256]{1,0:T(8,128)(2,1)S(1)}, u32[]{:S(2)}, u32[]{:S(2)}) %collective-permute-start.17) | collective-permute-done | bytes 163872 | tf_op jit(solution)/shard_map/ppermute | solution.py:323
  67.3 2.0 %collective-permute-start.20 = (bf16[320,256]{1,0:T(8,128)(2,1)S(1)}, bf16[320,256]{1,0:T(8,128)(2,1)S(1)}, u32[]{:S(2)}, u32[]{:S(2)}) collective-permute-start(bf16[320,256]{1,0:T(8,128)(2,1)S(1)} %collective-permute-done.16.refs_2_), channel_id=1, source_target_pairs={{0,4},{4,0},{8,12},{12,8},{1,5},{5,1},{9,13},{13,9},{2,6},{6,2},{1... | collective-permute-start | bytes 491528 | tf_op jit(solution)/shard_map/ppermute | solution.py:325
  69.4 1.5 %collective-permute-done.21.refs_0_ = bf16[320,256]{1,0:T(8,128)(2,1)S(1)} collective-permute-done((bf16[320,256]{1,0:T(8,128)(2,1)S(1)}, bf16[320,256]{1,0:T(8,128)(2,1)S(1)}, u32[]{:S(2)}, u32[]{:S(2)}) %collective-permute-start.21) | collective-permute-done | bytes 163872 | tf_op jit(solution)/shard_map/ppermute | solution.py:325
  70.8 1.6 %shard_map.110.refs_2_ = f32[320,1792]{1,0:T(8,128)S(1)} custom-call(s32[3]{0:T(128)S(1)} %pad_add_fusion.sc, bf16[320,256]{1,0:T(8,128)(2,1)S(1)} %collective-permute-done.21.refs_0_, bf16[320,256]{1,0:T(8,128)(2,1)S(1)} %collective-permute-done.17.refs_1_, bf16[320,256]{1,0:T(8,128)(2,1)S(1)} %collective-permute-done.16.refs_2_, ...), custom_call_target="tpu_custom_call", output_to_operand_aliasing={{}: (5, {})} | custom-call | flops 880803840 | bytes 2752512 | tf_op jit(solution)/shard_map/pallas_call | solution.py:108
  72.5 0.8 collective-permute-done.20.refs_0_
  73.2 0.8 shard_map.111.refs_3_
  74.2 0.9 %shard_map.112 = (f32[80,1792]{1,0:T(8,128)S(1)}, bf16[80,1792]{1,0:T(8,128)(2,1)S(1)}, f32[80,1792]{1,0:T(8,128)S(1)}) custom-call(s32[3]{0:T(128)S(1)} %pad_add_fusion.sc, bf16[320,256]{1,0:T(8,128)(2,1)S(1)} %collective-permute-done.20.refs_0_, bf16[1,256,1792]{2,1,0:T(8,128)(2,1)S(1)} %get-tuple-element.100.refs_1_, f32[320,1792]{1,0:T(8,128)S(1)} %shard_map.110.refs_2_, ...), custom_call_target="tpu_custom_call" | custom-call | flops 220200960 | bytes 3440640 | tf_op jit(solution)/shard_map/pallas_call | solution.py:108
  76.9 7.8 %collective-permute-done.24 = bf16[80,1792]{1,0:T(8,128)(2,1)S(1)} collective-permute-done((bf16[80,1792]{1,0:T(8,128)(2,1)S(1)}, bf16[80,1792]{1,0:T(8,128)(2,1)S(1)}, u32[]{:S(2)}, u32[]{:S(2)}) %collective-permute-start.24) | collective-permute-done | bytes 286752 | tf_op jit(solution)/shard_map/ppermute | solution.py:560
  84.7 0.8 add_convert_fusion.1
  (41 shorter events, 6.1 us)
Async XLA Ops:
  0.6 19.7 %copy-start.4 = (bf16[384,3072]{1,0:T(8,128)(2,1)S(1)}, bf16[384,3072]{1,0:T(8,128)(2,1)}, u32[]{:S(2)}) copy-start(bf16[384,3072]{1,0:T(8,128)(2,1)} %refs_19_.1) | copy-start | bytes 7077892
  0.6 19.7 %copy-start.1 = (bf16[384,64]{0,1:T(8,128)(2,1)S(1)}, bf16[384,64]{0,1:T(8,128)(2,1)}, u32[]{:S(2)}) copy-start(bf16[384,64]{0,1:T(8,128)(2,1)} %param.13) | copy-start | bytes 147460
  2.8 9.2 %collective-permute-start.4 = (bf16[128,384]{1,0:T(8,128)(2,1)S(1)}, bf16[128,384]{1,0:T(8,128)(2,1)S(1)}, u32[]{:S(2)}, u32[]{:S(2)}) collective-permute-start(bf16[128,384]{1,0:T(8,128)(2,1)S(1)} %get-tuple-element.58), channel_id=1, source_target_pairs={{0,4},{4,0},{8,12},{12,8},{1,5},{5,1},{9,13},{13,9},{2,6},{6,2},{1... | collective-permute-start | bytes 294920 | tf_op jit(solution)/shard_map/ppermute | solution.py:323
  5.9 14.1 %collective-permute-start.3 = (bf16[128,384]{1,0:T(8,128)(2,1)S(1)}, bf16[128,384]{1,0:T(8,128)(2,1)S(1)}, u32[]{:S(2)}, u32[]{:S(2)}) collective-permute-start(bf16[128,384]{1,0:T(8,128)(2,1)S(1)} %get-tuple-element.58), channel_id=1, source_target_pairs={{0,8},{4,12},{8,0},{12,4},{1,9},{5,13},{9,1},{13,5},{2,10},{6,14},... | collective-permute-start | bytes 294920 | tf_op jit(solution)/shard_map/ppermute | solution.py:322
  8.5 15.1 %collective-permute-start = (bf16[192,384]{1,0:T(8,128)(2,1)S(1)}, bf16[192,384]{1,0:T(8,128)(2,1)S(1)}, u32[]{:S(2)}, u32[]{:S(2)}) collective-permute-start(bf16[192,384]{1,0:T(8,128)(2,1)S(1)} %get-tuple-element.55), channel_id=1, source_target_pairs={{0,8},{4,12},{8,0},{12,4},{1,9},{5,13},{9,1},{13,5},{2,10},{6,14},... | collective-permute-start | bytes 442376 | tf_op jit(solution)/shard_map/ppermute | solution.py:439
  8.8 14.7 %collective-permute-start.1 = (bf16[192,384]{1,0:T(8,128)(2,1)S(1)}, bf16[192,384]{1,0:T(8,128)(2,1)S(1)}, u32[]{:S(2)}, u32[]{:S(2)}) collective-permute-start(bf16[192,384]{1,0:T(8,128)(2,1)S(1)} %get-tuple-element.56), channel_id=1, source_target_pairs={{0,12},{4,8},{8,4},{12,0},{1,13},{5,9},{9,5},{13,1},{2,14},{6,10},... | collective-permute-start | bytes 442376 | tf_op jit(solution)/shard_map/ppermute | solution.py:439
  11.3 12.3 %collective-permute-start.2 = (bf16[192,384]{1,0:T(8,128)(2,1)S(1)}, bf16[192,384]{1,0:T(8,128)(2,1)S(1)}, u32[]{:S(2)}, u32[]{:S(2)}) collective-permute-start(bf16[192,384]{1,0:T(8,128)(2,1)S(1)} %get-tuple-element.57), channel_id=1, source_target_pairs={{0,4},{4,0},{8,12},{12,8},{1,5},{5,1},{9,13},{13,9},{2,6},{6,2},{1... | collective-permute-start | bytes 442376 | tf_op jit(solution)/shard_map/ppermute | solution.py:439
  20.0 4.6 %collective-permute-start.5 = (bf16[128,384]{1,0:T(8,128)(2,1)S(1)}, bf16[128,384]{1,0:T(8,128)(2,1)S(1)}, u32[]{:S(2)}, u32[]{:S(2)}) collective-permute-start(bf16[128,384]{1,0:T(8,128)(2,1)S(1)} %collective-permute-done.3.refs_3_.refs_11_), channel_id=1, source_target_pairs={{0,4},{4,0},{8,12},{12,8},{1,5},{5,1},{9,13},{13,9},{2,6},{6,2},{1... | collective-permute-start | bytes 294920 | tf_op jit(solution)/shard_map/ppermute | solution.py:325
  25.2 15.0 %collective-permute-start.8 = (bf16[3,128,384]{2,1,0:T(8,128)(2,1)S(1)}, bf16[3,128,384]{2,1,0:T(8,128)(2,1)S(1)}, u32[]{:S(2)}, u32[]{:S(2)}) collective-permute-start(bf16[3,128,384]{2,1,0:T(8,128)(2,1)S(1)} %get-tuple-element.69), channel_id=1, source_target_pairs={{0,2},{1,3},{2,0},{3,1},{4,6},{5,7},{6,4},{7,5},{8,10},{9,11},{10,... | collective-permute-start | bytes 884744 | tf_op jit(solution)/shard_map/ppermute | solution.py:456
  26.7 13.4 %collective-permute-start.9 = (bf16[192,384]{1,0:T(8,128)(2,1)S(1)}, bf16[192,384]{1,0:T(8,128)(2,1)S(1)}, u32[]{:S(2)}, u32[]{:S(2)}) collective-permute-start(bf16[192,384]{1,0:T(8,128)(2,1)S(1)} %get-tuple-element.70), channel_id=1, source_target_pairs={{0,8},{4,12},{8,0},{12,4},{1,9},{5,13},{9,1},{13,5},{2,10},{6,14},... | collective-permute-start | bytes 442376 | tf_op jit(solution)/shard_map/ppermute | solution.py:439
  29.6 10.6 %collective-permute-start.10 = (bf16[192,384]{1,0:T(8,128)(2,1)S(1)}, bf16[192,384]{1,0:T(8,128)(2,1)S(1)}, u32[]{:S(2)}, u32[]{:S(2)}) collective-permute-start(bf16[192,384]{1,0:T(8,128)(2,1)S(1)} %get-tuple-element.71), channel_id=1, source_target_pairs={{0,12},{4,8},{8,4},{12,0},{1,13},{5,9},{9,5},{13,1},{2,14},{6,10},... | collective-permute-start | bytes 442376 | tf_op jit(solution)/shard_map/ppermute | solution.py:439
  31.0 9.2 %collective-permute-start.11 = (bf16[192,384]{1,0:T(8,128)(2,1)S(1)}, bf16[192,384]{1,0:T(8,128)(2,1)S(1)}, u32[]{:S(2)}, u32[]{:S(2)}) collective-permute-start(bf16[192,384]{1,0:T(8,128)(2,1)S(1)} %get-tuple-element.72), channel_id=1, source_target_pairs={{0,4},{4,0},{8,12},{12,8},{1,5},{5,1},{9,13},{13,9},{2,6},{6,2},{1... | collective-permute-start | bytes 442376 | tf_op jit(solution)/shard_map/ppermute | solution.py:439
  31.0 11.8 %copy-start = (bf16[80,1536]{1,0:T(8,128)(2,1)S(1)}, bf16[80,1536]{1,0:T(8,128)(2,1)}, u32[]{:S(2)}) copy-start(bf16[80,1536]{1,0:T(8,128)(2,1)} %refs_0_.3) | copy-start | bytes 737284
  31.0 11.8 %copy-start.2 = (bf16[80,576]{1,0:T(8,128)(2,1)S(1)}, bf16[80,576]{1,0:T(8,128)(2,1)}, u32[]{:S(2)}) copy-start(bf16[80,576]{1,0:T(8,128)(2,1)} %refs_1_.3) | copy-start | bytes 276484
  31.0 11.8 %copy-start.3 = (s32[80]{0:T(128)S(1)}, s32[80]{0:T(128)}, u32[]{:S(2)}) copy-start(s32[80]{0:T(128)} %param.11) | copy-start | bytes 964
  31.0 11.8 %collective-permute-start.6 = (bf16[3,192,384]{2,1,0:T(8,128)(2,1)S(1)}, bf16[3,192,384]{2,1,0:T(8,128)(2,1)S(1)}, u32[]{:S(2)}, u32[]{:S(2)}) collective-permute-start(bf16[3,192,384]{2,1,0:T(8,128)(2,1)S(1)} %get-tuple-element.68), channel_id=1, source_target_pairs={{0,16},{16,0},{1,17},{17,1},{2,18},{18,2},{3,19},{19,3},{4,20},{20... | collective-permute-start | bytes 1327112 | tf_op jit(solution)/shard_map/ppermute | solution.py:455
  40.1 2.6 %collective-permute-start.7 = (bf16[3,128,384]{2,1,0:T(8,128)(2,1)S(1)}, bf16[3,128,384]{2,1,0:T(8,128)(2,1)S(1)}, u32[]{:S(2)}, u32[]{:S(2)}) collective-permute-start(bf16[3,128,384]{2,1,0:T(8,128)(2,1)S(1)} %get-tuple-element.69), channel_id=1, source_target_pairs={{0,1},{1,0},{2,3},{3,2},{4,5},{5,4},{6,7},{7,6},{8,9},{9,8},{10,11... | collective-permute-start | bytes 884744 | tf_op jit(solution)/shard_map/ppermute | solution.py:469
  40.2 2.6 %collective-permute-start.12 = (bf16[3,128,384]{2,1,0:T(8,128)(2,1)S(1)}, bf16[3,128,384]{2,1,0:T(8,128)(2,1)S(1)}, u32[]{:S(2)}, u32[]{:S(2)}) collective-permute-start(bf16[3,128,384]{2,1,0:T(8,128)(2,1)S(1)} %collective-permute-done.8.refs_9_), channel_id=1, source_target_pairs={{0,1},{1,0},{2,3},{3,2},{4,5},{5,4},{6,7},{7,6},{8,9},{9,8},{10,11... | collective-permute-start | bytes 884744 | tf_op jit(solution)/shard_map/ppermute | solution.py:471
  40.7 10.4 %collective-permute-start.13 = (bf16[192,384]{1,0:T(8,128)(2,1)S(1)}, bf16[192,384]{1,0:T(8,128)(2,1)S(1)}, u32[]{:S(2)}, u32[]{:S(2)}) collective-permute-start(bf16[192,384]{1,0:T(8,128)(2,1)S(1)} %collective-permute-done.9.refs_4_), channel_id=1, source_target_pairs={{0,16},{16,0},{1,17},{17,1},{2,18},{18,2},{3,19},{19,3},{4,20},{20... | collective-permute-start | bytes 442376 | tf_op jit(solution)/shard_map/ppermute | solution.py:473
  42.3 8.9 %collective-permute-start.14 = (bf16[192,384]{1,0:T(8,128)(2,1)S(1)}, bf16[192,384]{1,0:T(8,128)(2,1)S(1)}, u32[]{:S(2)}, u32[]{:S(2)}) collective-permute-start(bf16[192,384]{1,0:T(8,128)(2,1)S(1)} %collective-permute-done.10.refs_5_), channel_id=1, source_target_pairs={{0,16},{16,0},{1,17},{17,1},{2,18},{18,2},{3,19},{19,3},{4,20},{20... | collective-permute-start | bytes 442376 | tf_op jit(solution)/shard_map/ppermute | solution.py:473
  47.1 5.8 %collective-permute-start.15 = (bf16[192,384]{1,0:T(8,128)(2,1)S(1)}, bf16[192,384]{1,0:T(8,128)(2,1)S(1)}, u32[]{:S(2)}, u32[]{:S(2)}) collective-permute-start(bf16[192,384]{1,0:T(8,128)(2,1)S(1)} %collective-permute-done.11.refs_6_), channel_id=1, source_target_pairs={{0,16},{16,0},{1,17},{17,1},{2,18},{18,2},{3,19},{19,3},{4,20},{20... | collective-permute-start | bytes 442376 | tf_op jit(solution)/shard_map/ppermute | solution.py:498
  48.6 10.2 %collective-permute-start.19 = (bf16[320,256]{1,0:T(8,128)(2,1)S(1)}, bf16[320,256]{1,0:T(8,128)(2,1)S(1)}, u32[]{:S(2)}, u32[]{:S(2)}) collective-permute-start(bf16[320,256]{1,0:T(8,128)(2,1)S(1)} %get-tuple-element.95.refs_0_), channel_id=1, source_target_pairs={{0,4},{4,0},{8,12},{12,8},{1,5},{5,1},{9,13},{13,9},{2,6},{6,2},{1... | collective-permute-start | bytes 491528 | tf_op jit(solution)/shard_map/ppermute | solution.py:323
  50.3 10.0 %collective-permute-start.18 = (bf16[320,256]{1,0:T(8,128)(2,1)S(1)}, bf16[320,256]{1,0:T(8,128)(2,1)S(1)}, u32[]{:S(2)}, u32[]{:S(2)}) collective-permute-start(bf16[320,256]{1,0:T(8,128)(2,1)S(1)} %get-tuple-element.95.refs_0_), channel_id=1, source_target_pairs={{0,8},{4,12},{8,0},{12,4},{1,9},{5,13},{9,1},{13,5},{2,10},{6,14},... | collective-permute-start | bytes 491528 | tf_op jit(solution)/shard_map/ppermute | solution.py:322
  56.2 11.1 %collective-permute-start.17 = (bf16[320,256]{1,0:T(8,128)(2,1)S(1)}, bf16[320,256]{1,0:T(8,128)(2,1)S(1)}, u32[]{:S(2)}, u32[]{:S(2)}) collective-permute-start(bf16[320,256]{1,0:T(8,128)(2,1)S(1)} %shard_map.108.refs_3_), channel_id=1, source_target_pairs={{0,4},{4,0},{8,12},{12,8},{1,5},{5,1},{9,13},{13,9},{2,6},{6,2},{1... | collective-permute-start | bytes 491528 | tf_op jit(solution)/shard_map/ppermute | solution.py:323
  58.3 9.1 %collective-permute-start.16 = (bf16[320,256]{1,0:T(8,128)(2,1)S(1)}, bf16[320,256]{1,0:T(8,128)(2,1)S(1)}, u32[]{:S(2)}, u32[]{:S(2)}) collective-permute-start(bf16[320,256]{1,0:T(8,128)(2,1)S(1)} %shard_map.108.refs_3_), channel_id=1, source_target_pairs={{0,8},{4,12},{8,0},{12,4},{1,9},{5,13},{9,1},{13,5},{2,10},{6,14},... | collective-permute-start | bytes 491528 | tf_op jit(solution)/shard_map/ppermute | solution.py:322
  60.3 10.6 %collective-permute-start.21 = (bf16[320,256]{1,0:T(8,128)(2,1)S(1)}, bf16[320,256]{1,0:T(8,128)(2,1)S(1)}, u32[]{:S(2)}, u32[]{:S(2)}) collective-permute-start(bf16[320,256]{1,0:T(8,128)(2,1)S(1)} %collective-permute-done.18.refs_2_), channel_id=1, source_target_pairs={{0,4},{4,0},{8,12},{12,8},{1,5},{5,1},{9,13},{13,9},{2,6},{6,2},{1... | collective-permute-start | bytes 491528 | tf_op jit(solution)/shard_map/ppermute | solution.py:325
  67.3 5.9 %collective-permute-start.20 = (bf16[320,256]{1,0:T(8,128)(2,1)S(1)}, bf16[320,256]{1,0:T(8,128)(2,1)S(1)}, u32[]{:S(2)}, u32[]{:S(2)}) collective-permute-start(bf16[320,256]{1,0:T(8,128)(2,1)S(1)} %collective-permute-done.16.refs_2_), channel_id=1, source_target_pairs={{0,4},{4,0},{8,12},{12,8},{1,5},{5,1},{9,13},{13,9},{2,6},{6,2},{1... | collective-permute-start | bytes 491528 | tf_op jit(solution)/shard_map/ppermute | solution.py:325
  74.1 1.6 %collective-permute-start.23 = (bf16[80,1792]{1,0:T(8,128)(2,1)S(1)}, bf16[80,1792]{1,0:T(8,128)(2,1)S(1)}, u32[]{:S(2)}, u32[]{:S(2)}) collective-permute-start(bf16[80,1792]{1,0:T(8,128)(2,1)S(1)} %shard_map.111.refs_3_), channel_id=1, source_target_pairs={{0,1},{1,0},{2,3},{3,2},{4,5},{5,4},{6,7},{7,6},{8,9},{9,8},{10,11... | collective-permute-start | bytes 860168 | tf_op jit(solution)/shard_map/ppermute | solution.py:559
  75.1 1.8 %collective-permute-start.22 = (bf16[80,1792]{1,0:T(8,128)(2,1)S(1)}, bf16[80,1792]{1,0:T(8,128)(2,1)S(1)}, u32[]{:S(2)}, u32[]{:S(2)}) collective-permute-start(bf16[80,1792]{1,0:T(8,128)(2,1)S(1)} %get-tuple-element.106), channel_id=1, source_target_pairs={{0,1},{1,0},{2,3},{3,2},{4,5},{5,4},{6,7},{7,6},{8,9},{9,8},{10,11... | collective-permute-start | bytes 860168 | tf_op jit(solution)/shard_map/ppermute | solution.py:561
  75.8 8.9 %collective-permute-start.24 = (bf16[80,1792]{1,0:T(8,128)(2,1)S(1)}, bf16[80,1792]{1,0:T(8,128)(2,1)S(1)}, u32[]{:S(2)}, u32[]{:S(2)}) collective-permute-start(bf16[80,1792]{1,0:T(8,128)(2,1)S(1)} %add_convert_fusion.2), channel_id=1, source_target_pairs={{0,2},{1,3},{2,0},{3,1},{4,6},{5,7},{6,4},{7,5},{8,10},{9,11},{10,... | collective-permute-start | bytes 860168 | tf_op jit(solution)/shard_map/ppermute | solution.py:560

commit v10 on v9

--- a/solution.py
+++ b/solution.py
@@ -450,7 +450,9 @@
     moved = [exchange(units[: n - 1])]
     held = lax.optimization_barrier((*moved[0], *packs, merged))
     moved[0], packs, merged = list(held[: n - 1]), list(held[n - 1 : -1]), held[-1]
-    moved.append(exchange(units[n - 1 :]))
+    later = dict(zip(partners(n), units[n - 1 :]))
+    later = {b: lax.ppermute(later[b], "seq", flipped(n, b)) for b in (3, 2, 1)}
+    moved.append([later[b] for b in partners(n)])
     share, stack = join(moved[0], packs)
     passed = [[lax.ppermute(share, "groups", flipped(2, 1))]]
     across = lax.ppermute(stack, "head", flipped(nh, 2))

time: 85.7 us -> 85.7 us (level)
    ppermute x0 -> x3, waiting for transfers between devices: none -> 5.85 us  [by_heads(): later = {b: lax.ppermute(later[b], 'seq', flipped(n, b)) for b in (3, 2, 1)}]
    ppermute x6 -> x3, waiting for transfers between devices: 5.85 us -> 0.01 us  [exchange(): lax.ppermute(p, 'seq', flipped(n, bits))]
    ppermute x0 -> x3, starting transfers between devices: none -> 4.23 us  [by_heads(): later = {b: lax.ppermute(later[b], 'seq', flipped(n, b)) for b in (3, 2, 1)}]
    ppermute x6 -> x3, starting transfers between devices: 7.72 us -> 3.49 us  [exchange(): lax.ppermute(p, 'seq', flipped(n, bits))]
where the time goes in v10:
time: 85.7 us; the launch traced here: 85.5 us
  waiting for transfers between devices  31.3 us (37%)
  starting transfers between devices  30 us (35%)
  Pallas kernels  19.3 us (23%)
  matrix products  3.19 us (4%)
  other arithmetic  0.95 us (1%)
    pallas_call x9, Pallas kernels, call(): pl.pallas_call(body, out_shape=outs, grid_spec=pltpu.PrefetchScalarGridSp...  19.3 us
    ppermute x3, waiting for transfers between devices, gather_line(): two = lax.ppermute(x, 'seq', flipped(4, 2))  9.47 us
    ppermute x1, waiting for transfers between devices, by_heads(): got = lax.ppermute(away.astype(bf), 'head', flipped(nh, 2))  7.84 us
    ppermute x3, starting transfers between devices, gather_line(): one = lax.ppermute(x, 'seq', flipped(4, 1))  6.79 us
    ppermute x3, waiting for transfers between devices, by_heads(): later = {b: lax.ppermute(later[b], 'seq', flipped(n, b)) for b in (3, 2, 1)}  5.85 us
    ppermute x3, starting transfers between devices, by_heads(): later = {b: lax.ppermute(later[b], 'seq', flipped(n, b)) for b in (3, 2, 1)}  4.23 us
    ppermute x3, starting transfers between devices, gather_line(): two = lax.ppermute(x, 'seq', flipped(4, 2))  4.01 us
    ppermute x3, starting transfers between devices, exchange(): lax.ppermute(p, 'seq', flipped(n, bits))  3.49 us
  transfers between devices with their start and end apart: 25, of which 10 were waited for; matrix products, arithmetic and copies ran while one was open for 4% of the time, Pallas kernels for 18%

profile of v10, /device:TPU:0, one launch (start us, length us, event | category | flops | bytes accessed | tf_op | source)
XLA Modules:
  0.0 85.5 jit_solution(6894444948958793593)
XLA Ops:
  0.7 2.0 %shard_map.104 = (bf16[128,384]{1,0:T(8,128)(2,1)S(1)}, bf16[192,384]{1,0:T(8,128)(2,1)S(1)}, bf16[192,384]{1,0:T(8,128)(2,1)S(1)}, bf16[192,384]{1,0:T(8,128)(2...) custom-call(s32[3]{0:T(128)S(1)} %pad_add_fusion.sc, ...), custom_call_target="tpu_custom_call" | custom-call | bytes 2359296 | tf_op jit(solution)/shard_map/pallas_call | solution.py:108
  2.8 3.1 %collective-permute-start.4 = (bf16[128,384]{1,0:T(8,128)(2,1)S(1)}, bf16[128,384]{1,0:T(8,128)(2,1)S(1)}, u32[]{:S(2)}, u32[]{:S(2)}) collective-permute-start(bf16[128,384]{1,0:T(8,128)(2,1)S(1)} %get-tuple-element.58), channel_id=1, source_target_pairs={{0,4},{4,0},{8,12},{12,8},{1,5},{5,1},{9,13},{13,9},{2,6},{6,2},{1... | collective-permute-start | bytes 294920 | tf_op jit(solution)/shard_map/ppermute | solution.py:323
  5.9 2.6 %collective-permute-start.3 = (bf16[128,384]{1,0:T(8,128)(2,1)S(1)}, bf16[128,384]{1,0:T(8,128)(2,1)S(1)}, u32[]{:S(2)}, u32[]{:S(2)}) collective-permute-start(bf16[128,384]{1,0:T(8,128)(2,1)S(1)} %get-tuple-element.58), channel_id=1, source_target_pairs={{0,8},{4,12},{8,0},{12,4},{1,9},{5,13},{9,1},{13,5},{2,10},{6,14},... | collective-permute-start | bytes 294920 | tf_op jit(solution)/shard_map/ppermute | solution.py:322
  8.8 2.5 %collective-permute-start.1 = (bf16[192,384]{1,0:T(8,128)(2,1)S(1)}, bf16[192,384]{1,0:T(8,128)(2,1)S(1)}, u32[]{:S(2)}, u32[]{:S(2)}) collective-permute-start(bf16[192,384]{1,0:T(8,128)(2,1)S(1)} %get-tuple-element.56), channel_id=1, source_target_pairs={{0,12},{4,8},{8,4},{12,0},{1,13},{5,9},{9,5},{13,1},{2,14},{6,10},... | collective-permute-start | bytes 442376 | tf_op jit(solution)/shard_map/ppermute | solution.py:439
  12.0 8.0 %collective-permute-done.3.refs_3_.refs_11_ = bf16[128,384]{1,0:T(8,128)(2,1)S(1)} collective-permute-done((bf16[128,384]{1,0:T(8,128)(2,1)S(1)}, bf16[128,384]{1,0:T(8,128)(2,1)S(1)}, u32[]{:S(2)}, u32[]{:S(2)}) %collective-permute-start.3) | collective-permute-done | bytes 98336 | tf_op jit(solution)/shard_map/ppermute | solution.py:322
  20.3 3.2 %add_convert_fusion = bf16[384,3072]{1,0:T(8,128)(2,1)} fusion(bf16[384,3072]{1,0:T(8,128)(2,1)S(1)} %copy-done.4, bf16[384,64]{0,1:T(8,128)(2,1)S(1)} %copy-done.1, bf16[64,3072]{1,0:T(8,128)(2,1)} %refs_18_.1), kind=kOutput, calls=%fused_computation | convolution fusion | flops 154533888 | bytes 5160960 | tf_op jit(solution)/shard_map/dot_general | solution.py:446
  23.5 1.0 %collective-permute-done.5.refs_4_.refs_12_ = bf16[128,384]{1,0:T(8,128)(2,1)S(1)} collective-permute-done((bf16[128,384]{1,0:T(8,128)(2,1)S(1)}, bf16[128,384]{1,0:T(8,128)(2,1)S(1)}, u32[]{:S(2)}, u32[]{:S(2)}) %collective-permute-start.5) | collective-permute-done | bytes 98336 | tf_op jit(solution)/shard_map/ppermute | solution.py:325
  25.2 1.6 %collective-permute-start.8 = (bf16[3,128,384]{2,1,0:T(8,128)(2,1)S(1)}, bf16[3,128,384]{2,1,0:T(8,128)(2,1)S(1)}, u32[]{:S(2)}, u32[]{:S(2)}) collective-permute-start(bf16[3,128,384]{2,1,0:T(8,128)(2,1)S(1)} %get-tuple-element.69), channel_id=1, source_target_pairs={{0,2},{1,3},{2,0},{3,1},{4,6},{5,7},{6,4},{7,5},{8,10},{9,11},{10,... | collective-permute-start | bytes 884744 | tf_op jit(solution)/shard_map/ppermute | solution.py:458
  26.7 2.8 %collective-permute-start.9 = (bf16[192,384]{1,0:T(8,128)(2,1)S(1)}, bf16[192,384]{1,0:T(8,128)(2,1)S(1)}, u32[]{:S(2)}, u32[]{:S(2)}) collective-permute-start(bf16[192,384]{1,0:T(8,128)(2,1)S(1)} %get-tuple-element.70), channel_id=1, source_target_pairs={{0,8},{4,12},{8,0},{12,4},{1,9},{5,13},{9,1},{13,5},{2,10},{6,14},... | collective-permute-start | bytes 442376 | tf_op jit(solution)/shard_map/ppermute | solution.py:454
  29.6 1.4 %collective-permute-start.10 = (bf16[192,384]{1,0:T(8,128)(2,1)S(1)}, bf16[192,384]{1,0:T(8,128)(2,1)S(1)}, u32[]{:S(2)}, u32[]{:S(2)}) collective-permute-start(bf16[192,384]{1,0:T(8,128)(2,1)S(1)} %get-tuple-element.71), channel_id=1, source_target_pairs={{0,12},{4,8},{8,4},{12,0},{1,13},{5,9},{9,5},{13,1},{2,14},{6,10},... | collective-permute-start | bytes 442376 | tf_op jit(solution)/shard_map/ppermute | solution.py:454
  31.0 1.6 %collective-permute-start.6 = (bf16[3,192,384]{2,1,0:T(8,128)(2,1)S(1)}, bf16[3,192,384]{2,1,0:T(8,128)(2,1)S(1)}, u32[]{:S(2)}, u32[]{:S(2)}) collective-permute-start(bf16[3,192,384]{2,1,0:T(8,128)(2,1)S(1)} %get-tuple-element.68), channel_id=1, source_target_pairs={{0,16},{16,0},{1,17},{17,1},{2,18},{18,2},{3,19},{19,3},{4,20},{20... | collective-permute-start | bytes 1327112 | tf_op jit(solution)/shard_map/ppermute | solution.py:457
  32.6 1.7 %shard_map.106 = (bf16[64,384]{1,0:T(8,128)(2,1)S(1)}, bf16[384,384]{1,0:T(8,128)(2,1)S(1)}, bf16[2,128,512]{2,1,0:T(8,128)(2,1)S(1)}, bf16[2,512,128]{2,1,0:T(8,128)(2,1)S(1)}) custom-call(s32[3]{0:T(128)S(1)} %pad_add_fusion.sc, bf16[64,3072]{1,0:T(8,128)(2,1)} %refs_18_.1, bf16[384,3072]{1,0:T(8,128)(2,1)} %refs_19_.1, bf16[16,128,512]{2,1,0:T(8,128)(2,1)} %refs_20_.1, ...), custom_call_target="tpu_custom_call" | custom-call | bytes 1736704 | tf_op jit(solution)/shard_map/pallas_call | solution.py:108
  34.3 5.8 %collective-permute-done.9.refs_4_ = bf16[192,384]{1,0:T(8,128)(2,1)S(1)} collective-permute-done((bf16[192,384]{1,0:T(8,128)(2,1)S(1)}, bf16[192,384]{1,0:T(8,128)(2,1)S(1)}, u32[]{:S(2)}, u32[]{:S(2)}) %collective-permute-start.9) | collective-permute-done | bytes 147488 | tf_op jit(solution)/shard_map/ppermute | solution.py:454
  40.7 1.5 %collective-permute-start.13 = (bf16[192,384]{1,0:T(8,128)(2,1)S(1)}, bf16[192,384]{1,0:T(8,128)(2,1)S(1)}, u32[]{:S(2)}, u32[]{:S(2)}) collective-permute-start(bf16[192,384]{1,0:T(8,128)(2,1)S(1)} %collective-permute-done.9.refs_4_), channel_id=1, source_target_pairs={{0,16},{16,0},{1,17},{17,1},{2,18},{18,2},{3,19},{19,3},{4,20},{20... | collective-permute-start | bytes 442376 | tf_op jit(solution)/shard_map/ppermute | solution.py:475
  42.8 4.3 %shard_map.107 = (bf16[320,256]{1,0:T(8,128)(2,1)S(1)}, bf16[320,1536]{1,0:T(8,128)(2,1)S(1)}, bf16[320,576]{1,0:T(8,128)(2,1)S(1)}, bf16[64,1536]{1,0:T(8,128)(...) custom-call(s32[3]{0:T(128)S(1)} %pad_add_fusion.sc, ...), custom_call_target="tpu_custom_call" | custom-call | flops 964689920 | bytes 2359296 | tf_op jit(solution)/shard_map/pallas_call | solution.py:108
  47.1 1.6 %collective-permute-start.15 = (bf16[192,384]{1,0:T(8,128)(2,1)S(1)}, bf16[192,384]{1,0:T(8,128)(2,1)S(1)}, u32[]{:S(2)}, u32[]{:S(2)}) collective-permute-start(bf16[192,384]{1,0:T(8,128)(2,1)S(1)} %collective-permute-done.11.refs_6_), channel_id=1, source_target_pairs={{0,16},{16,0},{1,17},{17,1},{2,18},{18,2},{3,19},{19,3},{4,20},{20... | collective-permute-start | bytes 442376 | tf_op jit(solution)/shard_map/ppermute | solution.py:500
  48.6 1.6 %collective-permute-start.19 = (bf16[320,256]{1,0:T(8,128)(2,1)S(1)}, bf16[320,256]{1,0:T(8,128)(2,1)S(1)}, u32[]{:S(2)}, u32[]{:S(2)}) collective-permute-start(bf16[320,256]{1,0:T(8,128)(2,1)S(1)} %get-tuple-element.95.refs_0_), channel_id=1, source_target_pairs={{0,4},{4,0},{8,12},{12,8},{1,5},{5,1},{9,13},{13,9},{2,6},{6,2},{1... | collective-permute-start | bytes 491528 | tf_op jit(solution)/shard_map/ppermute | solution.py:323
  50.3 0.9 %collective-permute-start.18 = (bf16[320,256]{1,0:T(8,128)(2,1)S(1)}, bf16[320,256]{1,0:T(8,128)(2,1)S(1)}, u32[]{:S(2)}, u32[]{:S(2)}) collective-permute-start(bf16[320,256]{1,0:T(8,128)(2,1)S(1)} %get-tuple-element.95.refs_0_), channel_id=1, source_target_pairs={{0,8},{4,12},{8,0},{12,4},{1,9},{5,13},{9,1},{13,5},{2,10},{6,14},... | collective-permute-start | bytes 491528 | tf_op jit(solution)/shard_map/ppermute | solution.py:322
  51.2 1.7 %collective-permute-done.15.refs_9_ = bf16[192,384]{1,0:T(8,128)(2,1)S(1)} collective-permute-done((bf16[192,384]{1,0:T(8,128)(2,1)S(1)}, bf16[192,384]{1,0:T(8,128)(2,1)S(1)}, u32[]{:S(2)}, u32[]{:S(2)}) %collective-permute-start.15) | collective-permute-done | bytes 147488 | tf_op jit(solution)/shard_map/ppermute | solution.py:500
  52.9 3.3 %shard_map.108.refs_3_ = bf16[320,256]{1,0:T(8,128)(2,1)S(1)} custom-call(s32[3]{0:T(128)S(1)} %pad_add_fusion.sc, bf16[320,1536]{1,0:T(8,128)(2,1)S(1)} %get-tuple-element.82.refs_0_, bf16[320,576]{1,0:T(8,128)(2,1)S(1)} %get-tuple-element.83.refs_1_, bf16[64,1536]{1,0:T(8,128)(2,1)S(1)} %get-tuple-element.84.refs_2_, ...), custom_call_target="tpu_custom_call" | custom-call | flops 964689920 | bytes 2359296 | tf_op jit(solution)/shard_map/pallas_call | solution.py:108
  56.2 2.1 %collective-permute-start.17 = (bf16[320,256]{1,0:T(8,128)(2,1)S(1)}, bf16[320,256]{1,0:T(8,128)(2,1)S(1)}, u32[]{:S(2)}, u32[]{:S(2)}) collective-permute-start(bf16[320,256]{1,0:T(8,128)(2,1)S(1)} %shard_map.108.refs_3_), channel_id=1, source_target_pairs={{0,4},{4,0},{8,12},{12,8},{1,5},{5,1},{9,13},{13,9},{2,6},{6,2},{1... | collective-permute-start | bytes 491528 | tf_op jit(solution)/shard_map/ppermute | solution.py:323
  58.8 1.5 %collective-permute-done.18.refs_2_ = bf16[320,256]{1,0:T(8,128)(2,1)S(1)} collective-permute-done((bf16[320,256]{1,0:T(8,128)(2,1)S(1)}, bf16[320,256]{1,0:T(8,128)(2,1)S(1)}, u32[]{:S(2)}, u32[]{:S(2)}) %collective-permute-start.18) | collective-permute-done | bytes 163872 | tf_op jit(solution)/shard_map/ppermute | solution.py:322
  60.8 4.0 %shard_map.109 = (f32[320,1792]{1,0:T(8,128)S(1)}, f32[8,128]{1,0:T(8,128)S(1)}, bf16[3,256,1792]{2,1,0:T(8,128)(2,1)S(1)}, bf16[1,256,1792]{2,1,0:T(8,128)(2,1)S(1)}) custom-call(s32[3]{0:T(128)S(1)} %pad_add_fusion.sc, bf16[320,256]{1,0:T(8,128)(2,1)S(1)} %get-tuple-element.95.refs_0_, bf16[320,256]{1,0:T(8,128)(2,1)S(1)} %collective-permute-done.19.refs_1_, ...), custom_call_target="tpu_custom_call" | custom-call | flops 1174405120 | bytes 3670016 | tf_op jit(solution)/shard_map/pallas_call | solution.py:108
  64.7 2.6 %collective-permute-done.17.refs_1_ = bf16[320,256]{1,0:T(8,128)(2,1)S(1)} collective-permute-done((bf16[320,256]{1,0:T(8,128)(2,1)S(1)}, bf16[320,256]{1,0:T(8,128)(2,1)S(1)}, u32[]{:S(2)}, u32[]{:S(2)}) %collective-permute-start.17) | collective-permute-done | bytes 163872 | tf_op jit(solution)/shard_map/ppermute | solution.py:323
  67.3 2.0 %collective-permute-start.20 = (bf16[320,256]{1,0:T(8,128)(2,1)S(1)}, bf16[320,256]{1,0:T(8,128)(2,1)S(1)}, u32[]{:S(2)}, u32[]{:S(2)}) collective-permute-start(bf16[320,256]{1,0:T(8,128)(2,1)S(1)} %collective-permute-done.16.refs_2_), channel_id=1, source_target_pairs={{0,4},{4,0},{8,12},{12,8},{1,5},{5,1},{9,13},{13,9},{2,6},{6,2},{1... | collective-permute-start | bytes 491528 | tf_op jit(solution)/shard_map/ppermute | solution.py:325
  69.4 1.5 %collective-permute-done.21.refs_0_ = bf16[320,256]{1,0:T(8,128)(2,1)S(1)} collective-permute-done((bf16[320,256]{1,0:T(8,128)(2,1)S(1)}, bf16[320,256]{1,0:T(8,128)(2,1)S(1)}, u32[]{:S(2)}, u32[]{:S(2)}) %collective-permute-start.21) | collective-permute-done | bytes 163872 | tf_op jit(solution)/shard_map/ppermute | solution.py:325
  70.8 1.6 %shard_map.110.refs_2_ = f32[320,1792]{1,0:T(8,128)S(1)} custom-call(s32[3]{0:T(128)S(1)} %pad_add_fusion.sc, bf16[320,256]{1,0:T(8,128)(2,1)S(1)} %collective-permute-done.21.refs_0_, bf16[320,256]{1,0:T(8,128)(2,1)S(1)} %collective-permute-done.17.refs_1_, bf16[320,256]{1,0:T(8,128)(2,1)S(1)} %collective-permute-done.16.refs_2_, ...), custom_call_target="tpu_custom_call", output_to_operand_aliasing={{}: (5, {})} | custom-call | flops 880803840 | bytes 2752512 | tf_op jit(solution)/shard_map/pallas_call | solution.py:108
  72.5 0.8 collective-permute-done.20.refs_0_
  73.2 0.8 shard_map.111.refs_3_
  74.2 0.9 %shard_map.112 = (f32[80,1792]{1,0:T(8,128)S(1)}, bf16[80,1792]{1,0:T(8,128)(2,1)S(1)}, f32[80,1792]{1,0:T(8,128)S(1)}) custom-call(s32[3]{0:T(128)S(1)} %pad_add_fusion.sc, bf16[320,256]{1,0:T(8,128)(2,1)S(1)} %collective-permute-done.20.refs_0_, bf16[1,256,1792]{2,1,0:T(8,128)(2,1)S(1)} %get-tuple-element.100.refs_1_, f32[320,1792]{1,0:T(8,128)S(1)} %shard_map.110.refs_2_, ...), custom_call_target="tpu_custom_call" | custom-call | flops 220200960 | bytes 3440640 | tf_op jit(solution)/shard_map/pallas_call | solution.py:108
  76.9 7.8 %collective-permute-done.24 = bf16[80,1792]{1,0:T(8,128)(2,1)S(1)} collective-permute-done((bf16[80,1792]{1,0:T(8,128)(2,1)S(1)}, bf16[80,1792]{1,0:T(8,128)(2,1)S(1)}, u32[]{:S(2)}, u32[]{:S(2)}) %collective-permute-start.24) | collective-permute-done | bytes 286752 | tf_op jit(solution)/shard_map/ppermute | solution.py:562
  84.7 0.8 add_convert_fusion.1
  (41 shorter events, 6.1 us)
Async XLA Ops:
  0.6 19.7 %copy-start.4 = (bf16[384,3072]{1,0:T(8,128)(2,1)S(1)}, bf16[384,3072]{1,0:T(8,128)(2,1)}, u32[]{:S(2)}) copy-start(bf16[384,3072]{1,0:T(8,128)(2,1)} %refs_19_.1) | copy-start | bytes 7077892
  0.6 19.7 %copy-start.1 = (bf16[384,64]{0,1:T(8,128)(2,1)S(1)}, bf16[384,64]{0,1:T(8,128)(2,1)}, u32[]{:S(2)}) copy-start(bf16[384,64]{0,1:T(8,128)(2,1)} %param.13) | copy-start | bytes 147460
  2.8 9.2 %collective-permute-start.4 = (bf16[128,384]{1,0:T(8,128)(2,1)S(1)}, bf16[128,384]{1,0:T(8,128)(2,1)S(1)}, u32[]{:S(2)}, u32[]{:S(2)}) collective-permute-start(bf16[128,384]{1,0:T(8,128)(2,1)S(1)} %get-tuple-element.58), channel_id=1, source_target_pairs={{0,4},{4,0},{8,12},{12,8},{1,5},{5,1},{9,13},{13,9},{2,6},{6,2},{1... | collective-permute-start | bytes 294920 | tf_op jit(solution)/shard_map/ppermute | solution.py:323
  5.9 14.1 %collective-permute-start.3 = (bf16[128,384]{1,0:T(8,128)(2,1)S(1)}, bf16[128,384]{1,0:T(8,128)(2,1)S(1)}, u32[]{:S(2)}, u32[]{:S(2)}) collective-permute-start(bf16[128,384]{1,0:T(8,128)(2,1)S(1)} %get-tuple-element.58), channel_id=1, source_target_pairs={{0,8},{4,12},{8,0},{12,4},{1,9},{5,13},{9,1},{13,5},{2,10},{6,14},... | collective-permute-start | bytes 294920 | tf_op jit(solution)/shard_map/ppermute | solution.py:322
  8.5 15.1 %collective-permute-start = (bf16[192,384]{1,0:T(8,128)(2,1)S(1)}, bf16[192,384]{1,0:T(8,128)(2,1)S(1)}, u32[]{:S(2)}, u32[]{:S(2)}) collective-permute-start(bf16[192,384]{1,0:T(8,128)(2,1)S(1)} %get-tuple-element.55), channel_id=1, source_target_pairs={{0,8},{4,12},{8,0},{12,4},{1,9},{5,13},{9,1},{13,5},{2,10},{6,14},... | collective-permute-start | bytes 442376 | tf_op jit(solution)/shard_map/ppermute | solution.py:439
  8.8 14.7 %collective-permute-start.1 = (bf16[192,384]{1,0:T(8,128)(2,1)S(1)}, bf16[192,384]{1,0:T(8,128)(2,1)S(1)}, u32[]{:S(2)}, u32[]{:S(2)}) collective-permute-start(bf16[192,384]{1,0:T(8,128)(2,1)S(1)} %get-tuple-element.56), channel_id=1, source_target_pairs={{0,12},{4,8},{8,4},{12,0},{1,13},{5,9},{9,5},{13,1},{2,14},{6,10},... | collective-permute-start | bytes 442376 | tf_op jit(solution)/shard_map/ppermute | solution.py:439
  11.3 12.3 %collective-permute-start.2 = (bf16[192,384]{1,0:T(8,128)(2,1)S(1)}, bf16[192,384]{1,0:T(8,128)(2,1)S(1)}, u32[]{:S(2)}, u32[]{:S(2)}) collective-permute-start(bf16[192,384]{1,0:T(8,128)(2,1)S(1)} %get-tuple-element.57), channel_id=1, source_target_pairs={{0,4},{4,0},{8,12},{12,8},{1,5},{5,1},{9,13},{13,9},{2,6},{6,2},{1... | collective-permute-start | bytes 442376 | tf_op jit(solution)/shard_map/ppermute | solution.py:439
  20.0 4.6 %collective-permute-start.5 = (bf16[128,384]{1,0:T(8,128)(2,1)S(1)}, bf16[128,384]{1,0:T(8,128)(2,1)S(1)}, u32[]{:S(2)}, u32[]{:S(2)}) collective-permute-start(bf16[128,384]{1,0:T(8,128)(2,1)S(1)} %collective-permute-done.3.refs_3_.refs_11_), channel_id=1, source_target_pairs={{0,4},{4,0},{8,12},{12,8},{1,5},{5,1},{9,13},{13,9},{2,6},{6,2},{1... | collective-permute-start | bytes 294920 | tf_op jit(solution)/shard_map/ppermute | solution.py:325
  25.2 15.0 %collective-permute-start.8 = (bf16[3,128,384]{2,1,0:T(8,128)(2,1)S(1)}, bf16[3,128,384]{2,1,0:T(8,128)(2,1)S(1)}, u32[]{:S(2)}, u32[]{:S(2)}) collective-permute-start(bf16[3,128,384]{2,1,0:T(8,128)(2,1)S(1)} %get-tuple-element.69), channel_id=1, source_target_pairs={{0,2},{1,3},{2,0},{3,1},{4,6},{5,7},{6,4},{7,5},{8,10},{9,11},{10,... | collective-permute-start | bytes 884744 | tf_op jit(solution)/shard_map/ppermute | solution.py:458
  26.7 13.4 %collective-permute-start.9 = (bf16[192,384]{1,0:T(8,128)(2,1)S(1)}, bf16[192,384]{1,0:T(8,128)(2,1)S(1)}, u32[]{:S(2)}, u32[]{:S(2)}) collective-permute-start(bf16[192,384]{1,0:T(8,128)(2,1)S(1)} %get-tuple-element.70), channel_id=1, source_target_pairs={{0,8},{4,12},{8,0},{12,4},{1,9},{5,13},{9,1},{13,5},{2,10},{6,14},... | collective-permute-start | bytes 442376 | tf_op jit(solution)/shard_map/ppermute | solution.py:454
  29.6 10.6 %collective-permute-start.10 = (bf16[192,384]{1,0:T(8,128)(2,1)S(1)}, bf16[192,384]{1,0:T(8,128)(2,1)S(1)}, u32[]{:S(2)}, u32[]{:S(2)}) collective-permute-start(bf16[192,384]{1,0:T(8,128)(2,1)S(1)} %get-tuple-element.71), channel_id=1, source_target_pairs={{0,12},{4,8},{8,4},{12,0},{1,13},{5,9},{9,5},{13,1},{2,14},{6,10},... | collective-permute-start | bytes 442376 | tf_op jit(solution)/shard_map/ppermute | solution.py:454
  31.0 9.2 %collective-permute-start.11 = (bf16[192,384]{1,0:T(8,128)(2,1)S(1)}, bf16[192,384]{1,0:T(8,128)(2,1)S(1)}, u32[]{:S(2)}, u32[]{:S(2)}) collective-permute-start(bf16[192,384]{1,0:T(8,128)(2,1)S(1)} %get-tuple-element.72), channel_id=1, source_target_pairs={{0,4},{4,0},{8,12},{12,8},{1,5},{5,1},{9,13},{13,9},{2,6},{6,2},{1... | collective-permute-start | bytes 442376 | tf_op jit(solution)/shard_map/ppermute | solution.py:454
  31.0 11.8 %copy-start = (bf16[80,1536]{1,0:T(8,128)(2,1)S(1)}, bf16[80,1536]{1,0:T(8,128)(2,1)}, u32[]{:S(2)}) copy-start(bf16[80,1536]{1,0:T(8,128)(2,1)} %refs_0_.3) | copy-start | bytes 737284
  31.0 11.8 %copy-start.2 = (bf16[80,576]{1,0:T(8,128)(2,1)S(1)}, bf16[80,576]{1,0:T(8,128)(2,1)}, u32[]{:S(2)}) copy-start(bf16[80,576]{1,0:T(8,128)(2,1)} %refs_1_.3) | copy-start | bytes 276484
  31.0 11.8 %copy-start.3 = (s32[80]{0:T(128)S(1)}, s32[80]{0:T(128)}, u32[]{:S(2)}) copy-start(s32[80]{0:T(128)} %param.11) | copy-start | bytes 964
  31.0 11.8 %collective-permute-start.6 = (bf16[3,192,384]{2,1,0:T(8,128)(2,1)S(1)}, bf16[3,192,384]{2,1,0:T(8,128)(2,1)S(1)}, u32[]{:S(2)}, u32[]{:S(2)}) collective-permute-start(bf16[3,192,384]{2,1,0:T(8,128)(2,1)S(1)} %get-tuple-element.68), channel_id=1, source_target_pairs={{0,16},{16,0},{1,17},{17,1},{2,18},{18,2},{3,19},{19,3},{4,20},{20... | collective-permute-start | bytes 1327112 | tf_op jit(solution)/shard_map/ppermute | solution.py:457
  40.1 2.6 %collective-permute-start.7 = (bf16[3,128,384]{2,1,0:T(8,128)(2,1)S(1)}, bf16[3,128,384]{2,1,0:T(8,128)(2,1)S(1)}, u32[]{:S(2)}, u32[]{:S(2)}) collective-permute-start(bf16[3,128,384]{2,1,0:T(8,128)(2,1)S(1)} %get-tuple-element.69), channel_id=1, source_target_pairs={{0,1},{1,0},{2,3},{3,2},{4,5},{5,4},{6,7},{7,6},{8,9},{9,8},{10,11... | collective-permute-start | bytes 884744 | tf_op jit(solution)/shard_map/ppermute | solution.py:471
  40.2 2.6 %collective-permute-start.12 = (bf16[3,128,384]{2,1,0:T(8,128)(2,1)S(1)}, bf16[3,128,384]{2,1,0:T(8,128)(2,1)S(1)}, u32[]{:S(2)}, u32[]{:S(2)}) collective-permute-start(bf16[3,128,384]{2,1,0:T(8,128)(2,1)S(1)} %collective-permute-done.8.refs_9_), channel_id=1, source_target_pairs={{0,1},{1,0},{2,3},{3,2},{4,5},{5,4},{6,7},{7,6},{8,9},{9,8},{10,11... | collective-permute-start | bytes 884744 | tf_op jit(solution)/shard_map/ppermute | solution.py:473
  40.7 10.4 %collective-permute-start.13 = (bf16[192,384]{1,0:T(8,128)(2,1)S(1)}, bf16[192,384]{1,0:T(8,128)(2,1)S(1)}, u32[]{:S(2)}, u32[]{:S(2)}) collective-permute-start(bf16[192,384]{1,0:T(8,128)(2,1)S(1)} %collective-permute-done.9.refs_4_), channel_id=1, source_target_pairs={{0,16},{16,0},{1,17},{17,1},{2,18},{18,2},{3,19},{19,3},{4,20},{20... | collective-permute-start | bytes 442376 | tf_op jit(solution)/shard_map/ppermute | solution.py:475
  42.3 8.9 %collective-permute-start.14 = (bf16[192,384]{1,0:T(8,128)(2,1)S(1)}, bf16[192,384]{1,0:T(8,128)(2,1)S(1)}, u32[]{:S(2)}, u32[]{:S(2)}) collective-permute-start(bf16[192,384]{1,0:T(8,128)(2,1)S(1)} %collective-permute-done.10.refs_5_), channel_id=1, source_target_pairs={{0,16},{16,0},{1,17},{17,1},{2,18},{18,2},{3,19},{19,3},{4,20},{20... | collective-permute-start | bytes 442376 | tf_op jit(solution)/shard_map/ppermute | solution.py:475
  47.1 5.8 %collective-permute-start.15 = (bf16[192,384]{1,0:T(8,128)(2,1)S(1)}, bf16[192,384]{1,0:T(8,128)(2,1)S(1)}, u32[]{:S(2)}, u32[]{:S(2)}) collective-permute-start(bf16[192,384]{1,0:T(8,128)(2,1)S(1)} %collective-permute-done.11.refs_6_), channel_id=1, source_target_pairs={{0,16},{16,0},{1,17},{17,1},{2,18},{18,2},{3,19},{19,3},{4,20},{20... | collective-permute-start | bytes 442376 | tf_op jit(solution)/shard_map/ppermute | solution.py:500
  48.6 10.2 %collective-permute-start.19 = (bf16[320,256]{1,0:T(8,128)(2,1)S(1)}, bf16[320,256]{1,0:T(8,128)(2,1)S(1)}, u32[]{:S(2)}, u32[]{:S(2)}) collective-permute-start(bf16[320,256]{1,0:T(8,128)(2,1)S(1)} %get-tuple-element.95.refs_0_), channel_id=1, source_target_pairs={{0,4},{4,0},{8,12},{12,8},{1,5},{5,1},{9,13},{13,9},{2,6},{6,2},{1... | collective-permute-start | bytes 491528 | tf_op jit(solution)/shard_map/ppermute | solution.py:323
  50.3 10.0 %collective-permute-start.18 = (bf16[320,256]{1,0:T(8,128)(2,1)S(1)}, bf16[320,256]{1,0:T(8,128)(2,1)S(1)}, u32[]{:S(2)}, u32[]{:S(2)}) collective-permute-start(bf16[320,256]{1,0:T(8,128)(2,1)S(1)} %get-tuple-element.95.refs_0_), channel_id=1, source_target_pairs={{0,8},{4,12},{8,0},{12,4},{1,9},{5,13},{9,1},{13,5},{2,10},{6,14},... | collective-permute-start | bytes 491528 | tf_op jit(solution)/shard_map/ppermute | solution.py:322
  56.2 11.1 %collective-permute-start.17 = (bf16[320,256]{1,0:T(8,128)(2,1)S(1)}, bf16[320,256]{1,0:T(8,128)(2,1)S(1)}, u32[]{:S(2)}, u32[]{:S(2)}) collective-permute-start(bf16[320,256]{1,0:T(8,128)(2,1)S(1)} %shard_map.108.refs_3_), channel_id=1, source_target_pairs={{0,4},{4,0},{8,12},{12,8},{1,5},{5,1},{9,13},{13,9},{2,6},{6,2},{1... | collective-permute-start | bytes 491528 | tf_op jit(solution)/shard_map/ppermute | solution.py:323
  58.3 9.1 %collective-permute-start.16 = (bf16[320,256]{1,0:T(8,128)(2,1)S(1)}, bf16[320,256]{1,0:T(8,128)(2,1)S(1)}, u32[]{:S(2)}, u32[]{:S(2)}) collective-permute-start(bf16[320,256]{1,0:T(8,128)(2,1)S(1)} %shard_map.108.refs_3_), channel_id=1, source_target_pairs={{0,8},{4,12},{8,0},{12,4},{1,9},{5,13},{9,1},{13,5},{2,10},{6,14},... | collective-permute-start | bytes 491528 | tf_op jit(solution)/shard_map/ppermute | solution.py:322
  60.3 10.6 %collective-permute-start.21 = (bf16[320,256]{1,0:T(8,128)(2,1)S(1)}, bf16[320,256]{1,0:T(8,128)(2,1)S(1)}, u32[]{:S(2)}, u32[]{:S(2)}) collective-permute-start(bf16[320,256]{1,0:T(8,128)(2,1)S(1)} %collective-permute-done.18.refs_2_), channel_id=1, source_target_pairs={{0,4},{4,0},{8,12},{12,8},{1,5},{5,1},{9,13},{13,9},{2,6},{6,2},{1... | collective-permute-start | bytes 491528 | tf_op jit(solution)/shard_map/ppermute | solution.py:325
  67.3 5.9 %collective-permute-start.20 = (bf16[320,256]{1,0:T(8,128)(2,1)S(1)}, bf16[320,256]{1,0:T(8,128)(2,1)S(1)}, u32[]{:S(2)}, u32[]{:S(2)}) collective-permute-start(bf16[320,256]{1,0:T(8,128)(2,1)S(1)} %collective-permute-done.16.refs_2_), channel_id=1, source_target_pairs={{0,4},{4,0},{8,12},{12,8},{1,5},{5,1},{9,13},{13,9},{2,6},{6,2},{1... | collective-permute-start | bytes 491528 | tf_op jit(solution)/shard_map/ppermute | solution.py:325
  74.1 1.6 %collective-permute-start.23 = (bf16[80,1792]{1,0:T(8,128)(2,1)S(1)}, bf16[80,1792]{1,0:T(8,128)(2,1)S(1)}, u32[]{:S(2)}, u32[]{:S(2)}) collective-permute-start(bf16[80,1792]{1,0:T(8,128)(2,1)S(1)} %shard_map.111.refs_3_), channel_id=1, source_target_pairs={{0,1},{1,0},{2,3},{3,2},{4,5},{5,4},{6,7},{7,6},{8,9},{9,8},{10,11... | collective-permute-start | bytes 860168 | tf_op jit(solution)/shard_map/ppermute | solution.py:561
  75.1 1.8 %collective-permute-start.22 = (bf16[80,1792]{1,0:T(8,128)(2,1)S(1)}, bf16[80,1792]{1,0:T(8,128)(2,1)S(1)}, u32[]{:S(2)}, u32[]{:S(2)}) collective-permute-start(bf16[80,1792]{1,0:T(8,128)(2,1)S(1)} %get-tuple-element.106), channel_id=1, source_target_pairs={{0,1},{1,0},{2,3},{3,2},{4,5},{5,4},{6,7},{7,6},{8,9},{9,8},{10,11... | collective-permute-start | bytes 860168 | tf_op jit(solution)/shard_map/ppermute | solution.py:563
  75.8 8.9 %collective-permute-start.24 = (bf16[80,1792]{1,0:T(8,128)(2,1)S(1)}, bf16[80,1792]{1,0:T(8,128)(2,1)S(1)}, u32[]{:S(2)}, u32[]{:S(2)}) collective-permute-start(bf16[80,1792]{1,0:T(8,128)(2,1)S(1)} %add_convert_fusion.2), channel_id=1, source_target_pairs={{0,2},{1,3},{2,0},{3,1},{4,6},{5,7},{6,4},{7,5},{8,10},{9,11},{10,... | collective-permute-start | bytes 860168 | tf_op jit(solution)/shard_map/ppermute | solution.py:562
